TPU v7x, 32 devices: a whole 2x2x4 slice. The times are simulated.
32 devices in a mesh: dp: 4 (over y, x), row: 2 (over core), col: 4 (over z).
Axes of the slice: x: 2, y: 2, z: 4, core: 2. Of those that a mesh axis runs over, the one named last changes fastest.
Arguments:
- tokens: bfloat16 [4, 2048, 1600], P('dp', 'row', 'col'), may hold values from -6 to 6
- cotangent: bfloat16 [4, 2048, 1600], P('dp', 'row', 'col'), may hold values from -6 to 6
- w_qkv: bfloat16 [3, 1600, 1600], P(None, 'row', 'col'), may hold values from -0.15625 to 0.15625
- q_bias: float32 [1600], P('col'), may hold values from -3 to 3
- v_bias: float32 [1600], P('col'), may hold values from -0.18 to 0.18
- w_out: bfloat16 [1600, 1600], P('row', 'col'), may hold values from -3 to 3
- out_bias: float32 [1600], P('col'), may hold values from -2 to 2
- w_up: bfloat16 [1600, 6400], P('row', 'col'), may hold values from -0.15625 to 0.15625
- up_bias: float32 [6400], P('col'), may hold values from -3 to 3
- w_down: bfloat16 [6400, 1600], P('row', 'col'), may hold values from -0.078125 to 0.078125
- down_bias: float32 [1600], P('col'), may hold values from -2 to 2
- ln1_gain: float32 [1600], P('col'), may hold values from 0.5 to 1.5
- ln1_bias: float32 [1600], P('col'), may hold values from -1.2 to 1.2
- ln2_gain: float32 [1600], P('col'), may hold values from 0.5 to 1.5
- ln2_bias: float32 [1600], P('col'), may hold values from -1.2 to 1.2
- key_start: int32 [25, 4], replicated, may hold values from 0 to 3, as said below
Outputs:
- outputs: bfloat16 [4, 2048, 1600], P('dp', 'row', 'col')
- input_grad: bfloat16 [4, 2048, 1600], P('dp', 'row', 'col')
- w_qkv_grad: float32 [3, 1600, 1600], P(None, 'row', 'col')
- q_bias_grad: float32 [1600], P('col')
- v_bias_grad: float32 [1600], P('col')
- w_out_grad: float32 [1600, 1600], P('row', 'col')
- out_bias_grad: float32 [1600], P('col')
- w_up_grad: float32 [1600, 6400], P('row', 'col')
- up_bias_grad: float32 [6400], P('col')
- w_down_grad: float32 [6400, 1600], P('row', 'col')
- down_bias_grad: float32 [1600], P('col')
- ln1_gain_grad: float32 [1600], P('col')
- ln1_bias_grad: float32 [1600], P('col')
- ln2_gain_grad: float32 [1600], P('col')
- ln2_bias_grad: float32 [1600], P('col')
Inputs may be any that keep to these rules, and one draw needn't show every extreme that they name: key_start[h, b] <= b for every head h and query block b; in every draw one head has 0 for every query block and another has b for every query block b.
All inputs are finite; a program needn't handle non-finite values.
Results may differ from a plain program's by a relative error of at most 0.034.
Values may be sent and summed in bfloat16 or wider, within the bound.
No kernel may reach another device: no remote copies, remote signals or barrier semaphores. Data moves between devices by JAX's collectives and lax.ppermute only.
A program may use at most 320 MiB of HBM per device.

v0:
```python
import functools

import jax
import jax.numpy as jnp
from jax import lax
from jax.experimental import pallas as pl
from jax.experimental.pallas import tpu as pltpu
from jax.sharding import PartitionSpec as P

BLK = 512
EPSILON = 1e-05
LOG2E = 1.4426950408889634
BF16 = jnp.bfloat16
F32 = jnp.float32

NT=(((0,),(0,)),((),()))
TN=(((1,),(1,)),((),()))

def plan_tiles(meta, ks, own, load, n_slots, n_blocks, n_row, n_heads):
    for i in range(n_row): load[i]=0
    def level(lv,_):
        cost=n_blocks-lv
        def tile(t,_):
            slot=t//n_blocks; qb=t%n_blocks
            head=meta[0]+slot
            here=head<n_heads
            hd=jnp.minimum(head,n_heads-1)
            n=qb+1-ks[hd,qb]
            mask=jnp.where(slot==0,meta[2],jnp.where(slot==n_slots-1,meta[3],(1<<n_blocks)-1))
            here=jnp.logical_and(here,((mask>>qb)&1)==1)
            @pl.when(cost==n_blocks)
            def _(): own[t]=-1
            @pl.when(jnp.logical_and(here,n==cost))
            def _():
                best=load[0]; who=jnp.int32(0)
                for i in range(1,n_row):
                    less=load[i]<best
                    best=jnp.where(less,load[i],best); who=jnp.where(less,i,who)
                own[t]=who
                load[who]=best+cost
            return 0
        lax.fori_loop(0,n_slots*n_blocks,tile,0)
        return 0
    lax.fori_loop(0,n_blocks,level,0)

def fetch(pieces, whole, sems, row, n_row, width):
    copies=[]
    for i,p in enumerate(pieces):
        at=lax.rem(row+i,n_row)*width
        c=pltpu.make_async_copy(p, whole.at[...,pl.ds(pl.multiple_of(at,width),width)], sems.at[i])
        c.start(); copies.append(c)
    return copies

def fwd_kernel(n_row,n_slots,hd,n_heads,meta,ks,*refs):
    pieces=refs[:n_row]; o_ref,lse_ref,whole,own,load,sems=refs[n_row:]
    S=whole.shape[2]; nb=S//BLK; width=S//n_row
    row=meta[1]
    copies=fetch(pieces,whole,sems,row,n_row,width)
    plan_tiles(meta,ks,own,load,n_slots,nb,n_row,n_heads)
    o_ref[...]=jnp.zeros_like(o_ref)
    for c in copies: c.wait()
    c2=hd**-0.5*LOG2E
    diag=lax.broadcasted_iota(jnp.int32,(BLK,BLK),0)<=lax.broadcasted_iota(jnp.int32,(BLK,BLK),1)
    def tile(t,_):
        @pl.when(own[t]==row)
        def _():
            slot=t//nb; qb=t%nb
            first=ks[meta[0]+slot,qb]
            hs=pl.ds(pl.multiple_of(slot*hd,hd),hd)
            qs=pl.ds(pl.multiple_of(qb*BLK,BLK),BLK)
            q=whole[0,hs,qs]
            def scores(kb_ds):
                return lax.dot_general(whole[1,hs,kb_ds],q,NT,preferred_element_type=jnp.float32)
            s=jnp.where(diag,scores(qs),-1e30)
            m=jnp.max(s,axis=0,keepdims=True)
            p=jnp.exp2((s-m)*c2)
            l=jnp.sum(p,axis=0,keepdims=True)
            acc=jnp.dot(whole[2,hs,qs],p.astype(jnp.bfloat16),preferred_element_type=jnp.float32)
            def step(kb,carry):
                m,l,acc=carry
                kd=pl.ds(pl.multiple_of(kb*BLK,BLK),BLK)
                s=scores(kd)
                mn=jnp.maximum(m,jnp.max(s,axis=0,keepdims=True))
                a=jnp.exp2((m-mn)*c2)
                p=jnp.exp2((s-mn)*c2)
                l=l*a+jnp.sum(p,axis=0,keepdims=True)
                acc=acc*a+jnp.dot(whole[2,hs,kd],p.astype(jnp.bfloat16),preferred_element_type=jnp.float32)
                return mn,l,acc
            m,l,acc=lax.fori_loop(first,qb,step,(m,l,acc))
            o_ref[hs,qs]=(acc/l).astype(jnp.bfloat16)
            lse_ref[pl.ds(slot,1),qs]=m*c2+jnp.log2(l)
        return 0
    lax.fori_loop(0,n_slots*nb,tile,0)

def bwd_kernel(n_row,n_slots,hd,n_heads,meta,ks,*refs):
    pieces=refs[:n_row]; das=refs[n_row:2*n_row]
    o_ref,lse_ref,d_ref,whole,da,acc,own,load,sems,sems2=refs[2*n_row:]
    S=whole.shape[2]; nb=S//BLK; width=S//n_row
    row=meta[1]
    copies=fetch(pieces,whole,sems,row,n_row,width)+fetch(das,da,sems2,row,n_row,width)
    plan_tiles(meta,ks,own,load,n_slots,nb,n_row,n_heads)
    d_ref[0]=jnp.zeros_like(d_ref[0])
    acc[...]=jnp.zeros_like(acc)
    for c in copies: c.wait()
    scale=hd**-0.5; c2=scale*LOG2E
    diag=lax.broadcasted_iota(jnp.int32,(BLK,BLK),0)<=lax.broadcasted_iota(jnp.int32,(BLK,BLK),1)
    def tile(t,_):
        @pl.when(own[t]==row)
        def _():
            slot=t//nb; qb=t%nb
            first=ks[meta[0]+slot,qb]
            hs=pl.ds(pl.multiple_of(slot*hd,hd),hd)
            qs=pl.ds(pl.multiple_of(qb*BLK,BLK),BLK)
            q=whole[0,hs,qs]
            up=da[hs,qs]
            lse=lse_ref[pl.ds(slot,1),qs]
            delta=jnp.sum(up.astype(jnp.float32)*o_ref[hs,qs].astype(jnp.float32),axis=0,keepdims=True)
            def block(kd,masked):
                k=whole[1,hs,kd]
                s=lax.dot_general(k,q,NT,preferred_element_type=jnp.float32)
                p=jnp.exp2(s*c2-lse)
                if masked: p=jnp.where(diag,p,0.0)
                dp=lax.dot_general(whole[2,hs,kd],up,NT,preferred_element_type=jnp.float32)
                ds=(p*(dp-delta)).astype(jnp.bfloat16)
                acc[1,hs,kd]+=lax.dot_general(up,p.astype(jnp.bfloat16),TN,preferred_element_type=jnp.float32)
                acc[0,hs,kd]+=lax.dot_general(q,ds,TN,preferred_element_type=jnp.float32)
                return jnp.dot(k,ds,preferred_element_type=jnp.float32)
            dq=block(qs,True)
            dq=lax.fori_loop(first,qb,lambda kb,dq:dq+block(pl.ds(pl.multiple_of(kb*BLK,BLK),BLK),False),dq)
            d_ref[0,hs,qs]=(dq*scale).astype(jnp.bfloat16)
        return 0
    lax.fori_loop(0,n_slots*nb,tile,0)
    d_ref[1]=(acc[0]*scale).astype(jnp.bfloat16)
    d_ref[2]=acc[1].astype(jnp.bfloat16)

V=pl.BlockSpec(memory_space=pltpu.VMEM); SM=pl.BlockSpec(memory_space=pltpu.SMEM); ANY=pl.BlockSpec(memory_space=pl.ANY)
def attn_fwd(meta,ks,pieces,n_slots,hd):
    n_row=len(pieces); _,H,T=pieces[0].shape; S=T*n_row; nb=S//BLK
    return pl.pallas_call(functools.partial(fwd_kernel,n_row,n_slots,hd,ks.shape[0]),
      out_shape=(jax.ShapeDtypeStruct((H,S),jnp.bfloat16),jax.ShapeDtypeStruct((n_slots,S),jnp.float32)),
      in_specs=[SM,SM]+[ANY]*n_row,out_specs=(V,V),
      scratch_shapes=[pltpu.VMEM((3,H,S),jnp.bfloat16),pltpu.SMEM((n_slots*nb,),jnp.int32),pltpu.SMEM((n_row,),jnp.int32),pltpu.SemaphoreType.DMA((n_row,))],
      compiler_params=pltpu.CompilerParams(vmem_limit_bytes=48*2**20),
      cost_estimate=pl.CostEstimate(flops=4*3*S*S//2*H//2,bytes_accessed=10**7,transcendentals=S*S),
    )(meta,ks,*pieces)
def attn_bwd(meta,ks,pieces,das,o,lse,n_slots,hd):
    n_row=len(pieces); _,H,T=pieces[0].shape; S=T*n_row; nb=S//BLK
    return pl.pallas_call(functools.partial(bwd_kernel,n_row,n_slots,hd,ks.shape[0]),
      out_shape=jax.ShapeDtypeStruct((3,H,S),jnp.bfloat16),
      in_specs=[SM,SM]+[ANY]*(2*n_row)+[V,V],out_specs=V,
      scratch_shapes=[pltpu.VMEM((3,H,S),jnp.bfloat16),pltpu.VMEM((H,S),jnp.bfloat16),pltpu.VMEM((2,H,S),jnp.float32),pltpu.SMEM((n_slots*nb,),jnp.int32),pltpu.SMEM((n_row,),jnp.int32),pltpu.SemaphoreType.DMA((n_row,)),pltpu.SemaphoreType.DMA((n_row,))],
      compiler_params=pltpu.CompilerParams(vmem_limit_bytes=56*2**20),
      cost_estimate=pl.CostEstimate(flops=10*3*S*S//2*H//2,bytes_accessed=10**7,transcendentals=S*S),
    )(meta,ks,*pieces,*das,o,lse)


def dot(a, b):
    return jnp.dot(a, b, preferred_element_type=F32)


def dot_nt(a, b):
    return lax.dot_general(a, b, TN, preferred_element_type=F32)


def dot_tn(a, b):
    return lax.dot_general(a, b, NT, preferred_element_type=F32)


def turn(value, axis, steps):
    size = lax.axis_size(axis)
    if steps % size == 0:
        return value
    return lax.ppermute(value, axis, [(i, (i + steps) % size) for i in range(size)])


def block(value, index, size, axis):
    return lax.dynamic_slice_in_dim(value, index * size, size, axis)


def place(whole, part, index, axis):
    return lax.dynamic_update_slice_in_dim(whole, part, index * part.shape[axis], axis)


def row_gather(value, axis):
    size = lax.axis_size("row")
    if size != 2:
        return lax.all_gather(value, "row", axis=axis, tiled=True)
    other = turn(value, "row", 1)
    low = lax.axis_index("row") == 0
    return jnp.concatenate([jnp.where(low, value, other), jnp.where(low, other, value)], axis)


def row_sum(value, axis):
    size = lax.axis_size("row")
    part = value.shape[axis] // size
    row = lax.axis_index("row")
    total = block(value, row, part, axis).astype(F32)
    for step in range(1, size):
        sent = block(value, (row + step) % size, part, axis).astype(BF16)
        total = total + turn(sent, "row", step).astype(F32)
    return total


def col_sum(value, axis):
    size = lax.axis_size("col")
    part = value.shape[axis] // size
    col = lax.axis_index("col")
    total = block(value, col, part, axis).astype(F32)
    for step in range(1, size):
        sent = block(value, (col + step) % size, part, axis).astype(BF16)
        total = total + turn(sent, "col", step).astype(F32)
    return total


def col_swap(value, split, join):
    size = lax.axis_size("col")
    part = value.shape[split] // size
    col = lax.axis_index("col")
    shape = list(value.shape)
    shape[split] = part
    shape[join] *= size
    whole = jnp.zeros(shape, value.dtype)
    for step in range(size):
        sent = block(value, (col + step) % size, part, split)
        whole = place(whole, turn(sent, "col", step), (col - step) % size, join)
    return whole


def swap_with(value, bit):
    return lax.ppermute(value, "dp", [(i, i ^ bit) for i in range(4)])


def pick(value, index, axis):
    return lax.dynamic_index_in_dim(value, index, axis, keepdims=False)


def dp_sum(value, first):
    if lax.axis_size("dp") != 4:
        return lax.psum(value.astype(BF16), "dp").astype(F32)
    shape = value.shape
    me = lax.axis_index("dp")
    bits = (me % 2, me // 2)
    second = 1 - first
    halves = value.astype(BF16).reshape(2, 2, -1, shape[-1])
    mine, theirs = pick(halves, bits[first], 0), pick(halves, 1 - bits[first], 0)
    half = mine.astype(F32) + swap_with(theirs, 1 << first).astype(F32)
    mine, theirs = pick(half, bits[second], 0), pick(half, 1 - bits[second], 0)
    quarter = mine + swap_with(theirs.astype(BF16), 1 << second).astype(F32)
    quarter = quarter.astype(BF16)
    other = swap_with(quarter, 1 << second)
    low = bits[second] == 0
    half = jnp.stack([jnp.where(low, quarter, other), jnp.where(low, other, quarter)])
    other = swap_with(half, 1 << first)
    low = bits[first] == 0
    whole = jnp.stack([jnp.where(low, half, other), jnp.where(low, other, half)])
    return whole.reshape(shape).astype(F32)


def small_sum(value, axes):
    return lax.psum(value, axes)


class Heads:
    def __init__(self, n_col, width, heads, blocks):
        self.size = n_col * width // heads
        self.firsts = [width * c // self.size for c in range(n_col)]
        lasts = [-(-width * (c + 1) // self.size) for c in range(n_col)]
        self.slots = max(b - a for a, b in zip(self.firsts, lasts))
        self.window = self.slots * self.size
        self.before = [width * c - f * self.size for c, f in enumerate(self.firsts)]
        self.after = [self.window - width - b for b in self.before]
        self.edge = max(self.before + self.after)
        full = (1 << blocks) - 1
        shares = {0: 0, 1: 2, 2: 9, 3: 13, 4: 15}

        def left_share(column):
            part = column % self.size
            return shares[round(4 * part / self.size)] if blocks == 4 else 0

        self.first_mask = [full & ~left_share(b) for b in self.before]
        self.last_mask = []
        for c, f in enumerate(self.firsts):
            end = width * (c + 1)
            begin = (f + self.slots - 1) * self.size
            if begin >= end:
                self.last_mask.append(0)
            elif begin + self.size <= end:
                self.last_mask.append(full)
            else:
                self.last_mask.append(left_share(end - begin))


def widen(value, axis, heads, col):
    size = lax.axis_size("col")
    edge, width = heads.edge, value.shape[axis]
    up = [(i, i + 1) for i in range(size - 1)]
    down = [(i + 1, i) for i in range(size - 1)]
    left = lax.ppermute(lax.slice_in_dim(value, width - edge, width, axis=axis), "col", up)
    right = lax.ppermute(lax.slice_in_dim(value, 0, edge, axis=axis), "col", down)
    wide = jnp.concatenate([left, value, right], axis)
    before = jnp.array(heads.before, jnp.int32)[col]
    return lax.dynamic_slice_in_dim(wide, edge - before, heads.window, axis)


def narrow(value, axis, heads, col, width):
    size = lax.axis_size("col")
    edge = heads.edge
    up = [(i, i + 1) for i in range(size - 1)]
    down = [(i + 1, i) for i in range(size - 1)]
    before = jnp.array(heads.before, jnp.int32)[col]
    shape = list(value.shape)
    shape[axis] = width + 2 * edge
    wide = lax.dynamic_update_slice_in_dim(
        jnp.zeros(shape, value.dtype), value, edge - before, axis
    )
    to_left = lax.slice_in_dim(wide, 0, edge, axis=axis)
    to_right = lax.slice_in_dim(wide, edge + width, width + 2 * edge, axis=axis)
    tail = lax.ppermute(to_left, "col", down)
    front = lax.ppermute(to_right, "col", up)
    pads = [(0, 0)] * value.ndim
    pads[axis] = (0, width - edge)
    own = lax.slice_in_dim(wide, edge, edge + width, axis=axis).astype(F32)
    own = own + jnp.pad(front, pads).astype(F32)
    pads[axis] = (width - edge, 0)
    return own + jnp.pad(tail, pads).astype(F32)


def moments(values):
    mean = jnp.mean(values, axis=0, keepdims=True)
    centred = values - mean
    variance = jnp.mean(centred * centred, axis=0, keepdims=True)
    return mean, lax.rsqrt(variance + EPSILON)


def gelu_parts(u):
    inner = 0.7978845608 * (u + 0.044715 * u * u * u)
    t = jnp.tanh(inner)
    value = 0.5 * u * (1.0 + t)
    slope = 0.5 * (1.0 + t) + 0.5 * u * (1.0 - t * t) * 0.7978845608 * (1.0 + 0.134145 * u * u)
    return value, slope


def body(
    tokens,
    cotangent,
    w_qkv,
    q_bias,
    v_bias,
    w_out,
    out_bias,
    w_up,
    up_bias,
    w_down,
    down_bias,
    ln1_gain,
    ln1_bias,
    ln2_gain,
    ln2_bias,
    key_start,
):
    n_row, n_col = lax.axis_size("row"), lax.axis_size("col")
    row, col = lax.axis_index("row"), lax.axis_index("col")
    seqs, rows, width = tokens.shape
    length = seqs * rows
    depth = width * n_col
    part = length // n_col
    in_rows = w_up.shape[0]
    ff = w_up.shape[1]
    ff_rows = w_down.shape[0]
    ff_part = ff_rows // n_col
    heads = Heads(n_col, width, key_start.shape[0], rows * n_row // BLK)
    size, window = heads.size, heads.window
    firsts = jnp.array(heads.firsts, jnp.int32) * size
    begin = firsts[col]

    x = tokens.reshape(length, width).T
    g = cotangent.reshape(length, width).T

    x_all = lax.all_gather(x, "col", axis=0, tiled=True)
    params = jnp.stack([ln1_gain, ln1_bias, ln2_gain, ln2_bias, out_bias, q_bias, v_bias])
    params = lax.all_gather(params, "col", axis=1, tiled=True)
    gain1, shift1, gain2, shift2, bias_out, bias_q, bias_v = [p[:, None] for p in params]

    w3 = row_gather(widen(w_qkv.transpose(0, 2, 1), 1, heads, col), 2)
    w3 = w3.reshape(3 * window, depth)
    up_all = row_gather(w_up, 0)
    out_all = lax.all_gather(w_out.T, "col", axis=0, tiled=True)
    out_all = row_gather(out_all, 1)
    down_own = w_down.T
    down_part = jnp.zeros((depth, ff_part), BF16)
    for step in range(n_col):
        pairs = []
        for r in range(n_row):
            for c in range(n_col):
                at = r * n_col + (step + c) % n_col
                pairs.append((r * n_col + c, (at % n_row) * n_col + at // n_row))
        sent = block(down_own, (step + col) % n_col, ff_part, 1)
        got = lax.ppermute(sent, ("row", "col"), pairs)
        at = col * n_row + row
        down_part = place(down_part, got, (at % n_col - step) % n_col, 0)
    down_all = row_gather(down_part, 1)

    g_source, unused = lax.optimization_barrier((g, x_all))
    g_all = lax.all_gather(g_source, "col", axis=0, tiled=True)

    x_float = x_all.astype(F32)
    mean1, rstd1 = moments(x_float)
    n1 = ((x_float - mean1) * rstd1 * gain1 + shift1).astype(BF16)
    bias3 = jnp.concatenate(
        [
            lax.dynamic_slice_in_dim(bias_q, begin, window, 0),
            jnp.zeros((window, 1), F32),
            lax.dynamic_slice_in_dim(bias_v, begin, window, 0),
        ]
    )
    qkv = (dot(w3, n1) + bias3).astype(BF16)
    triple = qkv.reshape(3, window, length)
    pieces = [turn(triple, "row", -step) for step in range(n_row)]
    meta = jnp.stack(
        [
            jnp.array(heads.firsts, jnp.int32)[col],
            row,
            jnp.array(heads.first_mask, jnp.int32)[col],
            jnp.array(heads.last_mask, jnp.int32)[col],
        ]
    )
    mixed, norms = attn_fwd(meta, key_start, pieces, heads.slots, size)
    mixed_own = row_sum(mixed, 1).astype(BF16)

    attention = jnp.zeros((depth, part), BF16)
    for step in range(n_col):
        sent = block(mixed_own, (col + step) % n_col, part, 1)
        got = turn(sent, "col", step)
        at = firsts[(col - step) % n_col]
        held = lax.dynamic_slice_in_dim(attention, at, window, 0)
        attention = lax.dynamic_update_slice_in_dim(attention, held + got, at, 0)
    resid = block(x_all, col, part, 1).astype(F32) + (dot(out_all, attention) + bias_out)
    mean2, rstd2 = moments(resid)
    hat2 = (resid - mean2) * rstd2
    n2_own = (hat2 * gain2 + shift2).astype(BF16)

    n2s, gs, hiddens, dus, parts2 = [], [], [], [], []
    summed = jnp.zeros((depth, length), BF16)
    for step in range(n_col):
        at = (col - step) % n_col
        n2 = turn(n2_own, "col", step)
        g_here = block(g_all, at, part, 1)
        u = dot_tn(up_all, n2) + up_bias[:, None]
        value, slope = gelu_parts(u)
        hidden = value.astype(BF16)
        shrunk = dot(down_all, hidden)
        if step == 0:
            shrunk = shrunk + resid
        summed = place(summed, shrunk.astype(BF16), at, 1)
        du = (dot_tn(down_all, g_here) * slope).astype(BF16)
        parts2.append(turn(dot(up_all, du).astype(BF16), "col", -step).astype(F32))
        n2s.append(n2)
        gs.append(g_here)
        hiddens.append(hidden)
        dus.append(du)
    outputs = col_sum(summed, 0) + down_bias[:, None]
    outputs = outputs.astype(BF16)

    dn2 = sum(parts2)
    up2 = dn2 * gain2
    pull2 = jnp.mean(up2, axis=0, keepdims=True)
    lean2 = jnp.mean(up2 * hat2, axis=0, keepdims=True)
    dr = gs[0].astype(F32) + rstd2 * (up2 - pull2 - hat2 * lean2)
    db = dr.astype(BF16)
    da = dot_tn(out_all, db).astype(BF16)
    da_own = jnp.zeros((window, length), BF16)
    for step in range(n_col):
        to = firsts[(col + step) % n_col]
        got = turn(lax.dynamic_slice_in_dim(da, to, window, 0), "col", step)
        da_own = place(da_own, got, (col - step) % n_col, 1)
    da_pieces = [turn(da_own, "row", -step) for step in range(n_row)]
    dqkv = attn_bwd(meta, key_start, pieces, da_pieces, mixed, norms, heads.slots, size)
    dqkv = row_sum(dqkv, 2).astype(BF16).reshape(3 * window, length)

    dn1_part = dot_tn(w3, dqkv).astype(BF16)
    dqkv_float = dqkv.astype(F32)
    weighed = dot(w3, gain1.astype(F32))
    plain = qkv.astype(F32) - (bias3 + dot(w3, shift1))
    stats = jnp.stack(
        [jnp.sum(dqkv_float * weighed, axis=0), jnp.sum(dqkv_float * plain, axis=0)]
    )
    stats = sum(turn(stats, "col", step) for step in range(n_col)) / depth
    dn1 = col_sum(dn1_part, 0)
    hat1 = (x.astype(F32) - mean1) * rstd1
    gain1_own = ln1_gain[:, None]
    dx = rstd1 * (dn1 * gain1_own - stats[0:1] - hat1 * stats[1:2])
    input_grad = (col_swap(db, 0, 1).astype(F32) + dx).astype(BF16)

    n2_all = jnp.concatenate(n2s, 1)
    g_turned = jnp.concatenate(gs, 1)
    hidden_all = jnp.concatenate(hiddens, 1)
    du_all = jnp.concatenate(dus, 1)
    up_grad = dp_sum(row_sum(dot_nt(n2_all, du_all).astype(BF16), 0), 0)
    down_grad = row_sum(dot_nt(g_turned, hidden_all).astype(BF16), 1).astype(BF16)
    down_home = jnp.zeros((width, ff_rows), BF16)
    for step in range(n_col):
        pairs = []
        for r in range(n_row):
            for c in range(n_col):
                at = r * n_col + (step + c) % n_col
                pairs.append(((at % n_row) * n_col + at // n_row, r * n_col + c))
        at = col * n_row + row
        sent = block(down_grad, (at % n_col - step) % n_col, width, 0)
        got = lax.ppermute(sent, ("row", "col"), pairs)
        down_home = place(down_home, got, (step + col) % n_col, 1)
    down_grad = dp_sum(down_home, 1)
    out_grad = dp_sum(col_sum(row_sum(dot_nt(db, attention).astype(BF16), 1).astype(BF16), 0), 0)
    qkv_grad = row_sum(dot_nt(dqkv, n1).astype(BF16).reshape(3, window, depth), 2)
    qkv_grad = dp_sum(narrow(qkv_grad.astype(BF16), 1, heads, col, width), 1)

    spread = jnp.zeros((2, depth), F32)
    dq_dv = jnp.sum(dqkv_float.reshape(3, window, length), axis=2)
    spread = lax.dynamic_update_slice_in_dim(spread, dq_dv[::2], begin, 1)
    everywhere = jnp.stack(
        [
            jnp.sum(db.astype(F32), axis=1),
            jnp.sum(dn2 * hat2, axis=1),
            jnp.sum(dn2, axis=1),
        ]
    )
    early = small_sum(jnp.concatenate([spread, everywhere]), ("dp", "row", "col"))
    early = lax.dynamic_slice_in_dim(early, col * width, width, 1)
    up_bias_grad = small_sum(jnp.sum(du_all.astype(F32), axis=1), ("dp", "row"))
    late = jnp.stack(
        [jnp.sum(g.astype(F32), axis=1), jnp.sum(dn1 * hat1, axis=1), jnp.sum(dn1, axis=1)]
    )
    late = small_sum(late, ("dp", "row"))
    return (
        outputs.T.reshape(tokens.shape),
        input_grad.T.reshape(tokens.shape),
        qkv_grad.transpose(0, 2, 1),
        early[0],
        early[1],
        out_grad.T,
        early[2],
        up_grad,
        up_bias_grad,
        down_grad.T,
        late[0],
        late[1],
        late[2],
        early[3],
        early[4],
    )


def solution(mesh):
    inputs = (
        P("dp", "row", "col"),
        P("dp", "row", "col"),
        P(None, "row", "col"),
        P("col"),
        P("col"),
        P("row", "col"),
        P("col"),
        P("row", "col"),
        P("col"),
        P("row", "col"),
        P("col"),
        P("col"),
        P("col"),
        P("col"),
        P("col"),
        P(),
    )
    return jax.shard_map(
        body, mesh=mesh, in_specs=inputs, out_specs=inputs[:15], check_vma=False
    )
```

profile of v0, /device:TPU:0, one launch (start us, length us, event | category | flops | bytes accessed | tf_op | source)
XLA Modules:
  0.0 1123.1 jit_solution(8432170276039910350)
XLA Ops:
  19.5 5.2 collective-permute-done.8
  27.7 14.7 %all-gather = f32[4,400,7]{1,2,0:T(8,128)S(1)} all-gather(f32[1,400,7]{1,2,0:T(8,128)S(1)} %bitcast.213), channel_id=1, replica_groups=mesh['dp'=4,'row'=2,'col'=4] {'col'}, dimensions={0}, use_global_device_ids=true | all-gather | bytes 56000 | tf_op jit(solution)/shard_map/all_gather | solution.py:381
  49.2 29.9 %all-gather.5.cloned.1.call-done = bf16[1600,1024]{1,0:T(8,128)(2,1)} async-done(((bf16[400,1024]{1,0:T(8,128)(2,1)}), bf16[1600,1024]{1,0:T(8,128)(2,1)}) %all-gather.5.cloned.1.call-update) | async-done | bytes 3276816 | tf_op jit(solution)/shard_map/all_gather | solution.py:379
  84.6 7.4 add_convert_fusion.2
  92.2 5.6 dynamic-slice_bitcast_fusion.3
  108.5 47.3 %collective-permute-start.3 = (bf16[400,800]{1,0:T(8,128)(2,1)}, bf16[400,800]{1,0:T(8,128)(2,1)}, u32[]{:S(2)}, u32[]{:S(2)}) collective-permute-start(bf16[400,800]{1,0:T(8,128)(2,1)} %get-tuple-element.71), channel_id=1, source_target_pairs={{0,5},{1,0},{2,4},{3,1},{4,7},{5,2},{6,6},{7,3},{8,13},{9,8},{10,1... | collective-permute-start | bytes 1920008 | tf_op jit(solution)/shard_map/ppermute | solution.py:398
  159.9 9.0 dynamic_update_slice.78
  171.2 9.4 dynamic_update_slice.79
  180.6 11.2 %collective-permute-done.2 = bf16[400,800]{1,0:T(8,128)(2,1)S(1)} collective-permute-done((bf16[400,800]{1,0:T(8,128)(2,1)}, bf16[400,800]{1,0:T(8,128)(2,1)S(1)}, u32[]{:S(2)}, u32[]{:S(2)}) %collective-permute-start.2) | collective-permute-done | bytes 640032 | tf_op jit(solution)/shard_map/ppermute | solution.py:398
  193.0 10.0 dynamic_update_slice.80
  205.4 10.1 dynamic_update_slice.81
  234.1 20.1 %shard_map.325 = (bf16[448,2048]{1,0:T(8,128)(2,1)S(1)}, f32[7,2048]{1,0:T(8,128)S(1)}) custom-call(s32[4]{0:T(128)S(1)} %pad_add_fusion.meta, s32[25,4]{1,0:T(8,128)S(1)} %copy.167.ks, bf16[3,448,1024]{2,1,0:T(8,128)(2,1)S(1)} %bitcast.187, bf16[3,448,1024]{2,1,0:T(8,128)(2,1)} %collective-permute-done.10.refs_1_), custom_call_target="tpu_custom_call" | custom-call | flops 5637144576 | bytes 10000000 | tf_op jit(solution)/shard_map/pallas_call | solution.py:139
  255.3 5.5 broadcast_select_fusion.1
  276.7 20.7 %collective-permute-done.13 = bf16[448,256]{1,0:T(8,128)(2,1)S(1)} collective-permute-done((bf16[448,256]{1,0:T(8,128)(2,1)S(1)}, bf16[448,256]{1,0:T(8,128)(2,1)S(1)}, u32[]{:S(2)}, u32[]{:S(2)}) %collective-permute-start.13) | collective-permute-done | bytes 229408 | tf_op jit(solution)/shard_map/ppermute | solution.py:173
  301.8 24.6 %collective-permute-start.15 = (bf16[1600,256]{1,0:T(8,128)(2,1)S(1)}, bf16[1600,256]{1,0:T(8,128)(2,1)S(1)}, u32[]{:S(2)}, u32[]{:S(2)}) collective-permute-start(bf16[1600,256]{1,0:T(8,128)(2,1)S(1)} %add_convert_fusion.11), channel_id=1, source_target_pairs={{0,1},{1,2},{2,3},{3,0},{4,5},{5,6},{6,7},{7,4},{8,9},{9,10},{10,1... | collective-permute-start | bytes 2457608 | tf_op jit(solution)/shard_map/ppermute | solution.py:173
  336.3 17.6 %collective-permute-done.15 = bf16[1600,256]{1,0:T(8,128)(2,1)S(1)} collective-permute-done((bf16[1600,256]{1,0:T(8,128)(2,1)S(1)}, bf16[1600,256]{1,0:T(8,128)(2,1)S(1)}, u32[]{:S(2)}, u32[]{:S(2)}) %collective-permute-start.15) | collective-permute-done | bytes 819232 | tf_op jit(solution)/shard_map/ppermute | solution.py:173
  357.3 39.0 %collective-permute-done.16 = bf16[1600,256]{1,0:T(8,128)(2,1)S(1)} collective-permute-done((bf16[1600,256]{1,0:T(8,128)(2,1)S(1)}, bf16[1600,256]{1,0:T(8,128)(2,1)S(1)}, u32[]{:S(2)}, u32[]{:S(2)}) %collective-permute-start.16) | collective-permute-done | bytes 819232 | tf_op jit(solution)/shard_map/ppermute | solution.py:173
  412.0 17.6 %collective-permute-start.20 = (bf16[400,1024]{1,0:T(8,128)(2,1)}, bf16[400,1024]{1,0:T(8,128)(2,1)}, u32[]{:S(2)}, u32[]{:S(2)}) collective-permute-start(bf16[400,1024]{1,0:T(8,128)(2,1)} %get-tuple-element.56), channel_id=1, source_target_pairs={{0,3},{1,0},{2,1},{3,2},{4,7},{5,4},{6,5},{7,6},{8,11},{9,8},{10,9... | collective-permute-start | bytes 2457608 | tf_op jit(solution)/shard_map/ppermute | solution.py:173
  434.4 5.7 fusion.37
  459.2 8.5 convolution_convert_fusion
  467.7 6.3 fusion.34
  474.0 8.8 convolution_convert_fusion.1
  482.8 6.3 convolution_convert_fusion.6
  497.1 38.4 %collective-permute-done.19 = bf16[400,1024]{1,0:T(8,128)(2,1)} collective-permute-done((bf16[400,1024]{1,0:T(8,128)(2,1)}, bf16[400,1024]{1,0:T(8,128)(2,1)}, u32[]{:S(2)}, u32[]{:S(2)}) %collective-permute-start.19) | collective-permute-done | bytes 819232 | tf_op jit(solution)/shard_map/ppermute | solution.py:173
  539.3 13.8 %collective-permute-done.22 = bf16[1600,256]{1,0:T(8,128)(2,1)} collective-permute-done((bf16[1600,256]{1,0:T(8,128)(2,1)}, bf16[1600,256]{1,0:T(8,128)(2,1)}, u32[]{:S(2)}, u32[]{:S(2)}) %collective-permute-start.22) | collective-permute-done | bytes 819232 | tf_op jit(solution)/shard_map/ppermute | solution.py:173
  562.2 17.9 %collective-permute-start.27 = (bf16[448,256]{1,0:T(8,128)(2,1)S(1)}, bf16[448,256]{1,0:T(8,128)(2,1)}, u32[]{:S(2)}, u32[]{:S(2)}) collective-permute-start(bf16[448,256]{1,0:T(8,128)(2,1)S(1)} %get-tuple-element.95), channel_id=1, source_target_pairs={{0,1},{1,2},{2,3},{3,0},{4,5},{5,6},{6,7},{7,4},{8,9},{9,10},{10,1... | collective-permute-start | bytes 688136 | tf_op jit(solution)/shard_map/ppermute | solution.py:173
  609.8 5.5 collective-permute-done.28
  627.1 6.9 collective-permute-start.59
  647.7 31.8 %collective-permute-start.30 = (bf16[448,1024]{1,0:T(8,128)(2,1)}, bf16[448,1024]{1,0:T(8,128)(2,1)}, u32[]{:S(2)}, u32[]{:S(2)}) collective-permute-start(bf16[448,1024]{1,0:T(8,128)(2,1)} %constant_dynamic-update-slice_fusion.refs_2_), channel_id=1, source_target_pairs={{0,4},{4,0},{1,5},{5,1},{2,6},{6,2},{3,7},{7,3},{8,12},{12,8},{9,1... | collective-permute-start | bytes 2752520 | tf_op jit(solution)/shard_map/ppermute | solution.py:173
  681.1 7.0 dynamic_update_slice.100
  689.6 7.7 dynamic_update_slice.101
  697.3 7.4 dynamic_update_slice.102
  704.8 6.8 dynamic_update_slice.103
  726.0 5.2 collective-permute-start.47
  735.8 7.1 collective-permute-done.48
  743.5 48.6 %collective-permute-done.47 = bf16[400,800]{1,0:T(8,128)(2,1)S(1)} collective-permute-done((bf16[400,800]{1,0:T(8,128)(2,1)S(1)}, bf16[400,800]{1,0:T(8,128)(2,1)S(1)}, u32[]{:S(2)}, u32[]{:S(2)}) %collective-permute-start.47) | collective-permute-done | bytes 640032 | tf_op jit(solution)/shard_map/ppermute | solution.py:173
  795.2 28.4 %shard_map.326 = bf16[3,448,2048]{2,1,0:T(8,128)(2,1)} custom-call(s32[4]{0:T(128)} %copy-done.5, s32[25,4]{1,0:T(8,128)} %copy-done.4, bf16[3,448,1024]{2,1,0:T(8,128)(2,1)} %bitcast.188, bf16[3,448,1024]{2,1,0:T(8,128)(2,1)} %collective-permute-done.10.refs_1_, bf16[448,1024]{1,0:T(8,128)(2,1)} %constant_dynamic-update-slice_fusion.refs_2_, ...), custom_call_target="tpu_custom_call" | custom-call | flops 14092861440 | bytes 10000000 | tf_op jit(solution)/shard_map/pallas_call | solution.py:148
  836.5 14.8 %collective-permute-done.51 = bf16[100,800]{1,0:T(8,128)(2,1)S(1)} collective-permute-done((bf16[100,800]{1,0:T(8,128)(2,1)S(1)}, bf16[100,800]{1,0:T(8,128)(2,1)S(1)}, u32[]{:S(2)}, u32[]{:S(2)}) %collective-permute-start.51) | collective-permute-done | bytes 160032 | tf_op jit(solution)/shard_map/ppermute | solution.py:230
  853.7 5.6 bitcast_convert_fusion
  864.8 5.4 convolution_convert_fusion.2
  876.6 40.8 %psum.21 = f32[5,1600]{1,0:T(8,128)} all-reduce(f32[5,1600]{1,0:T(8,128)} %pad_maximum_fusion.19), channel_id=1, replica_groups=mesh['dp'=4,'row'=2,'col'=4] {'dp','row','col'}, use_global_device_ids=true, to_apply=%region_12.13 | all-reduce | flops 8000 | bytes 64000 | tf_op jit(solution)/shard_map/psum | solution.py:260
  942.8 49.9 %collective-permute-done.33 = bf16[400,1024]{1,0:T(8,128)(2,1)} collective-permute-done((bf16[400,1024]{1,0:T(8,128)(2,1)}, bf16[400,1024]{1,0:T(8,128)(2,1)}, u32[]{:S(2)}, u32[]{:S(2)}) %collective-permute-start.33) | collective-permute-done | bytes 819232 | tf_op jit(solution)/shard_map/ppermute | solution.py:173
  1001.0 5.5 collective-permute-start.39
  1006.6 22.9 %all-reduce.2 = (f32[1600]{0:T(1024)}, f32[3,400]{1,0:T(4,128)S(1)}) all-reduce(f32[1600]{0:T(1024)S(1)} %copy-done.58, f32[3,400]{1,0:T(4,128)S(1)} %pad_maximum_fusion.21), channel_id=1, replica_groups=mesh['dp'=4,'row'=2,'col'=4] {'dp','row'}, use_global_device_ids=true, to_apply=%region_14.15 | all-reduce | flops 2800 | bytes 22400 | tf_op jit(solution)/shard_map/psum | solution.py:260
  1040.2 22.0 %collective-permute-done.41 = bf16[2,300,800]{2,0,1:T(2,128)(2,1)S(1)} collective-permute-done((bf16[2,300,800]{2,0,1:T(2,128)(2,1)S(1)}, bf16[2,300,800]{2,0,1:T(2,128)(2,1)S(1)}, u32[]{:S(2)}, u32[]{:S(2)}) %collective-permute-start.41) | collective-permute-done | bytes 960032 | tf_op jit(solution)/shard_map/ppermute | solution.py:230
  1064.5 8.6 collective-permute-done.42
  1078.0 6.0 collective-permute-done.43
  1095.6 13.8 %collective-permute-done.44 = bf16[2,300,800]{2,0,1:T(2,128)(2,1)S(1)} collective-permute-done((bf16[2,300,800]{2,0,1:T(2,128)(2,1)S(1)}, bf16[2,300,800]{2,0,1:T(2,128)(2,1)S(1)}, u32[]{:S(2)}, u32[]{:S(2)}) %collective-permute-start.44) | collective-permute-done | bytes 960032 | tf_op jit(solution)/shard_map/ppermute | solution.py:230
  (472 shorter events, 338.7 us)
Async XLA Ops:
  7.2 71.8 %all-gather.5.cloned.1.call-start = ((), (), s32[]{:S(2)}) async-start(), calls=%async_computation | async-start | bytes 4096000 | tf_op jit(solution)/shard_map/all_gather | solution.py:379
  7.9 220.5 %all-gather.7.cloned.1.call-start = ((), (), s32[]{:S(2)}) async-start(), calls=%async_computation.1 | async-start | bytes 3584000 | tf_op jit(solution)/shard_map/all_gather | solution.py:387
  27.6 402.6 %all-gather.9.cloned.1.call-start = ((), (), s32[]{:S(2)}) async-start(), calls=%async_computation.2 | async-start | bytes 4096000 | tf_op jit(solution)/shard_map/all_gather | solution.py:404
  92.1 141.9 %collective-permute-start.10 = (bf16[3,448,1024]{2,1,0:T(8,128)(2,1)S(1)}, bf16[3,448,1024]{2,1,0:T(8,128)(2,1)}, u32[]{:S(2)}, u32[]{:S(2)}) collective-permute-start(bf16[3,448,1024]{2,1,0:T(8,128)(2,1)S(1)} %bitcast.186), channel_id=1, source_target_pairs={{0,4},{4,0},{1,5},{5,1},{2,6},{6,2},{3,7},{7,3},{8,12},{12,8},{9,1... | collective-permute-start | bytes 8257544 | tf_op jit(solution)/shard_map/ppermute | solution.py:173
  99.3 156.0 %collective-permute-start.5 = (bf16[800,1600]{1,0:T(8,128)(2,1)}, bf16[800,1600]{1,0:T(8,128)(2,1)}, u32[]{:S(2)}, u32[]{:S(2)}) collective-permute-start(bf16[800,1600]{1,0:T(8,128)(2,1)} %param.29), channel_id=1, source_target_pairs={{0,4},{4,0},{1,5},{5,1},{2,6},{6,2},{3,7},{7,3},{8,12},{12,8},{9,1... | collective-permute-start | bytes 7680008 | tf_op jit(solution)/shard_map/ppermute | solution.py:173
  101.5 67.4 %collective-permute-start.1 = (bf16[400,800]{1,0:T(8,128)(2,1)}, bf16[400,800]{1,0:T(8,128)(2,1)}, u32[]{:S(2)}, u32[]{:S(2)}) collective-permute-start(bf16[400,800]{1,0:T(8,128)(2,1)} %get-tuple-element.72), channel_id=1, source_target_pairs={{0,4},{1,1},{2,5},{3,0},{4,6},{5,3},{6,7},{7,2},{8,12},{9,9},{10,1... | collective-permute-start | bytes 1920008 | tf_op jit(solution)/shard_map/ppermute | solution.py:398
  103.4 88.4 %collective-permute-start.2 = (bf16[400,800]{1,0:T(8,128)(2,1)}, bf16[400,800]{1,0:T(8,128)(2,1)S(1)}, u32[]{:S(2)}, u32[]{:S(2)}) collective-permute-start(bf16[400,800]{1,0:T(8,128)(2,1)} %get-tuple-element.74), channel_id=1, source_target_pairs={{0,1},{1,5},{2,0},{3,4},{4,3},{5,7},{6,2},{7,6},{8,9},{9,13},{10,8... | collective-permute-start | bytes 1920008 | tf_op jit(solution)/shard_map/ppermute | solution.py:398
  108.5 94.6 %collective-permute-start.3 = (bf16[400,800]{1,0:T(8,128)(2,1)}, bf16[400,800]{1,0:T(8,128)(2,1)}, u32[]{:S(2)}, u32[]{:S(2)}) collective-permute-start(bf16[400,800]{1,0:T(8,128)(2,1)} %get-tuple-element.71), channel_id=1, source_target_pairs={{0,5},{1,0},{2,4},{3,1},{4,7},{5,2},{6,6},{7,3},{8,13},{9,8},{10,1... | collective-permute-start | bytes 1920008 | tf_op jit(solution)/shard_map/ppermute | solution.py:398
  215.4 45.4 %collective-permute-start.4 = (bf16[1600,800]{0,1:T(8,128)(2,1)}, bf16[1600,800]{0,1:T(8,128)(2,1)}, u32[]{:S(2)}, u32[]{:S(2)}) collective-permute-start(bf16[1600,800]{0,1:T(8,128)(2,1)} %dynamic_update_slice.81), channel_id=1, source_target_pairs={{0,4},{4,0},{1,5},{5,1},{2,6},{6,2},{3,7},{7,3},{8,12},{12,8},{9,1... | collective-permute-start | bytes 7680008 | tf_op jit(solution)/shard_map/ppermute | solution.py:173
  233.5 32.7 %collective-permute-start.6 = (bf16[1600,800]{0,1:T(8,128)(2,1)}, bf16[1600,800]{0,1:T(8,128)(2,1)}, u32[]{:S(2)}, u32[]{:S(2)}) collective-permute-start(bf16[1600,800]{0,1:T(8,128)(2,1)} %copy.164), channel_id=1, source_target_pairs={{0,4},{4,0},{1,5},{5,1},{2,6},{6,2},{3,7},{7,3},{8,12},{12,8},{9,1... | collective-permute-start | bytes 7680008 | tf_op jit(solution)/shard_map/ppermute | solution.py:173
  269.7 27.7 %collective-permute-start.13 = (bf16[448,256]{1,0:T(8,128)(2,1)S(1)}, bf16[448,256]{1,0:T(8,128)(2,1)S(1)}, u32[]{:S(2)}, u32[]{:S(2)}) collective-permute-start(bf16[448,256]{1,0:T(8,128)(2,1)S(1)} %get-tuple-element.86), channel_id=1, source_target_pairs={{0,2},{1,3},{2,0},{3,1},{4,6},{5,7},{6,4},{7,5},{8,10},{9,11},{10,... | collective-permute-start | bytes 688136 | tf_op jit(solution)/shard_map/ppermute | solution.py:173
  269.7 27.7 %collective-permute-start.14 = (bf16[448,256]{1,0:T(8,128)(2,1)S(1)}, bf16[448,256]{1,0:T(8,128)(2,1)S(1)}, u32[]{:S(2)}, u32[]{:S(2)}) collective-permute-start(bf16[448,256]{1,0:T(8,128)(2,1)S(1)} %get-tuple-element.85), channel_id=1, source_target_pairs={{0,3},{1,0},{2,1},{3,2},{4,7},{5,4},{6,5},{7,6},{8,11},{9,8},{10,9... | collective-permute-start | bytes 688136 | tf_op jit(solution)/shard_map/ppermute | solution.py:173
  301.8 52.0 %collective-permute-start.15 = (bf16[1600,256]{1,0:T(8,128)(2,1)S(1)}, bf16[1600,256]{1,0:T(8,128)(2,1)S(1)}, u32[]{:S(2)}, u32[]{:S(2)}) collective-permute-start(bf16[1600,256]{1,0:T(8,128)(2,1)S(1)} %add_convert_fusion.11), channel_id=1, source_target_pairs={{0,1},{1,2},{2,3},{3,0},{4,5},{5,6},{6,7},{7,4},{8,9},{9,10},{10,1... | collective-permute-start | bytes 2457608 | tf_op jit(solution)/shard_map/ppermute | solution.py:173
  326.4 69.9 %collective-permute-start.16 = (bf16[1600,256]{1,0:T(8,128)(2,1)S(1)}, bf16[1600,256]{1,0:T(8,128)(2,1)S(1)}, u32[]{:S(2)}, u32[]{:S(2)}) collective-permute-start(bf16[1600,256]{1,0:T(8,128)(2,1)S(1)} %add_convert_fusion.11), channel_id=1, source_target_pairs={{0,2},{1,3},{2,0},{3,1},{4,6},{5,7},{6,4},{7,5},{8,10},{9,11},{10,... | collective-permute-start | bytes 2457608 | tf_op jit(solution)/shard_map/ppermute | solution.py:173
  326.4 77.1 %collective-permute-start.17 = (bf16[1600,256]{1,0:T(8,128)(2,1)S(1)}, bf16[1600,256]{1,0:T(8,128)(2,1)S(1)}, u32[]{:S(2)}, u32[]{:S(2)}) collective-permute-start(bf16[1600,256]{1,0:T(8,128)(2,1)S(1)} %add_convert_fusion.11), channel_id=1, source_target_pairs={{0,3},{1,0},{2,1},{3,2},{4,7},{5,4},{6,5},{7,6},{8,11},{9,8},{10,9... | collective-permute-start | bytes 2457608 | tf_op jit(solution)/shard_map/ppermute | solution.py:173
  412.0 78.9 %collective-permute-start.20 = (bf16[400,1024]{1,0:T(8,128)(2,1)}, bf16[400,1024]{1,0:T(8,128)(2,1)}, u32[]{:S(2)}, u32[]{:S(2)}) collective-permute-start(bf16[400,1024]{1,0:T(8,128)(2,1)} %get-tuple-element.56), channel_id=1, source_target_pairs={{0,3},{1,0},{2,1},{3,2},{4,7},{5,4},{6,5},{7,6},{8,11},{9,8},{10,9... | collective-permute-start | bytes 2457608 | tf_op jit(solution)/shard_map/ppermute | solution.py:173
  429.6 105.9 %collective-permute-start.19 = (bf16[400,1024]{1,0:T(8,128)(2,1)}, bf16[400,1024]{1,0:T(8,128)(2,1)}, u32[]{:S(2)}, u32[]{:S(2)}) collective-permute-start(bf16[400,1024]{1,0:T(8,128)(2,1)} %get-tuple-element.57), channel_id=1, source_target_pairs={{0,2},{1,3},{2,0},{3,1},{4,6},{5,7},{6,4},{7,5},{8,10},{9,11},{10,... | collective-permute-start | bytes 2457608 | tf_op jit(solution)/shard_map/ppermute | solution.py:173
  429.6 105.9 %collective-permute-start.18 = (bf16[400,1024]{1,0:T(8,128)(2,1)}, bf16[400,1024]{1,0:T(8,128)(2,1)}, u32[]{:S(2)}, u32[]{:S(2)}) collective-permute-start(bf16[400,1024]{1,0:T(8,128)(2,1)} %get-tuple-element.55), channel_id=1, source_target_pairs={{0,1},{1,2},{2,3},{3,0},{4,5},{5,6},{6,7},{7,4},{8,9},{9,10},{10,1... | collective-permute-start | bytes 2457608 | tf_op jit(solution)/shard_map/ppermute | solution.py:173
  442.7 96.6 %collective-permute-start.23 = (bf16[1600,256]{1,0:T(8,128)(2,1)}, bf16[1600,256]{1,0:T(8,128)(2,1)}, u32[]{:S(2)}, u32[]{:S(2)}) collective-permute-start(bf16[1600,256]{1,0:T(8,128)(2,1)} %convolution_convert_fusion.4), channel_id=1, source_target_pairs={{0,1},{1,2},{2,3},{3,0},{4,5},{5,6},{6,7},{7,4},{8,9},{9,10},{10,1... | collective-permute-start | bytes 2457608 | tf_op jit(solution)/shard_map/ppermute | solution.py:173
  453.2 99.9 %collective-permute-start.22 = (bf16[1600,256]{1,0:T(8,128)(2,1)}, bf16[1600,256]{1,0:T(8,128)(2,1)}, u32[]{:S(2)}, u32[]{:S(2)}) collective-permute-start(bf16[1600,256]{1,0:T(8,128)(2,1)} %convolution_convert_fusion.5), channel_id=1, source_target_pairs={{0,2},{1,3},{2,0},{3,1},{4,6},{5,7},{6,4},{7,5},{8,10},{9,11},{10,... | collective-permute-start | bytes 2457608 | tf_op jit(solution)/shard_map/ppermute | solution.py:173
  490.8 62.2 %collective-permute-start.21 = (bf16[1600,256]{1,0:T(8,128)(2,1)S(1)}, bf16[1600,256]{1,0:T(8,128)(2,1)S(1)}, u32[]{:S(2)}, u32[]{:S(2)}) collective-permute-start(bf16[1600,256]{1,0:T(8,128)(2,1)S(1)} %convolution_convert_fusion.6), channel_id=1, source_target_pairs={{0,3},{1,0},{2,1},{3,2},{4,7},{5,4},{6,5},{7,6},{8,11},{9,8},{10,9... | collective-permute-start | bytes 2457608 | tf_op jit(solution)/shard_map/ppermute | solution.py:173
  535.5 102.3 %collective-permute-start.53 = (bf16[800,1600]{1,0:T(8,128)(2,1)}, bf16[800,1600]{1,0:T(8,128)(2,1)}, u32[]{:S(2)}, u32[]{:S(2)}) collective-permute-start(bf16[800,1600]{1,0:T(8,128)(2,1)} %constant_dynamic-slice_fusion.5), channel_id=1, source_target_pairs={{0,4},{4,0},{1,5},{5,1},{2,6},{6,2},{3,7},{7,3},{8,12},{12,8},{9,1... | collective-permute-start | bytes 7680008 | tf_op jit(solution)/shard_map/ppermute | solution.py:173
  535.5 85.3 %collective-permute-start.58 = (bf16[1600,800]{0,1:T(8,128)(2,1)}, bf16[1600,800]{0,1:T(8,128)(2,1)}, u32[]{:S(2)}, u32[]{:S(2)}) collective-permute-start(bf16[1600,800]{0,1:T(8,128)(2,1)} %constant_dynamic-slice_fusion.4), channel_id=1, source_target_pairs={{0,4},{4,0},{1,5},{5,1},{2,6},{6,2},{3,7},{7,3},{8,12},{12,8},{9,1... | collective-permute-start | bytes 7680008 | tf_op jit(solution)/shard_map/ppermute | solution.py:173
  562.2 43.3 %collective-permute-start.27 = (bf16[448,256]{1,0:T(8,128)(2,1)S(1)}, bf16[448,256]{1,0:T(8,128)(2,1)}, u32[]{:S(2)}, u32[]{:S(2)}) collective-permute-start(bf16[448,256]{1,0:T(8,128)(2,1)S(1)} %get-tuple-element.95), channel_id=1, source_target_pairs={{0,1},{1,2},{2,3},{3,0},{4,5},{5,6},{6,7},{7,4},{8,9},{9,10},{10,1... | collective-permute-start | bytes 688136 | tf_op jit(solution)/shard_map/ppermute | solution.py:173
  604.8 112.4 %collective-permute-start.45 = (bf16[1600,800]{0,1:T(8,128)(2,1)}, bf16[1600,800]{0,1:T(8,128)(2,1)}, u32[]{:S(2)}, u32[]{:S(2)}) collective-permute-start(bf16[1600,800]{0,1:T(8,128)(2,1)} %copy.175), channel_id=1, source_target_pairs={{0,4},{4,0},{1,5},{5,1},{2,6},{6,2},{3,7},{7,3},{8,12},{12,8},{9,1... | collective-permute-start | bytes 7680008 | tf_op jit(solution)/shard_map/ppermute | solution.py:173
  635.1 53.0 %collective-permute-start.60 = (bf16[400,800]{1,0:T(8,128)(2,1)}, bf16[400,800]{1,0:T(8,128)(2,1)}, u32[]{:S(2)}, u32[]{:S(2)}) collective-permute-start(bf16[400,800]{1,0:T(8,128)(2,1)} %copy.178), channel_id=1, source_target_pairs={{4,0},{1,1},{5,2},{0,3},{6,4},{3,5},{7,6},{2,7},{12,8},{9,9},{13,1... | collective-permute-start | bytes 1920008 | tf_op jit(solution)/shard_map/ppermute | solution.py:509
  637.4 59.9 %collective-permute-start.61 = (bf16[400,800]{1,0:T(8,128)(2,1)S(1)}, bf16[400,800]{1,0:T(8,128)(2,1)S(1)}, u32[]{:S(2)}, u32[]{:S(2)}) collective-permute-start(bf16[400,800]{1,0:T(8,128)(2,1)S(1)} %copy.179), channel_id=1, source_target_pairs={{1,0},{5,1},{0,2},{4,3},{3,4},{7,5},{2,6},{6,7},{9,8},{13,9},{8,10... | collective-permute-start | bytes 1920008 | tf_op jit(solution)/shard_map/ppermute | solution.py:509
  637.8 67.0 %collective-permute-start.62 = (bf16[400,800]{1,0:T(8,128)(2,1)S(1)}, bf16[400,800]{1,0:T(8,128)(2,1)S(1)}, u32[]{:S(2)}, u32[]{:S(2)}) collective-permute-start(bf16[400,800]{1,0:T(8,128)(2,1)S(1)} %copy.180), channel_id=1, source_target_pairs={{5,0},{0,1},{4,2},{1,3},{7,4},{2,5},{6,6},{3,7},{13,8},{8,9},{12,1... | collective-permute-start | bytes 1920008 | tf_op jit(solution)/shard_map/ppermute | solution.py:509
  647.7 147.6 %collective-permute-start.30 = (bf16[448,1024]{1,0:T(8,128)(2,1)}, bf16[448,1024]{1,0:T(8,128)(2,1)}, u32[]{:S(2)}, u32[]{:S(2)}) collective-permute-start(bf16[448,1024]{1,0:T(8,128)(2,1)} %constant_dynamic-update-slice_fusion.refs_2_), channel_id=1, source_target_pairs={{0,4},{4,0},{1,5},{5,1},{2,6},{6,2},{3,7},{7,3},{8,12},{12,8},{9,1... | collective-permute-start | bytes 2752520 | tf_op jit(solution)/shard_map/ppermute | solution.py:173
  688.1 43.1 %collective-permute-start.54 = (bf16[2,200,1600]{2,1,0:T(8,128)(2,1)}, bf16[2,200,1600]{2,1,0:T(8,128)(2,1)}, u32[]{:S(2)}, u32[]{:S(2)}) collective-permute-start(bf16[2,200,1600]{2,1,0:T(8,128)(2,1)} %dynamic-slice_bitcast_fusion.1), channel_id=1, source_target_pairs={{0,8},{8,0},{16,24},{24,16},{1,9},{9,1},{17,25},{25,17},{2,10},{10... | collective-permute-start | bytes 3840008 | tf_op jit(solution)/shard_map/ppermute | solution.py:230
  715.7 113.7 %collective-permute-start.63 = (bf16[2,100,3200]{2,0,1:T(2,128)(2,1)}, bf16[2,100,3200]{2,0,1:T(2,128)(2,1)}, u32[]{:S(2)}, u32[]{:S(2)}) collective-permute-start(bf16[2,100,3200]{2,0,1:T(2,128)(2,1)} %copy.181), channel_id=1, source_target_pairs={{0,16},{8,24},{16,0},{24,8},{1,17},{9,25},{17,1},{25,9},{2,18},{10... | collective-permute-start | bytes 3840008 | tf_op jit(solution)/shard_map/ppermute | solution.py:230
  726.0 66.0 %collective-permute-start.47 = (bf16[400,800]{1,0:T(8,128)(2,1)S(1)}, bf16[400,800]{1,0:T(8,128)(2,1)S(1)}, u32[]{:S(2)}, u32[]{:S(2)}) collective-permute-start(bf16[400,800]{1,0:T(8,128)(2,1)S(1)} %get-tuple-element.60), channel_id=1, source_target_pairs={{0,2},{1,3},{2,0},{3,1},{4,6},{5,7},{6,4},{7,5},{8,10},{9,11},{10,... | collective-permute-start | bytes 1920008 | tf_op jit(solution)/shard_map/ppermute | solution.py:173
  731.2 60.8 %collective-permute-start.46 = (bf16[400,800]{1,0:T(8,128)(2,1)S(1)}, bf16[400,800]{1,0:T(8,128)(2,1)S(1)}, u32[]{:S(2)}, u32[]{:S(2)}) collective-permute-start(bf16[400,800]{1,0:T(8,128)(2,1)S(1)} %get-tuple-element.58), channel_id=1, source_target_pairs={{0,1},{1,2},{2,3},{3,0},{4,5},{5,6},{6,7},{7,4},{8,9},{9,10},{10,1... | collective-permute-start | bytes 1920008 | tf_op jit(solution)/shard_map/ppermute | solution.py:173
  743.0 83.5 %collective-permute-start.55 = (bf16[200,1600]{1,0:T(8,128)(2,1)}, bf16[200,1600]{1,0:T(8,128)(2,1)}, u32[]{:S(2)}, u32[]{:S(2)}) collective-permute-start(bf16[200,1600]{1,0:T(8,128)(2,1)} %fusion.74), channel_id=1, source_target_pairs={{0,16},{8,24},{16,0},{24,8},{1,17},{9,25},{17,1},{25,9},{2,18},{10... | collective-permute-start | bytes 1920008 | tf_op jit(solution)/shard_map/ppermute | solution.py:230
  794.6 31.1 %collective-permute-start.49 = (bf16[2,100,800]{2,1,0:T(8,128)(2,1)S(1)}, bf16[2,100,800]{2,1,0:T(8,128)(2,1)S(1)}, u32[]{:S(2)}, u32[]{:S(2)}) collective-permute-start(bf16[2,100,800]{2,1,0:T(8,128)(2,1)S(1)} %dynamic-slice_bitcast_fusion.7), channel_id=1, source_target_pairs={{0,8},{8,0},{16,24},{24,16},{1,9},{9,1},{17,25},{25,17},{2,10},{10... | collective-permute-start | bytes 960008 | tf_op jit(solution)/shard_map/ppermute | solution.py:230
  827.9 106.4 %collective-permute-start.56 = (bf16[200,1600]{1,0:T(8,128)(2,1)S(1)}, bf16[200,1600]{1,0:T(8,128)(2,1)}, u32[]{:S(2)}, u32[]{:S(2)}) collective-permute-start(bf16[200,1600]{1,0:T(8,128)(2,1)S(1)} %fusion.70), channel_id=1, source_target_pairs={{0,16},{8,24},{16,0},{24,8},{1,17},{9,25},{17,1},{25,9},{2,18},{10... | collective-permute-start | bytes 1920008 | tf_op jit(solution)/shard_map/ppermute | solution.py:230
  835.0 101.9 %collective-permute-start.64 = (bf16[100,3200]{1,0:T(8,128)(2,1)}, bf16[100,3200]{1,0:T(8,128)(2,1)}, u32[]{:S(2)}, u32[]{:S(2)}) collective-permute-start(bf16[100,3200]{1,0:T(8,128)(2,1)} %fusion.75), channel_id=1, source_target_pairs={{0,8},{8,0},{16,24},{24,16},{1,9},{9,1},{17,25},{25,17},{2,10},{10... | collective-permute-start | bytes 1920008 | tf_op jit(solution)/shard_map/ppermute | solution.py:230
  861.0 57.9 %collective-permute-start.37 = (f32[2,1024]{1,0:T(2,128)}, f32[2,1024]{1,0:T(2,128)}, u32[]{:S(2)}, u32[]{:S(2)}) collective-permute-start(f32[2,1024]{1,0:T(2,128)} %pad_maximum_fusion.20), channel_id=1, source_target_pairs={{0,3},{1,0},{2,1},{3,2},{4,7},{5,4},{6,5},{7,6},{8,11},{9,8},{10,9... | collective-permute-start | bytes 24584 | tf_op jit(solution)/shard_map/ppermute | solution.py:173
  861.0 60.3 %collective-permute-start.36 = (f32[2,1024]{1,0:T(2,128)}, f32[2,1024]{1,0:T(2,128)}, u32[]{:S(2)}, u32[]{:S(2)}) collective-permute-start(f32[2,1024]{1,0:T(2,128)} %pad_maximum_fusion.20), channel_id=1, source_target_pairs={{0,2},{1,3},{2,0},{3,1},{4,6},{5,7},{6,4},{7,5},{8,10},{9,11},{10,... | collective-permute-start | bytes 24584 | tf_op jit(solution)/shard_map/ppermute | solution.py:173
  861.0 62.6 %collective-permute-start.35 = (f32[2,1024]{1,0:T(2,128)}, f32[2,1024]{1,0:T(2,128)}, u32[]{:S(2)}, u32[]{:S(2)}) collective-permute-start(f32[2,1024]{1,0:T(2,128)} %pad_maximum_fusion.20), channel_id=1, source_target_pairs={{0,1},{1,2},{2,3},{3,0},{4,5},{5,6},{6,7},{7,4},{8,9},{9,10},{10,1... | collective-permute-start | bytes 24584 | tf_op jit(solution)/shard_map/ppermute | solution.py:173
  923.6 69.0 %collective-permute-start.33 = (bf16[400,1024]{1,0:T(8,128)(2,1)}, bf16[400,1024]{1,0:T(8,128)(2,1)}, u32[]{:S(2)}, u32[]{:S(2)}) collective-permute-start(bf16[400,1024]{1,0:T(8,128)(2,1)} %get-tuple-element.50), channel_id=1, source_target_pairs={{0,2},{1,3},{2,0},{3,1},{4,6},{5,7},{6,4},{7,5},{8,10},{9,11},{10,... | collective-permute-start | bytes 2457608 | tf_op jit(solution)/shard_map/ppermute | solution.py:173
  929.4 63.3 %collective-permute-start.32 = (bf16[400,1024]{1,0:T(8,128)(2,1)}, bf16[400,1024]{1,0:T(8,128)(2,1)}, u32[]{:S(2)}, u32[]{:S(2)}) collective-permute-start(bf16[400,1024]{1,0:T(8,128)(2,1)} %get-tuple-element.48), channel_id=1, source_target_pairs={{0,1},{1,2},{2,3},{3,0},{4,5},{5,6},{6,7},{7,4},{8,9},{9,10},{10,1... | collective-permute-start | bytes 2457608 | tf_op jit(solution)/shard_map/ppermute | solution.py:173
  934.3 62.6 %collective-permute-start.38 = (bf16[3,448,800]{2,1,0:T(8,128)(2,1)}, bf16[3,448,800]{2,1,0:T(8,128)(2,1)S(1)}, u32[]{:S(2)}, u32[]{:S(2)}) collective-permute-start(bf16[3,448,800]{2,1,0:T(8,128)(2,1)} %constant_dynamic-slice_fusion.10), channel_id=1, source_target_pairs={{0,4},{4,0},{1,5},{5,1},{2,6},{6,2},{3,7},{7,3},{8,12},{12,8},{9,1... | collective-permute-start | bytes 6451208 | tf_op jit(solution)/shard_map/ppermute | solution.py:173
  936.9 125.6 %collective-permute-start.57 = (bf16[2,200,1600]{2,1,0:T(8,128)(2,1)}, bf16[2,200,1600]{2,1,0:T(8,128)(2,1)}, u32[]{:S(2)}, u32[]{:S(2)}) collective-permute-start(bf16[2,200,1600]{2,1,0:T(8,128)(2,1)} %pad_maximum_fusion.14), channel_id=1, source_target_pairs={{0,8},{8,0},{16,24},{24,16},{1,9},{9,1},{17,25},{25,17},{2,10},{10... | collective-permute-start | bytes 3840008 | tf_op jit(solution)/shard_map/ppermute | solution.py:230
  942.7 92.9 %collective-permute-start.65 = (bf16[100,3200]{1,0:T(8,128)(2,1)}, bf16[100,3200]{1,0:T(8,128)(2,1)}, u32[]{:S(2)}, u32[]{:S(2)}) collective-permute-start(bf16[100,3200]{1,0:T(8,128)(2,1)} %fusion.69), channel_id=1, source_target_pairs={{0,8},{8,0},{16,24},{24,16},{1,9},{9,1},{17,25},{25,17},{2,10},{10... | collective-permute-start | bytes 1920008 | tf_op jit(solution)/shard_map/ppermute | solution.py:230
  999.8 30.3 %collective-permute-start.40 = (bf16[3,48,800]{2,1,0:T(8,128)(2,1)}, bf16[3,48,800]{2,1,0:T(8,128)(2,1)}, u32[]{:S(2)}, u32[]{:S(2)}) collective-permute-start(bf16[3,48,800]{2,1,0:T(8,128)(2,1)} %get-tuple-element.62), channel_id=1, source_target_pairs={{1,0},{2,1},{3,2},{5,4},{6,5},{7,6},{9,8},{10,9},{11,10},{13,12},{... | collective-permute-start | bytes 691208 | tf_op jit(solution)/shard_map/ppermute | solution.py:318
  1001.0 29.1 %collective-permute-start.39 = (bf16[3,48,800]{2,1,0:T(8,128)(2,1)}, bf16[3,48,800]{2,1,0:T(8,128)(2,1)}, u32[]{:S(2)}, u32[]{:S(2)}) collective-permute-start(bf16[3,48,800]{2,1,0:T(8,128)(2,1)} %get-tuple-element.61), channel_id=1, source_target_pairs={{0,1},{1,2},{2,3},{4,5},{5,6},{6,7},{8,9},{9,10},{10,11},{12,13},{... | collective-permute-start | bytes 691208 | tf_op jit(solution)/shard_map/ppermute | solution.py:319
  1038.1 50.1 %collective-permute-start.66 = (bf16[2,100,3200]{2,0,1:T(2,128)(2,1)S(1)}, bf16[2,100,3200]{2,0,1:T(2,128)(2,1)S(1)}, u32[]{:S(2)}, u32[]{:S(2)}) collective-permute-start(bf16[2,100,3200]{2,0,1:T(2,128)(2,1)S(1)} %copy.183), channel_id=1, source_target_pairs={{0,16},{8,24},{16,0},{24,8},{1,17},{9,25},{17,1},{25,9},{2,18},{10... | collective-permute-start | bytes 3840008 | tf_op jit(solution)/shard_map/ppermute | solution.py:230
  (116 other events, 1859.4 us)
Sparse Core Ops, SparseCore 0:
  9.6 69.3 all-gather.4
  80.6 78.8 all-gather.6
  265.7 127.5 all-gather.8
where the time goes:
time: 1140 us; the launch traced here: 1120 us
  waiting for transfers between devices  379 us (33%)
  starting transfers between devices  228 us (20%)
  local copies, waits for them, and re-layouts  175 us (15%)
  matrix products  108 us (9%)
  other arithmetic  89.8 us (8%)
  blocking collectives  78.4 us (7%)
  Pallas kernels  48.5 us (4%)
  between operations  16.1 us (1%)
    ppermute x39, waiting for transfers between devices, turn(): lax.ppermute(value, axis, [(i, (i + steps) % size) for i in range(size)])  255 us
    ppermute x39, starting transfers between devices, turn(): lax.ppermute(value, axis, [(i, (i + steps) % size) for i in range(size)])  127 us
    dynamic_update_slice x14, local copies, waits for them, and re-layouts, place(): lax.dynamic_update_slice_in_dim(whole, part, index * part.shape[axis], axis)  74.6 us
    ppermute x16, waiting for transfers between devices, swap_with(): return lax.ppermute(value, 'dp', [(i, i ^ bit) for i in range(4)])  72.5 us
    ppermute x8, starting transfers between devices, body(): got = lax.ppermute(sent, ('row', 'col'), pairs)  68.5 us
    psum x2, blocking collectives, small_sum(): return lax.psum(value, axes)  63.7 us
    dot_general x10, matrix products, dot_tn(): return lax.dot_general(a, b, NT, preferred_element_type=F32)  42.7 us
    dot_general x12, matrix products, dot(): return jnp.dot(a, b, preferred_element_type=F32)  40.7 us
  transfers between devices with their start and end apart: 70, of which 24 were waited for; matrix products, arithmetic and copies ran while one was open for 31% of the time, Pallas kernels for 4%

commit v1 on v0

v1 whole, which is shorter than its diff:
```python
import functools

import jax
import jax.numpy as jnp
from jax import lax
from jax.experimental import pallas as pl
from jax.experimental.pallas import tpu as pltpu
from jax.sharding import PartitionSpec as P

BLK = 512
EPSILON = 1e-05
LOG2E = 1.4426950408889634
BF16 = jnp.bfloat16
F32 = jnp.float32

FREE = pl.CostEstimate(flops=0, bytes_accessed=0, transcendentals=0)
ROOM = pltpu.CompilerParams(vmem_limit_bytes=56 * 2**20)

NT=(((0,),(0,)),((),()))
TN=(((1,),(1,)),((),()))

def plan_tiles(meta, ks, own, load, n_slots, n_blocks, n_row, n_heads):
    for i in range(n_row): load[i]=0
    def level(lv,_):
        cost=n_blocks-lv
        def tile(t,_):
            slot=t//n_blocks; qb=t%n_blocks
            head=meta[0]+slot
            here=head<n_heads
            hd=jnp.minimum(head,n_heads-1)
            n=qb+1-ks[hd,qb]
            mask=jnp.where(slot==0,meta[2],jnp.where(slot==n_slots-1,meta[3],(1<<n_blocks)-1))
            here=jnp.logical_and(here,((mask>>qb)&1)==1)
            @pl.when(cost==n_blocks)
            def _(): own[t]=-1
            @pl.when(jnp.logical_and(here,n==cost))
            def _():
                best=load[0]; who=jnp.int32(0)
                for i in range(1,n_row):
                    less=load[i]<best
                    best=jnp.where(less,load[i],best); who=jnp.where(less,i,who)
                own[t]=who
                load[who]=best+cost
            return 0
        lax.fori_loop(0,n_slots*n_blocks,tile,0)
        return 0
    lax.fori_loop(0,n_blocks,level,0)

def fetch(pieces, whole, sems, row, n_row, width):
    copies=[]
    for i,p in enumerate(pieces):
        at=lax.rem(row+i,n_row)*width
        c=pltpu.make_async_copy(p, whole.at[...,pl.ds(pl.multiple_of(at,width),width)], sems.at[i])
        c.start(); copies.append(c)
    return copies

def fwd_kernel(n_row,n_slots,hd,n_heads,meta,ks,*refs):
    pieces=refs[:n_row]; cuts=refs[n_row:2*n_row]; o_ref,lse_ref,whole,own,load,sems=refs[2*n_row:]
    S=whole.shape[2]; nb=S//BLK; width=S//n_row
    row=meta[1]
    copies=fetch(pieces,whole,sems,row,n_row,width)
    plan_tiles(meta,ks,own,load,n_slots,nb,n_row,n_heads)
    o_ref[...]=jnp.zeros_like(o_ref)
    for c in copies: c.wait()
    c2=hd**-0.5*LOG2E
    diag=lax.broadcasted_iota(jnp.int32,(BLK,BLK),0)<=lax.broadcasted_iota(jnp.int32,(BLK,BLK),1)
    def tile(t,_):
        @pl.when(own[t]==row)
        def _():
            slot=t//nb; qb=t%nb
            first=ks[meta[0]+slot,qb]
            hs=pl.ds(pl.multiple_of(slot*hd,hd),hd)
            qs=pl.ds(pl.multiple_of(qb*BLK,BLK),BLK)
            q=whole[0,hs,qs]
            def scores(kb_ds):
                return lax.dot_general(whole[1,hs,kb_ds],q,NT,preferred_element_type=jnp.float32)
            s=jnp.where(diag,scores(qs),-1e30)
            m=jnp.max(s,axis=0,keepdims=True)
            p=jnp.exp2((s-m)*c2)
            l=jnp.sum(p,axis=0,keepdims=True)
            acc=jnp.dot(whole[2,hs,qs],p.astype(jnp.bfloat16),preferred_element_type=jnp.float32)
            def step(kb,carry):
                m,l,acc=carry
                kd=pl.ds(pl.multiple_of(kb*BLK,BLK),BLK)
                s=scores(kd)
                mn=jnp.maximum(m,jnp.max(s,axis=0,keepdims=True))
                a=jnp.exp2((m-mn)*c2)
                p=jnp.exp2((s-mn)*c2)
                l=l*a+jnp.sum(p,axis=0,keepdims=True)
                acc=acc*a+jnp.dot(whole[2,hs,kd],p.astype(jnp.bfloat16),preferred_element_type=jnp.float32)
                return mn,l,acc
            m,l,acc=lax.fori_loop(first,qb,step,(m,l,acc))
            o_ref[hs,qs]=(acc/l).astype(jnp.bfloat16)
            lse_ref[pl.ds(slot,1),qs]=m*c2+jnp.log2(l)
        return 0
    lax.fori_loop(0,n_slots*nb,tile,0)
    for i,cut in enumerate(cuts):
        cut[...]=o_ref[:,pl.ds(pl.multiple_of(lax.rem(row+i,n_row)*width,width),width)]

def bwd_kernel(n_row,n_slots,hd,n_heads,meta,ks,*refs):
    pieces=refs[:n_row]; das=refs[n_row:2*n_row]
    o_ref,lse_ref=refs[2*n_row:2*n_row+2]; cuts=refs[2*n_row+2:3*n_row+2]
    d_ref,whole,da,acc,own,load,sems,sems2=refs[3*n_row+2:]
    S=whole.shape[2]; nb=S//BLK; width=S//n_row
    row=meta[1]
    copies=fetch(pieces,whole,sems,row,n_row,width)+fetch(das,da,sems2,row,n_row,width)
    plan_tiles(meta,ks,own,load,n_slots,nb,n_row,n_heads)
    d_ref[...]=jnp.zeros_like(d_ref)
    acc[...]=jnp.zeros_like(acc)
    for c in copies: c.wait()
    scale=hd**-0.5; c2=scale*LOG2E
    diag=lax.broadcasted_iota(jnp.int32,(BLK,BLK),0)<=lax.broadcasted_iota(jnp.int32,(BLK,BLK),1)
    def tile(t,_):
        @pl.when(own[t]==row)
        def _():
            slot=t//nb; qb=t%nb
            first=ks[meta[0]+slot,qb]
            hs=pl.ds(pl.multiple_of(slot*hd,hd),hd)
            qs=pl.ds(pl.multiple_of(qb*BLK,BLK),BLK)
            q=whole[0,hs,qs]
            up=da[hs,qs]
            lse=lse_ref[pl.ds(slot,1),qs]
            delta=jnp.sum(up.astype(jnp.float32)*o_ref[hs,qs].astype(jnp.float32),axis=0,keepdims=True)
            def block(kd,masked):
                k=whole[1,hs,kd]
                s=lax.dot_general(k,q,NT,preferred_element_type=jnp.float32)
                p=jnp.exp2(s*c2-lse)
                if masked: p=jnp.where(diag,p,0.0)
                dp=lax.dot_general(whole[2,hs,kd],up,NT,preferred_element_type=jnp.float32)
                ds=(p*(dp-delta)).astype(jnp.bfloat16)
                acc[1,hs,kd]+=lax.dot_general(up,p.astype(jnp.bfloat16),TN,preferred_element_type=jnp.float32)
                acc[0,hs,kd]+=lax.dot_general(q,ds,TN,preferred_element_type=jnp.float32)
                return jnp.dot(k,ds,preferred_element_type=jnp.float32)
            dq=block(qs,True)
            dq=lax.fori_loop(first,qb,lambda kb,dq:dq+block(pl.ds(pl.multiple_of(kb*BLK,BLK),BLK),False),dq)
            d_ref[hs,qs]=(dq*scale).astype(jnp.bfloat16)
        return 0
    lax.fori_loop(0,n_slots*nb,tile,0)
    for i,cut in enumerate(cuts):
        at=pl.ds(pl.multiple_of(lax.rem(row+i,n_row)*width,width),width)
        cut[0]=d_ref[:,at]
        cut[1]=(acc[0,:,at]*scale).astype(jnp.bfloat16)
        cut[2]=acc[1,:,at].astype(jnp.bfloat16)

V=pl.BlockSpec(memory_space=pltpu.VMEM); SM=pl.BlockSpec(memory_space=pltpu.SMEM); ANY=pl.BlockSpec(memory_space=pl.ANY)
def attn_fwd(meta,ks,pieces,n_slots,hd):
    n_row=len(pieces); _,H,T=pieces[0].shape; S=T*n_row; nb=S//BLK
    return pl.pallas_call(functools.partial(fwd_kernel,n_row,n_slots,hd,ks.shape[0]),
      out_shape=[jax.ShapeDtypeStruct((H,T),jnp.bfloat16)]*n_row+[jax.ShapeDtypeStruct((H,S),jnp.bfloat16),jax.ShapeDtypeStruct((n_slots,S),jnp.float32)],
      in_specs=[SM,SM]+[ANY]*n_row,out_specs=[V]*(n_row+2),
      scratch_shapes=[pltpu.VMEM((3,H,S),jnp.bfloat16),pltpu.SMEM((n_slots*nb,),jnp.int32),pltpu.SMEM((n_row,),jnp.int32),pltpu.SemaphoreType.DMA((n_row,))],
      compiler_params=pltpu.CompilerParams(vmem_limit_bytes=48*2**20),
      cost_estimate=FREE,
    )(meta,ks,*pieces)
def attn_bwd(meta,ks,pieces,das,o,lse,n_slots,hd):
    n_row=len(pieces); _,H,T=pieces[0].shape; S=T*n_row; nb=S//BLK
    return pl.pallas_call(functools.partial(bwd_kernel,n_row,n_slots,hd,ks.shape[0]),
      out_shape=[jax.ShapeDtypeStruct((3,H,T),jnp.bfloat16)]*n_row,
      in_specs=[SM,SM]+[ANY]*(2*n_row)+[V,V],out_specs=[V]*n_row,
      scratch_shapes=[pltpu.VMEM((H,S),jnp.bfloat16),pltpu.VMEM((3,H,S),jnp.bfloat16),pltpu.VMEM((H,S),jnp.bfloat16),pltpu.VMEM((2,H,S),jnp.float32),pltpu.SMEM((n_slots*nb,),jnp.int32),pltpu.SMEM((n_row,),jnp.int32),pltpu.SemaphoreType.DMA((n_row,)),pltpu.SemaphoreType.DMA((n_row,))],
      compiler_params=pltpu.CompilerParams(vmem_limit_bytes=56*2**20),
      cost_estimate=FREE,
    )(meta,ks,*pieces,*das,o,lse)


def rows_of(total, most):
    for rows in range(min(total, most) // 16 * 16, 0, -16):
        if total % rows == 0:
            return rows
    return total


def by_rows(i, *refs):
    return (i, 0)


def whole_block(i, *refs):
    return (0, 0)


def product_kernel(a_ref, b_ref, bias_ref, o_ref):
    o_ref[...] = (
        jnp.dot(a_ref[...], b_ref[...], preferred_element_type=F32) + bias_ref[...]
    ).astype(o_ref.dtype)


def product(a, b, bias):
    rows = rows_of(a.shape[0], 448)
    return pl.pallas_call(
        product_kernel,
        out_shape=jax.ShapeDtypeStruct((a.shape[0], b.shape[1]), BF16),
        grid=(a.shape[0] // rows,),
        in_specs=[
            pl.BlockSpec((rows, a.shape[1]), by_rows),
            pl.BlockSpec(b.shape, whole_block),
            pl.BlockSpec((rows, 1), by_rows),
        ],
        out_specs=pl.BlockSpec((rows, b.shape[1]), by_rows),
        compiler_params=ROOM,
        cost_estimate=FREE,
    )(a, b, bias)


def split_product(parts, b, row, bias, dtype):
    n = len(parts)
    total, depth = parts[0].shape
    width = b.shape[1]
    rows = rows_of(total, 400)

    def kernel(row_ref, b_ref, bias_ref, *refs):
        out = bias_ref[...] + jnp.zeros((rows, width), F32)
        for i in range(n):
            at = pl.multiple_of(lax.rem(row_ref[0] + i, n) * depth, 8)
            out = out + jnp.dot(refs[i][...], b_ref[pl.ds(at, depth), :], preferred_element_type=F32)
        refs[n][...] = out.astype(dtype)

    return pl.pallas_call(
        kernel,
        out_shape=jax.ShapeDtypeStruct((total, width), dtype),
        grid=(total // rows,),
        in_specs=[SM, pl.BlockSpec(b.shape, whole_block), pl.BlockSpec((rows, 1), by_rows)]
        + [pl.BlockSpec((rows, depth), by_rows)] * n,
        out_specs=pl.BlockSpec((rows, width), by_rows),
        compiler_params=ROOM,
        cost_estimate=FREE,
    )(row, b, bias, *parts)


def split_product_tn(parts, b, row):
    n = len(parts)
    depth = parts[0].shape[1]
    total, width = b.shape
    rows = rows_of(total, 400)
    steps = total // rows

    def kernel(row_ref, b_ref, *refs):
        o_ref, acc = refs[n:]

        @pl.when(pl.program_id(0) == 0)
        def start():
            acc[...] = jnp.zeros_like(acc)

        for i in range(n):
            at = pl.multiple_of(lax.rem(row_ref[0] + i, n) * depth, 8)
            acc[pl.ds(at, depth), :] += lax.dot_general(
                refs[i][...], b_ref[...], NT, preferred_element_type=F32
            )

        @pl.when(pl.program_id(0) == steps - 1)
        def end():
            o_ref[...] = acc[...].astype(BF16)

    return pl.pallas_call(
        kernel,
        out_shape=jax.ShapeDtypeStruct((n * depth, width), BF16),
        grid=(steps,),
        in_specs=[SM, pl.BlockSpec((rows, width), by_rows)]
        + [pl.BlockSpec((rows, depth), by_rows)] * n,
        out_specs=pl.BlockSpec((n * depth, width), whole_block),
        scratch_shapes=[pltpu.VMEM((n * depth, width), F32)],
        compiler_params=ROOM,
        cost_estimate=FREE,
    )(row, b, *parts)


def norm_product_tn(a, b, normed, gain, shift, scale):
    rows = rows_of(a.shape[0], 448)
    steps = a.shape[0] // rows
    depth, tokens = a.shape[1], b.shape[1]
    cut = rows_of(depth, 400)

    def kernel(a_ref, b_ref, n_ref, g_ref, s_ref, c_ref, o_ref, t_ref, f_ref, acc):
        @pl.when(pl.program_id(0) == 0)
        def start():
            acc[...] = lax.dot_general(a_ref[...], b_ref[...], NT, preferred_element_type=F32)

        @pl.when(pl.program_id(0) > 0)
        def more():
            acc[...] += lax.dot_general(a_ref[...], b_ref[...], NT, preferred_element_type=F32)

        @pl.when(pl.program_id(0) == steps - 1)
        def end():
            t_ref[...] = jnp.zeros_like(t_ref)
            for first in range(0, depth, cut):
                at = pl.ds(first, cut)
                p = acc[at, :]
                scaled = p * g_ref[at, :]
                o_ref[at, :] = (scaled * c_ref[...]).astype(BF16)
                moved = p * (n_ref[at, :].astype(F32) - s_ref[at, :])
                t_ref[0:1, :] += jnp.sum(scaled, axis=0, keepdims=True)
                t_ref[1:2, :] += jnp.sum(moved, axis=0, keepdims=True)
                f_ref[at, 0:1] = jnp.sum(moved, axis=1, keepdims=True)
                f_ref[at, 1:2] = jnp.sum(p, axis=1, keepdims=True)

    return pl.pallas_call(
        kernel,
        out_shape=[
            jax.ShapeDtypeStruct((depth, tokens), BF16),
            jax.ShapeDtypeStruct((2, tokens), F32),
            jax.ShapeDtypeStruct((depth, 2), F32),
        ],
        grid=(steps,),
        in_specs=[
            pl.BlockSpec((rows, depth), by_rows),
            pl.BlockSpec((rows, tokens), by_rows),
            pl.BlockSpec((depth, tokens), whole_block),
            pl.BlockSpec((depth, 1), whole_block),
            pl.BlockSpec((depth, 1), whole_block),
            pl.BlockSpec((1, tokens), whole_block),
        ],
        out_specs=[
            pl.BlockSpec((depth, tokens), whole_block),
            pl.BlockSpec((2, tokens), whole_block),
            pl.BlockSpec((depth, 2), whole_block),
        ],
        scratch_shapes=[pltpu.VMEM((depth, tokens), F32)],
        compiler_params=ROOM,
        cost_estimate=FREE,
    )(a, b, normed, gain, shift, scale)


def token_product(a, b, index, parts, of_a):
    rows_a = a.shape[0] // (parts if of_a else 1)
    rows_b = b.shape[0] // (1 if of_a else parts)
    rows = rows_of(rows_a, 448)
    steps = rows_a // rows

    def kernel(index_ref, a_ref, b_ref, o_ref):
        o_ref[...] = lax.dot_general(
            a_ref[...], b_ref[...], TN, preferred_element_type=F32
        ).astype(BF16)

    if of_a:
        a_map, b_map = (lambda i, r: (r[0] * steps + i, 0)), whole_block
    else:
        a_map, b_map = by_rows, (lambda i, r: (r[0], 0))
    return pl.pallas_call(
        kernel,
        out_shape=jax.ShapeDtypeStruct((rows_a, rows_b), BF16),
        grid_spec=pltpu.PrefetchScalarGridSpec(
            num_scalar_prefetch=1,
            grid=(steps,),
            in_specs=[
                pl.BlockSpec((rows, a.shape[1]), a_map),
                pl.BlockSpec((rows_b, b.shape[1]), b_map),
            ],
            out_specs=pl.BlockSpec((rows, rows_b), by_rows),
        ),
        compiler_params=ROOM,
        cost_estimate=FREE,
    )(index, a, b)


def gelu_parts(u):
    inner = 0.7978845608 * (u + 0.044715 * u * u * u)
    t = jnp.tanh(inner)
    value = 0.5 * u * (1.0 + t)
    slope = 0.5 * (1.0 + t) + 0.5 * u * (1.0 - t * t) * 0.7978845608 * (1.0 + 0.134145 * u * u)
    return value, slope


def hidden_layer(up, down, n, bias, n2, g, row):
    ff, depth = up.shape
    tokens = n2.shape[1]
    rows = rows_of(ff // n, 400)
    cuts = ff // n // rows
    steps = ff // rows

    def kernel(row_ref, up_ref, down_ref, bias_ref, n_ref, g_ref, h_ref, d_ref, p_ref, acc):
        step = pl.program_id(0)
        u = jnp.dot(up_ref[...], n_ref[...], preferred_element_type=F32) + bias_ref[...]
        value, slope = gelu_parts(u)
        h_ref[...] = value.astype(BF16)
        dh = jnp.dot(down_ref[...], g_ref[...], preferred_element_type=F32)
        du = (dh * slope).astype(BF16)
        d_ref[...] = du

        @pl.when(step == 0)
        def start():
            acc[...] = lax.dot_general(up_ref[...], du, NT, preferred_element_type=F32)

        @pl.when(step > 0)
        def more():
            acc[...] += lax.dot_general(up_ref[...], du, NT, preferred_element_type=F32)

        @pl.when(step == steps - 1)
        def end():
            p_ref[...] = acc[...].astype(BF16)

    mine = lambda i, r: (lax.rem(r[0] * cuts + i, steps), 0)
    full = lambda i, r: (0, 0)
    return pl.pallas_call(
        kernel,
        out_shape=[
            jax.ShapeDtypeStruct((ff, tokens), BF16),
            jax.ShapeDtypeStruct((ff, tokens), BF16),
            jax.ShapeDtypeStruct((depth, tokens), BF16),
        ],
        grid_spec=pltpu.PrefetchScalarGridSpec(
            num_scalar_prefetch=1,
            grid=(steps,),
            in_specs=[
                pl.BlockSpec((rows, depth), mine),
                pl.BlockSpec((rows, depth), lambda i, r: (i, 0)),
                pl.BlockSpec((rows, 1), mine),
                pl.BlockSpec((depth, tokens), full),
                pl.BlockSpec((depth, tokens), full),
            ],
            out_specs=[
                pl.BlockSpec((rows, tokens), mine),
                pl.BlockSpec((rows, tokens), mine),
                pl.BlockSpec((depth, tokens), full),
            ],
            scratch_shapes=[pltpu.VMEM((depth, tokens), F32)],
        ),
        compiler_params=ROOM,
        cost_estimate=FREE,
    )(row, up, down, bias, n2, g)


def gate(values, others):
    def kernel(*refs):
        pass

    out = pl.pallas_call(
        kernel,
        out_shape=[jax.ShapeDtypeStruct(v.shape, v.dtype) for v in values],
        in_specs=[ANY] * (len(values) + len(others)),
        out_specs=[ANY] * len(values),
        input_output_aliases={i: i for i in range(len(values))},
        cost_estimate=FREE,
    )(*values, *others)
    return list(out)


def turn(value, axis, steps):
    size = lax.axis_size(axis)
    if steps % size == 0:
        return value
    return lax.ppermute(value, axis, [(i, (i + steps) % size) for i in range(size)])


def block(value, index, size, axis):
    return lax.dynamic_slice_in_dim(value, index * size, size, axis)


def row_sum(parts):
    total = parts[0].astype(F32)
    for step in range(1, len(parts)):
        total = total + turn(parts[step], "row", step).astype(F32)
    return total


def swap_with(value, bit):
    return lax.ppermute(value, "dp", [(i, i ^ bit) for i in range(4)])


def pick(value, index, axis=0):
    return lax.dynamic_index_in_dim(value, index, axis, keepdims=False)


def dot(a, b):
    return jnp.dot(a, b, preferred_element_type=F32)


def ordered(parts, base, sign):
    size = len(parts)
    stacked = jnp.stack(parts)
    return [pick(stacked, (sign * (j - base)) % size) for j in range(size)]


class Shares:
    def __init__(self, rows):
        self.rows = rows
        self.size = -(-rows // 64) * 16
        self.starts = [(rows - self.size) * s // 48 * 16 for s in range(3)] + [rows - self.size]
        ends = self.starts[1:] + [rows]
        self.lengths = [b - a for a, b in zip(self.starts, ends)]

    def take(self, value, share, axis):
        start = jnp.array(self.starts, jnp.int32)[share]
        return lax.dynamic_slice_in_dim(value, start, self.size, axis)

    def join(self, parts, me, axis):
        stacked = jnp.stack(parts)
        laid = [
            lax.slice_in_dim(pick(stacked, me ^ s), 0, self.lengths[s], axis=axis)
            for s in range(4)
        ]
        return jnp.concatenate(laid, axis)


def assemble(parts, shares, me):
    n, wide = parts[0].shape[0], parts[0].shape[2]

    def kernel(me_ref, *refs):
        o_ref, sems = refs[-2:]
        for act in ("start", "wait"):
            for m in range(4):
                for s in range(4):

                    @pl.when(me_ref[0] ^ m == s)
                    def move():
                        rows = pl.ds(0, shares.lengths[s])
                        to = pl.ds(shares.starts[s], shares.lengths[s])
                        pairs = [(refs[m].at[:, rows], o_ref.at[:, to])]
                        if m == 3:
                            low, high = pl.ds(0, n // 2), pl.ds(n // 2, n // 2)
                            pairs = [
                                (refs[3].at[:, rows], o_ref.at[low, to]),
                                (refs[4].at[:, rows], o_ref.at[high, to]),
                            ]
                        for k, (source, target) in enumerate(pairs):
                            copy = pltpu.make_async_copy(source, target, sems.at[m + k])
                            getattr(copy, act)()

    return pl.pallas_call(
        kernel,
        out_shape=jax.ShapeDtypeStruct((n, shares.rows, wide), parts[0].dtype),
        in_specs=[SM] + [ANY] * 5,
        out_specs=V,
        scratch_shapes=[pltpu.SemaphoreType.DMA((5,))],
        compiler_params=ROOM,
        cost_estimate=FREE,
    )(me, *parts)


def small_sum(value, axes):
    for axis in axes:
        size = lax.axis_size(axis)
        if size & (size - 1):
            value = lax.psum(value, axis)
            continue
        bit = 1
        while bit < size:
            value = value + lax.ppermute(value, axis, [(i, i ^ bit) for i in range(size)])
            bit *= 2
    return value


def go_up(value, first, last):
    return lax.ppermute(value, "col", [(i, i + 1) for i in range(first, last + 1)])


def go_down(value, first, last):
    return lax.ppermute(value, "col", [(i, i - 1) for i in range(first, last + 1)])


def row_join(parts, axis):
    row = lax.axis_index("row")
    if len(parts) == 2:
        low = row == 0
        parts = [jnp.where(low, parts[0], parts[1]), jnp.where(low, parts[1], parts[0])]
    else:
        parts = ordered(parts, row, 1)
    return jnp.concatenate(parts, axis)


def swap_all(value):
    return [swap_with(value, 1), swap_with(value, 2), swap_with(value, 3)]


class Heads:
    def __init__(self, n_col, width, heads, blocks):
        self.size = n_col * width // heads
        self.firsts = [width * c // self.size for c in range(n_col)]
        lasts = [-(-width * (c + 1) // self.size) for c in range(n_col)]
        self.slots = max(b - a for a, b in zip(self.firsts, lasts))
        self.window = self.slots * self.size
        self.before = [width * c - f * self.size for c, f in enumerate(self.firsts)]
        self.after = [self.window - width - b for b in self.before]
        self.edge = max(self.before + self.after)
        full = (1 << blocks) - 1
        shares = {0: 0, 1: 2, 2: 9, 3: 13, 4: 15}

        def left_share(column):
            part = column % self.size
            return shares[round(4 * part / self.size)] if blocks == 4 else 0

        self.first_mask = [full & ~left_share(b) for b in self.before]
        self.last_mask = []
        for c, f in enumerate(self.firsts):
            end = width * (c + 1)
            begin = (f + self.slots - 1) * self.size
            if begin >= end:
                self.last_mask.append(0)
            elif begin + self.size <= end:
                self.last_mask.append(full)
            else:
                self.last_mask.append(left_share(end - begin))


def edges(value, axis, heads):
    n = lax.axis_size("col")
    edge, width = heads.edge, value.shape[axis]
    left = go_up(lax.slice_in_dim(value, width - edge, width, axis=axis), 0, n - 2)
    right = go_down(lax.slice_in_dim(value, 0, edge, axis=axis), 1, n - 1)
    return left, right


def widen(value, left, right, axis, heads, col):
    wide = jnp.concatenate([left, value, right], axis)
    before = jnp.array(heads.before, jnp.int32)[col]
    return lax.dynamic_slice_in_dim(wide, heads.edge - before, heads.window, axis)


def narrow_edges(value, axis, heads, col, width):
    n = lax.axis_size("col")
    edge = heads.edge
    before = jnp.array(heads.before, jnp.int32)[col]
    shape = list(value.shape)
    shape[axis] = width + 2 * edge
    wide = lax.dynamic_update_slice_in_dim(
        jnp.zeros(shape, value.dtype), value, edge - before, axis
    )
    tail = go_down(lax.slice_in_dim(wide, 0, edge, axis=axis), 1, n - 1)
    front = go_up(lax.slice_in_dim(wide, edge + width, width + 2 * edge, axis=axis), 0, n - 2)
    return wide, front, tail


def narrow(wide, front, tail, axis, heads, width):
    edge = heads.edge
    pads = [(0, 0)] * wide.ndim
    pads[axis] = (0, width - edge)
    own = lax.slice_in_dim(wide, edge, edge + width, axis=axis).astype(F32)
    own = own + jnp.pad(front, pads).astype(F32)
    pads[axis] = (width - edge, 0)
    return own + jnp.pad(tail, pads).astype(F32)


def moments(values):
    mean = jnp.mean(values, axis=0, keepdims=True)
    centred = values - mean
    variance = jnp.mean(centred * centred, axis=0, keepdims=True)
    return mean, lax.rsqrt(variance + EPSILON)


def body(
    tokens,
    cotangent,
    w_qkv,
    q_bias,
    v_bias,
    w_out,
    out_bias,
    w_up,
    up_bias,
    w_down,
    down_bias,
    ln1_gain,
    ln1_bias,
    ln2_gain,
    ln2_bias,
    key_start,
):
    n_row, n_col = lax.axis_size("row"), lax.axis_size("col")
    row, col = lax.axis_index("row"), lax.axis_index("col")
    seqs, rows, width = tokens.shape
    length = seqs * rows
    depth = width * n_col
    part = length // n_col
    in_rows = w_up.shape[0]
    ff = w_up.shape[1]
    ff_rows = w_down.shape[0]
    ff_part = ff_rows // n_col
    heads = Heads(n_col, width, key_start.shape[0], rows * n_row // BLK)
    size, window = heads.size, heads.window
    firsts = jnp.array(heads.firsts, jnp.int32) * size
    begin = firsts[col]

    shares = Shares(width)
    dp = lax.axis_index("dp")
    row_at = row[None].astype(jnp.int32)
    col_at = col[None].astype(jnp.int32)
    other_rows = [((row + i) % n_row)[None].astype(jnp.int32) for i in range(n_row)]


    x = tokens.reshape(length, width).T
    g = cotangent.reshape(length, width).T
    place_in = col * n_row + row

    def between_owners(value_of, back):
        got = []
        for step in range(n_col):
            pairs = []
            for r in range(n_row):
                for c in range(n_col):
                    to = r * n_col + (c - step) % n_col
                    here, there = r * n_col + c, (to % n_row) * n_col + to // n_row
                    pairs.append((there, here) if back else (here, there))
            got.append(lax.ppermute(value_of(step), ("row", "col"), pairs))
        return got

    x_all = lax.all_gather(x, "col", axis=0, tiled=True)
    wq = w_qkv.transpose(0, 2, 1)
    w3_own = widen(wq, *edges(wq, 1, heads), 1, heads, col)
    w3_parts = [w3_own] + [turn(w3_own, "row", -step) for step in range(1, n_row)]
    w3 = row_join(w3_parts, 2).reshape(3 * window, depth)
    params = jnp.stack([ln1_gain, ln1_bias, ln2_gain, ln2_bias, out_bias, q_bias, v_bias])
    params = [turn(params, "col", step) for step in range(n_col)]
    params = jnp.concatenate(ordered(params, col, -1), 1)
    gain1, shift1, gain2, shift2, bias_out, bias_q, bias_v = [p[:, None] for p in params]
    bias3 = jnp.concatenate(
        [
            lax.dynamic_slice_in_dim(bias_q, begin, window, 0),
            jnp.zeros((window, 1), F32),
            lax.dynamic_slice_in_dim(bias_v, begin, window, 0),
        ]
    )
    up_parts = [w_up] + [turn(w_up, "row", -step) for step in range(1, n_row)]
    up_turned = row_join(up_parts, 0).T
    out_own = shares.take(w_out.T, dp, 0)
    down_own = shares.take(w_down.T, dp, 0)
    x_all, g, out_own, down_own, w3 = gate([x_all, g, out_own, down_own, w3], [up_turned, bias3])

    moved_out = [out_own] + [turn(out_own, "col", -step) for step in range(1, n_col)]
    moved_down = between_owners(
        lambda step: block(down_own, (col - step) % n_col, ff_part, 1), False
    )
    x_float = x_all.astype(F32)
    mean1, rstd1 = moments(x_float)
    n1 = ((x_float - mean1) * rstd1 * gain1 + shift1).astype(BF16)
    triple = product(w3, n1, bias3).reshape(3, window, length)
    triple, g, *rest = gate([triple, g] + moved_out[1:] + moved_down, [])
    moved_out = jnp.stack(ordered(moved_out[:1] + rest[: n_col - 1], col, 1))
    moved_down = jnp.stack(ordered(rest[n_col - 1 :], place_in, 1))

    g_all = lax.all_gather(g, "col", axis=0, tiled=True)
    pieces = [triple] + [turn(triple, "row", -step) for step in range(1, n_row)]
    near_out = [swap_with(moved_out, 1), swap_with(moved_out, 2)]
    *pieces, near_x, near_y, moved_down = gate(pieces[1:] + near_out + [moved_down], [])
    pieces, near_out = [triple] + pieces, [near_x, near_y]

    half = n_col // 2

    def to_diagonal(near):
        return [swap_with(near[0][:half], 2), swap_with(near[1][half:], 1)]

    far_out = to_diagonal(near_out)
    near_down = [swap_with(moved_down, 1), swap_with(moved_down, 2)]
    meta = jnp.stack(
        [
            jnp.array(heads.firsts, jnp.int32)[col],
            row,
            jnp.array(heads.first_mask, jnp.int32)[col],
            jnp.array(heads.last_mask, jnp.int32)[col],
        ]
    )
    *cuts, mixed, norms = attn_fwd(meta, key_start, pieces, heads.slots, size)
    *cuts, a, b, c, d = gate(list(cuts) + far_out + near_down, [])
    far_out, near_down = [a, b], [c, d]

    dp_at = dp[None].astype(jnp.int32)
    far_down = to_diagonal(near_down)
    mixed_own = row_sum(cuts).astype(BF16)
    out_weights = assemble([moved_out] + near_out + far_out, shares, dp_at)
    mixed_own, out_weights, g_all, *far_down = gate(
        [mixed_own, out_weights, g_all] + far_down, []
    )

    got = [
        turn(block(mixed_own, (col + step) % n_col, part, 1), "col", step) for step in range(n_col)
    ]
    out_weights = [turn(out_weights, "row", -step) for step in range(n_row)]
    down_weights = assemble([moved_down] + near_down + far_down, shares, dp_at)
    *rest, down_weights = gate(got[1:] + out_weights[1:] + [down_weights], [])
    got = got[:1] + rest[: n_col - 1]
    out_weights = out_weights[:1] + rest[n_col - 1 :]
    out_weights = [w.reshape(depth, in_rows) for w in out_weights]

    down_weights = [turn(down_weights, "row", -step) for step in range(n_row)]
    got = ordered(got, col, -1)
    lapped = [heads.firsts[j] * size for j in range(n_col)]
    attention = sum(
        jnp.pad(piece, ((at, depth - at - window), (0, 0))) for piece, at in zip(got, lapped)
    )
    branch = split_product(out_weights, attention, row_at, bias_out, F32)
    resid = block(x_all, col, part, 1).astype(F32) + branch
    mean2, rstd2 = moments(resid)
    hat2 = (resid - mean2) * rstd2
    n2_own = (hat2 * gain2 + shift2).astype(BF16)
    n2_own, *rest = gate([n2_own] + down_weights[1:], [hat2])
    down_weights = down_weights[:1] + rest
    down_weights = [w.reshape(depth, ff_part) for w in down_weights]

    n2_all = lax.all_gather(n2_own, "col", axis=1, tiled=True)
    down_turned = jnp.concatenate([w.T for w in down_weights])
    g_sums = jnp.sum(g.astype(F32), axis=1)
    n2_all, down_turned = gate([n2_all, down_turned], [g_sums])

    hidden_all, du_all, part2 = hidden_layer(
        up_turned, down_turned, n_row, up_bias[:, None], n2_all, g_all, row_at
    )
    part2, hidden_all, du_all = gate([part2, hidden_all, du_all], [])

    dn2 = lax.psum_scatter(part2, "col", scatter_dimension=1, tiled=True)
    up_grad = [token_product(n2_all, du_all, r, n_row, True) for r in other_rows[::-1]][::-1]
    up_grad = row_sum(up_grad).astype(BF16)
    down_grad = [token_product(g_all, hidden_all, r, n_row, False) for r in other_rows[::-1]][::-1]
    down_grad = [d.reshape(n_col, width, ff_part) for d in down_grad]
    down_grad = row_sum(down_grad).astype(BF16)
    no_bias = jnp.zeros((depth, 1), F32)
    shrunk = split_product(down_weights, hidden_all, row_at, no_bias, BF16)
    own_sum = block(shrunk, col, part, 1).astype(F32) + resid
    shrunk = lax.dynamic_update_slice_in_dim(shrunk, own_sum.astype(BF16), col * part, 1)
    du_sums = jnp.sum(du_all.astype(F32), axis=1)
    up_rows = width if in_rows % width == 0 else in_rows
    up_shares = Shares(up_rows)
    up_grad = up_grad.reshape(in_rows // up_rows, up_rows, ff)
    dn2, up_grad, down_grad, shrunk = gate([dn2, up_grad, down_grad, shrunk], [du_sums])

    dn2 = dn2.astype(F32)
    up2 = dn2 * gain2
    pull2 = jnp.mean(up2, axis=0, keepdims=True)
    lean2 = jnp.mean(up2 * hat2, axis=0, keepdims=True)
    dr = block(g_all, col, part, 1).astype(F32) + rstd2 * (up2 - pull2 - hat2 * lean2)
    db = dr.astype(BF16)
    da = split_product_tn(out_weights, db, row_at)
    sums2 = jnp.stack(
        [
            jnp.sum(db.astype(F32), axis=1),
            jnp.sum(dn2 * hat2, axis=1),
            jnp.sum(dn2, axis=1),
        ]
    )
    da, db, shrunk, up_grad, down_grad = gate([da, db, shrunk, up_grad, down_grad], [sums2])

    outputs = lax.psum_scatter(shrunk, "col", scatter_dimension=0, tiled=True)
    got = []
    for step in range(n_col):
        to = firsts[(col + step) % n_col]
        got.append(turn(lax.dynamic_slice_in_dim(da, to, window, 0), "col", step))

    def first_sums(value, cut, bit):
        near = swap_with(cut.take(value, dp ^ bit, 1), bit)
        return [near, swap_with(cut.take(value, dp ^ 3, 1), bit)]

    def relay(value, far, cut, bit):
        sent = cut.take(value, dp ^ (3 - bit), 1).astype(F32) + far.astype(F32)
        return swap_with(sent.astype(BF16), 3 - bit)

    def share_sum(value, cut, near, relayed):
        own = cut.take(value, dp, 1).astype(F32)
        return (own + near.astype(F32) + relayed.astype(F32)).astype(BF16)

    up_first = first_sums(up_grad, up_shares, 1)
    down_first = first_sums(down_grad, shares, 2)
    out_grad = [token_product(db, attention, r, n_row, False) for r in other_rows[::-1]][::-1]
    out_grad = [o.reshape(n_col, width, in_rows) for o in out_grad]
    rest = gate(got[1:] + out_grad + up_first + down_first, [])
    got, rest = got[:1] + rest[: n_col - 1], rest[n_col - 1 :]
    out_grad, up_first, down_first = rest[:n_row], rest[n_row : n_row + 2], rest[n_row + 2 :]

    da_own = jnp.concatenate(ordered(got, col, -1), 1)
    da_pieces = [da_own] + [turn(da_own, "row", -step) for step in range(1, n_row)]
    up_relay = relay(up_grad, up_first[1], up_shares, 1)
    down_relay = relay(down_grad, down_first[1], shares, 2)
    out_grad = row_sum(out_grad).astype(BF16)
    *rest, out_grad, up_relay, down_relay = gate(
        da_pieces[1:] + [out_grad, up_relay, down_relay], []
    )
    da_pieces = [da_own] + rest

    out_first = first_sums(out_grad, shares, 1)
    dqkv = attn_bwd(meta, key_start, pieces, da_pieces, mixed, norms, heads.slots, size)
    *dqkv, outputs, down_relay, a, b = gate(list(dqkv) + [outputs, down_relay] + out_first, [])
    out_first = [a, b]

    down_share = share_sum(down_grad, shares, down_first[0], down_relay)
    down_home = between_owners(lambda step: pick(down_share, (place_in + step) % n_col), True)
    out_relay = relay(out_grad, out_first[1], shares, 1)
    dqkv = row_sum(dqkv).astype(BF16).reshape(3 * window, length)
    dqkv, out_relay, up_relay, *down_home = gate([dqkv, out_relay, up_relay] + down_home, [])

    out_share = share_sum(out_grad, shares, out_first[0], out_relay)
    out_home = [turn(pick(out_share, (col + step) % n_col), "col", step) for step in range(n_col)]
    up_share = share_sum(up_grad, up_shares, up_first[0], up_relay)
    up_near = [swap_with(up_share, 1), swap_with(up_share, 2)]
    dn1, stats, norm1 = norm_product_tn(w3, dqkv, n1, gain1, shift1, rstd1)
    riding = block(dn1, col, part, 1).astype(F32) + dr
    dn1 = lax.dynamic_update_slice_in_dim(dn1, riding.astype(BF16), col * part, 1)
    dn1, dqkv, stats, norm1, *rest = gate([dn1, dqkv, stats, norm1] + out_home[1:] + up_near, [])
    out_home, up_near = out_home[:1] + rest[: n_col - 1], rest[n_col - 1 :]

    dx = lax.psum_scatter(dn1, "col", scatter_dimension=0, tiled=True)
    qkv_parts = [token_product(dqkv, n1, r, n_row, False) for r in other_rows[::-1]][::-1]
    qkv_parts = [q.reshape(3, window, in_rows) for q in qkv_parts]
    qkv_grad = row_sum(qkv_parts).astype(BF16)
    up_half = up_share.shape[1] // 2 // 16 * 16
    up_far = [swap_with(up_near[0][:, :up_half], 2), swap_with(up_near[1][:, up_half:], 1)]
    out_home = sum(o.astype(F32) for o in out_home).astype(BF16)
    homes = jnp.stack([out_home] + ordered(down_home, col, -1))
    homes_near = [swap_with(homes, 1), swap_with(homes, 2)]
    stats = sum(turn(stats, "col", step) for step in range(n_col)) / depth
    dq_dv = jnp.sum(dqkv.astype(F32), axis=1).reshape(3, window)
    sums = lax.dynamic_update_slice_in_dim(jnp.zeros((2, depth), F32), dq_dv[::2], begin, 1)
    sums = jnp.concatenate([sums, (norm1[:, :1] / gain1).T, norm1[:, 1:].T, sums2]).reshape(-1)
    small = jnp.concatenate([sums, du_sums, g_sums])[None]
    small = small_sum(small, ("row",))
    outputs = (outputs.astype(F32) + down_bias[:, None]).astype(BF16)
    qkv_grad, small, *rest = gate([qkv_grad, small] + up_far + homes_near, [stats, outputs])
    up_far, homes_near = rest[:2], rest[2:]

    wide, front, tail = narrow_edges(qkv_grad, 1, heads, col, width)
    homes_far = [swap_with(homes_near[0][:2], 2), swap_with(homes_near[1][2:], 1)]
    small = small_sum(small, ("dp",))[0]
    up_grad = up_shares.join(
        [up_share] + up_near + [jnp.concatenate(up_far, 1)], dp, 1
    ).astype(F32)
    up_grad = up_grad.reshape(in_rows, ff)
    front, tail, small, *homes_far = gate([front, tail, small] + homes_far, [up_grad])

    qkv_grad = narrow(wide, front, tail, 1, heads, width).astype(BF16)
    qkv_got = [swap_with(shares.take(qkv_grad, dp ^ m, 1), m) for m in (1, 2, 3)]
    sums, local = small[: 7 * depth].reshape(7, depth), small[7 * depth :]
    sums = small_sum(sums, ("col",))
    sums = lax.dynamic_slice_in_dim(sums, col * width, width, 1)
    homes = shares.join(
        [homes] + homes_near + [jnp.concatenate(homes_far)], dp, 1
    ).astype(F32)
    out_grad = homes[0]
    down_grad = jnp.concatenate([homes[1 + j] for j in range(n_col)], 1)
    qkv_got = gate(qkv_got, [out_grad, down_grad, sums])

    qkv_share = shares.take(qkv_grad, dp, 1).astype(F32)
    qkv_share = (qkv_share + sum(q.astype(F32) for q in qkv_got)).astype(BF16)
    qkv_all = swap_all(qkv_share)
    hat1 = (x.astype(F32) - mean1) * rstd1
    input_grad = (dx.astype(F32) - rstd1 * (stats[0:1] + hat1 * stats[1:2])).astype(BF16)
    qkv_grad = shares.join([qkv_share] + qkv_all, dp, 1).astype(F32)
    return (
        outputs.T.reshape(tokens.shape),
        input_grad.T.reshape(tokens.shape),
        qkv_grad.transpose(0, 2, 1),
        sums[0],
        sums[1],
        out_grad.T,
        sums[4],
        up_grad,
        local[:ff],
        down_grad.T,
        local[ff:],
        sums[2],
        sums[3],
        sums[5],
        sums[6],
    )


def solution(mesh):
    inputs = (
        P("dp", "row", "col"),
        P("dp", "row", "col"),
        P(None, "row", "col"),
        P("col"),
        P("col"),
        P("row", "col"),
        P("col"),
        P("row", "col"),
        P("col"),
        P("row", "col"),
        P("col"),
        P("col"),
        P("col"),
        P("col"),
        P("col"),
        P(),
    )
    return jax.shard_map(
        body, mesh=mesh, in_specs=inputs, out_specs=inputs[:15], check_vma=False
    )
```

time: 1140 us -> 765 us (0.67)
  waiting for transfers between devices: 379 us -> 238 us
  Pallas kernels: 48.5 us -> 178 us
  starting transfers between devices: 228 us -> 119 us
  matrix products: 108 us -> 0 us
  local copies, waits for them, and re-layouts: 175 us -> 83.6 us
  blocking collectives: 78.4 us -> 0 us
  other arithmetic: 89.8 us -> 118 us
    ppermute x39 -> x30, waiting for transfers between devices: 255 us -> 57.8 us  [turn(): lax.ppermute(value, axis, [(i, (i + steps) % size) for i in range(size)])]
    pallas_call x0 -> x35, Pallas kernels: none -> 131 us  [the longest x8 50 us: token_product(): pl.pallas_call(kernel, out_shape=jax.ShapeDtypeStruct((rows_a, rows_b), B...]
    dot_general x26 -> x0, matrix products: 108 us -> none  [the longest x10 42.7 us: dot_tn(): return lax.dot_general(a, b, NT, preferred_element_type=F32)]
    ppermute x39 -> x30, starting transfers between devices: 127 us -> 33.8 us  [turn(): lax.ppermute(value, axis, [(i, (i + steps) % size) for i in range(size)])]
    dynamic_update_slice x15 -> x2, local copies, waits for them, and re-layouts: 74.9 us -> 0.64 us  [the longest x1 0.39 us: narrow_edges(): lax.dynamic_update_slice_in_dim(jnp.zeros(shape, value.dtype), value, edg...]
    psum x2 -> x0, blocking collectives: 63.7 us -> none  [small_sum(): return lax.psum(value, axes)]
    all_gather x2, waiting for transfers between devices: 0.01 us -> 46.7 us  [the longest x1 46.7 us: body(): n2_all = lax.all_gather(n2_own, 'col', axis=1, tiled=True)]
    ppermute x12 -> x17, starting transfers between devices: 81.6 us -> 49.8 us  [the longest x8 36.2 us: between_owners(): got.append(lax.ppermute(value_of(step), ('row', 'col'), pairs))]
  transfers between devices with their start and end apart: 70 -> 84, of which waited for: 24 -> 28; matrix products, arithmetic and copies ran while one was open for 31% -> 24% of each run, Pallas kernels for 4% -> 18%
where the time goes in v1:
time: 765 us; the launch traced here: 753 us
  waiting for transfers between devices  238 us (31%)
  Pallas kernels  178 us (23%)
  starting transfers between devices  119 us (16%)
  other arithmetic  118 us (15%)
  local copies, waits for them, and re-layouts  83.6 us (11%)
  between operations  16.3 us (2%)
    ppermute x31, waiting for transfers between devices, swap_with(): return lax.ppermute(value, 'dp', [(i, i ^ bit) for i in range(4)])  82.9 us
    ppermute x30, waiting for transfers between devices, turn(): lax.ppermute(value, axis, [(i, (i + steps) % size) for i in range(size)])  57.8 us
    pallas_call x8, Pallas kernels, token_product(): pl.pallas_call(kernel, out_shape=jax.ShapeDtypeStruct((rows_a, rows_b), B...  50 us
    all_gather x1, waiting for transfers between devices, body(): n2_all = lax.all_gather(n2_own, 'col', axis=1, tiled=True)  46.7 us
    ppermute x8, starting transfers between devices, between_owners(): got.append(lax.ppermute(value_of(step), ('row', 'col'), pairs))  36.2 us
    ppermute x31, starting transfers between devices, swap_with(): return lax.ppermute(value, 'dp', [(i, i ^ bit) for i in range(4)])  34.7 us
    ppermute x30, starting transfers between devices, turn(): lax.ppermute(value, axis, [(i, (i + steps) % size) for i in range(size)])  33.8 us
    pallas_call x1, Pallas kernels, attn_bwd(): pl.pallas_call(functools.partial(bwd_kernel, n_row, n_slots, hd, ks.shape...  27.7 us
  transfers between devices with their start and end apart: 84, of which 28 were waited for; matrix products, arithmetic and copies ran while one was open for 24% of the time, Pallas kernels for 18%

profile of v1, /device:TPU:0, one launch (start us, length us, event | category | flops | bytes accessed | tf_op | source)
XLA Modules:
  0.0 753.3 jit_solution(2715746926399682322)
XLA Ops:
  11.3 4.9 collective-permute-start
  17.7 4.3 collective-permute-done
  25.8 4.4 fusion.9
  38.9 4.3 copy.173
  51.8 5.2 copy.174
  59.4 4.1 maximum_bitcast_fusion.refs_5_.up_ref
  63.5 23.5 %all-gather.4.cloned.1.call-done.refs_0_ = bf16[1600,1024]{1,0:T(8,128)(2,1)} async-done(((bf16[400,1024]{1,0:T(8,128)(2,1)}), bf16[1600,1024]{1,0:T(8,128)(2,1)}) %all-gather.4.cloned.1.call-update) | async-done | bytes 3276816 | tf_op jit(solution)/shard_map/all_gather | solution.py:694
  94.3 4.2 collective-permute-start.11
  98.6 16.4 %collective-permute-start.12 = (bf16[112,800]{1,0:T(8,128)(2,1)S(1)}, bf16[112,800]{1,0:T(8,128)(2,1)S(1)}, u32[]{:S(2)}, u32[]{:S(2)}) collective-permute-start(bf16[112,800]{1,0:T(8,128)(2,1)S(1)} %get-tuple-element.318), channel_id=1, source_target_pairs={{0,1},{1,5},{2,0},{3,4},{4,3},{5,7},{6,2},{7,6},{8,9},{9,13},{10,8... | collective-permute-start | bytes 537608 | tf_op jit(solution)/shard_map/ppermute | solution.py:691
  121.2 9.4 %shard_map.488 = bf16[1344,1024]{1,0:T(8,128)(2,1)} custom-call(bf16[1344,1600]{1,0:T(8,128)(2,1)} %get-tuple-element.126.a_ref, bf16[1600,1024]{1,0:T(8,128)(2,1)} %fusion.5.b_ref.n_ref, f32[1344,1]{1,0:T(8,128)} %copy.177.refs_6_.bias_ref), custom_call_target="tpu_custom_call" | custom-call | tf_op jit(solution)/shard_map/pallas_call | solution.py:189
  140.2 15.3 %collective-permute-done.15.refs_1_ = bf16[4,112,800]{2,1,0:T(8,128)(2,1)} collective-permute-done((bf16[4,112,800]{2,1,0:T(8,128)(2,1)}, bf16[4,112,800]{2,1,0:T(8,128)(2,1)}, u32[]{:S(2)}, u32[]{:S(2)}) %collective-permute-start.15) | collective-permute-done | bytes 716832 | tf_op jit(solution)/shard_map/ppermute | solution.py:455
  167.1 19.3 %shard_map.491 = (bf16[448,1024]{1,0:T(8,128)(2,1)S(1)}, bf16[448,1024]{1,0:T(8,128)(2,1)S(1)}, bf16[448,2048]{1,0:T(8,128)(2,1)S(1)}, f32[7,2048]{1,0:T(8,128)S(1)}) custom-call(s32[4]{0:T(128)S(1)} %pad_add_fusion.1.meta, s32[25,4]{1,0:T(8,128)S(1)} %copy.183.ks, bf16[3,448,1024]{2,1,0:T(8,128)(2,1)} %get-tuple-element.131.refs_0_, ...), custom_call_target="tpu_custom_call" | custom-call | tf_op jit(solution)/shard_map/pallas_call | solution.py:148
  217.3 9.4 %collective-permute-done.25.refs_1_ = bf16[448,256]{1,0:T(8,128)(2,1)} collective-permute-done((bf16[448,256]{1,0:T(8,128)(2,1)S(1)}, bf16[448,256]{1,0:T(8,128)(2,1)}, u32[]{:S(2)}, u32[]{:S(2)}) %collective-permute-start.25) | collective-permute-done | bytes 229408 | tf_op jit(solution)/shard_map/ppermute | solution.py:440
  230.3 6.1 shard_map.497
  244.4 6.7 pad_maximum_fusion
  251.1 9.7 %copy.181.refs_1_ = bf16[1600,1600]{1,0:T(8,128)(2,1)} copy(bf16[1600,1600]{0,1:T(8,128)(2,1)} %pad_maximum_fusion) | data formatting | bytes 10240000 | tf_op jit(solution)/shard_map/concatenate | solution.py:787
  260.8 46.7 %all-gather.8.cloned.1.call-done.refs_0_ = bf16[1600,1024]{1,0:T(8,128)(2,1)} async-done(((bf16[1600,256]{1,0:T(8,128)(2,1)}), bf16[1600,1024]{1,0:T(8,128)(2,1)}) %all-gather.8.cloned.1.call-update) | async-done | bytes 3276816 | tf_op jit(solution)/shard_map/all_gather | solution.py:786
  307.5 27.3 %shard_map.500 = (bf16[1600,1024]{1,0:T(8,128)(2,1)}, bf16[1600,1024]{1,0:T(8,128)(2,1)}, bf16[1600,1024]{1,0:T(8,128)(2,1)}) custom-call(s32[1]{0:T(128)} %bitcast.1.row_ref, bf16[1600,1600]{1,0:T(8,128)(2,1)} %maximum_bitcast_fusion.refs_5_.up_ref, bf16[1600,1600]{1,0:T(8,128)(2,1)} %get-tuple-element.164.down_ref, f32[1600,1]{1,0:T(8,128)} %broadcast_in_dim.44.bias_ref, ...), custom_call_target="tpu_custom_call" | custom-call | tf_op jit(solution)/shard_map/pallas_call | solution.py:392
  335.4 7.3 shard_map.505
  342.7 6.7 shard_map.503
  349.9 7.2 shard_map.504
  357.1 6.7 shard_map.502
  364.7 11.3 %shard_map.506 = bf16[1600,1024]{1,0:T(8,128)(2,1)} custom-call(s32[1]{0:T(128)} %bitcast.1.row_ref, bf16[1600,1024]{1,0:T(8,128)(2,1)} %get-tuple-element.171.b_ref, f32[1600,1]{1,0:T(8,128)} %broadcast_in_dim.40.bias_ref, bf16[1600,800]{1,0:T(8,128)(2,1)} %bitcast.207, bf16[1600,800]{1,0:T(8,128)(2,1)} %bitcast.51.refs_1_), custom_call_target="tpu_custom_call" | custom-call | tf_op jit(solution)/shard_map/pallas_call | solution.py:217
  380.0 4.3 fusion.6.refs_2_
  388.3 7.3 reduce-scatter.4.cloned.1.call-done.refs_0_
  400.4 6.8 shard_map.508.refs_0_
  415.2 12.7 %collective-permute-done.31.refs_0_ = bf16[448,256]{1,0:T(8,128)(2,1)} collective-permute-done((bf16[448,256]{1,0:T(8,128)(2,1)S(1)}, bf16[448,256]{1,0:T(8,128)(2,1)}, u32[]{:S(2)}, u32[]{:S(2)}) %collective-permute-start.31) | collective-permute-done | bytes 229408 | tf_op jit(solution)/shard_map/ppermute | solution.py:440
  427.9 9.6 %collective-permute-start.32 = (bf16[448,256]{1,0:T(8,128)(2,1)S(1)}, bf16[448,256]{1,0:T(8,128)(2,1)}, u32[]{:S(2)}, u32[]{:S(2)}) collective-permute-start(bf16[448,256]{1,0:T(8,128)(2,1)S(1)} %get-tuple-element.300), channel_id=1, source_target_pairs={{0,2},{1,3},{2,0},{3,1},{4,6},{5,7},{6,4},{7,5},{8,10},{9,11},{10,... | collective-permute-start | bytes 688136 | tf_op jit(solution)/shard_map/ppermute | solution.py:440
  437.5 22.3 %collective-permute-done.32.refs_1_ = bf16[448,256]{1,0:T(8,128)(2,1)} collective-permute-done((bf16[448,256]{1,0:T(8,128)(2,1)S(1)}, bf16[448,256]{1,0:T(8,128)(2,1)}, u32[]{:S(2)}, u32[]{:S(2)}) %collective-permute-start.32) | collective-permute-done | bytes 229408 | tf_op jit(solution)/shard_map/ppermute | solution.py:440
  460.5 4.6 shard_map.511
  465.1 4.6 shard_map.510
  469.8 6.2 collective-permute-done.33.refs_2_
  486.7 11.5 %collective-permute-done.41.refs_3_ = bf16[4,112,800]{2,1,0:T(8,128)(2,1)} collective-permute-done((bf16[4,112,800]{2,1,0:T(8,128)(2,1)S(1)}, bf16[4,112,800]{2,1,0:T(8,128)(2,1)}, u32[]{:S(2)}, u32[]{:S(2)}) %collective-permute-start.41) | collective-permute-done | bytes 716832 | tf_op jit(solution)/shard_map/ppermute | solution.py:455
  505.3 27.7 %shard_map.514 = (bf16[3,448,1024]{2,1,0:T(8,128)(2,1)}, bf16[3,448,1024]{2,1,0:T(8,128)(2,1)}) custom-call(s32[4]{0:T(128)} %copy-done.8, s32[25,4]{1,0:T(8,128)} %copy-done.6, bf16[3,448,1024]{2,1,0:T(8,128)(2,1)} %get-tuple-element.131.refs_0_, bf16[3,448,1024]{2,1,0:T(8,128)(2,1)} %get-tuple-element.139.refs_1_, bf16[448,1024]{1,0:T(8,128)(2,1)} %copy-done.32, ...), custom_call_target="tpu_custom_call" | custom-call | tf_op jit(solution)/shard_map/pallas_call | solution.py:157
  533.0 6.9 collective-permute-done.43.refs_5_
  554.2 5.4 collective-permute-start.49
  559.7 4.6 add_convert_fusion.1
  577.7 13.5 %shard_map.517 = (bf16[1600,1024]{1,0:T(8,128)(2,1)}, f32[2,1024]{1,0:T(2,128)}, f32[1600,2]{1,0:T(8,128)}) custom-call(bf16[1344,1600]{1,0:T(8,128)(2,1)} %get-tuple-element.126.a_ref, bf16[1344,1024]{1,0:T(8,128)(2,1)} %get-tuple-element.202.b_ref.refs_1_, bf16[1600,1024]{1,0:T(8,128)(2,1)} %fusion.5.b_ref.n_ref, f32[1600,1]{1,0:T(8,128)} %copy.184.g_ref, ...), custom_call_target="tpu_custom_call" | custom-call | tf_op jit(solution)/shard_map/pallas_call | solution.py:295
  594.7 6.5 shard_map.520
  612.7 4.1 collective-permute-done.55
  617.8 6.4 shard_map.519
  635.3 6.0 collective-permute-done.60.refs_2_
  661.2 5.8 collective-permute-done.67
  667.7 4.9 collective-permute-done.65.refs_1_
  690.1 6.9 concatenate.59.refs_4_
  699.1 12.0 %collective-permute-done.71.refs_1_ = bf16[3,112,800]{2,1,0:T(8,128)(2,1)S(1)} collective-permute-done((bf16[3,112,800]{2,1,0:T(8,128)(2,1)}, bf16[3,112,800]{2,1,0:T(8,128)(2,1)S(1)}, u32[]{:S(2)}, u32[]{:S(2)}) %collective-permute-start.71) | collective-permute-done | bytes 537632 | tf_op jit(solution)/shard_map/ppermute | solution.py:455
  721.8 8.7 %collective-permute-done.75 = bf16[3,112,800]{2,1,0:T(8,128)(2,1)S(1)} collective-permute-done((bf16[3,112,800]{2,1,0:T(8,128)(2,1)S(1)}, bf16[3,112,800]{2,1,0:T(8,128)(2,1)S(1)}, u32[]{:S(2)}, u32[]{:S(2)}) %collective-permute-start.75) | collective-permute-done | bytes 537632 | tf_op jit(solution)/shard_map/ppermute | solution.py:455
  730.4 9.6 %collective-permute-done.76 = bf16[3,112,800]{2,1,0:T(8,128)(2,1)S(1)} collective-permute-done((bf16[3,112,800]{2,1,0:T(8,128)(2,1)S(1)}, bf16[3,112,800]{2,1,0:T(8,128)(2,1)S(1)}, u32[]{:S(2)}, u32[]{:S(2)}) %collective-permute-start.76) | collective-permute-done | bytes 537632 | tf_op jit(solution)/shard_map/ppermute | solution.py:455
  (479 shorter events, 257.7 us)
Async XLA Ops:
  7.2 79.8 %all-gather.4.cloned.1.call-start = ((), (), s32[]{:S(2)}) async-start(), calls=%async_computation.3 | async-start | bytes 4096000 | tf_op jit(solution)/shard_map/all_gather | solution.py:694
  17.6 187.8 %all-gather.6.cloned.1.call-start = ((), (), s32[]{:S(2)}) async-start(), calls=%async_computation.4 | async-start | bytes 4096000 | tf_op jit(solution)/shard_map/all_gather | solution.py:728
  30.2 21.6 %collective-permute-start.3 = (bf16[800,1600]{1,0:T(8,128)(2,1)}, bf16[800,1600]{1,0:T(8,128)(2,1)}, u32[]{:S(2)}, u32[]{:S(2)}) collective-permute-start(bf16[800,1600]{1,0:T(8,128)(2,1)} %param.47), channel_id=1, source_target_pairs={{0,4},{4,0},{1,5},{5,1},{2,6},{6,2},{3,7},{7,3},{8,12},{12,8},{9,1... | collective-permute-start | bytes 7680008 | tf_op jit(solution)/shard_map/ppermute | solution.py:440
  87.0 43.6 %collective-permute-start.7 = (bf16[112,800]{1,0:T(8,128)(2,1)}, bf16[112,800]{1,0:T(8,128)(2,1)S(1)}, u32[]{:S(2)}, u32[]{:S(2)}) collective-permute-start(bf16[112,800]{1,0:T(8,128)(2,1)} %get-tuple-element.129), channel_id=1, source_target_pairs={{0,3},{1,0},{2,1},{3,2},{4,7},{5,4},{6,5},{7,6},{8,11},{9,8},{10,9... | collective-permute-start | bytes 537608 | tf_op jit(solution)/shard_map/ppermute | solution.py:440
  87.8 42.9 %collective-permute-start.8 = (bf16[112,800]{1,0:T(8,128)(2,1)}, bf16[112,800]{1,0:T(8,128)(2,1)S(1)}, u32[]{:S(2)}, u32[]{:S(2)}) collective-permute-start(bf16[112,800]{1,0:T(8,128)(2,1)} %get-tuple-element.129), channel_id=1, source_target_pairs={{0,2},{1,3},{2,0},{3,1},{4,6},{5,7},{6,4},{7,5},{8,10},{9,11},{10,... | collective-permute-start | bytes 537608 | tf_op jit(solution)/shard_map/ppermute | solution.py:440
  87.8 42.9 %collective-permute-start.9 = (bf16[112,800]{1,0:T(8,128)(2,1)}, bf16[112,800]{1,0:T(8,128)(2,1)S(1)}, u32[]{:S(2)}, u32[]{:S(2)}) collective-permute-start(bf16[112,800]{1,0:T(8,128)(2,1)} %get-tuple-element.129), channel_id=1, source_target_pairs={{0,1},{1,2},{2,3},{3,0},{4,5},{5,6},{6,7},{7,4},{8,9},{9,10},{10,1... | collective-permute-start | bytes 537608 | tf_op jit(solution)/shard_map/ppermute | solution.py:440
  94.3 20.7 %collective-permute-start.11 = (bf16[112,800]{1,0:T(8,128)(2,1)S(1)}, bf16[112,800]{1,0:T(8,128)(2,1)S(1)}, u32[]{:S(2)}, u32[]{:S(2)}) collective-permute-start(bf16[112,800]{1,0:T(8,128)(2,1)S(1)} %get-tuple-element.319), channel_id=1, source_target_pairs={{0,5},{1,0},{2,4},{3,1},{4,7},{5,2},{6,6},{7,3},{8,13},{9,8},{10,1... | collective-permute-start | bytes 537608 | tf_op jit(solution)/shard_map/ppermute | solution.py:691
  98.6 32.0 %collective-permute-start.12 = (bf16[112,800]{1,0:T(8,128)(2,1)S(1)}, bf16[112,800]{1,0:T(8,128)(2,1)S(1)}, u32[]{:S(2)}, u32[]{:S(2)}) collective-permute-start(bf16[112,800]{1,0:T(8,128)(2,1)S(1)} %get-tuple-element.318), channel_id=1, source_target_pairs={{0,1},{1,5},{2,0},{3,4},{4,3},{5,7},{6,2},{7,6},{8,9},{9,13},{10,8... | collective-permute-start | bytes 537608 | tf_op jit(solution)/shard_map/ppermute | solution.py:691
  131.6 176.0 %all-gather.8.cloned.1.call-start = ((), (), s32[]{:S(2)}) async-start(), calls=%async_computation.5 | async-start | bytes 4096000 | tf_op jit(solution)/shard_map/all_gather | solution.py:786
  131.6 25.1 %collective-permute-start.14 = (bf16[3,448,1024]{2,1,0:T(8,128)(2,1)}, bf16[3,448,1024]{2,1,0:T(8,128)(2,1)}, u32[]{:S(2)}, u32[]{:S(2)}) collective-permute-start(bf16[3,448,1024]{2,1,0:T(8,128)(2,1)} %get-tuple-element.131.refs_0_), channel_id=1, source_target_pairs={{0,4},{4,0},{1,5},{5,1},{2,6},{6,2},{3,7},{7,3},{8,12},{12,8},{9,1... | collective-permute-start | bytes 8257544 | tf_op jit(solution)/shard_map/ppermute | solution.py:440
  134.9 20.7 %collective-permute-start.15 = (bf16[4,112,800]{2,1,0:T(8,128)(2,1)}, bf16[4,112,800]{2,1,0:T(8,128)(2,1)}, u32[]{:S(2)}, u32[]{:S(2)}) collective-permute-start(bf16[4,112,800]{2,1,0:T(8,128)(2,1)} %pad_maximum_fusion.10.refs_0_), channel_id=1, source_target_pairs={{0,8},{8,0},{16,24},{24,16},{1,9},{9,1},{17,25},{25,17},{2,10},{10... | collective-permute-start | bytes 2150408 | tf_op jit(solution)/shard_map/ppermute | solution.py:455
  136.3 20.4 %collective-permute-start.16 = (bf16[4,112,800]{2,1,0:T(8,128)(2,1)}, bf16[4,112,800]{2,1,0:T(8,128)(2,1)}, u32[]{:S(2)}, u32[]{:S(2)}) collective-permute-start(bf16[4,112,800]{2,1,0:T(8,128)(2,1)} %pad_maximum_fusion.10.refs_0_), channel_id=1, source_target_pairs={{0,16},{8,24},{16,0},{24,8},{1,17},{9,25},{17,1},{25,9},{2,18},{10... | collective-permute-start | bytes 2150408 | tf_op jit(solution)/shard_map/ppermute | solution.py:455
  156.7 33.4 %collective-permute-start.19 = (bf16[4,112,800]{2,1,0:T(8,128)(2,1)}, bf16[4,112,800]{2,1,0:T(8,128)(2,1)}, u32[]{:S(2)}, u32[]{:S(2)}) collective-permute-start(bf16[4,112,800]{2,1,0:T(8,128)(2,1)} %get-tuple-element.144.refs_0_), channel_id=1, source_target_pairs={{0,8},{8,0},{16,24},{24,16},{1,9},{9,1},{17,25},{25,17},{2,10},{10... | collective-permute-start | bytes 2150408 | tf_op jit(solution)/shard_map/ppermute | solution.py:455
  157.3 32.9 %collective-permute-start.20 = (bf16[4,112,800]{2,1,0:T(8,128)(2,1)}, bf16[4,112,800]{2,1,0:T(8,128)(2,1)}, u32[]{:S(2)}, u32[]{:S(2)}) collective-permute-start(bf16[4,112,800]{2,1,0:T(8,128)(2,1)} %get-tuple-element.144.refs_0_), channel_id=1, source_target_pairs={{0,16},{8,24},{16,0},{24,8},{1,17},{9,25},{17,1},{25,9},{2,18},{10... | collective-permute-start | bytes 2150408 | tf_op jit(solution)/shard_map/ppermute | solution.py:455
  160.6 29.5 %collective-permute-start.17 = (bf16[2,112,800]{2,1,0:T(8,128)(2,1)}, bf16[2,112,800]{2,1,0:T(8,128)(2,1)}, u32[]{:S(2)}, u32[]{:S(2)}) collective-permute-start(bf16[2,112,800]{2,1,0:T(8,128)(2,1)} %slice.131), channel_id=1, source_target_pairs={{0,16},{8,24},{16,0},{24,8},{1,17},{9,25},{17,1},{25,9},{2,18},{10... | collective-permute-start | bytes 1075208 | tf_op jit(solution)/shard_map/ppermute | solution.py:455
  162.9 27.2 %collective-permute-start.18 = (bf16[2,112,800]{2,1,0:T(8,128)(2,1)}, bf16[2,112,800]{2,1,0:T(8,128)(2,1)}, u32[]{:S(2)}, u32[]{:S(2)}) collective-permute-start(bf16[2,112,800]{2,1,0:T(8,128)(2,1)} %slice.132), channel_id=1, source_target_pairs={{0,8},{8,0},{16,24},{24,16},{1,9},{9,1},{17,25},{25,17},{2,10},{10... | collective-permute-start | bytes 1075208 | tf_op jit(solution)/shard_map/ppermute | solution.py:455
  205.4 21.3 %collective-permute-start.27 = (bf16[4,400,800]{2,1,0:T(8,128)(2,1)}, bf16[4,400,800]{2,1,0:T(8,128)(2,1)}, u32[]{:S(2)}, u32[]{:S(2)}) collective-permute-start(bf16[4,400,800]{2,1,0:T(8,128)(2,1)} %get-tuple-element.154), channel_id=1, source_target_pairs={{0,4},{4,0},{1,5},{5,1},{2,6},{6,2},{3,7},{7,3},{8,12},{12,8},{9,1... | collective-permute-start | bytes 7680008 | tf_op jit(solution)/shard_map/ppermute | solution.py:440
  240.6 154.9 %reduce-scatter.4.cloned.1.call-start = ((), (), s32[]{:S(2)}) async-start(), calls=%async_computation.6 | async-start | bytes 4096000 | tf_op jit(solution)/shard_map/reduce_scatter | solution.py:796
  334.9 205.0 %reduce-scatter.6.cloned.1.call-start = ((), (), s32[]{:S(2)}) async-start(), calls=%async_computation.7 | async-start | bytes 4096000 | tf_op jit(solution)/shard_map/reduce_scatter | solution.py:828
  342.7 37.3 %collective-permute-start.30 = (bf16[4,400,800]{2,1,0:T(8,128)(2,1)}, bf16[4,400,800]{2,1,0:T(8,128)(2,1)}, u32[]{:S(2)}, u32[]{:S(2)}) collective-permute-start(bf16[4,400,800]{2,1,0:T(8,128)(2,1)} %bitcast.222), channel_id=1, source_target_pairs={{0,4},{4,0},{1,5},{5,1},{2,6},{6,2},{3,7},{7,3},{8,12},{12,8},{9,1... | collective-permute-start | bytes 7680008 | tf_op jit(solution)/shard_map/ppermute | solution.py:440
  349.4 34.9 %collective-permute-start.29 = (bf16[800,1600]{1,0:T(8,128)(2,1)}, bf16[800,1600]{1,0:T(8,128)(2,1)}, u32[]{:S(2)}, u32[]{:S(2)}) collective-permute-start(bf16[800,1600]{1,0:T(8,128)(2,1)} %shard_map.503), channel_id=1, source_target_pairs={{0,4},{4,0},{1,5},{5,1},{2,6},{6,2},{3,7},{7,3},{8,12},{12,8},{9,1... | collective-permute-start | bytes 7680008 | tf_op jit(solution)/shard_map/ppermute | solution.py:440
  407.8 335.6 %reduce-scatter.8.cloned.1.call-start = ((), (), s32[]{:S(2)}) async-start(), calls=%async_computation.8 | async-start | bytes 4096000 | tf_op jit(solution)/shard_map/reduce_scatter | solution.py:885
  409.7 66.3 %collective-permute-start.36 = (bf16[4,112,800]{2,1,0:T(8,128)(2,1)S(1)}, bf16[4,112,800]{2,1,0:T(8,128)(2,1)}, u32[]{:S(2)}, u32[]{:S(2)}) collective-permute-start(bf16[4,112,800]{2,1,0:T(8,128)(2,1)S(1)} %get-tuple-element.272), channel_id=1, source_target_pairs={{0,16},{8,24},{16,0},{24,8},{1,17},{9,25},{17,1},{25,9},{2,18},{10... | collective-permute-start | bytes 2150408 | tf_op jit(solution)/shard_map/ppermute | solution.py:455
  411.2 64.7 %collective-permute-start.37 = (bf16[4,112,800]{2,1,0:T(8,128)(2,1)S(1)}, bf16[4,112,800]{2,1,0:T(8,128)(2,1)}, u32[]{:S(2)}, u32[]{:S(2)}) collective-permute-start(bf16[4,112,800]{2,1,0:T(8,128)(2,1)S(1)} %get-tuple-element.271), channel_id=1, source_target_pairs={{0,16},{8,24},{16,0},{24,8},{1,17},{9,25},{17,1},{25,9},{2,18},{10... | collective-permute-start | bytes 2150408 | tf_op jit(solution)/shard_map/ppermute | solution.py:455
  411.9 64.1 %collective-permute-start.34 = (bf16[2,112,1600]{2,1,0:T(8,128)(2,1)S(1)}, bf16[2,112,1600]{2,1,0:T(8,128)(2,1)}, u32[]{:S(2)}, u32[]{:S(2)}) collective-permute-start(bf16[2,112,1600]{2,1,0:T(8,128)(2,1)S(1)} %get-tuple-element.276), channel_id=1, source_target_pairs={{0,8},{8,0},{16,24},{24,16},{1,9},{9,1},{17,25},{25,17},{2,10},{10... | collective-permute-start | bytes 2150408 | tf_op jit(solution)/shard_map/ppermute | solution.py:455
  413.4 62.6 %collective-permute-start.35 = (bf16[2,112,1600]{2,1,0:T(8,128)(2,1)S(1)}, bf16[2,112,1600]{2,1,0:T(8,128)(2,1)}, u32[]{:S(2)}, u32[]{:S(2)}) collective-permute-start(bf16[2,112,1600]{2,1,0:T(8,128)(2,1)S(1)} %get-tuple-element.275), channel_id=1, source_target_pairs={{0,8},{8,0},{16,24},{24,16},{1,9},{9,1},{17,25},{25,17},{2,10},{10... | collective-permute-start | bytes 2150408 | tf_op jit(solution)/shard_map/ppermute | solution.py:455
  427.9 31.9 %collective-permute-start.32 = (bf16[448,256]{1,0:T(8,128)(2,1)S(1)}, bf16[448,256]{1,0:T(8,128)(2,1)}, u32[]{:S(2)}, u32[]{:S(2)}) collective-permute-start(bf16[448,256]{1,0:T(8,128)(2,1)S(1)} %get-tuple-element.300), channel_id=1, source_target_pairs={{0,2},{1,3},{2,0},{3,1},{4,6},{5,7},{6,4},{7,5},{8,10},{9,11},{10,... | collective-permute-start | bytes 688136 | tf_op jit(solution)/shard_map/ppermute | solution.py:440
  477.7 20.5 %collective-permute-start.41 = (bf16[4,112,800]{2,1,0:T(8,128)(2,1)S(1)}, bf16[4,112,800]{2,1,0:T(8,128)(2,1)}, u32[]{:S(2)}, u32[]{:S(2)}) collective-permute-start(bf16[4,112,800]{2,1,0:T(8,128)(2,1)S(1)} %add_convert_fusion.12), channel_id=1, source_target_pairs={{0,8},{8,0},{16,24},{24,16},{1,9},{9,1},{17,25},{25,17},{2,10},{10... | collective-permute-start | bytes 2150408 | tf_op jit(solution)/shard_map/ppermute | solution.py:455
  480.3 21.4 %collective-permute-start.38 = (bf16[448,1024]{1,0:T(8,128)(2,1)S(1)}, bf16[448,1024]{1,0:T(8,128)(2,1)}, u32[]{:S(2)}, u32[]{:S(2)}) collective-permute-start(bf16[448,1024]{1,0:T(8,128)(2,1)S(1)} %pad_maximum_fusion.8.refs_2_), channel_id=1, source_target_pairs={{0,4},{4,0},{1,5},{5,1},{2,6},{6,2},{3,7},{7,3},{8,12},{12,8},{9,1... | collective-permute-start | bytes 2752520 | tf_op jit(solution)/shard_map/ppermute | solution.py:440
  482.7 19.1 %collective-permute-start.40 = (bf16[2,112,1600]{2,1,0:T(8,128)(2,1)S(1)}, bf16[2,112,1600]{2,1,0:T(8,128)(2,1)}, u32[]{:S(2)}, u32[]{:S(2)}) collective-permute-start(bf16[2,112,1600]{2,1,0:T(8,128)(2,1)S(1)} %add_convert_fusion.14), channel_id=1, source_target_pairs={{0,16},{8,24},{16,0},{24,8},{1,17},{9,25},{17,1},{25,9},{2,18},{10... | collective-permute-start | bytes 2150408 | tf_op jit(solution)/shard_map/ppermute | solution.py:455
  503.2 29.8 %collective-permute-start.42 = (bf16[4,112,800]{2,1,0:T(8,128)(2,1)S(1)}, bf16[4,112,800]{2,1,0:T(8,128)(2,1)}, u32[]{:S(2)}, u32[]{:S(2)}) collective-permute-start(bf16[4,112,800]{2,1,0:T(8,128)(2,1)S(1)} %get-tuple-element.270), channel_id=1, source_target_pairs={{0,8},{8,0},{16,24},{24,16},{1,9},{9,1},{17,25},{25,17},{2,10},{10... | collective-permute-start | bytes 2150408 | tf_op jit(solution)/shard_map/ppermute | solution.py:455
  504.3 35.6 %collective-permute-start.43 = (bf16[4,112,800]{2,1,0:T(8,128)(2,1)S(1)}, bf16[4,112,800]{2,1,0:T(8,128)(2,1)}, u32[]{:S(2)}, u32[]{:S(2)}) collective-permute-start(bf16[4,112,800]{2,1,0:T(8,128)(2,1)S(1)} %get-tuple-element.269), channel_id=1, source_target_pairs={{0,8},{8,0},{16,24},{24,16},{1,9},{9,1},{17,25},{25,17},{2,10},{10... | collective-permute-start | bytes 2150408 | tf_op jit(solution)/shard_map/ppermute | solution.py:455
  544.6 20.8 %collective-permute-start.45 = (bf16[4,112,800]{2,1,0:T(8,128)(2,1)S(1)}, bf16[4,112,800]{2,1,0:T(8,128)(2,1)}, u32[]{:S(2)}, u32[]{:S(2)}) collective-permute-start(bf16[4,112,800]{2,1,0:T(8,128)(2,1)S(1)} %add_convert_fusion.11), channel_id=1, source_target_pairs={{0,16},{8,24},{16,0},{24,8},{1,17},{9,25},{17,1},{25,9},{2,18},{10... | collective-permute-start | bytes 2150408 | tf_op jit(solution)/shard_map/ppermute | solution.py:455
  567.3 26.7 %collective-permute-start.53 = (bf16[2,112,1600]{2,1,0:T(8,128)(2,1)S(1)}, bf16[2,112,1600]{2,1,0:T(8,128)(2,1)}, u32[]{:S(2)}, u32[]{:S(2)}) collective-permute-start(bf16[2,112,1600]{2,1,0:T(8,128)(2,1)S(1)} %add_convert_fusion.13), channel_id=1, source_target_pairs={{0,8},{8,0},{16,24},{24,16},{1,9},{9,1},{17,25},{25,17},{2,10},{10... | collective-permute-start | bytes 2150408 | tf_op jit(solution)/shard_map/ppermute | solution.py:455
  568.0 26.0 %collective-permute-start.54 = (bf16[2,112,1600]{2,1,0:T(8,128)(2,1)S(1)}, bf16[2,112,1600]{2,1,0:T(8,128)(2,1)}, u32[]{:S(2)}, u32[]{:S(2)}) collective-permute-start(bf16[2,112,1600]{2,1,0:T(8,128)(2,1)S(1)} %add_convert_fusion.13), channel_id=1, source_target_pairs={{0,16},{8,24},{16,0},{24,8},{1,17},{9,25},{17,1},{25,9},{2,18},{10... | collective-permute-start | bytes 2150408 | tf_op jit(solution)/shard_map/ppermute | solution.py:455
  571.0 22.9 %collective-permute-start.50 = (bf16[112,800]{1,0:T(8,128)(2,1)S(1)}, bf16[112,800]{1,0:T(8,128)(2,1)S(1)}, u32[]{:S(2)}, u32[]{:S(2)}) collective-permute-start(bf16[112,800]{1,0:T(8,128)(2,1)S(1)} %get-tuple-element.304), channel_id=1, source_target_pairs={{0,1},{1,2},{2,3},{3,0},{4,5},{5,6},{6,7},{7,4},{8,9},{9,10},{10,1... | collective-permute-start | bytes 537608 | tf_op jit(solution)/shard_map/ppermute | solution.py:440
  571.1 22.8 %collective-permute-start.51 = (bf16[112,800]{1,0:T(8,128)(2,1)S(1)}, bf16[112,800]{1,0:T(8,128)(2,1)S(1)}, u32[]{:S(2)}, u32[]{:S(2)}) collective-permute-start(bf16[112,800]{1,0:T(8,128)(2,1)S(1)} %get-tuple-element.303), channel_id=1, source_target_pairs={{0,2},{1,3},{2,0},{3,1},{4,6},{5,7},{6,4},{7,5},{8,10},{9,11},{10,... | collective-permute-start | bytes 537608 | tf_op jit(solution)/shard_map/ppermute | solution.py:440
  574.6 19.3 %collective-permute-start.52 = (bf16[112,800]{1,0:T(8,128)(2,1)S(1)}, bf16[112,800]{1,0:T(8,128)(2,1)S(1)}, u32[]{:S(2)}, u32[]{:S(2)}) collective-permute-start(bf16[112,800]{1,0:T(8,128)(2,1)S(1)} %get-tuple-element.302), channel_id=1, source_target_pairs={{0,3},{1,0},{2,1},{3,2},{4,7},{5,4},{6,5},{7,6},{8,11},{9,8},{10,9... | collective-permute-start | bytes 537608 | tf_op jit(solution)/shard_map/ppermute | solution.py:440
  601.2 30.0 %collective-permute-start.58 = (bf16[3,448,800]{2,1,0:T(8,128)(2,1)}, bf16[3,448,800]{2,1,0:T(8,128)(2,1)}, u32[]{:S(2)}, u32[]{:S(2)}) collective-permute-start(bf16[3,448,800]{2,1,0:T(8,128)(2,1)} %bitcast.224), channel_id=1, source_target_pairs={{0,4},{4,0},{1,5},{5,1},{2,6},{6,2},{3,7},{7,3},{8,12},{12,8},{9,1... | collective-permute-start | bytes 6451208 | tf_op jit(solution)/shard_map/ppermute | solution.py:440
  608.6 33.9 %collective-permute-start.62 = (bf16[5,112,800]{2,1,0:T(8,128)(2,1)}, bf16[5,112,800]{2,1,0:T(8,128)(2,1)}, u32[]{:S(2)}, u32[]{:S(2)}) collective-permute-start(bf16[5,112,800]{2,1,0:T(8,128)(2,1)} %dynamic-slice_dynamic-update-slice_fusion), channel_id=1, source_target_pairs={{0,8},{8,0},{16,24},{24,16},{1,9},{9,1},{17,25},{25,17},{2,10},{10... | collective-permute-start | bytes 2688008 | tf_op jit(solution)/shard_map/ppermute | solution.py:455
  610.0 32.4 %collective-permute-start.63 = (bf16[5,112,800]{2,1,0:T(8,128)(2,1)}, bf16[5,112,800]{2,1,0:T(8,128)(2,1)}, u32[]{:S(2)}, u32[]{:S(2)}) collective-permute-start(bf16[5,112,800]{2,1,0:T(8,128)(2,1)} %dynamic-slice_dynamic-update-slice_fusion), channel_id=1, source_target_pairs={{0,16},{8,24},{16,0},{24,8},{1,17},{9,25},{17,1},{25,9},{2,18},{10... | collective-permute-start | bytes 2688008 | tf_op jit(solution)/shard_map/ppermute | solution.py:455
  648.4 19.3 %collective-permute-start.64 = (bf16[3,48,800]{2,1,0:T(8,128)(2,1)S(1)}, bf16[3,48,800]{2,1,0:T(8,128)(2,1)}, u32[]{:S(2)}, u32[]{:S(2)}) collective-permute-start(bf16[3,48,800]{2,1,0:T(8,128)(2,1)S(1)} %get-tuple-element.274), channel_id=1, source_target_pairs={{0,1},{1,2},{2,3},{4,5},{5,6},{6,7},{8,9},{9,10},{10,11},{12,13},{... | collective-permute-start | bytes 691208 | tf_op jit(solution)/shard_map/ppermute | solution.py:542
  651.0 21.6 %collective-permute-start.65 = (bf16[3,48,800]{2,1,0:T(8,128)(2,1)S(1)}, bf16[3,48,800]{2,1,0:T(8,128)(2,1)}, u32[]{:S(2)}, u32[]{:S(2)}) collective-permute-start(bf16[3,48,800]{2,1,0:T(8,128)(2,1)S(1)} %get-tuple-element.273), channel_id=1, source_target_pairs={{1,0},{2,1},{3,2},{5,4},{6,5},{7,6},{9,8},{10,9},{11,10},{13,12},{... | collective-permute-start | bytes 691208 | tf_op jit(solution)/shard_map/ppermute | solution.py:546
  653.4 19.2 %collective-permute-start.69 = (bf16[3,112,800]{2,1,0:T(8,128)(2,1)S(1)}, bf16[3,112,800]{2,1,0:T(8,128)(2,1)}, u32[]{:S(2)}, u32[]{:S(2)}) collective-permute-start(bf16[3,112,800]{2,1,0:T(8,128)(2,1)S(1)} %slice.146), channel_id=1, source_target_pairs={{0,8},{8,0},{16,24},{24,16},{1,9},{9,1},{17,25},{25,17},{2,10},{10... | collective-permute-start | bytes 1612808 | tf_op jit(solution)/shard_map/ppermute | solution.py:455
  683.6 27.4 %collective-permute-start.71 = (bf16[3,112,800]{2,1,0:T(8,128)(2,1)}, bf16[3,112,800]{2,1,0:T(8,128)(2,1)S(1)}, u32[]{:S(2)}, u32[]{:S(2)}) collective-permute-start(bf16[3,112,800]{2,1,0:T(8,128)(2,1)} %get-tuple-element.282), channel_id=1, source_target_pairs={{0,16},{8,24},{16,0},{24,8},{1,17},{9,25},{17,1},{25,9},{2,18},{10... | collective-permute-start | bytes 1612808 | tf_op jit(solution)/shard_map/ppermute | solution.py:455
  685.0 26.1 %collective-permute-start.72 = (bf16[3,112,800]{2,1,0:T(8,128)(2,1)}, bf16[3,112,800]{2,1,0:T(8,128)(2,1)}, u32[]{:S(2)}, u32[]{:S(2)}) collective-permute-start(bf16[3,112,800]{2,1,0:T(8,128)(2,1)} %get-tuple-element.281), channel_id=1, source_target_pairs={{0,24},{8,16},{16,8},{24,0},{1,25},{9,17},{17,9},{25,1},{2,26},{10... | collective-permute-start | bytes 1612808 | tf_op jit(solution)/shard_map/ppermute | solution.py:455
  714.0 26.0 %collective-permute-start.76 = (bf16[3,112,800]{2,1,0:T(8,128)(2,1)S(1)}, bf16[3,112,800]{2,1,0:T(8,128)(2,1)S(1)}, u32[]{:S(2)}, u32[]{:S(2)}) collective-permute-start(bf16[3,112,800]{2,1,0:T(8,128)(2,1)S(1)} %add_convert_fusion.15), channel_id=1, source_target_pairs={{0,16},{8,24},{16,0},{24,8},{1,17},{9,25},{17,1},{25,9},{2,18},{10... | collective-permute-start | bytes 1612808 | tf_op jit(solution)/shard_map/ppermute | solution.py:455
  716.0 24.1 %collective-permute-start.77 = (bf16[3,112,800]{2,1,0:T(8,128)(2,1)S(1)}, bf16[3,112,800]{2,1,0:T(8,128)(2,1)S(1)}, u32[]{:S(2)}, u32[]{:S(2)}) collective-permute-start(bf16[3,112,800]{2,1,0:T(8,128)(2,1)S(1)} %add_convert_fusion.15), channel_id=1, source_target_pairs={{0,24},{8,16},{16,8},{24,0},{1,25},{9,17},{17,9},{25,1},{2,26},{10... | collective-permute-start | bytes 1612808 | tf_op jit(solution)/shard_map/ppermute | solution.py:455
  (117 other events, 1078.7 us)
Sparse Core Ops, SparseCore 0:
  17.7 69.3 all-gather.3
  131.7 67.6 all-gather.5
  240.7 66.7 all-gather.7
  335.0 60.4 reduce-scatter.3
  408.0 77.8 reduce-scatter.5
  628.6 67.9 reduce-scatter.7

commit v2 on v1

--- a/solution.py
+++ b/solution.py
@@ -201,14 +201,14 @@
     )(a, b, bias)
 
 
-def split_product(parts, b, row, bias, dtype):
+def split_product(parts, b, row, columns, which, dtype):
     n = len(parts)
     total, depth = parts[0].shape
     width = b.shape[1]
     rows = rows_of(total, 400)
 
     def kernel(row_ref, b_ref, bias_ref, *refs):
-        out = bias_ref[...] + jnp.zeros((rows, width), F32)
+        out = bias_ref[:, which : which + 1] + jnp.zeros((rows, width), F32)
         for i in range(n):
             at = pl.multiple_of(lax.rem(row_ref[0] + i, n) * depth, 8)
             out = out + jnp.dot(refs[i][...], b_ref[pl.ds(at, depth), :], preferred_element_type=F32)
@@ -218,12 +218,16 @@
         kernel,
         out_shape=jax.ShapeDtypeStruct((total, width), dtype),
         grid=(total // rows,),
-        in_specs=[SM, pl.BlockSpec(b.shape, whole_block), pl.BlockSpec((rows, 1), by_rows)]
+        in_specs=[
+            SM,
+            pl.BlockSpec(b.shape, whole_block),
+            pl.BlockSpec((rows, columns.shape[1]), by_rows),
+        ]
         + [pl.BlockSpec((rows, depth), by_rows)] * n,
         out_specs=pl.BlockSpec((rows, width), by_rows),
         compiler_params=ROOM,
         cost_estimate=FREE,
-    )(row, b, bias, *parts)
+    )(row, b, columns, *parts)
 
 
 def split_product_tn(parts, b, row):
@@ -263,13 +267,13 @@
     )(row, b, *parts)
 
 
-def norm_product_tn(a, b, normed, gain, shift, scale):
+def norm_product_tn(a, b, normed, columns, scale, riding, col, n_col):
     rows = rows_of(a.shape[0], 448)
     steps = a.shape[0] // rows
     depth, tokens = a.shape[1], b.shape[1]
-    cut = rows_of(depth, 400)
-
-    def kernel(a_ref, b_ref, n_ref, g_ref, s_ref, c_ref, o_ref, t_ref, f_ref, acc):
+    cut, part = depth // n_col, tokens // n_col
+
+    def kernel(col_ref, a_ref, b_ref, n_ref, g_ref, c_ref, r_ref, o_ref, f_ref, acc):
         @pl.when(pl.program_id(0) == 0)
         def start():
             acc[...] = lax.dot_general(a_ref[...], b_ref[...], NT, preferred_element_type=F32)
@@ -280,43 +284,58 @@
 
         @pl.when(pl.program_id(0) == steps - 1)
         def end():
-            t_ref[...] = jnp.zeros_like(t_ref)
-            for first in range(0, depth, cut):
-                at = pl.ds(first, cut)
+            first = jnp.zeros((1, tokens), F32)
+            second = jnp.zeros((1, tokens), F32)
+            for j in range(n_col):
+                at = pl.ds(j * cut, cut)
                 p = acc[at, :]
-                scaled = p * g_ref[at, :]
-                o_ref[at, :] = (scaled * c_ref[...]).astype(BF16)
-                moved = p * (n_ref[at, :].astype(F32) - s_ref[at, :])
-                t_ref[0:1, :] += jnp.sum(scaled, axis=0, keepdims=True)
-                t_ref[1:2, :] += jnp.sum(moved, axis=0, keepdims=True)
+                scaled = p * g_ref[at, 0:1]
+                o_ref[j, 0:cut, :] = (scaled * c_ref[...]).astype(BF16)
+                moved = p * (n_ref[at, :].astype(F32) - g_ref[at, 1:2])
+                first += jnp.sum(scaled, axis=0, keepdims=True)
+                second += jnp.sum(moved, axis=0, keepdims=True)
                 f_ref[at, 0:1] = jnp.sum(moved, axis=1, keepdims=True)
                 f_ref[at, 1:2] = jnp.sum(p, axis=1, keepdims=True)
+                for c in range(n_col):
+
+                    @pl.when(col_ref[0] == c)
+                    def ride():
+                        here = slice(c * part, (c + 1) * part)
+                        own = scaled[:, here] * c_ref[:, here] + r_ref[at, :]
+                        o_ref[j, 0:cut, here] = own.astype(BF16)
+
+            lines = []
+            for line in (first, second):
+                high = line.astype(BF16).astype(F32)
+                lines += [high, line - high]
+            lines = jnp.concatenate(lines + [jnp.zeros((12, tokens), F32)]).astype(BF16)
+            for j in range(n_col):
+                o_ref[j, cut : cut + 16, :] = lines
 
     return pl.pallas_call(
         kernel,
         out_shape=[
-            jax.ShapeDtypeStruct((depth, tokens), BF16),
-            jax.ShapeDtypeStruct((2, tokens), F32),
+            jax.ShapeDtypeStruct((n_col, cut + 16, tokens), BF16),
             jax.ShapeDtypeStruct((depth, 2), F32),
         ],
         grid=(steps,),
         in_specs=[
+            SM,
             pl.BlockSpec((rows, depth), by_rows),
             pl.BlockSpec((rows, tokens), by_rows),
             pl.BlockSpec((depth, tokens), whole_block),
-            pl.BlockSpec((depth, 1), whole_block),
-            pl.BlockSpec((depth, 1), whole_block),
+            pl.BlockSpec(columns.shape, whole_block),
             pl.BlockSpec((1, tokens), whole_block),
+            pl.BlockSpec((depth, part), whole_block),
         ],
         out_specs=[
-            pl.BlockSpec((depth, tokens), whole_block),
-            pl.BlockSpec((2, tokens), whole_block),
+            pl.BlockSpec((n_col, cut + 16, tokens), lambda i: (0, 0, 0)),
             pl.BlockSpec((depth, 2), whole_block),
         ],
         scratch_shapes=[pltpu.VMEM((depth, tokens), F32)],
         compiler_params=ROOM,
         cost_estimate=FREE,
-    )(a, b, normed, gain, shift, scale)
+    )(col, a, b, normed, columns, scale, riding)
 
 
 def token_product(a, b, index, parts, of_a):
@@ -418,6 +437,31 @@
     )(row, up, down, bias, n2, g)
 
 
+def turned(parts):
+    n = len(parts)
+    depth, wide = parts[0].shape
+
+    def kernel(*refs):
+        o_ref = refs[n]
+        for i in range(n):
+            for first in range(0, wide, 256):
+                size = min(256, wide - first)
+                at = lax.broadcasted_iota(jnp.int32, (size, size), 0)
+                ones = (at == lax.broadcasted_iota(jnp.int32, (size, size), 1)).astype(BF16)
+                cut = refs[i][:, first : first + size]
+                out = lax.dot_general(ones, cut, TN, preferred_element_type=F32)
+                o_ref[i * wide + first : i * wide + first + size, :] = out.astype(BF16)
+
+    return pl.pallas_call(
+        kernel,
+        out_shape=jax.ShapeDtypeStruct((n * wide, depth), BF16),
+        in_specs=[V] * n,
+        out_specs=V,
+        compiler_params=ROOM,
+        cost_estimate=FREE,
+    )(*parts)
+
+
 def gate(values, others):
     def kernel(*refs):
         pass
@@ -504,7 +548,7 @@
                         rows = pl.ds(0, shares.lengths[s])
                         to = pl.ds(shares.starts[s], shares.lengths[s])
                         pairs = [(refs[m].at[:, rows], o_ref.at[:, to])]
-                        if m == 3:
+                        if m == 3 and len(parts) == 5:
                             low, high = pl.ds(0, n // 2), pl.ds(n // 2, n // 2)
                             pairs = [
                                 (refs[3].at[:, rows], o_ref.at[low, to]),
@@ -517,7 +561,7 @@
     return pl.pallas_call(
         kernel,
         out_shape=jax.ShapeDtypeStruct((n, shares.rows, wide), parts[0].dtype),
-        in_specs=[SM] + [ANY] * 5,
+        in_specs=[SM] + [ANY] * len(parts),
         out_specs=V,
         scratch_shapes=[pltpu.SemaphoreType.DMA((5,))],
         compiler_params=ROOM,
@@ -678,10 +722,11 @@
     x = tokens.reshape(length, width).T
     g = cotangent.reshape(length, width).T
     place_in = col * n_row + row
-
-    def between_owners(value_of, back):
+    half = n_col // 2
+
+    def between_owners(value_of, steps, back):
         got = []
-        for step in range(n_col):
+        for step in steps:
             pairs = []
             for r in range(n_row):
                 for c in range(n_col):
@@ -707,37 +752,7 @@
             lax.dynamic_slice_in_dim(bias_v, begin, window, 0),
         ]
     )
-    up_parts = [w_up] + [turn(w_up, "row", -step) for step in range(1, n_row)]
-    up_turned = row_join(up_parts, 0).T
-    out_own = shares.take(w_out.T, dp, 0)
-    down_own = shares.take(w_down.T, dp, 0)
-    x_all, g, out_own, down_own, w3 = gate([x_all, g, out_own, down_own, w3], [up_turned, bias3])
-
-    moved_out = [out_own] + [turn(out_own, "col", -step) for step in range(1, n_col)]
-    moved_down = between_owners(
-        lambda step: block(down_own, (col - step) % n_col, ff_part, 1), False
-    )
-    x_float = x_all.astype(F32)
-    mean1, rstd1 = moments(x_float)
-    n1 = ((x_float - mean1) * rstd1 * gain1 + shift1).astype(BF16)
-    triple = product(w3, n1, bias3).reshape(3, window, length)
-    triple, g, *rest = gate([triple, g] + moved_out[1:] + moved_down, [])
-    moved_out = jnp.stack(ordered(moved_out[:1] + rest[: n_col - 1], col, 1))
-    moved_down = jnp.stack(ordered(rest[n_col - 1 :], place_in, 1))
-
-    g_all = lax.all_gather(g, "col", axis=0, tiled=True)
-    pieces = [triple] + [turn(triple, "row", -step) for step in range(1, n_row)]
-    near_out = [swap_with(moved_out, 1), swap_with(moved_out, 2)]
-    *pieces, near_x, near_y, moved_down = gate(pieces[1:] + near_out + [moved_down], [])
-    pieces, near_out = [triple] + pieces, [near_x, near_y]
-
-    half = n_col // 2
-
-    def to_diagonal(near):
-        return [swap_with(near[0][:half], 2), swap_with(near[1][half:], 1)]
-
-    far_out = to_diagonal(near_out)
-    near_down = [swap_with(moved_down, 1), swap_with(moved_down, 2)]
+    columns = jnp.concatenate([gain1, shift1, bias_out, jnp.zeros((depth, 1), F32)], 1)
     meta = jnp.stack(
         [
             jnp.array(heads.firsts, jnp.int32)[col],
@@ -746,45 +761,69 @@
             jnp.array(heads.last_mask, jnp.int32)[col],
         ]
     )
+    up_parts = [w_up] + [turn(w_up, "row", -step) for step in range(1, n_row)]
+    up_turned = row_join(up_parts, 0).T
+    out_own = shares.take(w_out.T, dp, 0)
+    down_own = shares.take(w_down.T, dp, 0)
+    x_all, g, out_own, down_own, w3, meta, columns, bias3 = gate(
+        [x_all, g, out_own, down_own, w3, meta, columns, bias3], [up_turned]
+    )
+
+    g_all = lax.all_gather(g, "col", axis=0, tiled=True)
+    moved_out = [out_own] + [turn(out_own, "col", -step) for step in range(1, n_col)]
+    x_float = x_all.astype(F32)
+    mean1, rstd1 = moments(x_float)
+    n1 = ((x_float - mean1) * rstd1 * gain1 + shift1).astype(BF16)
+    triple = product(w3, n1, bias3).reshape(3, window, length)
+    triple, *rest = gate([triple] + moved_out[1:], [])
+    moved_out = moved_out[:1] + rest
+
+    pieces = [triple] + [turn(triple, "row", -step) for step in range(1, n_row)]
+    moved_out = jnp.stack(ordered(moved_out, col, 1))
+    moved_out, *rest = gate([moved_out] + pieces[1:], [])
+    pieces = pieces[:1] + rest
+
+    near_out = [swap_with(moved_out, 1), swap_with(moved_out, 2)]
     *cuts, mixed, norms = attn_fwd(meta, key_start, pieces, heads.slots, size)
-    *cuts, a, b, c, d = gate(list(cuts) + far_out + near_down, [])
-    far_out, near_down = [a, b], [c, d]
+    *cuts, near_x, near_y, g_all = gate(list(cuts) + near_out + [g_all], [])
+
+    half = n_col // 2
+    far_out = [swap_with(near_x[:half], 2), swap_with(near_y[half:], 1)]
+    mixed_own = row_sum(cuts).astype(BF16)
+    mixed_own, *far_out = gate([mixed_own] + far_out, [])
 
     dp_at = dp[None].astype(jnp.int32)
-    far_down = to_diagonal(near_down)
-    mixed_own = row_sum(cuts).astype(BF16)
-    out_weights = assemble([moved_out] + near_out + far_out, shares, dp_at)
-    mixed_own, out_weights, g_all, *far_down = gate(
-        [mixed_own, out_weights, g_all] + far_down, []
-    )
-
     got = [
         turn(block(mixed_own, (col + step) % n_col, part, 1), "col", step) for step in range(n_col)
     ]
-    out_weights = [turn(out_weights, "row", -step) for step in range(n_row)]
-    down_weights = assemble([moved_down] + near_down + far_down, shares, dp_at)
-    *rest, down_weights = gate(got[1:] + out_weights[1:] + [down_weights], [])
+    out_weights = assemble([moved_out, near_x, near_y] + far_out, shares, dp_at)
+    out_weights = [out_weights] + [turn(out_weights, "row", -step) for step in range(1, n_row)]
+    down_own, *rest = gate([down_own] + got[1:] + out_weights[1:], [])
     got = got[:1] + rest[: n_col - 1]
     out_weights = out_weights[:1] + rest[n_col - 1 :]
     out_weights = [w.reshape(depth, in_rows) for w in out_weights]
 
-    down_weights = [turn(down_weights, "row", -step) for step in range(n_row)]
+    moved_down = between_owners(
+        lambda step: block(down_own, (col - step) % n_col, ff_part, 1), range(n_col), False
+    )
     got = ordered(got, col, -1)
     lapped = [heads.firsts[j] * size for j in range(n_col)]
     attention = sum(
         jnp.pad(piece, ((at, depth - at - window), (0, 0))) for piece, at in zip(got, lapped)
     )
-    branch = split_product(out_weights, attention, row_at, bias_out, F32)
+    branch = split_product(out_weights, attention, row_at, columns, 2, F32)
     resid = block(x_all, col, part, 1).astype(F32) + branch
     mean2, rstd2 = moments(resid)
     hat2 = (resid - mean2) * rstd2
     n2_own = (hat2 * gain2 + shift2).astype(BF16)
-    n2_own, *rest = gate([n2_own] + down_weights[1:], [hat2])
-    down_weights = down_weights[:1] + rest
+    n2_own, g, *moved_down = gate([n2_own, g] + moved_down, [hat2])
+
+    n2_all = lax.all_gather(n2_own, "col", axis=1, tiled=True)
+    moved_down = jnp.stack(ordered(moved_down, place_in, 1))
+    down_weights = assemble([moved_down] + swap_all(moved_down), shares, dp_at)
+    down_weights = [turn(down_weights, "row", -step) for step in range(n_row)]
     down_weights = [w.reshape(depth, ff_part) for w in down_weights]
-
-    n2_all = lax.all_gather(n2_own, "col", axis=1, tiled=True)
-    down_turned = jnp.concatenate([w.T for w in down_weights])
+    down_turned = turned(down_weights)
     g_sums = jnp.sum(g.astype(F32), axis=1)
     n2_all, down_turned = gate([n2_all, down_turned], [g_sums])
 
@@ -795,19 +834,38 @@
 
     dn2 = lax.psum_scatter(part2, "col", scatter_dimension=1, tiled=True)
     up_grad = [token_product(n2_all, du_all, r, n_row, True) for r in other_rows[::-1]][::-1]
-    up_grad = row_sum(up_grad).astype(BF16)
     down_grad = [token_product(g_all, hidden_all, r, n_row, False) for r in other_rows[::-1]][::-1]
     down_grad = [d.reshape(n_col, width, ff_part) for d in down_grad]
-    down_grad = row_sum(down_grad).astype(BF16)
-    no_bias = jnp.zeros((depth, 1), F32)
-    shrunk = split_product(down_weights, hidden_all, row_at, no_bias, BF16)
+    up_grad = up_grad[:1] + [turn(p, "row", i) for i, p in enumerate(up_grad) if i]
+    down_grad = down_grad[:1] + [turn(p, "row", i) for i, p in enumerate(down_grad) if i]
+    hidden_all, *rest = gate([hidden_all] + up_grad + down_grad, [])
+    up_grad, down_grad = rest[:n_row], rest[n_row:]
+
+    up_grad = sum(p.astype(F32) for p in up_grad).astype(BF16)
+    down_grad = sum(p.astype(F32) for p in down_grad).astype(BF16)
+    up_rows = width if in_rows % width == 0 else in_rows
+    up_shares = Shares(up_rows)
+    up_grad = up_grad.reshape(in_rows // up_rows, up_rows, ff)
+
+    def first_sum(value, cut, bit):
+        sent = [cut.take(value, dp ^ bit, 1), cut.take(value, dp ^ 3, 1)]
+        return swap_with(jnp.stack(sent), bit)
+
+    def relay(value, first, cut, bit):
+        sent = cut.take(value, dp ^ (3 - bit), 1).astype(F32) + first[1].astype(F32)
+        return swap_with(sent.astype(BF16), 3 - bit)
+
+    def share_sum(value, cut, first, relayed):
+        own = cut.take(value, dp, 1).astype(F32)
+        return (own + first[0].astype(F32) + relayed.astype(F32)).astype(BF16)
+
+    up_first = first_sum(up_grad, up_shares, 1)
+    down_first = first_sum(down_grad, shares, 2)
+    shrunk = split_product(down_weights, hidden_all, row_at, columns, 3, BF16)
     own_sum = block(shrunk, col, part, 1).astype(F32) + resid
     shrunk = lax.dynamic_update_slice_in_dim(shrunk, own_sum.astype(BF16), col * part, 1)
     du_sums = jnp.sum(du_all.astype(F32), axis=1)
-    up_rows = width if in_rows % width == 0 else in_rows
-    up_shares = Shares(up_rows)
-    up_grad = up_grad.reshape(in_rows // up_rows, up_rows, ff)
-    dn2, up_grad, down_grad, shrunk = gate([dn2, up_grad, down_grad, shrunk], [du_sums])
+    dn2, shrunk = gate([dn2, shrunk], [du_sums])
 
     dn2 = dn2.astype(F32)
     up2 = dn2 * gain2
@@ -823,110 +881,109 @@
             jnp.sum(dn2, axis=1),
         ]
     )
-    da, db, shrunk, up_grad, down_grad = gate([da, db, shrunk, up_grad, down_grad], [sums2])
-
-    outputs = lax.psum_scatter(shrunk, "col", scatter_dimension=0, tiled=True)
+    da, db, shrunk, up_first, down_first = gate([da, db, shrunk, up_first, down_first], [sums2])
+
     got = []
     for step in range(n_col):
         to = firsts[(col + step) % n_col]
         got.append(turn(lax.dynamic_slice_in_dim(da, to, window, 0), "col", step))
-
-    def first_sums(value, cut, bit):
-        near = swap_with(cut.take(value, dp ^ bit, 1), bit)
-        return [near, swap_with(cut.take(value, dp ^ 3, 1), bit)]
-
-    def relay(value, far, cut, bit):
-        sent = cut.take(value, dp ^ (3 - bit), 1).astype(F32) + far.astype(F32)
-        return swap_with(sent.astype(BF16), 3 - bit)
-
-    def share_sum(value, cut, near, relayed):
-        own = cut.take(value, dp, 1).astype(F32)
-        return (own + near.astype(F32) + relayed.astype(F32)).astype(BF16)
-
-    up_first = first_sums(up_grad, up_shares, 1)
-    down_first = first_sums(down_grad, shares, 2)
+    up_relay = relay(up_grad, up_first, up_shares, 1)
+    down_relay = relay(down_grad, down_first, shares, 2)
     out_grad = [token_product(db, attention, r, n_row, False) for r in other_rows[::-1]][::-1]
     out_grad = [o.reshape(n_col, width, in_rows) for o in out_grad]
-    rest = gate(got[1:] + out_grad + up_first + down_first, [])
+    rest = gate(got[1:] + out_grad + [up_relay, down_relay, shrunk], [])
     got, rest = got[:1] + rest[: n_col - 1], rest[n_col - 1 :]
-    out_grad, up_first, down_first = rest[:n_row], rest[n_row : n_row + 2], rest[n_row + 2 :]
-
+    out_grad, (up_relay, down_relay, shrunk) = rest[:n_row], rest[n_row:]
+
+    outputs = lax.psum_scatter(shrunk, "col", scatter_dimension=0, tiled=True)
     da_own = jnp.concatenate(ordered(got, col, -1), 1)
     da_pieces = [da_own] + [turn(da_own, "row", -step) for step in range(1, n_row)]
-    up_relay = relay(up_grad, up_first[1], up_shares, 1)
-    down_relay = relay(down_grad, down_first[1], shares, 2)
     out_grad = row_sum(out_grad).astype(BF16)
-    *rest, out_grad, up_relay, down_relay = gate(
-        da_pieces[1:] + [out_grad, up_relay, down_relay], []
-    )
-    da_pieces = [da_own] + rest
-
-    out_first = first_sums(out_grad, shares, 1)
+    up_share = share_sum(up_grad, up_shares, up_first, up_relay)
+    down_share = share_sum(down_grad, shares, down_first, down_relay)
+    out_cuts = [(out_grad[:half], 1), (out_grad[half:], 2)]
+    out_sent = [
+        jnp.stack([shares.take(v, dp ^ bit, 1), shares.take(v, dp ^ 3, 1)]) for v, bit in out_cuts
+    ]
+    *rest, up_share, down_share = gate(da_pieces[1:] + out_sent + [up_share, down_share], [])
+    da_pieces, out_sent = [da_own] + rest[: n_row - 1], rest[n_row - 1 :]
+
+    out_first = [swap_with(v, bit) for v, (_, bit) in zip(out_sent, out_cuts)]
+    up_near = [swap_with(up_share, 1), swap_with(up_share, 2)]
     dqkv = attn_bwd(meta, key_start, pieces, da_pieces, mixed, norms, heads.slots, size)
-    *dqkv, outputs, down_relay, a, b = gate(list(dqkv) + [outputs, down_relay] + out_first, [])
-    out_first = [a, b]
-
-    down_share = share_sum(down_grad, shares, down_first[0], down_relay)
-    down_home = between_owners(lambda step: pick(down_share, (place_in + step) % n_col), True)
-    out_relay = relay(out_grad, out_first[1], shares, 1)
+    *rest, down_share = gate(list(dqkv) + up_near + out_first + [down_share], [])
+    dqkv, up_near, out_first = rest[:n_row], rest[n_row : n_row + 2], rest[n_row + 2 :]
+
+    down_home = between_owners(
+        lambda step: pick(down_share, (place_in + step) % n_col), range(n_col), True
+    )
     dqkv = row_sum(dqkv).astype(BF16).reshape(3 * window, length)
-    dqkv, out_relay, up_relay, *down_home = gate([dqkv, out_relay, up_relay] + down_home, [])
-
-    out_share = share_sum(out_grad, shares, out_first[0], out_relay)
-    out_home = [turn(pick(out_share, (col + step) % n_col), "col", step) for step in range(n_col)]
-    up_share = share_sum(up_grad, up_shares, up_first[0], up_relay)
-    up_near = [swap_with(up_share, 1), swap_with(up_share, 2)]
-    dn1, stats, norm1 = norm_product_tn(w3, dqkv, n1, gain1, shift1, rstd1)
-    riding = block(dn1, col, part, 1).astype(F32) + dr
-    dn1 = lax.dynamic_update_slice_in_dim(dn1, riding.astype(BF16), col * part, 1)
-    dn1, dqkv, stats, norm1, *rest = gate([dn1, dqkv, stats, norm1] + out_home[1:] + up_near, [])
-    out_home, up_near = out_home[:1] + rest[: n_col - 1], rest[n_col - 1 :]
-
-    dx = lax.psum_scatter(dn1, "col", scatter_dimension=0, tiled=True)
+    *rest, dqkv, outputs = gate(down_home + out_first + up_near + [dqkv, outputs], [])
+    down_home, out_first, up_near = rest[:n_col], rest[n_col : n_col + 2], rest[n_col + 2 :]
+
+    homes = jnp.stack(ordered(down_home, col, -1))
+    homes_near = [swap_with(homes, 1), swap_with(homes, 2)]
+    out_relay = [relay(v, f, shares, bit) for (v, bit), f in zip(out_cuts, out_first)]
     qkv_parts = [token_product(dqkv, n1, r, n_row, False) for r in other_rows[::-1]][::-1]
     qkv_parts = [q.reshape(3, window, in_rows) for q in qkv_parts]
     qkv_grad = row_sum(qkv_parts).astype(BF16)
-    up_half = up_share.shape[1] // 2 // 16 * 16
-    up_far = [swap_with(up_near[0][:, :up_half], 2), swap_with(up_near[1][:, up_half:], 1)]
-    out_home = sum(o.astype(F32) for o in out_home).astype(BF16)
-    homes = jnp.stack([out_home] + ordered(down_home, col, -1))
-    homes_near = [swap_with(homes, 1), swap_with(homes, 2)]
-    stats = sum(turn(stats, "col", step) for step in range(n_col)) / depth
+    dqkv, qkv_grad, *rest = gate([dqkv, qkv_grad] + out_relay + homes_near, [])
+    out_relay, homes_near = rest[:2], rest[2:]
+
+    out_share = [
+        share_sum(v, shares, f, r) for (v, _), f, r in zip(out_cuts, out_first, out_relay)
+    ]
+    out_home = lax.psum_scatter(
+        jnp.concatenate(out_share), "col", scatter_dimension=0, tiled=True
+    )
+    wide, front, tail = narrow_edges(qkv_grad, 1, heads, col, width)
+    homes_far = swap_with(homes_near[0], 2)
+    up_far = swap_with(up_near[1], 1)
+    dn1, norm1 = norm_product_tn(w3, dqkv, n1, columns, rstd1, dr, col_at, n_col)
+    dn1, front, tail, dqkv, out_home, homes_far, up_far, outputs = gate(
+        [dn1, front, tail, dqkv, out_home, homes_far, up_far, outputs], [norm1]
+    )
+
+    dx = lax.psum_scatter(dn1, "col", scatter_dimension=0, tiled=True)
+    qkv_grad = narrow(wide, front, tail, 1, heads, width).astype(BF16)
+    qkv_got = [swap_with(shares.take(qkv_grad, dp ^ m, 1), m) for m in (1, 2, 3)]
+    out_near = [swap_with(out_home, 1), swap_with(out_home, 2)]
     dq_dv = jnp.sum(dqkv.astype(F32), axis=1).reshape(3, window)
     sums = lax.dynamic_update_slice_in_dim(jnp.zeros((2, depth), F32), dq_dv[::2], begin, 1)
     sums = jnp.concatenate([sums, (norm1[:, :1] / gain1).T, norm1[:, 1:].T, sums2]).reshape(-1)
     small = jnp.concatenate([sums, du_sums, g_sums])[None]
-    small = small_sum(small, ("row",))
-    outputs = (outputs.astype(F32) + down_bias[:, None]).astype(BF16)
-    qkv_grad, small, *rest = gate([qkv_grad, small] + up_far + homes_near, [stats, outputs])
-    up_far, homes_near = rest[:2], rest[2:]
-
-    wide, front, tail = narrow_edges(qkv_grad, 1, heads, col, width)
-    homes_far = [swap_with(homes_near[0][:2], 2), swap_with(homes_near[1][2:], 1)]
-    small = small_sum(small, ("dp",))[0]
-    up_grad = up_shares.join(
-        [up_share] + up_near + [jnp.concatenate(up_far, 1)], dp, 1
-    ).astype(F32)
-    up_grad = up_grad.reshape(in_rows, ff)
-    front, tail, small, *homes_far = gate([front, tail, small] + homes_far, [up_grad])
-
-    qkv_grad = narrow(wide, front, tail, 1, heads, width).astype(BF16)
-    qkv_got = [swap_with(shares.take(qkv_grad, dp ^ m, 1), m) for m in (1, 2, 3)]
+    small, outputs, up_far, homes_far, *rest = gate(
+        [small, outputs, up_far, homes_far] + out_near + qkv_got, []
+    )
+    out_near, qkv_got = rest[:2], rest[2:]
+
+    qkv_share = shares.take(qkv_grad, dp, 1).astype(F32)
+    qkv_share = (qkv_share + sum(q.astype(F32) for q in qkv_got)).astype(BF16)
+    qkv_all = swap_all(qkv_share)
+    out_far = swap_with(out_near[0], 2)
+    small = small_sum(small, ("row",))[0]
     sums, local = small[: 7 * depth].reshape(7, depth), small[7 * depth :]
     sums = small_sum(sums, ("col",))
     sums = lax.dynamic_slice_in_dim(sums, col * width, width, 1)
-    homes = shares.join(
-        [homes] + homes_near + [jnp.concatenate(homes_far)], dp, 1
-    ).astype(F32)
-    out_grad = homes[0]
-    down_grad = jnp.concatenate([homes[1 + j] for j in range(n_col)], 1)
-    qkv_got = gate(qkv_got, [out_grad, down_grad, sums])
-
-    qkv_share = shares.take(qkv_grad, dp, 1).astype(F32)
-    qkv_share = (qkv_share + sum(q.astype(F32) for q in qkv_got)).astype(BF16)
-    qkv_all = swap_all(qkv_share)
+    small = jnp.concatenate([sums.reshape(-1), local])[None]
+    small = small_sum(small, ("dp",))[0]
+    sums, local = small[: 7 * width].reshape(7, width), small[7 * width :]
+    up_grad = up_shares.join([up_share] + up_near + [up_far], dp, 1).astype(F32)
+    up_grad = up_grad.reshape(in_rows, ff)
+    homes = shares.join([homes] + homes_near + [homes_far], dp, 1).astype(F32)
+    down_grad = jnp.concatenate([homes[j] for j in range(n_col)], 1)
+    outputs = (outputs.astype(F32) + down_bias[:, None]).astype(BF16)
     hat1 = (x.astype(F32) - mean1) * rstd1
-    input_grad = (dx.astype(F32) - rstd1 * (stats[0:1] + hat1 * stats[1:2])).astype(BF16)
+    dx = dx.reshape(width + 16, length)
+    lines = dx[width : width + 4].astype(F32)
+    lines = (lines[0::2] + lines[1::2]) / depth
+    input_grad = dx[:width].astype(F32) - rstd1 * (lines[0:1] + hat1 * lines[1:2])
+    input_grad = input_grad.astype(BF16)
+    out_far, *qkv_all = gate(
+        [out_far] + qkv_all, [sums, local, up_grad, down_grad, outputs, input_grad]
+    )
+
+    out_grad = shares.join([out_home] + out_near + [out_far], dp, 1).astype(F32)[0]
     qkv_grad = shares.join([qkv_share] + qkv_all, dp, 1).astype(F32)
     return (
         outputs.T.reshape(tokens.shape),

time: 765 us -> 707 us (0.924)
  waiting for transfers between devices: 238 us -> 210 us
  starting transfers between devices: 119 us -> 101 us
  local copies, waits for them, and re-layouts: 83.6 us -> 71.8 us
  Pallas kernels: 178 us -> 188 us
    all_gather x1, waiting for transfers between devices: 46.7 us -> 9.19 us  [body(): n2_all = lax.all_gather(n2_own, 'col', axis=1, tiled=True)]
    ppermute x30 -> x24, waiting for transfers between devices: 57.8 us -> 33.9 us  [turn(): lax.ppermute(value, axis, [(i, (i + steps) % size) for i in range(size)])]
    all_gather x1, waiting for transfers between devices: 0.01 us -> 14.5 us  [body(): g_all = lax.all_gather(g, 'col', axis=0, tiled=True)]
    ppermute x8, waiting for transfers between devices: 1.1 us -> 12.1 us  [between_owners(): got.append(lax.ppermute(value_of(step), ('row', 'col'), pairs))]
    ppermute x30 -> x24, starting transfers between devices: 33.8 us -> 23.1 us  [turn(): lax.ppermute(value, axis, [(i, (i + steps) % size) for i in range(size)])]
    ppermute x8, starting transfers between devices: 36.2 us -> 26.6 us  [between_owners(): got.append(lax.ppermute(value_of(step), ('row', 'col'), pairs))]
    slice x10 -> x8, local copies, waits for them, and re-layouts: 12.7 us -> 3.07 us  [the longest x2 2.06 us: body(): far_out = [swap_with(near_x[:half], 2), swap_with(near_y[half:], 1)]]
    unnamed x168 -> x187, local copies, waits for them, and re-layouts: 18 us -> 27.4 us
  transfers between devices with their start and end apart: 84 -> 78, of which waited for: 28 -> 31; matrix products, arithmetic and copies ran while one was open for 24% -> 20% of each run, Pallas kernels for 18% -> 21%
where the time goes in v2:
time: 707 us; the launch traced here: 698 us
  waiting for transfers between devices  210 us (30%)
  Pallas kernels  188 us (27%)
  other arithmetic  111 us (16%)
  starting transfers between devices  101 us (14%)
  local copies, waits for them, and re-layouts  71.8 us (10%)
  between operations  16 us (2%)
    ppermute x30, waiting for transfers between devices, swap_with(): return lax.ppermute(value, 'dp', [(i, i ^ bit) for i in range(4)])  89.4 us
    pallas_call x8, Pallas kernels, token_product(): pl.pallas_call(kernel, out_shape=jax.ShapeDtypeStruct((rows_a, rows_b), B...  50.1 us
    ppermute x30, starting transfers between devices, swap_with(): return lax.ppermute(value, 'dp', [(i, i ^ bit) for i in range(4)])  37.2 us
    ppermute x24, waiting for transfers between devices, turn(): lax.ppermute(value, axis, [(i, (i + steps) % size) for i in range(size)])  33.9 us
    pallas_call x1, Pallas kernels, attn_bwd(): pl.pallas_call(functools.partial(bwd_kernel, n_row, n_slots, hd, ks.shape...  28.5 us
    pallas_call x1, Pallas kernels, hidden_layer(): pl.pallas_call(kernel, out_shape=[jax.ShapeDtypeStruct((ff, tokens), BF16...  27.4 us
    unnamed x187, local copies, waits for them, and re-layouts  27.4 us
    ppermute x8, starting transfers between devices, between_owners(): got.append(lax.ppermute(value_of(step), ('row', 'col'), pairs))  26.6 us
  transfers between devices with their start and end apart: 78, of which 31 were waited for; matrix products, arithmetic and copies ran while one was open for 20% of the time, Pallas kernels for 21%

profile of v2, /device:TPU:0, one launch (start us, length us, event | category | flops | bytes accessed | tf_op | source)
XLA Modules:
  0.0 698.0 jit_solution(6345615497523972825)
XLA Ops:
  11.3 4.9 collective-permute-start
  17.7 4.3 collective-permute-done
  25.8 4.4 fusion.8
  40.5 4.3 copy.185
  54.2 5.2 copy.186
  61.8 4.1 maximum_bitcast_fusion.refs_8_.up_ref
  65.9 21.1 %all-gather.4.cloned.1.call-done.refs_0_ = bf16[1600,1024]{1,0:T(8,128)(2,1)} async-done(((bf16[400,1024]{1,0:T(8,128)(2,1)}), bf16[1600,1024]{1,0:T(8,128)(2,1)}) %all-gather.4.cloned.1.call-update) | async-done | bytes 3276816 | tf_op jit(solution)/shard_map/all_gather | solution.py:739
  96.5 9.6 %shard_map.524 = bf16[1344,1024]{1,0:T(8,128)(2,1)} custom-call(bf16[1344,1600]{1,0:T(8,128)(2,1)} %get-tuple-element.133.a_ref, bf16[1600,1024]{1,0:T(8,128)(2,1)} %fusion.5.b_ref.n_ref, f32[1344,1]{1,0:T(8,128)} %get-tuple-element.136.bias_ref), custom_call_target="tpu_custom_call" | custom-call | tf_op jit(solution)/shard_map/pallas_call | solution.py:189
  106.0 6.6 collective-permute-done.8.refs_2_
  121.1 20.0 %shard_map.527 = (bf16[448,1024]{1,0:T(8,128)(2,1)S(1)}, bf16[448,1024]{1,0:T(8,128)(2,1)S(1)}, bf16[448,2048]{1,0:T(8,128)(2,1)S(1)}, f32[7,2048]{1,0:T(8,128)S(1)}) custom-call(s32[4]{0:T(128)S(1)} %copy-done.7, s32[25,4]{1,0:T(8,128)S(1)} %copy.191.ks, bf16[3,448,1024]{2,1,0:T(8,128)(2,1)} %get-tuple-element.138.refs_0_, ...), custom_call_target="tpu_custom_call" | custom-call | tf_op jit(solution)/shard_map/pallas_call | solution.py:148
  144.8 14.5 %all-gather.6.cloned.1.call-done.refs_4_ = bf16[1600,1024]{1,0:T(8,128)(2,1)} async-done(((bf16[400,1024]{1,0:T(8,128)(2,1)}), bf16[1600,1024]{1,0:T(8,128)(2,1)}) %all-gather.6.cloned.1.call-update) | async-done | bytes 3276816 | tf_op jit(solution)/shard_map/all_gather | solution.py:772
  167.0 5.3 collective-permute-done.14.refs_1_
  184.4 6.5 collective-permute-done.16.refs_1_
  190.9 9.3 %collective-permute-done.17.refs_2_ = bf16[448,256]{1,0:T(8,128)(2,1)} collective-permute-done((bf16[448,256]{1,0:T(8,128)(2,1)}, bf16[448,256]{1,0:T(8,128)(2,1)}, u32[]{:S(2)}, u32[]{:S(2)}) %collective-permute-start.17) | collective-permute-done | bytes 229408 | tf_op jit(solution)/shard_map/ppermute | solution.py:484
  202.6 6.1 shard_map.532
  212.1 8.2 %collective-permute-start.21 = (bf16[112,800]{1,0:T(8,128)(2,1)S(1)}, bf16[112,800]{1,0:T(8,128)(2,1)}, u32[]{:S(2)}, u32[]{:S(2)}) collective-permute-start(bf16[112,800]{1,0:T(8,128)(2,1)S(1)} %get-tuple-element.343), channel_id=1, source_target_pairs={{0,5},{1,0},{2,4},{3,1},{4,7},{5,2},{6,6},{7,3},{8,13},{9,8},{10,1... | collective-permute-start | bytes 537608 | tf_op jit(solution)/shard_map/ppermute | solution.py:736
  220.7 4.4 collective-permute-start.23
  227.0 9.9 %collective-permute-done.22.refs_4_ = bf16[112,800]{1,0:T(8,128)(2,1)} collective-permute-done((bf16[112,800]{1,0:T(8,128)(2,1)S(1)}, bf16[112,800]{1,0:T(8,128)(2,1)}, u32[]{:S(2)}, u32[]{:S(2)}) %collective-permute-start.22) | collective-permute-done | bytes 179232 | tf_op jit(solution)/shard_map/ppermute | solution.py:736
  242.4 17.3 %collective-permute-done.24.refs_1_ = bf16[4,112,800]{2,1,0:T(8,128)(2,1)S(1)} collective-permute-done((bf16[4,112,800]{2,1,0:T(8,128)(2,1)S(1)}, bf16[4,112,800]{2,1,0:T(8,128)(2,1)S(1)}, u32[]{:S(2)}, u32[]{:S(2)}) %collective-permute-start.24) | collective-permute-done | bytes 716832 | tf_op jit(solution)/shard_map/ppermute | solution.py:499
  259.7 13.5 %collective-permute-done.25.refs_2_ = bf16[4,112,800]{2,1,0:T(8,128)(2,1)S(1)} collective-permute-done((bf16[4,112,800]{2,1,0:T(8,128)(2,1)S(1)}, bf16[4,112,800]{2,1,0:T(8,128)(2,1)S(1)}, u32[]{:S(2)}, u32[]{:S(2)}) %collective-permute-start.25) | collective-permute-done | bytes 716832 | tf_op jit(solution)/shard_map/ppermute | solution.py:499
  285.6 6.9 shard_map.535.refs_1_
  292.5 9.2 %all-gather.8.cloned.1.call-done.refs_0_ = bf16[1600,1024]{1,0:T(8,128)(2,1)} async-done(((bf16[1600,256]{1,0:T(8,128)(2,1)}), bf16[1600,1024]{1,0:T(8,128)(2,1)}) %all-gather.8.cloned.1.call-update) | async-done | bytes 3276816 | tf_op jit(solution)/shard_map/all_gather | solution.py:821
  301.7 27.4 %shard_map.537 = (bf16[1600,1024]{1,0:T(8,128)(2,1)}, bf16[1600,1024]{1,0:T(8,128)(2,1)}, bf16[1600,1024]{1,0:T(8,128)(2,1)}) custom-call(s32[1]{0:T(128)} %bitcast.10.row_ref, bf16[1600,1600]{1,0:T(8,128)(2,1)} %maximum_bitcast_fusion.refs_8_.up_ref, bf16[1600,1600]{1,0:T(8,128)(2,1)} %get-tuple-element.168.down_ref, f32[1600,1]{1,0:T(8,128)} %broadcast_in_dim.52.bias_ref, ...), custom_call_target="tpu_custom_call" | custom-call | tf_op jit(solution)/shard_map/pallas_call | solution.py:411
  329.4 6.7 shard_map.540
  336.1 7.2 %shard_map.542 = bf16[1600,800]{1,0:T(8,128)(2,1)} custom-call(s32[1]{0:T(128)} %bitcast.55.index_ref, bf16[1600,1024]{1,0:T(8,128)(2,1)} %get-tuple-element.147.g_ref.a_ref, bf16[1600,1024]{1,0:T(8,128)(2,1)} %get-tuple-element.174.b_ref.refs_0_), custom_call_target="tpu_custom_call" | custom-call | tf_op jit(solution)/shard_map/pallas_call | solution.py:356
  343.8 6.7 shard_map.539.refs_1_
  350.6 7.3 %shard_map.541 = bf16[1600,800]{1,0:T(8,128)(2,1)} custom-call(s32[1]{0:T(128)} %bitcast.54.index_ref, bf16[1600,1024]{1,0:T(8,128)(2,1)} %get-tuple-element.147.g_ref.a_ref, bf16[1600,1024]{1,0:T(8,128)(2,1)} %get-tuple-element.174.b_ref.refs_0_), custom_call_target="tpu_custom_call" | custom-call | tf_op jit(solution)/shard_map/pallas_call | solution.py:356
  359.0 11.3 %shard_map.544 = bf16[1600,1024]{1,0:T(8,128)(2,1)} custom-call(s32[1]{0:T(128)} %bitcast.10.row_ref, bf16[1600,1024]{1,0:T(8,128)(2,1)} %get-tuple-element.176.b_ref, f32[1600,4]{1,0:T(8,128)} %get-tuple-element.159.bias_ref.g_ref, bf16[1600,800]{1,0:T(8,128)(2,1)} %bitcast.261, bf16[1600,800]{1,0:T(8,128)(2,1)} %bitcast.269), custom_call_target="tpu_custom_call" | custom-call | tf_op jit(solution)/shard_map/pallas_call | solution.py:217
  385.0 4.8 reduce-scatter.5.cloned.1.call-done.refs_0_
  395.2 6.7 shard_map.546.refs_0_
  402.6 7.2 %collective-permute-done.30.refs_3_ = bf16[2,2,112,1600]{3,2,1,0:T(8,128)(2,1)} collective-permute-done((bf16[2,2,112,1600]{3,2,1,0:T(8,128)(2,1)}, bf16[2,2,112,1600]{3,2,1,0:T(8,128)(2,1)}, u32[]{:S(2)}, u32[]{:S(2)}) %collective-permute-start.30) | collective-permute-done | bytes 1433632 | tf_op jit(solution)/shard_map/ppermute | solution.py:499
  409.8 8.4 %collective-permute-done.31.refs_4_ = bf16[2,4,112,800]{3,2,1,0:T(8,128)(2,1)} collective-permute-done((bf16[2,4,112,800]{3,2,1,0:T(8,128)(2,1)}, bf16[2,4,112,800]{3,2,1,0:T(8,128)(2,1)}, u32[]{:S(2)}, u32[]{:S(2)}) %collective-permute-start.31) | collective-permute-done | bytes 1433632 | tf_op jit(solution)/shard_map/ppermute | solution.py:499
  431.6 4.6 shard_map.548
  436.2 4.6 shard_map.549
  440.8 5.0 collective-permute-done.33.refs_1_
  464.4 28.5 %shard_map.552 = (bf16[3,448,1024]{2,1,0:T(8,128)(2,1)}, bf16[3,448,1024]{2,1,0:T(8,128)(2,1)}) custom-call(s32[4]{0:T(128)} %get-tuple-element.134.meta, s32[25,4]{1,0:T(8,128)} %copy-done.5, bf16[3,448,1024]{2,1,0:T(8,128)(2,1)} %get-tuple-element.138.refs_0_, bf16[3,448,1024]{2,1,0:T(8,128)(2,1)} %get-tuple-element.142.refs_1_, ...), custom_call_target="tpu_custom_call" | custom-call | tf_op jit(solution)/shard_map/pallas_call | solution.py:157
  499.8 6.7 collective-permute-start.44
  512.1 4.7 add_convert_fusion.2
  519.8 6.5 shard_map.556
  526.2 6.5 collective-permute-start.48
  538.1 6.5 shard_map.555
  549.6 14.1 %collective-permute-done.49.refs_2_ = bf16[2,112,800]{2,1,0:T(8,128)(2,1)S(1)} collective-permute-done((bf16[2,112,800]{2,1,0:T(8,128)(2,1)S(1)}, bf16[2,112,800]{2,1,0:T(8,128)(2,1)S(1)}, u32[]{:S(2)}, u32[]{:S(2)}) %collective-permute-start.49) | collective-permute-done | bytes 358432 | tf_op jit(solution)/shard_map/ppermute | solution.py:499
  575.0 14.2 %shard_map.558 = (bf16[4,416,1024]{2,1,0:T(8,128)(2,1)}, f32[1600,2]{1,0:T(8,128)}) custom-call(s32[1]{0:T(128)} %bitcast.col_ref, bf16[1344,1600]{1,0:T(8,128)(2,1)} %get-tuple-element.133.a_ref, bf16[1344,1024]{1,0:T(8,128)(2,1)} %get-tuple-element.219.b_ref.refs_3_, bf16[1600,1024]{1,0:T(8,128)(2,1)} %fusion.5.b_ref.n_ref, ...), custom_call_target="tpu_custom_call" | custom-call | tf_op jit(solution)/shard_map/pallas_call | solution.py:315
  590.7 4.0 reduce-scatter.9.cloned.1.call-done.refs_4_
  615.8 16.4 %collective-permute-done.57.refs_4_ = bf16[1,112,800]{2,1,0:T(8,128)(2,1)} collective-permute-done((bf16[1,112,800]{2,1,0:T(8,128)(2,1)S(1)}, bf16[1,112,800]{2,1,0:T(8,128)(2,1)}, u32[]{:S(2)}, u32[]{:S(2)}) %collective-permute-start.57) | collective-permute-done | bytes 179232 | tf_op jit(solution)/shard_map/ppermute | solution.py:499
  651.9 5.2 collective-permute-done.67
  657.7 5.1 collective-permute-done.68
  670.1 6.4 concatenate.73.refs_7_
  (501 shorter events, 253.7 us)
Async XLA Ops:
  7.2 79.8 %all-gather.4.cloned.1.call-start = ((), (), s32[]{:S(2)}) async-start(), calls=%async_computation.4 | async-start | bytes 4096000 | tf_op jit(solution)/shard_map/all_gather | solution.py:739
  17.6 141.7 %all-gather.6.cloned.1.call-start = ((), (), s32[]{:S(2)}) async-start(), calls=%async_computation.5 | async-start | bytes 4096000 | tf_op jit(solution)/shard_map/all_gather | solution.py:772
  30.2 17.6 %collective-permute-start.2 = (bf16[3,448,800]{2,1,0:T(8,128)(2,1)}, bf16[3,448,800]{2,1,0:T(8,128)(2,1)}, u32[]{:S(2)}, u32[]{:S(2)}) collective-permute-start(bf16[3,448,800]{2,1,0:T(8,128)(2,1)} %fusion.8), channel_id=1, source_target_pairs={{0,4},{4,0},{1,5},{5,1},{2,6},{6,2},{3,7},{7,3},{8,12},{12,8},{9,1... | collective-permute-start | bytes 6451208 | tf_op jit(solution)/shard_map/ppermute | solution.py:484
  34.9 19.3 %collective-permute-start.6 = (bf16[800,1600]{1,0:T(8,128)(2,1)}, bf16[800,1600]{1,0:T(8,128)(2,1)}, u32[]{:S(2)}, u32[]{:S(2)}) collective-permute-start(bf16[800,1600]{1,0:T(8,128)(2,1)} %param.51), channel_id=1, source_target_pairs={{0,4},{4,0},{1,5},{5,1},{2,6},{6,2},{3,7},{7,3},{8,12},{12,8},{9,1... | collective-permute-start | bytes 7680008 | tf_op jit(solution)/shard_map/ppermute | solution.py:484
  87.0 19.0 %collective-permute-start.7 = (bf16[112,800]{1,0:T(8,128)(2,1)}, bf16[112,800]{1,0:T(8,128)(2,1)}, u32[]{:S(2)}, u32[]{:S(2)}) collective-permute-start(bf16[112,800]{1,0:T(8,128)(2,1)} %get-tuple-element.137), channel_id=1, source_target_pairs={{0,3},{1,0},{2,1},{3,2},{4,7},{5,4},{6,5},{7,6},{8,11},{9,8},{10,9... | collective-permute-start | bytes 537608 | tf_op jit(solution)/shard_map/ppermute | solution.py:484
  87.8 24.9 %collective-permute-start.8 = (bf16[112,800]{1,0:T(8,128)(2,1)}, bf16[112,800]{1,0:T(8,128)(2,1)}, u32[]{:S(2)}, u32[]{:S(2)}) collective-permute-start(bf16[112,800]{1,0:T(8,128)(2,1)} %get-tuple-element.137), channel_id=1, source_target_pairs={{0,2},{1,3},{2,0},{3,1},{4,6},{5,7},{6,4},{7,5},{8,10},{9,11},{10,... | collective-permute-start | bytes 537608 | tf_op jit(solution)/shard_map/ppermute | solution.py:484
  87.8 24.9 %collective-permute-start.9 = (bf16[112,800]{1,0:T(8,128)(2,1)}, bf16[112,800]{1,0:T(8,128)(2,1)}, u32[]{:S(2)}, u32[]{:S(2)}) collective-permute-start(bf16[112,800]{1,0:T(8,128)(2,1)} %get-tuple-element.137), channel_id=1, source_target_pairs={{0,1},{1,2},{2,3},{3,0},{4,5},{5,6},{6,7},{7,4},{8,9},{9,10},{10,1... | collective-permute-start | bytes 537608 | tf_op jit(solution)/shard_map/ppermute | solution.py:484
  92.3 209.4 %all-gather.8.cloned.1.call-start = ((), (), s32[]{:S(2)}) async-start(), calls=%async_computation.6 | async-start | bytes 4096000 | tf_op jit(solution)/shard_map/all_gather | solution.py:821
  118.1 26.8 %collective-permute-start.11 = (bf16[4,112,800]{2,1,0:T(8,128)(2,1)}, bf16[4,112,800]{2,1,0:T(8,128)(2,1)}, u32[]{:S(2)}, u32[]{:S(2)}) collective-permute-start(bf16[4,112,800]{2,1,0:T(8,128)(2,1)} %get-tuple-element.145.refs_0_), channel_id=1, source_target_pairs={{0,8},{8,0},{16,24},{24,16},{1,9},{9,1},{17,25},{25,17},{2,10},{10... | collective-permute-start | bytes 2150408 | tf_op jit(solution)/shard_map/ppermute | solution.py:499
  119.5 25.3 %collective-permute-start.12 = (bf16[4,112,800]{2,1,0:T(8,128)(2,1)}, bf16[4,112,800]{2,1,0:T(8,128)(2,1)}, u32[]{:S(2)}, u32[]{:S(2)}) collective-permute-start(bf16[4,112,800]{2,1,0:T(8,128)(2,1)} %get-tuple-element.145.refs_0_), channel_id=1, source_target_pairs={{0,16},{8,24},{16,0},{24,8},{1,17},{9,25},{17,1},{25,9},{2,18},{10... | collective-permute-start | bytes 2150408 | tf_op jit(solution)/shard_map/ppermute | solution.py:499
  178.0 22.3 %collective-permute-start.19 = (bf16[4,400,800]{2,1,0:T(8,128)(2,1)}, bf16[4,400,800]{2,1,0:T(8,128)(2,1)}, u32[]{:S(2)}, u32[]{:S(2)}) collective-permute-start(bf16[4,400,800]{2,1,0:T(8,128)(2,1)} %shard_map.530), channel_id=1, source_target_pairs={{0,4},{4,0},{1,5},{5,1},{2,6},{6,2},{3,7},{7,3},{8,12},{12,8},{9,1... | collective-permute-start | bytes 7680008 | tf_op jit(solution)/shard_map/ppermute | solution.py:484
  180.8 19.5 %collective-permute-start.17 = (bf16[448,256]{1,0:T(8,128)(2,1)}, bf16[448,256]{1,0:T(8,128)(2,1)}, u32[]{:S(2)}, u32[]{:S(2)}) collective-permute-start(bf16[448,256]{1,0:T(8,128)(2,1)} %get-tuple-element.313), channel_id=1, source_target_pairs={{0,2},{1,3},{2,0},{3,1},{4,6},{5,7},{6,4},{7,5},{8,10},{9,11},{10,... | collective-permute-start | bytes 688136 | tf_op jit(solution)/shard_map/ppermute | solution.py:484
  236.9 152.9 %reduce-scatter.5.cloned.1.call-start = ((), (), s32[]{:S(2)}) async-start(), calls=%async_computation.7 | async-start | bytes 4096000 | tf_op jit(solution)/shard_map/reduce_scatter | solution.py:835
  238.8 20.9 %collective-permute-start.24 = (bf16[4,112,800]{2,1,0:T(8,128)(2,1)S(1)}, bf16[4,112,800]{2,1,0:T(8,128)(2,1)S(1)}, u32[]{:S(2)}, u32[]{:S(2)}) collective-permute-start(bf16[4,112,800]{2,1,0:T(8,128)(2,1)S(1)} %pad_maximum_fusion.13.refs_0_), channel_id=1, source_target_pairs={{0,8},{8,0},{16,24},{24,16},{1,9},{9,1},{17,25},{25,17},{2,10},{10... | collective-permute-start | bytes 2150408 | tf_op jit(solution)/shard_map/ppermute | solution.py:499
  240.4 32.9 %collective-permute-start.25 = (bf16[4,112,800]{2,1,0:T(8,128)(2,1)S(1)}, bf16[4,112,800]{2,1,0:T(8,128)(2,1)S(1)}, u32[]{:S(2)}, u32[]{:S(2)}) collective-permute-start(bf16[4,112,800]{2,1,0:T(8,128)(2,1)S(1)} %pad_maximum_fusion.13.refs_0_), channel_id=1, source_target_pairs={{0,16},{8,24},{16,0},{24,8},{1,17},{9,25},{17,1},{25,9},{2,18},{10... | collective-permute-start | bytes 2150408 | tf_op jit(solution)/shard_map/ppermute | solution.py:499
  240.9 32.3 %collective-permute-start.26 = (bf16[4,112,800]{2,1,0:T(8,128)(2,1)S(1)}, bf16[4,112,800]{2,1,0:T(8,128)(2,1)S(1)}, u32[]{:S(2)}, u32[]{:S(2)}) collective-permute-start(bf16[4,112,800]{2,1,0:T(8,128)(2,1)S(1)} %pad_maximum_fusion.13.refs_0_), channel_id=1, source_target_pairs={{0,24},{8,16},{16,8},{24,0},{1,25},{9,17},{17,9},{25,1},{2,26},{10... | collective-permute-start | bytes 2150408 | tf_op jit(solution)/shard_map/ppermute | solution.py:499
  329.1 189.9 %reduce-scatter.7.cloned.1.call-start = ((), (), s32[]{:S(2)}) async-start(), calls=%async_computation.8 | async-start | bytes 4096000 | tf_op jit(solution)/shard_map/reduce_scatter | solution.py:898
  336.1 22.9 %collective-permute-start.28 = (bf16[800,1600]{1,0:T(8,128)(2,1)}, bf16[800,1600]{1,0:T(8,128)(2,1)}, u32[]{:S(2)}, u32[]{:S(2)}) collective-permute-start(bf16[800,1600]{1,0:T(8,128)(2,1)} %shard_map.540), channel_id=1, source_target_pairs={{0,4},{4,0},{1,5},{5,1},{2,6},{6,2},{3,7},{7,3},{8,12},{12,8},{9,1... | collective-permute-start | bytes 7680008 | tf_op jit(solution)/shard_map/ppermute | solution.py:484
  374.9 34.9 %collective-permute-start.30 = (bf16[2,2,112,1600]{3,2,1,0:T(8,128)(2,1)}, bf16[2,2,112,1600]{3,2,1,0:T(8,128)(2,1)}, u32[]{:S(2)}, u32[]{:S(2)}) collective-permute-start(bf16[2,2,112,1600]{3,2,1,0:T(8,128)(2,1)} %pad_maximum_fusion.6), channel_id=1, source_target_pairs={{0,8},{8,0},{16,24},{24,16},{1,9},{9,1},{17,25},{25,17},{2,10},{10... | collective-permute-start | bytes 4300808 | tf_op jit(solution)/shard_map/ppermute | solution.py:499
  381.0 37.1 %collective-permute-start.31 = (bf16[2,4,112,800]{3,2,1,0:T(8,128)(2,1)}, bf16[2,4,112,800]{3,2,1,0:T(8,128)(2,1)}, u32[]{:S(2)}, u32[]{:S(2)}) collective-permute-start(bf16[2,4,112,800]{3,2,1,0:T(8,128)(2,1)} %pad_maximum_fusion.5), channel_id=1, source_target_pairs={{0,16},{8,24},{16,0},{24,8},{1,17},{9,25},{17,1},{25,9},{2,18},{10... | collective-permute-start | bytes 4300808 | tf_op jit(solution)/shard_map/ppermute | solution.py:499
  420.7 25.1 %collective-permute-start.35 = (bf16[2,112,1600]{2,1,0:T(8,128)(2,1)}, bf16[2,112,1600]{2,1,0:T(8,128)(2,1)}, u32[]{:S(2)}, u32[]{:S(2)}) collective-permute-start(bf16[2,112,1600]{2,1,0:T(8,128)(2,1)} %fusion.23), channel_id=1, source_target_pairs={{0,16},{8,24},{16,0},{24,8},{1,17},{9,25},{17,1},{25,9},{2,18},{10... | collective-permute-start | bytes 2150408 | tf_op jit(solution)/shard_map/ppermute | solution.py:499
  424.5 21.4 %collective-permute-start.36 = (bf16[4,112,800]{2,1,0:T(8,128)(2,1)}, bf16[4,112,800]{2,1,0:T(8,128)(2,1)}, u32[]{:S(2)}, u32[]{:S(2)}) collective-permute-start(bf16[4,112,800]{2,1,0:T(8,128)(2,1)} %fusion.20), channel_id=1, source_target_pairs={{0,8},{8,0},{16,24},{24,16},{1,9},{9,1},{17,25},{25,17},{2,10},{10... | collective-permute-start | bytes 2150408 | tf_op jit(solution)/shard_map/ppermute | solution.py:499
  427.8 18.0 %collective-permute-start.33 = (bf16[448,256]{1,0:T(8,128)(2,1)S(1)}, bf16[448,256]{1,0:T(8,128)(2,1)S(1)}, u32[]{:S(2)}, u32[]{:S(2)}) collective-permute-start(bf16[448,256]{1,0:T(8,128)(2,1)S(1)} %get-tuple-element.317), channel_id=1, source_target_pairs={{0,2},{1,3},{2,0},{3,1},{4,6},{5,7},{6,4},{7,5},{8,10},{9,11},{10,... | collective-permute-start | bytes 688136 | tf_op jit(solution)/shard_map/ppermute | solution.py:484
  446.5 148.2 %reduce-scatter.9.cloned.1.call-start = ((), (), s32[]{:S(2)}) async-start(), calls=%async_computation.9 | async-start | bytes 1003520 | tf_op jit(solution)/shard_map/reduce_scatter | solution.py:936
  460.3 32.7 %collective-permute-start.39 = (bf16[2,112,1600]{2,1,0:T(8,128)(2,1)}, bf16[2,112,1600]{2,1,0:T(8,128)(2,1)S(1)}, u32[]{:S(2)}, u32[]{:S(2)}) collective-permute-start(bf16[2,112,1600]{2,1,0:T(8,128)(2,1)} %get-tuple-element.200), channel_id=1, source_target_pairs={{0,8},{8,0},{16,24},{24,16},{1,9},{9,1},{17,25},{25,17},{2,10},{10... | collective-permute-start | bytes 2150408 | tf_op jit(solution)/shard_map/ppermute | solution.py:499
  460.4 32.6 %collective-permute-start.40 = (bf16[2,112,1600]{2,1,0:T(8,128)(2,1)}, bf16[2,112,1600]{2,1,0:T(8,128)(2,1)}, u32[]{:S(2)}, u32[]{:S(2)}) collective-permute-start(bf16[2,112,1600]{2,1,0:T(8,128)(2,1)} %get-tuple-element.200), channel_id=1, source_target_pairs={{0,16},{8,24},{16,0},{24,8},{1,17},{9,25},{17,1},{25,9},{2,18},{10... | collective-permute-start | bytes 2150408 | tf_op jit(solution)/shard_map/ppermute | solution.py:499
  461.3 35.4 %collective-permute-start.41 = (bf16[2,2,112,800]{3,2,1,0:T(8,128)(2,1)}, bf16[2,2,112,800]{3,2,1,0:T(8,128)(2,1)S(1)}, u32[]{:S(2)}, u32[]{:S(2)}) collective-permute-start(bf16[2,2,112,800]{3,2,1,0:T(8,128)(2,1)} %get-tuple-element.201), channel_id=1, source_target_pairs={{0,8},{8,0},{16,24},{24,16},{1,9},{9,1},{17,25},{25,17},{2,10},{10... | collective-permute-start | bytes 2150408 | tf_op jit(solution)/shard_map/ppermute | solution.py:499
  462.5 34.2 %collective-permute-start.42 = (bf16[2,2,112,800]{3,2,1,0:T(8,128)(2,1)}, bf16[2,2,112,800]{3,2,1,0:T(8,128)(2,1)S(1)}, u32[]{:S(2)}, u32[]{:S(2)}) collective-permute-start(bf16[2,2,112,800]{3,2,1,0:T(8,128)(2,1)} %get-tuple-element.202), channel_id=1, source_target_pairs={{0,16},{8,24},{16,0},{24,8},{1,17},{9,25},{17,1},{25,9},{2,18},{10... | collective-permute-start | bytes 2150408 | tf_op jit(solution)/shard_map/ppermute | solution.py:499
  499.1 17.6 %collective-permute-start.43 = (bf16[112,800]{1,0:T(8,128)(2,1)S(1)}, bf16[112,800]{1,0:T(8,128)(2,1)S(1)}, u32[]{:S(2)}, u32[]{:S(2)}) collective-permute-start(bf16[112,800]{1,0:T(8,128)(2,1)S(1)} %get-tuple-element.332), channel_id=1, source_target_pairs={{0,0},{4,1},{1,2},{5,3},{2,4},{6,5},{3,6},{7,7},{8,8},{12,9},{9,10... | collective-permute-start | bytes 537608 | tf_op jit(solution)/shard_map/ppermute | solution.py:736
  499.8 18.3 %collective-permute-start.44 = (bf16[112,800]{1,0:T(8,128)(2,1)S(1)}, bf16[112,800]{1,0:T(8,128)(2,1)S(1)}, u32[]{:S(2)}, u32[]{:S(2)}) collective-permute-start(bf16[112,800]{1,0:T(8,128)(2,1)S(1)} %get-tuple-element.331), channel_id=1, source_target_pairs={{5,0},{0,1},{4,2},{1,3},{7,4},{2,5},{6,6},{3,7},{13,8},{8,9},{12,1... | collective-permute-start | bytes 537608 | tf_op jit(solution)/shard_map/ppermute | solution.py:736
  526.2 19.7 %collective-permute-start.48 = (bf16[3,448,800]{2,1,0:T(8,128)(2,1)}, bf16[3,448,800]{2,1,0:T(8,128)(2,1)S(1)}, u32[]{:S(2)}, u32[]{:S(2)}) collective-permute-start(bf16[3,448,800]{2,1,0:T(8,128)(2,1)} %bitcast.281), channel_id=1, source_target_pairs={{0,4},{4,0},{1,5},{5,1},{2,6},{6,2},{3,7},{7,3},{8,12},{12,8},{9,1... | collective-permute-start | bytes 6451208 | tf_op jit(solution)/shard_map/ppermute | solution.py:484
  534.0 29.6 %collective-permute-start.51 = (bf16[4,112,800]{2,1,0:T(8,128)(2,1)S(1)}, bf16[4,112,800]{2,1,0:T(8,128)(2,1)}, u32[]{:S(2)}, u32[]{:S(2)}) collective-permute-start(bf16[4,112,800]{2,1,0:T(8,128)(2,1)S(1)} %get-tuple-element.324), channel_id=1, source_target_pairs={{0,8},{8,0},{16,24},{24,16},{1,9},{9,1},{17,25},{25,17},{2,10},{10... | collective-permute-start | bytes 2150408 | tf_op jit(solution)/shard_map/ppermute | solution.py:499
  535.5 28.2 %collective-permute-start.52 = (bf16[4,112,800]{2,1,0:T(8,128)(2,1)S(1)}, bf16[4,112,800]{2,1,0:T(8,128)(2,1)}, u32[]{:S(2)}, u32[]{:S(2)}) collective-permute-start(bf16[4,112,800]{2,1,0:T(8,128)(2,1)S(1)} %get-tuple-element.324), channel_id=1, source_target_pairs={{0,16},{8,24},{16,0},{24,8},{1,17},{9,25},{17,1},{25,9},{2,18},{10... | collective-permute-start | bytes 2150408 | tf_op jit(solution)/shard_map/ppermute | solution.py:499
  544.6 19.0 %collective-permute-start.49 = (bf16[2,112,800]{2,1,0:T(8,128)(2,1)S(1)}, bf16[2,112,800]{2,1,0:T(8,128)(2,1)S(1)}, u32[]{:S(2)}, u32[]{:S(2)}) collective-permute-start(bf16[2,112,800]{2,1,0:T(8,128)(2,1)S(1)} %fusion.31), channel_id=1, source_target_pairs={{0,16},{8,24},{16,0},{24,8},{1,17},{9,25},{17,1},{25,9},{2,18},{10... | collective-permute-start | bytes 1075208 | tf_op jit(solution)/shard_map/ppermute | solution.py:499
  545.3 18.3 %collective-permute-start.50 = (bf16[2,112,800]{2,1,0:T(8,128)(2,1)S(1)}, bf16[2,112,800]{2,1,0:T(8,128)(2,1)}, u32[]{:S(2)}, u32[]{:S(2)}) collective-permute-start(bf16[2,112,800]{2,1,0:T(8,128)(2,1)S(1)} %fusion.30), channel_id=1, source_target_pairs={{0,8},{8,0},{16,24},{24,16},{1,9},{9,1},{17,25},{25,17},{2,10},{10... | collective-permute-start | bytes 1075208 | tf_op jit(solution)/shard_map/ppermute | solution.py:499
  567.0 112.4 %reduce-scatter.11.cloned.1.call-start = ((), (), s32[]{:S(2)}) async-start(), calls=%async_computation.10 | async-start | bytes 4259840 | tf_op jit(solution)/shard_map/reduce_scatter | solution.py:947
  567.0 22.2 %collective-permute-start.56 = (bf16[2,112,1600]{2,1,0:T(8,128)(2,1)}, bf16[2,112,1600]{2,1,0:T(8,128)(2,1)S(1)}, u32[]{:S(2)}, u32[]{:S(2)}) collective-permute-start(bf16[2,112,1600]{2,1,0:T(8,128)(2,1)} %get-tuple-element.225), channel_id=1, source_target_pairs={{0,8},{8,0},{16,24},{24,16},{1,9},{9,1},{17,25},{25,17},{2,10},{10... | collective-permute-start | bytes 2150408 | tf_op jit(solution)/shard_map/ppermute | solution.py:499
  567.6 23.1 %collective-permute-start.55 = (bf16[4,112,800]{2,1,0:T(8,128)(2,1)}, bf16[4,112,800]{2,1,0:T(8,128)(2,1)S(1)}, u32[]{:S(2)}, u32[]{:S(2)}) collective-permute-start(bf16[4,112,800]{2,1,0:T(8,128)(2,1)} %get-tuple-element.224), channel_id=1, source_target_pairs={{0,16},{8,24},{16,0},{24,8},{1,17},{9,25},{17,1},{25,9},{2,18},{10... | collective-permute-start | bytes 2150408 | tf_op jit(solution)/shard_map/ppermute | solution.py:499
  571.3 18.0 %collective-permute-start.53 = (bf16[3,48,800]{2,1,0:T(8,128)(2,1)S(1)}, bf16[3,48,800]{2,1,0:T(8,128)(2,1)S(1)}, u32[]{:S(2)}, u32[]{:S(2)}) collective-permute-start(bf16[3,48,800]{2,1,0:T(8,128)(2,1)S(1)} %get-tuple-element.287), channel_id=1, source_target_pairs={{0,1},{1,2},{2,3},{4,5},{5,6},{6,7},{8,9},{9,10},{10,11},{12,13},{... | collective-permute-start | bytes 691208 | tf_op jit(solution)/shard_map/ppermute | solution.py:586
  599.4 33.9 %collective-permute-start.59 = (bf16[3,112,800]{2,1,0:T(8,128)(2,1)}, bf16[3,112,800]{2,1,0:T(8,128)(2,1)S(1)}, u32[]{:S(2)}, u32[]{:S(2)}) collective-permute-start(bf16[3,112,800]{2,1,0:T(8,128)(2,1)} %get-tuple-element.296), channel_id=1, source_target_pairs={{0,8},{8,0},{16,24},{24,16},{1,9},{9,1},{17,25},{25,17},{2,10},{10... | collective-permute-start | bytes 1612808 | tf_op jit(solution)/shard_map/ppermute | solution.py:499
  600.9 32.4 %collective-permute-start.60 = (bf16[3,112,800]{2,1,0:T(8,128)(2,1)}, bf16[3,112,800]{2,1,0:T(8,128)(2,1)}, u32[]{:S(2)}, u32[]{:S(2)}) collective-permute-start(bf16[3,112,800]{2,1,0:T(8,128)(2,1)} %get-tuple-element.295), channel_id=1, source_target_pairs={{0,16},{8,24},{16,0},{24,8},{1,17},{9,25},{17,1},{25,9},{2,18},{10... | collective-permute-start | bytes 1612808 | tf_op jit(solution)/shard_map/ppermute | solution.py:499
  602.4 31.0 %collective-permute-start.61 = (bf16[3,112,800]{2,1,0:T(8,128)(2,1)}, bf16[3,112,800]{2,1,0:T(8,128)(2,1)}, u32[]{:S(2)}, u32[]{:S(2)}) collective-permute-start(bf16[3,112,800]{2,1,0:T(8,128)(2,1)} %get-tuple-element.294), channel_id=1, source_target_pairs={{0,24},{8,16},{16,8},{24,0},{1,25},{9,17},{17,9},{25,1},{2,26},{10... | collective-permute-start | bytes 1612808 | tf_op jit(solution)/shard_map/ppermute | solution.py:499
  608.4 23.7 %collective-permute-start.57 = (bf16[1,112,800]{2,1,0:T(8,128)(2,1)S(1)}, bf16[1,112,800]{2,1,0:T(8,128)(2,1)}, u32[]{:S(2)}, u32[]{:S(2)}) collective-permute-start(bf16[1,112,800]{2,1,0:T(8,128)(2,1)S(1)} %copy-done.68), channel_id=1, source_target_pairs={{0,8},{8,0},{16,24},{24,16},{1,9},{9,1},{17,25},{25,17},{2,10},{10... | collective-permute-start | bytes 537608 | tf_op jit(solution)/shard_map/ppermute | solution.py:499
  609.9 23.4 %collective-permute-start.58 = (bf16[1,112,800]{2,1,0:T(8,128)(2,1)S(1)}, bf16[1,112,800]{2,1,0:T(8,128)(2,1)}, u32[]{:S(2)}, u32[]{:S(2)}) collective-permute-start(bf16[1,112,800]{2,1,0:T(8,128)(2,1)S(1)} %copy-done.68), channel_id=1, source_target_pairs={{0,16},{8,24},{16,0},{24,8},{1,17},{9,25},{17,1},{25,9},{2,18},{10... | collective-permute-start | bytes 537608 | tf_op jit(solution)/shard_map/ppermute | solution.py:499
  636.3 46.6 %collective-permute-start.63 = (bf16[3,112,800]{2,1,0:T(8,128)(2,1)S(1)}, bf16[3,112,800]{2,1,0:T(8,128)(2,1)}, u32[]{:S(2)}, u32[]{:S(2)}) collective-permute-start(bf16[3,112,800]{2,1,0:T(8,128)(2,1)S(1)} %add_convert_fusion.9), channel_id=1, source_target_pairs={{0,8},{8,0},{16,24},{24,16},{1,9},{9,1},{17,25},{25,17},{2,10},{10... | collective-permute-start | bytes 1612808 | tf_op jit(solution)/shard_map/ppermute | solution.py:499
  636.8 46.1 %collective-permute-start.64 = (bf16[3,112,800]{2,1,0:T(8,128)(2,1)S(1)}, bf16[3,112,800]{2,1,0:T(8,128)(2,1)}, u32[]{:S(2)}, u32[]{:S(2)}) collective-permute-start(bf16[3,112,800]{2,1,0:T(8,128)(2,1)S(1)} %add_convert_fusion.9), channel_id=1, source_target_pairs={{0,16},{8,24},{16,0},{24,8},{1,17},{9,25},{17,1},{25,9},{2,18},{10... | collective-permute-start | bytes 1612808 | tf_op jit(solution)/shard_map/ppermute | solution.py:499
  638.3 44.6 %collective-permute-start.65 = (bf16[3,112,800]{2,1,0:T(8,128)(2,1)S(1)}, bf16[3,112,800]{2,1,0:T(8,128)(2,1)}, u32[]{:S(2)}, u32[]{:S(2)}) collective-permute-start(bf16[3,112,800]{2,1,0:T(8,128)(2,1)S(1)} %add_convert_fusion.9), channel_id=1, source_target_pairs={{0,24},{8,16},{16,8},{24,0},{1,25},{9,17},{17,9},{25,1},{2,26},{10... | collective-permute-start | bytes 1612808 | tf_op jit(solution)/shard_map/ppermute | solution.py:499
  639.8 43.1 %collective-permute-start.62 = (bf16[1,112,800]{2,1,0:T(8,128)(2,1)}, bf16[1,112,800]{2,1,0:T(8,128)(2,1)}, u32[]{:S(2)}, u32[]{:S(2)}) collective-permute-start(bf16[1,112,800]{2,1,0:T(8,128)(2,1)} %get-tuple-element.240), channel_id=1, source_target_pairs={{0,16},{8,24},{16,0},{24,8},{1,17},{9,25},{17,1},{25,9},{2,18},{10... | collective-permute-start | bytes 537608 | tf_op jit(solution)/shard_map/ppermute | solution.py:499
  (122 other events, 1015.9 us)
Sparse Core Ops, SparseCore 0:
  17.7 69.2 all-gather.3
  92.4 66.9 all-gather.5
  237.0 64.6 all-gather.7
  329.3 60.4 reduce-scatter.4
  446.7 62.9 reduce-scatter.6
  567.1 27.6 reduce-scatter.8
  597.6 64.4 reduce-scatter.10

commit v3 on v2

--- a/solution.py
+++ b/solution.py
@@ -294,7 +294,7 @@
                 moved = p * (n_ref[at, :].astype(F32) - g_ref[at, 1:2])
                 first += jnp.sum(scaled, axis=0, keepdims=True)
                 second += jnp.sum(moved, axis=0, keepdims=True)
-                f_ref[at, 0:1] = jnp.sum(moved, axis=1, keepdims=True)
+                f_ref[at, 0:1] = jnp.sum(moved, axis=1, keepdims=True) / g_ref[at, 0:1]
                 f_ref[at, 1:2] = jnp.sum(p, axis=1, keepdims=True)
                 for c in range(n_col):
 
@@ -385,7 +385,7 @@
     cuts = ff // n // rows
     steps = ff // rows
 
-    def kernel(row_ref, up_ref, down_ref, bias_ref, n_ref, g_ref, h_ref, d_ref, p_ref, acc):
+    def kernel(row_ref, up_ref, down_ref, bias_ref, n_ref, g_ref, h_ref, d_ref, p_ref, s_ref, acc):
         step = pl.program_id(0)
         u = jnp.dot(up_ref[...], n_ref[...], preferred_element_type=F32) + bias_ref[...]
         value, slope = gelu_parts(u)
@@ -393,6 +393,7 @@
         dh = jnp.dot(down_ref[...], g_ref[...], preferred_element_type=F32)
         du = (dh * slope).astype(BF16)
         d_ref[...] = du
+        s_ref[...] = jnp.sum(du.astype(F32), axis=1, keepdims=True)
 
         @pl.when(step == 0)
         def start():
@@ -414,6 +415,7 @@
             jax.ShapeDtypeStruct((ff, tokens), BF16),
             jax.ShapeDtypeStruct((ff, tokens), BF16),
             jax.ShapeDtypeStruct((depth, tokens), BF16),
+            jax.ShapeDtypeStruct((ff, 1), F32),
         ],
         grid_spec=pltpu.PrefetchScalarGridSpec(
             num_scalar_prefetch=1,
@@ -429,6 +431,7 @@
                 pl.BlockSpec((rows, tokens), mine),
                 pl.BlockSpec((rows, tokens), mine),
                 pl.BlockSpec((depth, tokens), full),
+                pl.BlockSpec((rows, 1), mine),
             ],
             scratch_shapes=[pltpu.VMEM((depth, tokens), F32)],
         ),
@@ -514,10 +517,11 @@
 
 
 class Shares:
-    def __init__(self, rows):
+    def __init__(self, rows, tile):
         self.rows = rows
-        self.size = -(-rows // 64) * 16
-        self.starts = [(rows - self.size) * s // 48 * 16 for s in range(3)] + [rows - self.size]
+        self.size = -(-rows // (4 * tile)) * tile
+        self.starts = [(rows - self.size) * s // (3 * tile) * tile for s in range(3)]
+        self.starts.append(rows - self.size)
         ends = self.starts[1:] + [rows]
         self.lengths = [b - a for a, b in zip(self.starts, ends)]
 
@@ -525,13 +529,22 @@
         start = jnp.array(self.starts, jnp.int32)[share]
         return lax.dynamic_slice_in_dim(value, start, self.size, axis)
 
+    def lay(self, parts, axis):
+        return jnp.concatenate(
+            [lax.slice_in_dim(p, 0, n, axis=axis) for p, n in zip(parts, self.lengths)], axis
+        )
+
     def join(self, parts, me, axis):
-        stacked = jnp.stack(parts)
-        laid = [
-            lax.slice_in_dim(pick(stacked, me ^ s), 0, self.lengths[s], axis=axis)
+        odd, high = me % 2 == 1, me // 2 == 1
+        picked = [
+            jnp.where(
+                high,
+                jnp.where(odd, parts[3 ^ s], parts[2 ^ s]),
+                jnp.where(odd, parts[1 ^ s], parts[s]),
+            )
             for s in range(4)
         ]
-        return jnp.concatenate(laid, axis)
+        return self.lay(picked, axis)
 
 
 def assemble(parts, shares, me):
@@ -648,8 +661,7 @@
     return lax.dynamic_slice_in_dim(wide, heads.edge - before, heads.window, axis)
 
 
-def narrow_edges(value, axis, heads, col, width):
-    n = lax.axis_size("col")
+def narrow_cuts(value, axis, heads, col, width):
     edge = heads.edge
     before = jnp.array(heads.before, jnp.int32)[col]
     shape = list(value.shape)
@@ -657,9 +669,9 @@
     wide = lax.dynamic_update_slice_in_dim(
         jnp.zeros(shape, value.dtype), value, edge - before, axis
     )
-    tail = go_down(lax.slice_in_dim(wide, 0, edge, axis=axis), 1, n - 1)
-    front = go_up(lax.slice_in_dim(wide, edge + width, width + 2 * edge, axis=axis), 0, n - 2)
-    return wide, front, tail
+    to_left = lax.slice_in_dim(wide, 0, edge, axis=axis)
+    to_right = lax.slice_in_dim(wide, edge + width, width + 2 * edge, axis=axis)
+    return wide, to_left, to_right
 
 
 def narrow(wide, front, tail, axis, heads, width):
@@ -712,7 +724,7 @@
     firsts = jnp.array(heads.firsts, jnp.int32) * size
     begin = firsts[col]
 
-    shares = Shares(width)
+    shares = Shares(width, 16)
     dp = lax.axis_index("dp")
     row_at = row[None].astype(jnp.int32)
     col_at = col[None].astype(jnp.int32)
@@ -785,12 +797,19 @@
 
     near_out = [swap_with(moved_out, 1), swap_with(moved_out, 2)]
     *cuts, mixed, norms = attn_fwd(meta, key_start, pieces, heads.slots, size)
-    *cuts, near_x, near_y, g_all = gate(list(cuts) + near_out + [g_all], [])
-
-    half = n_col // 2
-    far_out = [swap_with(near_x[:half], 2), swap_with(near_y[half:], 1)]
+    far_cuts = [near_out[0][:half], near_out[1][half:]]
+    *cuts, near_x, near_y, far_x, far_y, g_all, down_own = gate(
+        list(cuts) + near_out + far_cuts + [g_all, down_own], []
+    )
+
+    def move_down(step):
+        return block(down_own, (col - step) % n_col, ff_part, 1)
+
+    far_out = [swap_with(far_x, 2), swap_with(far_y, 1)]
+    moved_down = between_owners(move_down, range(half), False)
     mixed_own = row_sum(cuts).astype(BF16)
-    mixed_own, *far_out = gate([mixed_own] + far_out, [])
+    mixed_own, *rest = gate([mixed_own] + moved_down + far_out, [])
+    moved_down, far_out = rest[:half], rest[half:]
 
     dp_at = dp[None].astype(jnp.int32)
     got = [
@@ -803,9 +822,7 @@
     out_weights = out_weights[:1] + rest[n_col - 1 :]
     out_weights = [w.reshape(depth, in_rows) for w in out_weights]
 
-    moved_down = between_owners(
-        lambda step: block(down_own, (col - step) % n_col, ff_part, 1), range(n_col), False
-    )
+    moved_down = moved_down + between_owners(move_down, range(half, n_col), False)
     got = ordered(got, col, -1)
     lapped = [heads.firsts[j] * size for j in range(n_col)]
     attention = sum(
@@ -816,10 +833,10 @@
     mean2, rstd2 = moments(resid)
     hat2 = (resid - mean2) * rstd2
     n2_own = (hat2 * gain2 + shift2).astype(BF16)
-    n2_own, g, *moved_down = gate([n2_own, g] + moved_down, [hat2])
+    moved_down = jnp.stack(ordered(moved_down, place_in, 1))
+    n2_own, g, moved_down = gate([n2_own, g, moved_down], [hat2])
 
     n2_all = lax.all_gather(n2_own, "col", axis=1, tiled=True)
-    moved_down = jnp.stack(ordered(moved_down, place_in, 1))
     down_weights = assemble([moved_down] + swap_all(moved_down), shares, dp_at)
     down_weights = [turn(down_weights, "row", -step) for step in range(n_row)]
     down_weights = [w.reshape(depth, ff_part) for w in down_weights]
@@ -827,45 +844,58 @@
     g_sums = jnp.sum(g.astype(F32), axis=1)
     n2_all, down_turned = gate([n2_all, down_turned], [g_sums])
 
-    hidden_all, du_all, part2 = hidden_layer(
+    hidden_all, du_all, part2, du_sums = hidden_layer(
         up_turned, down_turned, n_row, up_bias[:, None], n2_all, g_all, row_at
     )
     part2, hidden_all, du_all = gate([part2, hidden_all, du_all], [])
 
+    def relay_cut(value, far, cut, bit):
+        return (cut.take(value, dp ^ (3 - bit), 1).astype(F32) + far.astype(F32)).astype(BF16)
+
+    def share_sum(value, cut, near, relayed):
+        own = cut.take(value, dp, 1).astype(F32)
+        return (own + near.astype(F32) + relayed.astype(F32)).astype(BF16)
+
+    def up_product(r):
+        return token_product(n2_all, du_all, r, n_row, True)
+
+    def down_product(r):
+        return token_product(g_all, hidden_all, r, n_row, False).reshape(n_col, width, ff_part)
+
     dn2 = lax.psum_scatter(part2, "col", scatter_dimension=1, tiled=True)
-    up_grad = [token_product(n2_all, du_all, r, n_row, True) for r in other_rows[::-1]][::-1]
-    down_grad = [token_product(g_all, hidden_all, r, n_row, False) for r in other_rows[::-1]][::-1]
-    down_grad = [d.reshape(n_col, width, ff_part) for d in down_grad]
-    up_grad = up_grad[:1] + [turn(p, "row", i) for i, p in enumerate(up_grad) if i]
-    down_grad = down_grad[:1] + [turn(p, "row", i) for i, p in enumerate(down_grad) if i]
+    up_grad = [up_product(r) for r in other_rows[1:]]
+    n2_all, hidden_all, *up_grad = gate([n2_all, hidden_all] + up_grad, [])
+
+    up_grad = [turn(p, "row", i + 1) for i, p in enumerate(up_grad)]
+    up_grad = [up_product(other_rows[0])] + up_grad
+    down_grad = [down_product(r) for r in other_rows[1:]]
     hidden_all, *rest = gate([hidden_all] + up_grad + down_grad, [])
     up_grad, down_grad = rest[:n_row], rest[n_row:]
-
+    up_rows = width if in_rows % width == 0 else in_rows
+    up_shares, fine = Shares(up_rows, 8), Shares(width, 8)
     up_grad = sum(p.astype(F32) for p in up_grad).astype(BF16)
+    up_grad = up_grad.reshape(in_rows // up_rows, up_rows, ff)
+    up_far = up_shares.take(up_grad, dp ^ 3, 1)
+    up_far, hidden_all, *down_grad = gate([up_far, hidden_all] + down_grad, [])
+
+    up_far = swap_with(up_far, 1)
+    down_grad = [turn(p, "row", i + 1) for i, p in enumerate(down_grad)]
+    down_grad = [down_product(other_rows[0])] + down_grad
+    hidden_all, *down_grad = gate([hidden_all] + down_grad, [])
     down_grad = sum(p.astype(F32) for p in down_grad).astype(BF16)
-    up_rows = width if in_rows % width == 0 else in_rows
-    up_shares = Shares(up_rows)
-    up_grad = up_grad.reshape(in_rows // up_rows, up_rows, ff)
-
-    def first_sum(value, cut, bit):
-        sent = [cut.take(value, dp ^ bit, 1), cut.take(value, dp ^ 3, 1)]
-        return swap_with(jnp.stack(sent), bit)
-
-    def relay(value, first, cut, bit):
-        sent = cut.take(value, dp ^ (3 - bit), 1).astype(F32) + first[1].astype(F32)
-        return swap_with(sent.astype(BF16), 3 - bit)
-
-    def share_sum(value, cut, first, relayed):
-        own = cut.take(value, dp, 1).astype(F32)
-        return (own + first[0].astype(F32) + relayed.astype(F32)).astype(BF16)
-
-    up_first = first_sum(up_grad, up_shares, 1)
-    down_first = first_sum(down_grad, shares, 2)
+    down_far = fine.take(down_grad, dp ^ 3, 1)
+    down_far, hidden_all = gate([down_far, hidden_all], [])
+
+    down_far = swap_with(down_far, 2)
+    up_near = up_shares.take(up_grad, dp ^ 1, 1)
+    down_near = fine.take(down_grad, dp ^ 2, 1)
+    du_row = du_sums[:, 0]
     shrunk = split_product(down_weights, hidden_all, row_at, columns, 3, BF16)
     own_sum = block(shrunk, col, part, 1).astype(F32) + resid
     shrunk = lax.dynamic_update_slice_in_dim(shrunk, own_sum.astype(BF16), col * part, 1)
-    du_sums = jnp.sum(du_all.astype(F32), axis=1)
-    dn2, shrunk = gate([dn2, shrunk], [du_sums])
+    dn2, shrunk, up_far, down_far, up_near, down_near, du_row = gate(
+        [dn2, shrunk, up_far, down_far, up_near, down_near, du_row], []
+    )
 
     dn2 = dn2.astype(F32)
     up2 = dn2 * gain2
@@ -881,14 +911,22 @@
             jnp.sum(dn2, axis=1),
         ]
     )
-    da, db, shrunk, up_first, down_first = gate([da, db, shrunk, up_first, down_first], [sums2])
-
-    got = []
-    for step in range(n_col):
-        to = firsts[(col + step) % n_col]
-        got.append(turn(lax.dynamic_slice_in_dim(da, to, window, 0), "col", step))
-    up_relay = relay(up_grad, up_first, up_shares, 1)
-    down_relay = relay(down_grad, down_first, shares, 2)
+    early = jnp.concatenate([sums2.reshape(-1), du_row, g_sums])
+    da_cuts = [
+        lax.dynamic_slice_in_dim(da, firsts[(col + step) % n_col], window, 0)
+        for step in range(n_col)
+    ]
+    up_near = swap_with(up_near, 1)
+    down_near = swap_with(down_near, 2)
+    up_relay = relay_cut(up_grad, up_far, up_shares, 1)
+    down_relay = relay_cut(down_grad, down_far, fine, 2)
+    db, shrunk, up_near, down_near, up_relay, down_relay, *da_cuts = gate(
+        [db, shrunk, up_near, down_near, up_relay, down_relay] + da_cuts, [early]
+    )
+
+    got = [turn(cut, "col", step) for step, cut in enumerate(da_cuts)]
+    up_relay = swap_with(up_relay, 2)
+    down_relay = swap_with(down_relay, 1)
     out_grad = [token_product(db, attention, r, n_row, False) for r in other_rows[::-1]][::-1]
     out_grad = [o.reshape(n_col, width, in_rows) for o in out_grad]
     rest = gate(got[1:] + out_grad + [up_relay, down_relay, shrunk], [])
@@ -899,92 +937,96 @@
     da_own = jnp.concatenate(ordered(got, col, -1), 1)
     da_pieces = [da_own] + [turn(da_own, "row", -step) for step in range(1, n_row)]
     out_grad = row_sum(out_grad).astype(BF16)
-    up_share = share_sum(up_grad, up_shares, up_first, up_relay)
-    down_share = share_sum(down_grad, shares, down_first, down_relay)
-    out_cuts = [(out_grad[:half], 1), (out_grad[half:], 2)]
-    out_sent = [
-        jnp.stack([shares.take(v, dp ^ bit, 1), shares.take(v, dp ^ 3, 1)]) for v, bit in out_cuts
-    ]
-    *rest, up_share, down_share = gate(da_pieces[1:] + out_sent + [up_share, down_share], [])
-    da_pieces, out_sent = [da_own] + rest[: n_row - 1], rest[n_row - 1 :]
-
-    out_first = [swap_with(v, bit) for v, (_, bit) in zip(out_sent, out_cuts)]
-    up_near = [swap_with(up_share, 1), swap_with(up_share, 2)]
+    up_share = share_sum(up_grad, up_shares, up_near, up_relay)
+    down_share = share_sum(down_grad, fine, down_near, down_relay)
+    out_sent = jnp.stack([fine.take(out_grad, dp ^ 1, 1), fine.take(out_grad, dp ^ 3, 1)])
+    *rest, out_sent, up_share, down_share = gate(
+        da_pieces[1:] + [out_sent, up_share, down_share], []
+    )
+    da_pieces = [da_own] + rest
+
+    out_first = swap_with(out_sent, 1)
+    up_y = swap_with(up_share, 2)
+
+    def move_home(step):
+        return pick(down_share, (place_in + step) % n_col)
+
+    down_home = between_owners(move_home, range(n_col - 1), True)
     dqkv = attn_bwd(meta, key_start, pieces, da_pieces, mixed, norms, heads.slots, size)
-    *rest, down_share = gate(list(dqkv) + up_near + out_first + [down_share], [])
-    dqkv, up_near, out_first = rest[:n_row], rest[n_row : n_row + 2], rest[n_row + 2 :]
-
-    down_home = between_owners(
-        lambda step: pick(down_share, (place_in + step) % n_col), range(n_col), True
-    )
+    *rest, out_first, up_y, up_share, down_share = gate(
+        list(dqkv) + down_home + [out_first, up_y, up_share, down_share], []
+    )
+    dqkv, down_home = rest[:n_row], rest[n_row:]
+    out_near, out_far = out_first[0], out_first[1]
+    out_relay = relay_cut(out_grad, out_far, fine, 1)
+
+    out_relay = swap_with(out_relay, 2)
+    up_x = swap_with(up_share, 1)
+    down_home = down_home + between_owners(move_home, range(n_col - 1, n_col), True)
     dqkv = row_sum(dqkv).astype(BF16).reshape(3 * window, length)
-    *rest, dqkv, outputs = gate(down_home + out_first + up_near + [dqkv, outputs], [])
-    down_home, out_first, up_near = rest[:n_col], rest[n_col : n_col + 2], rest[n_col + 2 :]
-
     homes = jnp.stack(ordered(down_home, col, -1))
+    out_share = share_sum(out_grad, fine, out_near, out_relay)
+    dqkv, homes, outputs, up_x, out_share = gate([dqkv, homes, outputs, up_x, out_share], [])
+
     homes_near = [swap_with(homes, 1), swap_with(homes, 2)]
-    out_relay = [relay(v, f, shares, bit) for (v, bit), f in zip(out_cuts, out_first)]
     qkv_parts = [token_product(dqkv, n1, r, n_row, False) for r in other_rows[::-1]][::-1]
     qkv_parts = [q.reshape(3, window, in_rows) for q in qkv_parts]
     qkv_grad = row_sum(qkv_parts).astype(BF16)
-    dqkv, qkv_grad, *rest = gate([dqkv, qkv_grad] + out_relay + homes_near, [])
-    out_relay, homes_near = rest[:2], rest[2:]
-
-    out_share = [
-        share_sum(v, shares, f, r) for (v, _), f, r in zip(out_cuts, out_first, out_relay)
-    ]
-    out_home = lax.psum_scatter(
-        jnp.concatenate(out_share), "col", scatter_dimension=0, tiled=True
-    )
-    wide, front, tail = narrow_edges(qkv_grad, 1, heads, col, width)
-    homes_far = swap_with(homes_near[0], 2)
-    up_far = swap_with(up_near[1], 1)
+    wide, to_left, to_right = narrow_cuts(qkv_grad, 1, heads, col, width)
+    dqkv, wide, to_left, to_right, out_share, up_y, *homes_near = gate(
+        [dqkv, wide, to_left, to_right, out_share, up_y] + homes_near, []
+    )
+
+    out_home = lax.psum_scatter(out_share, "col", scatter_dimension=0, tiled=True)
+    tail, front = go_down(to_left, 1, n_col - 1), go_up(to_right, 0, n_col - 2)
+    homes_far = swap_with(homes_near[1], 1)
+    up_far = swap_with(up_x, 2)
     dn1, norm1 = norm_product_tn(w3, dqkv, n1, columns, rstd1, dr, col_at, n_col)
-    dn1, front, tail, dqkv, out_home, homes_far, up_far, outputs = gate(
-        [dn1, front, tail, dqkv, out_home, homes_far, up_far, outputs], [norm1]
+    qkv_grad = narrow(wide, front, tail, 1, heads, width).astype(BF16)
+    qkv_sent = [fine.take(qkv_grad, dp ^ m, 1) for m in (1, 2, 3)]
+    dn1, dqkv, homes_far, up_far, out_home, *qkv_sent = gate(
+        [dn1, dqkv, homes_far, up_far, out_home] + qkv_sent, [norm1]
     )
 
     dx = lax.psum_scatter(dn1, "col", scatter_dimension=0, tiled=True)
-    qkv_grad = narrow(wide, front, tail, 1, heads, width).astype(BF16)
-    qkv_got = [swap_with(shares.take(qkv_grad, dp ^ m, 1), m) for m in (1, 2, 3)]
-    out_near = [swap_with(out_home, 1), swap_with(out_home, 2)]
+    qkv_got = [swap_with(v, m) for v, m in zip(qkv_sent, (1, 2, 3))]
+    out_all = [swap_with(out_home, 1), swap_with(out_home, 2)]
+    homes, homes_far, norm1, outputs, dqkv = gate(
+        [homes, homes_far, norm1, outputs, dqkv], qkv_sent
+    )
+    homes = fine.join([homes] + homes_near + [homes_far], dp, 1).astype(F32)
+    down_grad = jnp.concatenate([homes[j] for j in range(n_col)], 1)
+    outputs = (outputs.astype(F32) + down_bias[:, None]).astype(BF16)
     dq_dv = jnp.sum(dqkv.astype(F32), axis=1).reshape(3, window)
     sums = lax.dynamic_update_slice_in_dim(jnp.zeros((2, depth), F32), dq_dv[::2], begin, 1)
-    sums = jnp.concatenate([sums, (norm1[:, :1] / gain1).T, norm1[:, 1:].T, sums2]).reshape(-1)
-    small = jnp.concatenate([sums, du_sums, g_sums])[None]
-    small, outputs, up_far, homes_far, *rest = gate(
-        [small, outputs, up_far, homes_far] + out_near + qkv_got, []
-    )
-    out_near, qkv_got = rest[:2], rest[2:]
-
-    qkv_share = shares.take(qkv_grad, dp, 1).astype(F32)
-    qkv_share = (qkv_share + sum(q.astype(F32) for q in qkv_got)).astype(BF16)
-    qkv_all = swap_all(qkv_share)
-    out_far = swap_with(out_near[0], 2)
+    small = jnp.concatenate([sums.reshape(-1), norm1.T.reshape(-1), early])[None]
     small = small_sum(small, ("row",))[0]
     sums, local = small[: 7 * depth].reshape(7, depth), small[7 * depth :]
     sums = small_sum(sums, ("col",))
     sums = lax.dynamic_slice_in_dim(sums, col * width, width, 1)
     small = jnp.concatenate([sums.reshape(-1), local])[None]
+    qkv_share = fine.take(qkv_grad, dp, 1).astype(F32)
+    qkv_share = (qkv_share + sum(q.astype(F32) for q in qkv_got)).astype(BF16)
+    small, up_far, qkv_share, *out_all = gate(
+        [small, up_far, qkv_share] + out_all, [down_grad, outputs]
+    )
+
+    qkv_all = swap_all(qkv_share)
+    out_all.append(swap_with(out_all[0], 2))
     small = small_sum(small, ("dp",))[0]
     sums, local = small[: 7 * width].reshape(7, width), small[7 * width :]
-    up_grad = up_shares.join([up_share] + up_near + [up_far], dp, 1).astype(F32)
+    up_grad = up_shares.join([up_share, up_x, up_y, up_far], dp, 1).astype(F32)
     up_grad = up_grad.reshape(in_rows, ff)
-    homes = shares.join([homes] + homes_near + [homes_far], dp, 1).astype(F32)
-    down_grad = jnp.concatenate([homes[j] for j in range(n_col)], 1)
-    outputs = (outputs.astype(F32) + down_bias[:, None]).astype(BF16)
     hat1 = (x.astype(F32) - mean1) * rstd1
     dx = dx.reshape(width + 16, length)
     lines = dx[width : width + 4].astype(F32)
     lines = (lines[0::2] + lines[1::2]) / depth
     input_grad = dx[:width].astype(F32) - rstd1 * (lines[0:1] + hat1 * lines[1:2])
     input_grad = input_grad.astype(BF16)
-    out_far, *qkv_all = gate(
-        [out_far] + qkv_all, [sums, local, up_grad, down_grad, outputs, input_grad]
-    )
-
-    out_grad = shares.join([out_home] + out_near + [out_far], dp, 1).astype(F32)[0]
-    qkv_grad = shares.join([qkv_share] + qkv_all, dp, 1).astype(F32)
+    *out_all, a, b, c = gate(out_all + qkv_all, [sums, local, up_grad, input_grad])
+
+    out_grad = fine.join([out_home] + out_all, dp, 1).astype(F32)[0]
+    qkv_grad = fine.join([qkv_share, a, b, c], dp, 1).astype(F32)
     return (
         outputs.T.reshape(tokens.shape),
         input_grad.T.reshape(tokens.shape),

time: 707 us -> 671 us (0.949)
  waiting for transfers between devices: 210 us -> 169 us
  between operations: 16 us -> 23.3 us
    ppermute x30, waiting for transfers between devices: 89.4 us -> 46.3 us  [swap_with(): return lax.ppermute(value, 'dp', [(i, i ^ bit) for i in range(4)])]
    ppermute x5, waiting for transfers between devices: 12.5 us -> 25.7 us  [small_sum(): lax.ppermute(value, axis, [(i, i ^ bit) for i in range(size)])]
    another operation x9 -> x2, other arithmetic: 12.6 us -> 2.64 us  [the longest x1 1.65 us: body(): jnp.stack([fine.take(out_grad, dp ^ 1, 1), fine.take(out_grad, dp ^ 3, 1)])]
    ppermute x8, waiting for transfers between devices: 12.1 us -> 19.4 us  [between_owners(): got.append(lax.ppermute(value_of(step), ('row', 'col'), pairs))]
    unnamed x187 -> x227, local copies, waits for them, and re-layouts: 27.4 us -> 34.4 us
    convert_element_type x10 -> x8, other arithmetic: 20.5 us -> 16.4 us  [the longest x3 7.14 us: share_sum(): return (own + near.astype(F32) + relayed.astype(F32)).astype(BF16)]
  transfers between devices with their start and end apart: 78 -> 78, of which waited for: 31 -> 27; matrix products, arithmetic and copies ran while one was open for 20% -> 21% of each run, Pallas kernels for 21% -> 20%
where the time goes in v3:
time: 671 us; the launch traced here: 662 us
  Pallas kernels  184 us (27%)
  waiting for transfers between devices  169 us (25%)
  other arithmetic  106 us (16%)
  starting transfers between devices  101 us (15%)
  local copies, waits for them, and re-layouts  78.4 us (12%)
  between operations  23.3 us (3%)
    pallas_call x8, Pallas kernels, token_product(): pl.pallas_call(kernel, out_shape=jax.ShapeDtypeStruct((rows_a, rows_b), B...  49.9 us
    ppermute x30, waiting for transfers between devices, swap_with(): return lax.ppermute(value, 'dp', [(i, i ^ bit) for i in range(4)])  46.3 us
    unnamed x227, local copies, waits for them, and re-layouts  34.4 us
    ppermute x30, starting transfers between devices, swap_with(): return lax.ppermute(value, 'dp', [(i, i ^ bit) for i in range(4)])  33.5 us
    ppermute x24, waiting for transfers between devices, turn(): lax.ppermute(value, axis, [(i, (i + steps) % size) for i in range(size)])  28.6 us
    pallas_call x1, Pallas kernels, hidden_layer(): pl.pallas_call(kernel, out_shape=[jax.ShapeDtypeStruct((ff, tokens), BF16...  27.8 us
    ppermute x8, starting transfers between devices, between_owners(): got.append(lax.ppermute(value_of(step), ('row', 'col'), pairs))  26.7 us
    pallas_call x1, Pallas kernels, attn_bwd(): pl.pallas_call(functools.partial(bwd_kernel, n_row, n_slots, hd, ks.shape...  26.1 us
  transfers between devices with their start and end apart: 78, of which 27 were waited for; matrix products, arithmetic and copies ran while one was open for 21% of the time, Pallas kernels for 20%

profile of v3, /device:TPU:0, one launch (start us, length us, event | category | flops | bytes accessed | tf_op | source)
XLA Modules:
  0.0 661.9 jit_solution(842501483805173833)
XLA Ops:
  11.3 4.9 collective-permute-start
  17.7 4.3 collective-permute-done
  22.0 3.8 collective-permute-done.1
  25.8 4.4 fusion.8
  41.0 5.3 copy.204
  55.6 5.2 copy.205
  64.1 4.2 maximum_bitcast_fusion.refs_8_.up_ref
  68.3 18.7 %all-gather.4.cloned.1.call-done.refs_0_ = bf16[1600,1024]{1,0:T(8,128)(2,1)} async-done(((bf16[400,1024]{1,0:T(8,128)(2,1)}), bf16[1600,1024]{1,0:T(8,128)(2,1)}) %all-gather.4.cloned.1.call-update) | async-done | bytes 3276816 | tf_op jit(solution)/shard_map/all_gather | solution.py:751
  95.5 4.0 fusion.5.b_ref.n_ref
  99.5 9.8 %shard_map.488 = bf16[1344,1024]{1,0:T(8,128)(2,1)} custom-call(bf16[1344,1600]{1,0:T(8,128)(2,1)} %get-tuple-element.158.a_ref, bf16[1600,1024]{1,0:T(8,128)(2,1)} %fusion.5.b_ref.n_ref, f32[1344,1]{1,0:T(8,128)} %get-tuple-element.160.bias_ref), custom_call_target="tpu_custom_call" | custom-call | tf_op jit(solution)/shard_map/pallas_call | solution.py:189
  121.8 18.0 %shard_map.491 = (bf16[448,1024]{1,0:T(8,128)(2,1)S(1)}, bf16[448,1024]{1,0:T(8,128)(2,1)S(1)}, bf16[448,2048]{1,0:T(8,128)(2,1)S(1)}, f32[7,2048]{1,0:T(8,128)S(1)}) custom-call(s32[4]{0:T(128)S(1)} %copy-done.7, s32[25,4]{1,0:T(8,128)S(1)} %copy.210.ks, bf16[3,448,1024]{2,1,0:T(8,128)(2,1)} %get-tuple-element.162.refs_0_, ...), custom_call_target="tpu_custom_call" | custom-call | tf_op jit(solution)/shard_map/pallas_call | solution.py:148
  146.1 13.2 %all-gather.6.cloned.1.call-done.refs_6_ = bf16[1600,1024]{1,0:T(8,128)(2,1)} async-done(((bf16[400,1024]{1,0:T(8,128)(2,1)}), bf16[1600,1024]{1,0:T(8,128)(2,1)}) %all-gather.6.cloned.1.call-update) | async-done | bytes 3276816 | tf_op jit(solution)/shard_map/all_gather | solution.py:784
  174.4 3.5 shard_map.494
  177.9 4.7 collective-permute-start.21
  182.9 3.7 collective-permute-start.20
  186.6 6.6 collective-permute-done.18.refs_1_
  193.2 8.9 %collective-permute-done.19.refs_2_ = bf16[448,256]{1,0:T(8,128)(2,1)S(1)} collective-permute-done((bf16[448,256]{1,0:T(8,128)(2,1)S(1)}, bf16[448,256]{1,0:T(8,128)(2,1)S(1)}, u32[]{:S(2)}, u32[]{:S(2)}) %collective-permute-start.19) | collective-permute-done | bytes 229408 | tf_op jit(solution)/shard_map/ppermute | solution.py:487
  205.1 6.2 shard_map.496
  221.2 4.4 collective-permute-done.23
  225.6 4.8 collective-permute-done.22
  235.9 17.6 %collective-permute-done.24.refs_1_ = bf16[4,112,800]{2,1,0:T(8,128)(2,1)S(1)} collective-permute-done((bf16[4,112,800]{2,1,0:T(8,128)(2,1)}, bf16[4,112,800]{2,1,0:T(8,128)(2,1)S(1)}, u32[]{:S(2)}, u32[]{:S(2)}) %collective-permute-start.24) | collective-permute-done | bytes 716832 | tf_op jit(solution)/shard_map/ppermute | solution.py:502
  253.4 15.7 %collective-permute-done.25.refs_2_ = bf16[4,112,800]{2,1,0:T(8,128)(2,1)S(1)} collective-permute-done((bf16[4,112,800]{2,1,0:T(8,128)(2,1)}, bf16[4,112,800]{2,1,0:T(8,128)(2,1)S(1)}, u32[]{:S(2)}, u32[]{:S(2)}) %collective-permute-start.25) | collective-permute-done | bytes 716832 | tf_op jit(solution)/shard_map/ppermute | solution.py:502
  276.4 3.6 collective-permute-done.27
  280.0 6.9 %shard_map.499.refs_1_ = bf16[1600,1600]{1,0:T(8,128)(2,1)} custom-call(bf16[1600,800]{1,0:T(8,128)(2,1)} %bitcast.189, bf16[1600,800]{1,0:T(8,128)(2,1)} %bitcast.52.refs_1_), custom_call_target="tpu_custom_call" | custom-call | tf_op jit(solution)/shard_map/pallas_call | solution.py:458
  286.9 7.0 %all-gather.8.cloned.1.call-done.refs_0_ = bf16[1600,1024]{1,0:T(8,128)(2,1)} async-done(((bf16[1600,256]{1,0:T(8,128)(2,1)}), bf16[1600,1024]{1,0:T(8,128)(2,1)}) %all-gather.8.cloned.1.call-update) | async-done | bytes 3276816 | tf_op jit(solution)/shard_map/all_gather | solution.py:839
  294.0 27.8 %shard_map.501 = (bf16[1600,1024]{1,0:T(8,128)(2,1)}, bf16[1600,1024]{1,0:T(8,128)(2,1)}, bf16[1600,1024]{1,0:T(8,128)(2,1)}, f32[1600,1]{1,0:T(8,128)}) custom-call(s32[1]{0:T(128)} %bitcast.9.row_ref, bf16[1600,1600]{1,0:T(8,128)(2,1)} %maximum_bitcast_fusion.refs_8_.up_ref, bf16[1600,1600]{1,0:T(8,128)(2,1)} %get-tuple-element.194.down_ref, ...), custom_call_target="tpu_custom_call" | custom-call | tf_op jit(solution)/shard_map/pallas_call | solution.py:412
  321.7 6.7 %shard_map.503.refs_2_ = bf16[800,1600]{1,0:T(8,128)(2,1)} custom-call(s32[1]{0:T(128)} %bitcast.53.index_ref, bf16[1600,1024]{1,0:T(8,128)(2,1)} %get-tuple-element.195.n_ref.a_ref.refs_0_, bf16[1600,1024]{1,0:T(8,128)(2,1)} %get-tuple-element.201.b_ref), custom_call_target="tpu_custom_call" | custom-call | tf_op jit(solution)/shard_map/pallas_call | solution.py:356
  333.6 7.2 %shard_map.506 = bf16[1600,800]{1,0:T(8,128)(2,1)} custom-call(s32[1]{0:T(128)} %bitcast.53.index_ref, bf16[1600,1024]{1,0:T(8,128)(2,1)} %get-tuple-element.172.g_ref.a_ref, bf16[1600,1024]{1,0:T(8,128)(2,1)} %get-tuple-element.202.b_ref.refs_0_), custom_call_target="tpu_custom_call" | custom-call | tf_op jit(solution)/shard_map/pallas_call | solution.py:356
  340.8 6.7 %shard_map.505.refs_1_ = bf16[800,1600]{1,0:T(8,128)(2,1)} custom-call(s32[1]{0:T(128)} %bitcast.54.index_ref, bf16[1600,1024]{1,0:T(8,128)(2,1)} %get-tuple-element.203.a_ref, bf16[1600,1024]{1,0:T(8,128)(2,1)} %get-tuple-element.201.b_ref), custom_call_target="tpu_custom_call" | custom-call | tf_op jit(solution)/shard_map/pallas_call | solution.py:356
  355.4 7.3 %shard_map.509 = bf16[1600,800]{1,0:T(8,128)(2,1)} custom-call(s32[1]{0:T(128)} %bitcast.54.index_ref, bf16[1600,1024]{1,0:T(8,128)(2,1)} %get-tuple-element.172.g_ref.a_ref, bf16[1600,1024]{1,0:T(8,128)(2,1)} %get-tuple-element.209.b_ref.refs_0_), custom_call_target="tpu_custom_call" | custom-call | tf_op jit(solution)/shard_map/pallas_call | solution.py:356
  373.9 11.2 %shard_map.512 = bf16[1600,1024]{1,0:T(8,128)(2,1)} custom-call(s32[1]{0:T(128)} %bitcast.9.row_ref, bf16[1600,1024]{1,0:T(8,128)(2,1)} %get-tuple-element.214.b_ref, f32[1600,4]{1,0:T(8,128)} %get-tuple-element.186.bias_ref.g_ref, bf16[1600,800]{1,0:T(8,128)(2,1)} %bitcast.190, bf16[1600,800]{1,0:T(8,128)(2,1)} %bitcast.52.refs_1_), custom_call_target="tpu_custom_call" | custom-call | tf_op jit(solution)/shard_map/pallas_call | solution.py:217
  401.3 6.8 %shard_map.514 = bf16[1600,256]{1,0:T(8,128)(2,1)} custom-call(s32[1]{0:T(128)} %bitcast.9.row_ref, bf16[1600,256]{1,0:T(8,128)(2,1)} %get-tuple-element.332.b_ref.refs_0_, bf16[1600,800]{1,0:T(8,128)(2,1)} %bitcast.188, bf16[1600,800]{1,0:T(8,128)(2,1)} %bitcast.46.refs_1_), custom_call_target="tpu_custom_call" | custom-call | tf_op jit(solution)/shard_map/pallas_call | solution.py:257
  421.1 4.6 shard_map.516
  425.7 4.6 shard_map.517
  453.2 8.6 %collective-permute-start.42 = (bf16[104,800]{1,0:T(8,128)(2,1)S(1)}, bf16[104,800]{1,0:T(8,128)(2,1)S(1)}, u32[]{:S(2)}, u32[]{:S(2)}) collective-permute-start(bf16[104,800]{1,0:T(8,128)(2,1)S(1)} %get-tuple-element.398), channel_id=1, source_target_pairs={{5,0},{0,1},{4,2},{1,3},{7,4},{2,5},{6,6},{3,7},{13,8},{8,9},{12,1... | collective-permute-start | bytes 499208 | tf_op jit(solution)/shard_map/ppermute | solution.py:748
  464.9 26.1 %shard_map.520 = (bf16[3,448,1024]{2,1,0:T(8,128)(2,1)}, bf16[3,448,1024]{2,1,0:T(8,128)(2,1)}) custom-call(s32[4]{0:T(128)} %get-tuple-element.157.meta, s32[25,4]{1,0:T(8,128)} %copy-done.5, bf16[3,448,1024]{2,1,0:T(8,128)(2,1)} %get-tuple-element.162.refs_0_, bf16[3,448,1024]{2,1,0:T(8,128)(2,1)} %get-tuple-element.166.refs_1_, ...), custom_call_target="tpu_custom_call" | custom-call | tf_op jit(solution)/shard_map/pallas_call | solution.py:157
  495.7 5.1 collective-permute-start.47
  500.9 7.2 %collective-permute-done.47 = bf16[104,800]{1,0:T(8,128)(2,1)S(1)} collective-permute-done((bf16[104,800]{1,0:T(8,128)(2,1)S(1)}, bf16[104,800]{1,0:T(8,128)(2,1)S(1)}, u32[]{:S(2)}, u32[]{:S(2)}) %collective-permute-start.47) | collective-permute-done | bytes 166432 | tf_op jit(solution)/shard_map/ppermute | solution.py:748
  509.3 3.9 collective-permute-done.49
  515.5 4.2 add_convert_fusion.2
  519.7 6.5 shard_map.524
  529.9 6.4 shard_map.523
  541.1 5.2 collective-permute-done.51.refs_6_
  549.1 5.0 collective-permute-start.55
  556.9 14.3 %shard_map.526 = (bf16[4,416,1024]{2,1,0:T(8,128)(2,1)}, f32[1600,2]{1,0:T(8,128)}) custom-call(s32[1]{0:T(128)} %bitcast.85.col_ref, bf16[1344,1600]{1,0:T(8,128)(2,1)} %get-tuple-element.158.a_ref, bf16[1344,1024]{1,0:T(8,128)(2,1)} %get-tuple-element.263.b_ref.refs_1_, bf16[1600,1024]{1,0:T(8,128)(2,1)} %fusion.5.b_ref.n_ref, ...), custom_call_target="tpu_custom_call" | custom-call | tf_op jit(solution)/shard_map/pallas_call | solution.py:315
  587.8 6.8 %collective-permute-done.58 = f32[7,1600]{1,0:T(8,128)S(1)} collective-permute-done((f32[7,1600]{1,0:T(8,128)S(1)}, f32[7,1600]{1,0:T(8,128)S(1)}, u32[]{:S(2)}, u32[]{:S(2)}) %collective-permute-start.58) | collective-permute-done | bytes 44832 | tf_op jit(solution)/shard_map/ppermute | solution.py:593
  597.0 7.0 %concatenate.68.refs_5_ = f32[400,3200]{1,0:T(8,128)} concatenate(f32[400,800]{1,0:T(8,128)} %get-tuple-element.339, f32[400,800]{1,0:T(8,128)} %get-tuple-element.338, f32[400,800]{1,0:T(8,128)} %get-tuple-element.337, f32[400,800]{1,0:T(8,128)S(1)} %get-tuple-element.336), dimensions={1} | concatenate | bytes 10240000 | tf_op jit(solution)/shard_map/concatenate | solution.py:998
  617.5 17.8 %collective-permute-done.69 = f32[1,4800]{1,0:T(1,128)S(1)} collective-permute-done((f32[1,4800]{1,0:T(1,128)}, f32[1,4800]{1,0:T(1,128)S(1)}, u32[]{:S(2)}, u32[]{:S(2)}) %collective-permute-start.69) | collective-permute-done | bytes 19232 | tf_op jit(solution)/shard_map/ppermute | solution.py:593
  (531 shorter events, 242.2 us)
Async XLA Ops:
  7.2 79.8 %all-gather.4.cloned.1.call-start = ((), (), s32[]{:S(2)}) async-start(), calls=%async_computation.4 | async-start | bytes 4096000 | tf_op jit(solution)/shard_map/all_gather | solution.py:751
  17.7 141.7 %all-gather.6.cloned.1.call-start = ((), (), s32[]{:S(2)}) async-start(), calls=%async_computation.5 | async-start | bytes 4096000 | tf_op jit(solution)/shard_map/all_gather | solution.py:784
  30.2 19.0 %collective-permute-start.2 = (bf16[3,448,800]{2,1,0:T(8,128)(2,1)}, bf16[3,448,800]{2,1,0:T(8,128)(2,1)}, u32[]{:S(2)}, u32[]{:S(2)}) collective-permute-start(bf16[3,448,800]{2,1,0:T(8,128)(2,1)} %fusion.8), channel_id=1, source_target_pairs={{0,4},{4,0},{1,5},{5,1},{2,6},{6,2},{3,7},{7,3},{8,12},{12,8},{9,1... | collective-permute-start | bytes 6451208 | tf_op jit(solution)/shard_map/ppermute | solution.py:487
  30.2 25.4 %collective-permute-start.6 = (bf16[800,1600]{1,0:T(8,128)(2,1)}, bf16[800,1600]{1,0:T(8,128)(2,1)}, u32[]{:S(2)}, u32[]{:S(2)}) collective-permute-start(bf16[800,1600]{1,0:T(8,128)(2,1)} %param.47), channel_id=1, source_target_pairs={{0,4},{4,0},{1,5},{5,1},{2,6},{6,2},{3,7},{7,3},{8,12},{12,8},{9,1... | collective-permute-start | bytes 7680008 | tf_op jit(solution)/shard_map/ppermute | solution.py:487
  87.0 22.3 %collective-permute-start.7 = (bf16[112,800]{1,0:T(8,128)(2,1)}, bf16[112,800]{1,0:T(8,128)(2,1)S(1)}, u32[]{:S(2)}, u32[]{:S(2)}) collective-permute-start(bf16[112,800]{1,0:T(8,128)(2,1)} %get-tuple-element.161), channel_id=1, source_target_pairs={{0,3},{1,0},{2,1},{3,2},{4,7},{5,4},{6,5},{7,6},{8,11},{9,8},{10,9... | collective-permute-start | bytes 537608 | tf_op jit(solution)/shard_map/ppermute | solution.py:487
  87.8 24.8 %collective-permute-start.8 = (bf16[112,800]{1,0:T(8,128)(2,1)}, bf16[112,800]{1,0:T(8,128)(2,1)S(1)}, u32[]{:S(2)}, u32[]{:S(2)}) collective-permute-start(bf16[112,800]{1,0:T(8,128)(2,1)} %get-tuple-element.161), channel_id=1, source_target_pairs={{0,2},{1,3},{2,0},{3,1},{4,6},{5,7},{6,4},{7,5},{8,10},{9,11},{10,... | collective-permute-start | bytes 537608 | tf_op jit(solution)/shard_map/ppermute | solution.py:487
  87.8 24.8 %collective-permute-start.9 = (bf16[112,800]{1,0:T(8,128)(2,1)}, bf16[112,800]{1,0:T(8,128)(2,1)S(1)}, u32[]{:S(2)}, u32[]{:S(2)}) collective-permute-start(bf16[112,800]{1,0:T(8,128)(2,1)} %get-tuple-element.161), channel_id=1, source_target_pairs={{0,1},{1,2},{2,3},{3,0},{4,5},{5,6},{6,7},{7,4},{8,9},{9,10},{10,1... | collective-permute-start | bytes 537608 | tf_op jit(solution)/shard_map/ppermute | solution.py:487
  92.3 201.7 %all-gather.8.cloned.1.call-start = ((), (), s32[]{:S(2)}) async-start(), calls=%async_computation.6 | async-start | bytes 4096000 | tf_op jit(solution)/shard_map/all_gather | solution.py:839
  118.7 24.8 %collective-permute-start.11 = (bf16[4,112,800]{2,1,0:T(8,128)(2,1)}, bf16[4,112,800]{2,1,0:T(8,128)(2,1)S(1)}, u32[]{:S(2)}, u32[]{:S(2)}) collective-permute-start(bf16[4,112,800]{2,1,0:T(8,128)(2,1)} %get-tuple-element.169.refs_0_), channel_id=1, source_target_pairs={{0,8},{8,0},{16,24},{24,16},{1,9},{9,1},{17,25},{25,17},{2,10},{10... | collective-permute-start | bytes 2150408 | tf_op jit(solution)/shard_map/ppermute | solution.py:502
  120.2 24.2 %collective-permute-start.12 = (bf16[4,112,800]{2,1,0:T(8,128)(2,1)}, bf16[4,112,800]{2,1,0:T(8,128)(2,1)}, u32[]{:S(2)}, u32[]{:S(2)}) collective-permute-start(bf16[4,112,800]{2,1,0:T(8,128)(2,1)} %get-tuple-element.169.refs_0_), channel_id=1, source_target_pairs={{0,16},{8,24},{16,0},{24,8},{1,17},{9,25},{17,1},{25,9},{2,18},{10... | collective-permute-start | bytes 2150408 | tf_op jit(solution)/shard_map/ppermute | solution.py:502
  177.9 24.1 %collective-permute-start.21 = (bf16[4,400,800]{2,1,0:T(8,128)(2,1)}, bf16[4,400,800]{2,1,0:T(8,128)(2,1)}, u32[]{:S(2)}, u32[]{:S(2)}) collective-permute-start(bf16[4,400,800]{2,1,0:T(8,128)(2,1)} %shard_map.494), channel_id=1, source_target_pairs={{0,4},{4,0},{1,5},{5,1},{2,6},{6,2},{3,7},{7,3},{8,12},{12,8},{9,1... | collective-permute-start | bytes 7680008 | tf_op jit(solution)/shard_map/ppermute | solution.py:487
  182.8 19.3 %collective-permute-start.19 = (bf16[448,256]{1,0:T(8,128)(2,1)S(1)}, bf16[448,256]{1,0:T(8,128)(2,1)S(1)}, u32[]{:S(2)}, u32[]{:S(2)}) collective-permute-start(bf16[448,256]{1,0:T(8,128)(2,1)S(1)} %get-tuple-element.376), channel_id=1, source_target_pairs={{0,2},{1,3},{2,0},{3,1},{4,6},{5,7},{6,4},{7,5},{8,10},{9,11},{10,... | collective-permute-start | bytes 688136 | tf_op jit(solution)/shard_map/ppermute | solution.py:487
  182.9 19.2 %collective-permute-start.20 = (bf16[448,256]{1,0:T(8,128)(2,1)S(1)}, bf16[448,256]{1,0:T(8,128)(2,1)S(1)}, u32[]{:S(2)}, u32[]{:S(2)}) collective-permute-start(bf16[448,256]{1,0:T(8,128)(2,1)S(1)} %get-tuple-element.375), channel_id=1, source_target_pairs={{0,3},{1,0},{2,1},{3,2},{4,7},{5,4},{6,5},{7,6},{8,11},{9,8},{10,9... | collective-permute-start | bytes 688136 | tf_op jit(solution)/shard_map/ppermute | solution.py:487
  231.7 157.6 %reduce-scatter.7.cloned.1.call-start = ((), (), s32[]{:S(2)}) async-start(), calls=%async_computation.7 | async-start | bytes 4096000 | tf_op jit(solution)/shard_map/reduce_scatter | solution.py:865
  232.3 21.1 %collective-permute-start.24 = (bf16[4,112,800]{2,1,0:T(8,128)(2,1)}, bf16[4,112,800]{2,1,0:T(8,128)(2,1)S(1)}, u32[]{:S(2)}, u32[]{:S(2)}) collective-permute-start(bf16[4,112,800]{2,1,0:T(8,128)(2,1)} %get-tuple-element.192.refs_0_), channel_id=1, source_target_pairs={{0,8},{8,0},{16,24},{24,16},{1,9},{9,1},{17,25},{25,17},{2,10},{10... | collective-permute-start | bytes 2150408 | tf_op jit(solution)/shard_map/ppermute | solution.py:502
  232.9 36.2 %collective-permute-start.25 = (bf16[4,112,800]{2,1,0:T(8,128)(2,1)}, bf16[4,112,800]{2,1,0:T(8,128)(2,1)S(1)}, u32[]{:S(2)}, u32[]{:S(2)}) collective-permute-start(bf16[4,112,800]{2,1,0:T(8,128)(2,1)} %get-tuple-element.192.refs_0_), channel_id=1, source_target_pairs={{0,16},{8,24},{16,0},{24,8},{1,17},{9,25},{17,1},{25,9},{2,18},{10... | collective-permute-start | bytes 2150408 | tf_op jit(solution)/shard_map/ppermute | solution.py:502
  233.5 35.7 %collective-permute-start.26 = (bf16[4,112,800]{2,1,0:T(8,128)(2,1)}, bf16[4,112,800]{2,1,0:T(8,128)(2,1)S(1)}, u32[]{:S(2)}, u32[]{:S(2)}) collective-permute-start(bf16[4,112,800]{2,1,0:T(8,128)(2,1)} %get-tuple-element.192.refs_0_), channel_id=1, source_target_pairs={{0,24},{8,16},{16,8},{24,0},{1,25},{9,17},{17,9},{25,1},{2,26},{10... | collective-permute-start | bytes 2150408 | tf_op jit(solution)/shard_map/ppermute | solution.py:502
  328.4 19.1 %collective-permute-start.28 = (bf16[800,1600]{1,0:T(8,128)(2,1)}, bf16[800,1600]{1,0:T(8,128)(2,1)}, u32[]{:S(2)}, u32[]{:S(2)}) collective-permute-start(bf16[800,1600]{1,0:T(8,128)(2,1)} %get-tuple-element.204), channel_id=1, source_target_pairs={{0,4},{4,0},{1,5},{5,1},{2,6},{6,2},{3,7},{7,3},{8,12},{12,8},{9,1... | collective-permute-start | bytes 7680008 | tf_op jit(solution)/shard_map/ppermute | solution.py:487
  328.5 191.2 %reduce-scatter.9.cloned.1.call-start = ((), (), s32[]{:S(2)}) async-start(), calls=%async_computation.8 | async-start | bytes 4096000 | tf_op jit(solution)/shard_map/reduce_scatter | solution.py:936
  362.6 25.0 %collective-permute-start.30 = (bf16[2,104,1600]{2,1,0:T(8,128)(2,1)}, bf16[2,104,1600]{2,1,0:T(8,128)(2,1)S(1)}, u32[]{:S(2)}, u32[]{:S(2)}) collective-permute-start(bf16[2,104,1600]{2,1,0:T(8,128)(2,1)} %get-tuple-element.215), channel_id=1, source_target_pairs={{0,8},{8,0},{16,24},{24,16},{1,9},{9,1},{17,25},{25,17},{2,10},{10... | collective-permute-start | bytes 1996808 | tf_op jit(solution)/shard_map/ppermute | solution.py:502
  370.4 18.8 %collective-permute-start.31 = (bf16[4,104,800]{2,1,0:T(8,128)(2,1)}, bf16[4,104,800]{2,1,0:T(8,128)(2,1)S(1)}, u32[]{:S(2)}, u32[]{:S(2)}) collective-permute-start(bf16[4,104,800]{2,1,0:T(8,128)(2,1)} %get-tuple-element.216), channel_id=1, source_target_pairs={{0,16},{8,24},{16,0},{24,8},{1,17},{9,25},{17,1},{25,9},{2,18},{10... | collective-permute-start | bytes 1996808 | tf_op jit(solution)/shard_map/ppermute | solution.py:502
  393.5 19.7 %collective-permute-start.32 = (bf16[2,104,1600]{2,1,0:T(8,128)(2,1)}, bf16[2,104,1600]{2,1,0:T(8,128)(2,1)}, u32[]{:S(2)}, u32[]{:S(2)}) collective-permute-start(bf16[2,104,1600]{2,1,0:T(8,128)(2,1)} %get-tuple-element.220), channel_id=1, source_target_pairs={{0,8},{8,0},{16,24},{24,16},{1,9},{9,1},{17,25},{25,17},{2,10},{10... | collective-permute-start | bytes 1996808 | tf_op jit(solution)/shard_map/ppermute | solution.py:502
  394.3 18.9 %collective-permute-start.33 = (bf16[4,104,800]{2,1,0:T(8,128)(2,1)}, bf16[4,104,800]{2,1,0:T(8,128)(2,1)S(1)}, u32[]{:S(2)}, u32[]{:S(2)}) collective-permute-start(bf16[4,104,800]{2,1,0:T(8,128)(2,1)} %get-tuple-element.221), channel_id=1, source_target_pairs={{0,16},{8,24},{16,0},{24,8},{1,17},{9,25},{17,1},{25,9},{2,18},{10... | collective-permute-start | bytes 1996808 | tf_op jit(solution)/shard_map/ppermute | solution.py:502
  414.1 19.4 %collective-permute-start.37 = (bf16[2,104,1600]{2,1,0:T(8,128)(2,1)}, bf16[2,104,1600]{2,1,0:T(8,128)(2,1)S(1)}, u32[]{:S(2)}, u32[]{:S(2)}) collective-permute-start(bf16[2,104,1600]{2,1,0:T(8,128)(2,1)} %get-tuple-element.230), channel_id=1, source_target_pairs={{0,16},{8,24},{16,0},{24,8},{1,17},{9,25},{17,1},{25,9},{2,18},{10... | collective-permute-start | bytes 1996808 | tf_op jit(solution)/shard_map/ppermute | solution.py:502
  414.8 18.7 %collective-permute-start.38 = (bf16[4,104,800]{2,1,0:T(8,128)(2,1)}, bf16[4,104,800]{2,1,0:T(8,128)(2,1)S(1)}, u32[]{:S(2)}, u32[]{:S(2)}) collective-permute-start(bf16[4,104,800]{2,1,0:T(8,128)(2,1)} %get-tuple-element.231), channel_id=1, source_target_pairs={{0,8},{8,0},{16,24},{24,16},{1,9},{9,1},{17,25},{25,17},{2,10},{10... | collective-permute-start | bytes 1996808 | tf_op jit(solution)/shard_map/ppermute | solution.py:502
  434.9 139.8 %reduce-scatter.13.cloned.1.call-start = ((), (), s32[]{:S(2)}) async-start(), calls=%async_computation.10 | async-start | bytes 931840
  448.7 42.3 %collective-permute-start.44 = (bf16[2,4,104,800]{3,2,1,0:T(8,128)(2,1)}, bf16[2,4,104,800]{3,2,1,0:T(8,128)(2,1)S(1)}, u32[]{:S(2)}, u32[]{:S(2)}) collective-permute-start(bf16[2,4,104,800]{3,2,1,0:T(8,128)(2,1)} %get-tuple-element.248), channel_id=1, source_target_pairs={{0,8},{8,0},{16,24},{24,16},{1,9},{9,1},{17,25},{25,17},{2,10},{10... | collective-permute-start | bytes 3993608 | tf_op jit(solution)/shard_map/ppermute | solution.py:502
  449.9 41.1 %collective-permute-start.45 = (bf16[2,104,1600]{2,1,0:T(8,128)(2,1)}, bf16[2,104,1600]{2,1,0:T(8,128)(2,1)S(1)}, u32[]{:S(2)}, u32[]{:S(2)}) collective-permute-start(bf16[2,104,1600]{2,1,0:T(8,128)(2,1)} %get-tuple-element.249.refs_7_), channel_id=1, source_target_pairs={{0,16},{8,24},{16,0},{24,8},{1,17},{9,25},{17,1},{25,9},{2,18},{10... | collective-permute-start | bytes 1996808 | tf_op jit(solution)/shard_map/ppermute | solution.py:502
  452.5 38.4 %collective-permute-start.41 = (bf16[104,800]{1,0:T(8,128)(2,1)S(1)}, bf16[104,800]{1,0:T(8,128)(2,1)S(1)}, u32[]{:S(2)}, u32[]{:S(2)}) collective-permute-start(bf16[104,800]{1,0:T(8,128)(2,1)S(1)} %get-tuple-element.399), channel_id=1, source_target_pairs={{0,0},{4,1},{1,2},{5,3},{2,4},{6,5},{3,6},{7,7},{8,8},{12,9},{9,10... | collective-permute-start | bytes 499208 | tf_op jit(solution)/shard_map/ppermute | solution.py:748
  453.2 37.7 %collective-permute-start.42 = (bf16[104,800]{1,0:T(8,128)(2,1)S(1)}, bf16[104,800]{1,0:T(8,128)(2,1)S(1)}, u32[]{:S(2)}, u32[]{:S(2)}) collective-permute-start(bf16[104,800]{1,0:T(8,128)(2,1)S(1)} %get-tuple-element.398), channel_id=1, source_target_pairs={{5,0},{0,1},{4,2},{1,3},{7,4},{2,5},{6,6},{3,7},{13,8},{8,9},{12,1... | collective-permute-start | bytes 499208 | tf_op jit(solution)/shard_map/ppermute | solution.py:748
  461.8 29.2 %collective-permute-start.43 = (bf16[104,800]{1,0:T(8,128)(2,1)S(1)}, bf16[104,800]{1,0:T(8,128)(2,1)S(1)}, u32[]{:S(2)}, u32[]{:S(2)}) collective-permute-start(bf16[104,800]{1,0:T(8,128)(2,1)S(1)} %get-tuple-element.397), channel_id=1, source_target_pairs={{1,0},{5,1},{0,2},{4,3},{3,4},{7,5},{2,6},{6,7},{9,8},{13,9},{8,10... | collective-permute-start | bytes 499208 | tf_op jit(solution)/shard_map/ppermute | solution.py:748
  492.5 23.0 %collective-permute-start.46 = (bf16[3,448,1024]{2,1,0:T(8,128)(2,1)}, bf16[3,448,1024]{2,1,0:T(8,128)(2,1)}, u32[]{:S(2)}, u32[]{:S(2)}) collective-permute-start(bf16[3,448,1024]{2,1,0:T(8,128)(2,1)} %get-tuple-element.251), channel_id=1, source_target_pairs={{0,4},{4,0},{1,5},{5,1},{2,6},{6,2},{3,7},{7,3},{8,12},{12,8},{9,1... | collective-permute-start | bytes 8257544 | tf_op jit(solution)/shard_map/ppermute | solution.py:487
  494.1 19.1 %collective-permute-start.49 = (bf16[4,104,800]{2,1,0:T(8,128)(2,1)S(1)}, bf16[4,104,800]{2,1,0:T(8,128)(2,1)S(1)}, u32[]{:S(2)}, u32[]{:S(2)}) collective-permute-start(bf16[4,104,800]{2,1,0:T(8,128)(2,1)S(1)} %fusion.19), channel_id=1, source_target_pairs={{0,16},{8,24},{16,0},{24,8},{1,17},{9,25},{17,1},{25,9},{2,18},{10... | collective-permute-start | bytes 1996808 | tf_op jit(solution)/shard_map/ppermute | solution.py:502
  500.8 18.9 %collective-permute-start.48 = (bf16[2,104,1600]{2,1,0:T(8,128)(2,1)}, bf16[2,104,1600]{2,1,0:T(8,128)(2,1)}, u32[]{:S(2)}, u32[]{:S(2)}) collective-permute-start(bf16[2,104,1600]{2,1,0:T(8,128)(2,1)} %get-tuple-element.257), channel_id=1, source_target_pairs={{0,8},{8,0},{16,24},{24,16},{1,9},{9,1},{17,25},{25,17},{2,10},{10... | collective-permute-start | bytes 1996808 | tf_op jit(solution)/shard_map/ppermute | solution.py:502
  527.8 18.6 %collective-permute-start.51 = (bf16[4,104,800]{2,1,0:T(8,128)(2,1)S(1)}, bf16[4,104,800]{2,1,0:T(8,128)(2,1)S(1)}, u32[]{:S(2)}, u32[]{:S(2)}) collective-permute-start(bf16[4,104,800]{2,1,0:T(8,128)(2,1)S(1)} %copy-done.19), channel_id=1, source_target_pairs={{0,8},{8,0},{16,24},{24,16},{1,9},{9,1},{17,25},{25,17},{2,10},{10... | collective-permute-start | bytes 1996808 | tf_op jit(solution)/shard_map/ppermute | solution.py:502
  547.7 95.4 %reduce-scatter.11.cloned.1.call-start = ((), (), s32[]{:S(2)}) async-start(), calls=%async_computation.9 | async-start | bytes 4259840 | tf_op jit(solution)/shard_map/reduce_scatter | solution.py:991
  547.8 23.3 %collective-permute-start.56 = (bf16[3,48,800]{2,1,0:T(8,128)(2,1)}, bf16[3,48,800]{2,1,0:T(8,128)(2,1)S(1)}, u32[]{:S(2)}, u32[]{:S(2)}) collective-permute-start(bf16[3,48,800]{2,1,0:T(8,128)(2,1)} %get-tuple-element.270), channel_id=1, source_target_pairs={{1,0},{2,1},{3,2},{5,4},{6,5},{7,6},{9,8},{10,9},{11,10},{13,12},{... | collective-permute-start | bytes 691208 | tf_op jit(solution)/shard_map/ppermute | solution.py:603
  549.1 22.1 %collective-permute-start.55 = (bf16[3,48,800]{2,1,0:T(8,128)(2,1)}, bf16[3,48,800]{2,1,0:T(8,128)(2,1)S(1)}, u32[]{:S(2)}, u32[]{:S(2)}) collective-permute-start(bf16[3,48,800]{2,1,0:T(8,128)(2,1)} %get-tuple-element.269), channel_id=1, source_target_pairs={{0,1},{1,2},{2,3},{4,5},{5,6},{6,7},{8,9},{9,10},{10,11},{12,13},{... | collective-permute-start | bytes 691208 | tf_op jit(solution)/shard_map/ppermute | solution.py:599
  554.1 18.7 %collective-permute-start.54 = (bf16[2,104,1600]{2,1,0:T(8,128)(2,1)}, bf16[2,104,1600]{2,1,0:T(8,128)(2,1)}, u32[]{:S(2)}, u32[]{:S(2)}) collective-permute-start(bf16[2,104,1600]{2,1,0:T(8,128)(2,1)} %get-tuple-element.266), channel_id=1, source_target_pairs={{0,16},{8,24},{16,0},{24,8},{1,17},{9,25},{17,1},{25,9},{2,18},{10... | collective-permute-start | bytes 1996808 | tf_op jit(solution)/shard_map/ppermute | solution.py:502
  574.8 30.4 %collective-permute-start.62 = (bf16[3,104,800]{2,1,0:T(8,128)(2,1)}, bf16[3,104,800]{2,1,0:T(8,128)(2,1)}, u32[]{:S(2)}, u32[]{:S(2)}) collective-permute-start(bf16[3,104,800]{2,1,0:T(8,128)(2,1)} %get-tuple-element.277.refs_7_), channel_id=1, source_target_pairs={{0,24},{8,16},{16,8},{24,0},{1,25},{9,17},{17,9},{25,1},{2,26},{10... | collective-permute-start | bytes 1497608 | tf_op jit(solution)/shard_map/ppermute | solution.py:502
  576.4 28.7 %collective-permute-start.61 = (bf16[3,104,800]{2,1,0:T(8,128)(2,1)}, bf16[3,104,800]{2,1,0:T(8,128)(2,1)}, u32[]{:S(2)}, u32[]{:S(2)}) collective-permute-start(bf16[3,104,800]{2,1,0:T(8,128)(2,1)} %get-tuple-element.276.refs_6_), channel_id=1, source_target_pairs={{0,16},{8,24},{16,0},{24,8},{1,17},{9,25},{17,1},{25,9},{2,18},{10... | collective-permute-start | bytes 1497608 | tf_op jit(solution)/shard_map/ppermute | solution.py:502
  577.4 27.8 %collective-permute-start.60 = (bf16[3,104,800]{2,1,0:T(8,128)(2,1)}, bf16[3,104,800]{2,1,0:T(8,128)(2,1)}, u32[]{:S(2)}, u32[]{:S(2)}) collective-permute-start(bf16[3,104,800]{2,1,0:T(8,128)(2,1)} %get-tuple-element.275.refs_5_), channel_id=1, source_target_pairs={{0,8},{8,0},{16,24},{24,16},{1,9},{9,1},{17,25},{25,17},{2,10},{10... | collective-permute-start | bytes 1497608 | tf_op jit(solution)/shard_map/ppermute | solution.py:502
  581.7 26.1 %collective-permute-start.63 = (bf16[1,104,800]{2,1,0:T(8,128)(2,1)S(1)}, bf16[1,104,800]{2,1,0:T(8,128)(2,1)S(1)}, u32[]{:S(2)}, u32[]{:S(2)}) collective-permute-start(bf16[1,104,800]{2,1,0:T(8,128)(2,1)S(1)} %copy-done.85), channel_id=1, source_target_pairs={{0,8},{8,0},{16,24},{24,16},{1,9},{9,1},{17,25},{25,17},{2,10},{10... | collective-permute-start | bytes 499208 | tf_op jit(solution)/shard_map/ppermute | solution.py:502
  610.4 36.1 %collective-permute-start.66 = (bf16[3,104,800]{2,1,0:T(8,128)(2,1)}, bf16[3,104,800]{2,1,0:T(8,128)(2,1)S(1)}, u32[]{:S(2)}, u32[]{:S(2)}) collective-permute-start(bf16[3,104,800]{2,1,0:T(8,128)(2,1)} %get-tuple-element.289), channel_id=1, source_target_pairs={{0,8},{8,0},{16,24},{24,16},{1,9},{9,1},{17,25},{25,17},{2,10},{10... | collective-permute-start | bytes 1497608 | tf_op jit(solution)/shard_map/ppermute | solution.py:502
  611.1 35.4 %collective-permute-start.67 = (bf16[3,104,800]{2,1,0:T(8,128)(2,1)}, bf16[3,104,800]{2,1,0:T(8,128)(2,1)}, u32[]{:S(2)}, u32[]{:S(2)}) collective-permute-start(bf16[3,104,800]{2,1,0:T(8,128)(2,1)} %get-tuple-element.289), channel_id=1, source_target_pairs={{0,16},{8,24},{16,0},{24,8},{1,17},{9,25},{17,1},{25,9},{2,18},{10... | collective-permute-start | bytes 1497608 | tf_op jit(solution)/shard_map/ppermute | solution.py:502
  611.8 34.7 %collective-permute-start.68 = (bf16[3,104,800]{2,1,0:T(8,128)(2,1)}, bf16[3,104,800]{2,1,0:T(8,128)(2,1)}, u32[]{:S(2)}, u32[]{:S(2)}) collective-permute-start(bf16[3,104,800]{2,1,0:T(8,128)(2,1)} %get-tuple-element.289), channel_id=1, source_target_pairs={{0,24},{8,16},{16,8},{24,0},{1,25},{9,17},{17,9},{25,1},{2,26},{10... | collective-permute-start | bytes 1497608 | tf_op jit(solution)/shard_map/ppermute | solution.py:502
  613.9 32.6 %collective-permute-start.65 = (bf16[1,104,800]{2,1,0:T(8,128)(2,1)}, bf16[1,104,800]{2,1,0:T(8,128)(2,1)S(1)}, u32[]{:S(2)}, u32[]{:S(2)}) collective-permute-start(bf16[1,104,800]{2,1,0:T(8,128)(2,1)} %get-tuple-element.287.refs_0_), channel_id=1, source_target_pairs={{0,16},{8,24},{16,0},{24,8},{1,17},{9,25},{17,1},{25,9},{2,18},{10... | collective-permute-start | bytes 499208 | tf_op jit(solution)/shard_map/ppermute | solution.py:502
  614.2 21.2 %collective-permute-start.69 = (f32[1,4800]{1,0:T(1,128)}, f32[1,4800]{1,0:T(1,128)S(1)}, u32[]{:S(2)}, u32[]{:S(2)}) collective-permute-start(f32[1,4800]{1,0:T(1,128)} %get-tuple-element.290), channel_id=1, source_target_pairs={{0,8},{8,0},{16,24},{24,16},{1,9},{9,1},{17,25},{25,17},{2,10},{10... | collective-permute-start | bytes 57608 | tf_op jit(solution)/shard_map/ppermute | solution.py:593
  (142 other events, 1016.7 us)
Sparse Core Ops, SparseCore 0:
  17.7 69.2 all-gather.3
  92.4 66.9 all-gather.5
  231.8 62.0 all-gather.7
  328.6 60.6 reduce-scatter.6
  435.0 78.1 reduce-scatter.8
  547.9 26.8 reduce-scatter.12
  577.7 65.1 reduce-scatter.10

commit v4 on v3

--- a/solution.py
+++ b/solution.py
@@ -230,41 +230,127 @@
     )(row, b, columns, *parts)
 
 
-def split_product_tn(parts, b, row):
+def mixed_norm(parts, b, row, columns, x):
+    n = len(parts)
+    total, depth = parts[0].shape
+    width = b.shape[1]
+    rows = rows_of(total, 400)
+    steps = total // rows
+
+    def kernel(row_ref, b_ref, c_ref, x_ref, *refs):
+        o_ref, hat_ref, norm_ref, scale_ref = refs[n:]
+        step = pl.program_id(0)
+        at = pl.ds(pl.multiple_of(step * rows, 8), rows)
+        out = c_ref[at, 2:3] + x_ref[...].astype(F32)
+        for i in range(n):
+            here = pl.multiple_of(lax.rem(row_ref[0] + i, n) * depth, 8)
+            out = out + jnp.dot(
+                refs[i][...], b_ref[pl.ds(here, depth), :], preferred_element_type=F32
+            )
+        o_ref[at, :] = out
+
+        @pl.when(step == steps - 1)
+        def end():
+            mean = jnp.sum(o_ref[...], axis=0, keepdims=True) / total
+            centred = o_ref[...] - mean
+            scale = lax.rsqrt(jnp.sum(centred * centred, axis=0, keepdims=True) / total + EPSILON)
+            hat = centred * scale
+            hat_ref[...] = hat
+            norm_ref[...] = (hat * c_ref[:, 3:4] + c_ref[:, 4:5]).astype(BF16)
+            scale_ref[...] = scale
+
+    return pl.pallas_call(
+        kernel,
+        out_shape=[
+            jax.ShapeDtypeStruct((total, width), F32),
+            jax.ShapeDtypeStruct((total, width), F32),
+            jax.ShapeDtypeStruct((total, width), BF16),
+            jax.ShapeDtypeStruct((1, width), F32),
+        ],
+        grid=(steps,),
+        in_specs=[
+            SM,
+            pl.BlockSpec(b.shape, whole_block),
+            pl.BlockSpec(columns.shape, whole_block),
+            pl.BlockSpec((rows, width), by_rows),
+        ]
+        + [pl.BlockSpec((rows, depth), by_rows)] * n,
+        out_specs=[
+            pl.BlockSpec((total, width), whole_block),
+            pl.BlockSpec((total, width), whole_block),
+            pl.BlockSpec((total, width), whole_block),
+            pl.BlockSpec((1, width), whole_block),
+        ],
+        compiler_params=ROOM,
+        cost_estimate=FREE,
+    )(row, b, columns, x, *parts)
+
+
+def mixed_norm_back(parts, dn, hat, scale, g, row, columns):
     n = len(parts)
     depth = parts[0].shape[1]
-    total, width = b.shape
+    total, width = dn.shape
     rows = rows_of(total, 400)
     steps = total // rows
 
-    def kernel(row_ref, b_ref, *refs):
-        o_ref, acc = refs[n:]
-
-        @pl.when(pl.program_id(0) == 0)
+    def kernel(row_ref, dn_ref, hat_ref, scale_ref, g_ref, c_ref, *refs):
+        o_ref, low_ref, a_ref, s_ref, acc = refs[n:]
+        step = pl.program_id(0)
+
+        @pl.when(step == 0)
         def start():
+            grad = dn_ref[...].astype(F32)
+            up = grad * c_ref[:, 3:4]
+            hat = hat_ref[...]
+            pull = jnp.sum(up, axis=0, keepdims=True) / total
+            lean = jnp.sum(up * hat, axis=0, keepdims=True) / total
+            out = g_ref[...].astype(F32) + scale_ref[...] * (up - pull - hat * lean)
+            low = out.astype(BF16)
+            o_ref[...] = out
+            low_ref[...] = low
+            s_ref[:, 0:1] = jnp.sum(low.astype(F32), axis=1, keepdims=True)
+            s_ref[:, 1:2] = jnp.sum(grad * hat, axis=1, keepdims=True)
+            s_ref[:, 2:3] = jnp.sum(grad, axis=1, keepdims=True)
             acc[...] = jnp.zeros_like(acc)
 
+        cut = low_ref[pl.ds(pl.multiple_of(step * rows, 8), rows), :]
         for i in range(n):
-            at = pl.multiple_of(lax.rem(row_ref[0] + i, n) * depth, 8)
-            acc[pl.ds(at, depth), :] += lax.dot_general(
-                refs[i][...], b_ref[...], NT, preferred_element_type=F32
-            )
-
-        @pl.when(pl.program_id(0) == steps - 1)
+            here = pl.ds(pl.multiple_of(lax.rem(row_ref[0] + i, n) * depth, 8), depth)
+            acc[here, :] += lax.dot_general(refs[i][...], cut, NT, preferred_element_type=F32)
+
+        @pl.when(step == steps - 1)
         def end():
-            o_ref[...] = acc[...].astype(BF16)
-
+            a_ref[...] = acc[...].astype(BF16)
+
+    full = pl.BlockSpec((total, width), whole_block)
     return pl.pallas_call(
         kernel,
-        out_shape=jax.ShapeDtypeStruct((n * depth, width), BF16),
+        out_shape=[
+            jax.ShapeDtypeStruct((total, width), F32),
+            jax.ShapeDtypeStruct((total, width), BF16),
+            jax.ShapeDtypeStruct((n * depth, width), BF16),
+            jax.ShapeDtypeStruct((total, 3), F32),
+        ],
         grid=(steps,),
-        in_specs=[SM, pl.BlockSpec((rows, width), by_rows)]
+        in_specs=[
+            SM,
+            full,
+            full,
+            pl.BlockSpec((1, width), whole_block),
+            full,
+            pl.BlockSpec(columns.shape, whole_block),
+        ]
         + [pl.BlockSpec((rows, depth), by_rows)] * n,
-        out_specs=pl.BlockSpec((n * depth, width), whole_block),
+        out_specs=[
+            full,
+            full,
+            pl.BlockSpec((n * depth, width), whole_block),
+            pl.BlockSpec((total, 3), whole_block),
+        ],
         scratch_shapes=[pltpu.VMEM((n * depth, width), F32)],
         compiler_params=ROOM,
         cost_estimate=FREE,
-    )(row, b, *parts)
+    )(row, dn, hat, scale, g, columns, *parts)
 
 
 def norm_product_tn(a, b, normed, columns, scale, riding, col, n_col):
@@ -764,7 +850,8 @@
             lax.dynamic_slice_in_dim(bias_v, begin, window, 0),
         ]
     )
-    columns = jnp.concatenate([gain1, shift1, bias_out, jnp.zeros((depth, 1), F32)], 1)
+    no_bias = jnp.zeros((depth, 1), F32)
+    columns = jnp.concatenate([gain1, shift1, bias_out, gain2, shift2, no_bias], 1)
     meta = jnp.stack(
         [
             jnp.array(heads.firsts, jnp.int32)[col],
@@ -798,8 +885,8 @@
     near_out = [swap_with(moved_out, 1), swap_with(moved_out, 2)]
     *cuts, mixed, norms = attn_fwd(meta, key_start, pieces, heads.slots, size)
     far_cuts = [near_out[0][:half], near_out[1][half:]]
-    *cuts, near_x, near_y, far_x, far_y, g_all, down_own = gate(
-        list(cuts) + near_out + far_cuts + [g_all, down_own], []
+    *cuts, near_x, near_y, far_x, far_y, down_own = gate(
+        list(cuts) + near_out + far_cuts + [down_own], []
     )
 
     def move_down(step):
@@ -808,7 +895,7 @@
     far_out = [swap_with(far_x, 2), swap_with(far_y, 1)]
     moved_down = between_owners(move_down, range(half), False)
     mixed_own = row_sum(cuts).astype(BF16)
-    mixed_own, *rest = gate([mixed_own] + moved_down + far_out, [])
+    mixed_own, g_all, *rest = gate([mixed_own, g_all] + moved_down + far_out, [])
     moved_down, far_out = rest[:half], rest[half:]
 
     dp_at = dp[None].astype(jnp.int32)
@@ -817,7 +904,8 @@
     ]
     out_weights = assemble([moved_out, near_x, near_y] + far_out, shares, dp_at)
     out_weights = [out_weights] + [turn(out_weights, "row", -step) for step in range(1, n_row)]
-    down_own, *rest = gate([down_own] + got[1:] + out_weights[1:], [])
+    x_part = block(x_all, col, part, 1)
+    down_own, x_part, *rest = gate([down_own, x_part] + got[1:] + out_weights[1:], [])
     got = got[:1] + rest[: n_col - 1]
     out_weights = out_weights[:1] + rest[n_col - 1 :]
     out_weights = [w.reshape(depth, in_rows) for w in out_weights]
@@ -828,13 +916,9 @@
     attention = sum(
         jnp.pad(piece, ((at, depth - at - window), (0, 0))) for piece, at in zip(got, lapped)
     )
-    branch = split_product(out_weights, attention, row_at, columns, 2, F32)
-    resid = block(x_all, col, part, 1).astype(F32) + branch
-    mean2, rstd2 = moments(resid)
-    hat2 = (resid - mean2) * rstd2
-    n2_own = (hat2 * gain2 + shift2).astype(BF16)
+    resid, hat2, n2_own, rstd2 = mixed_norm(out_weights, attention, row_at, columns, x_part)
     moved_down = jnp.stack(ordered(moved_down, place_in, 1))
-    n2_own, g, moved_down = gate([n2_own, g, moved_down], [hat2])
+    n2_own, g, moved_down = gate([n2_own, g, moved_down], [])
 
     n2_all = lax.all_gather(n2_own, "col", axis=1, tiled=True)
     down_weights = assemble([moved_down] + swap_all(moved_down), shares, dp_at)
@@ -890,38 +974,26 @@
     up_near = up_shares.take(up_grad, dp ^ 1, 1)
     down_near = fine.take(down_grad, dp ^ 2, 1)
     du_row = du_sums[:, 0]
-    shrunk = split_product(down_weights, hidden_all, row_at, columns, 3, BF16)
+    shrunk = split_product(down_weights, hidden_all, row_at, columns, 5, BF16)
     own_sum = block(shrunk, col, part, 1).astype(F32) + resid
     shrunk = lax.dynamic_update_slice_in_dim(shrunk, own_sum.astype(BF16), col * part, 1)
-    dn2, shrunk, up_far, down_far, up_near, down_near, du_row = gate(
-        [dn2, shrunk, up_far, down_far, up_near, down_near, du_row], []
-    )
-
-    dn2 = dn2.astype(F32)
-    up2 = dn2 * gain2
-    pull2 = jnp.mean(up2, axis=0, keepdims=True)
-    lean2 = jnp.mean(up2 * hat2, axis=0, keepdims=True)
-    dr = block(g_all, col, part, 1).astype(F32) + rstd2 * (up2 - pull2 - hat2 * lean2)
-    db = dr.astype(BF16)
-    da = split_product_tn(out_weights, db, row_at)
-    sums2 = jnp.stack(
-        [
-            jnp.sum(db.astype(F32), axis=1),
-            jnp.sum(dn2 * hat2, axis=1),
-            jnp.sum(dn2, axis=1),
-        ]
-    )
-    early = jnp.concatenate([sums2.reshape(-1), du_row, g_sums])
+    up_relay = relay_cut(up_grad, up_far, up_shares, 1)
+    down_relay = relay_cut(down_grad, down_far, fine, 2)
+    g_part = block(g_all, col, part, 1)
+    dn2, shrunk, up_relay, down_relay, up_near, down_near, du_row, g_part = gate(
+        [dn2, shrunk, up_relay, down_relay, up_near, down_near, du_row, g_part], []
+    )
+
+    up_near = swap_with(up_near, 1)
+    down_near = swap_with(down_near, 2)
+    dr, db, da, sums2 = mixed_norm_back(out_weights, dn2, hat2, rstd2, g_part, row_at, columns)
+    early = jnp.concatenate([sums2.T.reshape(-1), du_row, g_sums])
     da_cuts = [
         lax.dynamic_slice_in_dim(da, firsts[(col + step) % n_col], window, 0)
         for step in range(n_col)
     ]
-    up_near = swap_with(up_near, 1)
-    down_near = swap_with(down_near, 2)
-    up_relay = relay_cut(up_grad, up_far, up_shares, 1)
-    down_relay = relay_cut(down_grad, down_far, fine, 2)
     db, shrunk, up_near, down_near, up_relay, down_relay, *da_cuts = gate(
-        [db, shrunk, up_near, down_near, up_relay, down_relay] + da_cuts, [early]
+        [db, shrunk, up_near, down_near, up_relay, down_relay] + da_cuts, []
     )
 
     got = [turn(cut, "col", step) for step, cut in enumerate(da_cuts)]
@@ -951,7 +1023,7 @@
     def move_home(step):
         return pick(down_share, (place_in + step) % n_col)
 
-    down_home = between_owners(move_home, range(n_col - 1), True)
+    down_home = between_owners(move_home, range(half), True)
     dqkv = attn_bwd(meta, key_start, pieces, da_pieces, mixed, norms, heads.slots, size)
     *rest, out_first, up_y, up_share, down_share = gate(
         list(dqkv) + down_home + [out_first, up_y, up_share, down_share], []
@@ -962,16 +1034,22 @@
 
     out_relay = swap_with(out_relay, 2)
     up_x = swap_with(up_share, 1)
-    down_home = down_home + between_owners(move_home, range(n_col - 1, n_col), True)
+    down_home = down_home + between_owners(move_home, range(half, n_col), True)
     dqkv = row_sum(dqkv).astype(BF16).reshape(3 * window, length)
+    out_near, out_grad, *down_home = gate([out_near, out_grad] + down_home, [dqkv])
     homes = jnp.stack(ordered(down_home, col, -1))
     out_share = share_sum(out_grad, fine, out_near, out_relay)
-    dqkv, homes, outputs, up_x, out_share = gate([dqkv, homes, outputs, up_x, out_share], [])
+    qkv_parts = [
+        token_product(dqkv, n1, r, n_row, False).reshape(3, window, in_rows)
+        for r in other_rows[:0:-1]
+    ][::-1]
+    dqkv, homes, outputs, up_x, out_share, *qkv_parts = gate(
+        [dqkv, homes, outputs, up_x, out_share] + qkv_parts, []
+    )
 
     homes_near = [swap_with(homes, 1), swap_with(homes, 2)]
-    qkv_parts = [token_product(dqkv, n1, r, n_row, False) for r in other_rows[::-1]][::-1]
-    qkv_parts = [q.reshape(3, window, in_rows) for q in qkv_parts]
-    qkv_grad = row_sum(qkv_parts).astype(BF16)
+    own = token_product(dqkv, n1, other_rows[0], n_row, False).reshape(3, window, in_rows)
+    qkv_grad = row_sum([own] + qkv_parts).astype(BF16)
     wide, to_left, to_right = narrow_cuts(qkv_grad, 1, heads, col, width)
     dqkv, wide, to_left, to_right, out_share, up_y, *homes_near = gate(
         [dqkv, wide, to_left, to_right, out_share, up_y] + homes_near, []
@@ -1004,17 +1082,20 @@
     sums, local = small[: 7 * depth].reshape(7, depth), small[7 * depth :]
     sums = small_sum(sums, ("col",))
     sums = lax.dynamic_slice_in_dim(sums, col * width, width, 1)
-    small = jnp.concatenate([sums.reshape(-1), local])[None]
+    small = jnp.concatenate([sums.reshape(-1), local])
+    deep = -(-small.shape[0] // in_rows)
+    small = jnp.pad(small, (0, deep * in_rows - small.shape[0])).reshape(deep, in_rows)
+    rounded = lax.reduce_precision(small, 8, 7)
+    rest = (small - rounded).astype(BF16)
+    rounded = rounded.astype(BF16)
     qkv_share = fine.take(qkv_grad, dp, 1).astype(F32)
     qkv_share = (qkv_share + sum(q.astype(F32) for q in qkv_got)).astype(BF16)
-    small, up_far, qkv_share, *out_all = gate(
-        [small, up_far, qkv_share] + out_all, [down_grad, outputs]
-    )
-
-    qkv_all = swap_all(qkv_share)
+    ends = 3 * fine.size
+    payload = jnp.concatenate([qkv_share.reshape(ends, in_rows), rounded, rest])
+    up_far, payload, *out_all = gate([up_far, payload] + out_all, [down_grad, outputs])
+
+    qkv_all = swap_all(payload)
     out_all.append(swap_with(out_all[0], 2))
-    small = small_sum(small, ("dp",))[0]
-    sums, local = small[: 7 * width].reshape(7, width), small[7 * width :]
     up_grad = up_shares.join([up_share, up_x, up_y, up_far], dp, 1).astype(F32)
     up_grad = up_grad.reshape(in_rows, ff)
     hat1 = (x.astype(F32) - mean1) * rstd1
@@ -1023,10 +1104,14 @@
     lines = (lines[0::2] + lines[1::2]) / depth
     input_grad = dx[:width].astype(F32) - rstd1 * (lines[0:1] + hat1 * lines[1:2])
     input_grad = input_grad.astype(BF16)
-    *out_all, a, b, c = gate(out_all + qkv_all, [sums, local, up_grad, input_grad])
+    *out_all, a, b, c = gate(out_all + qkv_all, [up_grad, input_grad])
 
     out_grad = fine.join([out_home] + out_all, dp, 1).astype(F32)[0]
-    qkv_grad = fine.join([qkv_share, a, b, c], dp, 1).astype(F32)
+    small = sum(v[ends:].astype(F32) for v in (payload, a, b, c))
+    small = (small[:deep] + small[deep:]).reshape(-1)
+    sums, local = small[: 7 * width].reshape(7, width), small[7 * width : 8 * width + ff]
+    qkv_all = [v[:ends].reshape(3, fine.size, in_rows) for v in (payload, a, b, c)]
+    qkv_grad = fine.join(qkv_all, dp, 1).astype(F32)
     return (
         outputs.T.reshape(tokens.shape),
         input_grad.T.reshape(tokens.shape),

time: 671 us -> 651 us (0.970)
  waiting for transfers between devices: 169 us -> 144 us
  starting transfers between devices: 101 us -> 109 us
    ppermute x5 -> x3, waiting for transfers between devices: 25.7 us -> 4.74 us  [small_sum(): lax.ppermute(value, axis, [(i, i ^ bit) for i in range(size)])]
    reduce_scatter x1, waiting for transfers between devices: 0.01 us -> 20.3 us  [body(): dx = lax.psum_scatter(dn1, 'col', scatter_dimension=0, tiled=True)]
    ppermute x8, waiting for transfers between devices: 19.4 us -> 4.19 us  [between_owners(): got.append(lax.ppermute(value_of(step), ('row', 'col'), pairs))]
    all_gather x1, waiting for transfers between devices: 13.2 us -> 0.01 us  [body(): g_all = lax.all_gather(g, 'col', axis=0, tiled=True)]
    pallas_call x1 -> x2, Pallas kernels: 6.81 us -> 18.6 us  [the longest x1 10.4 us: mixed_norm_back(): pl.pallas_call(kernel, out_shape=[jax.ShapeDtypeStruct((total, width), F3...]
    ppermute x8, starting transfers between devices: 26.7 us -> 37.4 us  [between_owners(): got.append(lax.ppermute(value_of(step), ('row', 'col'), pairs))]
    unnamed x227 -> x161, local copies, waits for them, and re-layouts: 34.4 us -> 27.7 us
    pallas_call x2 -> x1, Pallas kernels: 17.4 us -> 11.2 us  [split_product(): pl.pallas_call(kernel, out_shape=jax.ShapeDtypeStruct((total, width), dty...]
  transfers between devices with their start and end apart: 78 -> 76, of which waited for: 27 -> 24; matrix products, arithmetic and copies ran while one was open for 21% -> 22% of each run, Pallas kernels for 20% -> 23%
where the time goes in v4:
time: 651 us; the launch traced here: 642 us
  Pallas kernels  188 us (29%)
  waiting for transfers between devices  144 us (22%)
  starting transfers between devices  109 us (17%)
  other arithmetic  102 us (16%)
  local copies, waits for them, and re-layouts  76.1 us (12%)
  between operations  23.1 us (4%)
    ppermute x30, waiting for transfers between devices, swap_with(): return lax.ppermute(value, 'dp', [(i, i ^ bit) for i in range(4)])  51.6 us
    pallas_call x8, Pallas kernels, token_product(): pl.pallas_call(kernel, out_shape=jax.ShapeDtypeStruct((rows_a, rows_b), B...  49.9 us
    ppermute x8, starting transfers between devices, between_owners(): got.append(lax.ppermute(value_of(step), ('row', 'col'), pairs))  37.4 us
    ppermute x30, starting transfers between devices, swap_with(): return lax.ppermute(value, 'dp', [(i, i ^ bit) for i in range(4)])  35.6 us
    pallas_call x1, Pallas kernels, hidden_layer(): pl.pallas_call(kernel, out_shape=[jax.ShapeDtypeStruct((ff, tokens), BF16...  27.8 us
    unnamed x161, local copies, waits for them, and re-layouts  27.7 us
    ppermute x24, waiting for transfers between devices, turn(): lax.ppermute(value, axis, [(i, (i + steps) % size) for i in range(size)])  26.8 us
    pallas_call x1, Pallas kernels, attn_bwd(): pl.pallas_call(functools.partial(bwd_kernel, n_row, n_slots, hd, ks.shape...  25.3 us
  transfers between devices with their start and end apart: 76, of which 24 were waited for; matrix products, arithmetic and copies ran while one was open for 22% of the time, Pallas kernels for 23%

profile of v4, /device:TPU:0, one launch (start us, length us, event | category | flops | bytes accessed | tf_op | source)
XLA Modules:
  0.0 641.6 jit_solution(658414609241134380)
XLA Ops:
  11.3 4.9 collective-permute-start
  17.7 4.3 collective-permute-done
  22.0 3.8 collective-permute-done.1
  25.8 4.4 fusion.8
  41.0 4.3 copy.214
  51.1 3.5 pad_maximum_fusion
  54.6 5.2 copy.215
  62.2 4.1 maximum_bitcast_fusion.refs_8_.up_ref
  66.3 20.7 %all-gather.4.cloned.1.call-done.refs_0_ = bf16[1600,1024]{1,0:T(8,128)(2,1)} async-done(((bf16[400,1024]{1,0:T(8,128)(2,1)}), bf16[1600,1024]{1,0:T(8,128)(2,1)}) %all-gather.4.cloned.1.call-update) | async-done | bytes 3276816 | tf_op jit(solution)/shard_map/all_gather | solution.py:837
  96.3 9.4 %shard_map.488 = bf16[1344,1024]{1,0:T(8,128)(2,1)} custom-call(bf16[1344,1600]{1,0:T(8,128)(2,1)} %get-tuple-element.173.a_ref, bf16[1600,1024]{1,0:T(8,128)(2,1)} %fusion.5.b_ref.n_ref, f32[1344,1]{1,0:T(8,128)} %get-tuple-element.175.bias_ref), custom_call_target="tpu_custom_call" | custom-call | tf_op jit(solution)/shard_map/pallas_call | solution.py:189
  105.7 3.4 collective-permute-done.8.refs_2_
  117.6 17.3 %shard_map.491 = (bf16[448,1024]{1,0:T(8,128)(2,1)S(1)}, bf16[448,1024]{1,0:T(8,128)(2,1)S(1)}, bf16[448,2048]{1,0:T(8,128)(2,1)S(1)}, f32[7,2048]{1,0:T(8,128)S(1)}) custom-call(s32[4]{0:T(128)S(1)} %copy-done.7, s32[25,4]{1,0:T(8,128)S(1)} %copy.220.ks, bf16[3,448,1024]{2,1,0:T(8,128)(2,1)} %get-tuple-element.177.refs_0_, ...), custom_call_target="tpu_custom_call" | custom-call | tf_op jit(solution)/shard_map/pallas_call | solution.py:148
  145.2 14.3 %collective-permute-start.15 = (bf16[112,800]{1,0:T(8,128)(2,1)S(1)}, bf16[112,800]{1,0:T(8,128)(2,1)}, u32[]{:S(2)}, u32[]{:S(2)}) collective-permute-start(bf16[112,800]{1,0:T(8,128)(2,1)S(1)} %get-tuple-element.417), channel_id=1, source_target_pairs={{0,5},{1,0},{2,4},{3,1},{4,7},{5,2},{6,6},{7,3},{8,13},{9,8},{10,1... | collective-permute-start | bytes 537608 | tf_op jit(solution)/shard_map/ppermute | solution.py:834
  164.8 3.5 shard_map.494
  179.5 3.5 collective-permute-done.18.refs_2_
  183.1 9.1 %collective-permute-done.19.refs_3_ = bf16[448,256]{1,0:T(8,128)(2,1)} collective-permute-done((bf16[448,256]{1,0:T(8,128)(2,1)S(1)}, bf16[448,256]{1,0:T(8,128)(2,1)}, u32[]{:S(2)}, u32[]{:S(2)}) %collective-permute-start.19) | collective-permute-done | bytes 229408 | tf_op jit(solution)/shard_map/ppermute | solution.py:573
  195.7 3.9 collective-permute-start.22
  200.6 8.2 %shard_map.496 = (f32[1600,256]{1,0:T(8,128)}, f32[1600,256]{1,0:T(8,128)}, bf16[1600,256]{1,0:T(8,128)(2,1)}, f32[1,256]{1,0:T(1,128)}) custom-call(s32[1]{0:T(128)} %bitcast.9.row_ref, bf16[1600,256]{1,0:T(8,128)(2,1)} %pad_add_fusion.b_ref, f32[1600,6]{1,0:T(8,128)} %get-tuple-element.200.c_ref.bias_ref.g_ref, ...), custom_call_target="tpu_custom_call" | custom-call | tf_op jit(solution)/shard_map/pallas_call | solution.py:262
  217.8 17.4 %collective-permute-done.24.refs_1_ = bf16[4,112,800]{2,1,0:T(8,128)(2,1)S(1)} collective-permute-done((bf16[4,112,800]{2,1,0:T(8,128)(2,1)}, bf16[4,112,800]{2,1,0:T(8,128)(2,1)S(1)}, u32[]{:S(2)}, u32[]{:S(2)}) %collective-permute-start.24) | collective-permute-done | bytes 716832 | tf_op jit(solution)/shard_map/ppermute | solution.py:588
  235.2 18.3 %collective-permute-done.25.refs_2_ = bf16[4,112,800]{2,1,0:T(8,128)(2,1)S(1)} collective-permute-done((bf16[4,112,800]{2,1,0:T(8,128)(2,1)}, bf16[4,112,800]{2,1,0:T(8,128)(2,1)S(1)}, u32[]{:S(2)}, u32[]{:S(2)}) %collective-permute-start.25) | collective-permute-done | bytes 716832 | tf_op jit(solution)/shard_map/ppermute | solution.py:588
  255.3 3.5 shard_map.498
  260.8 3.6 collective-permute-done.27
  264.5 6.9 %shard_map.499.refs_1_ = bf16[1600,1600]{1,0:T(8,128)(2,1)} custom-call(bf16[1600,800]{1,0:T(8,128)(2,1)} %bitcast.190, bf16[1600,800]{1,0:T(8,128)(2,1)} %bitcast.54.refs_1_), custom_call_target="tpu_custom_call" | custom-call | tf_op jit(solution)/shard_map/pallas_call | solution.py:544
  271.4 7.0 %all-gather.8.cloned.1.call-done.refs_0_ = bf16[1600,1024]{1,0:T(8,128)(2,1)} async-done(((bf16[1600,256]{1,0:T(8,128)(2,1)}), bf16[1600,1024]{1,0:T(8,128)(2,1)}) %all-gather.8.cloned.1.call-update) | async-done | bytes 3276816 | tf_op jit(solution)/shard_map/all_gather | solution.py:923
  278.4 27.8 %shard_map.501 = (bf16[1600,1024]{1,0:T(8,128)(2,1)}, bf16[1600,1024]{1,0:T(8,128)(2,1)}, bf16[1600,1024]{1,0:T(8,128)(2,1)}, f32[1600,1]{1,0:T(8,128)}) custom-call(s32[1]{0:T(128)} %bitcast.9.row_ref, bf16[1600,1600]{1,0:T(8,128)(2,1)} %maximum_bitcast_fusion.refs_8_.up_ref, bf16[1600,1600]{1,0:T(8,128)(2,1)} %get-tuple-element.210.down_ref, ...), custom_call_target="tpu_custom_call" | custom-call | tf_op jit(solution)/shard_map/pallas_call | solution.py:498
  306.2 6.7 %shard_map.503.refs_2_ = bf16[800,1600]{1,0:T(8,128)(2,1)} custom-call(s32[1]{0:T(128)} %bitcast.55.index_ref, bf16[1600,1024]{1,0:T(8,128)(2,1)} %get-tuple-element.211.n_ref.a_ref.refs_0_, bf16[1600,1024]{1,0:T(8,128)(2,1)} %get-tuple-element.218.b_ref), custom_call_target="tpu_custom_call" | custom-call | tf_op jit(solution)/shard_map/pallas_call | solution.py:442
  318.1 7.2 %shard_map.506 = bf16[1600,800]{1,0:T(8,128)(2,1)} custom-call(s32[1]{0:T(128)} %bitcast.55.index_ref, bf16[1600,1024]{1,0:T(8,128)(2,1)} %get-tuple-element.212.g_ref.a_ref, bf16[1600,1024]{1,0:T(8,128)(2,1)} %get-tuple-element.219.b_ref.refs_0_), custom_call_target="tpu_custom_call" | custom-call | tf_op jit(solution)/shard_map/pallas_call | solution.py:442
  325.3 6.7 %shard_map.505.refs_1_ = bf16[800,1600]{1,0:T(8,128)(2,1)} custom-call(s32[1]{0:T(128)} %bitcast.56.index_ref, bf16[1600,1024]{1,0:T(8,128)(2,1)} %get-tuple-element.220.a_ref, bf16[1600,1024]{1,0:T(8,128)(2,1)} %get-tuple-element.218.b_ref), custom_call_target="tpu_custom_call" | custom-call | tf_op jit(solution)/shard_map/pallas_call | solution.py:442
  333.5 3.3 add_convert_fusion.3
  347.1 7.2 %shard_map.509 = bf16[1600,800]{1,0:T(8,128)(2,1)} custom-call(s32[1]{0:T(128)} %bitcast.56.index_ref, bf16[1600,1024]{1,0:T(8,128)(2,1)} %get-tuple-element.212.g_ref.a_ref, bf16[1600,1024]{1,0:T(8,128)(2,1)} %get-tuple-element.226.b_ref.refs_0_), custom_call_target="tpu_custom_call" | custom-call | tf_op jit(solution)/shard_map/pallas_call | solution.py:442
  355.9 3.4 add_convert_fusion.1
  364.4 11.2 %shard_map.512 = bf16[1600,1024]{1,0:T(8,128)(2,1)} custom-call(s32[1]{0:T(128)} %bitcast.9.row_ref, bf16[1600,1024]{1,0:T(8,128)(2,1)} %get-tuple-element.231.b_ref, f32[1600,6]{1,0:T(8,128)} %get-tuple-element.200.c_ref.bias_ref.g_ref, bf16[1600,800]{1,0:T(8,128)(2,1)} %bitcast.191, bf16[1600,800]{1,0:T(8,128)(2,1)} %bitcast.54.refs_1_), custom_call_target="tpu_custom_call" | custom-call | tf_op jit(solution)/shard_map/pallas_call | solution.py:217
  382.7 10.4 %shard_map.514 = (f32[1600,256]{1,0:T(8,128)}, bf16[1600,256]{1,0:T(8,128)(2,1)}, bf16[1600,256]{1,0:T(8,128)(2,1)}, f32[1600,3]{1,0:T(8,128)}) custom-call(s32[1]{0:T(128)} %bitcast.9.row_ref, bf16[1600,256]{1,0:T(8,128)(2,1)} %get-tuple-element.236.dn_ref, f32[1600,256]{1,0:T(8,128)} %get-tuple-element.237.hat_ref, f32[1,256]{1,0:T(1,128)} %get-tuple-element.238.scale_ref, ...), custom_call_target="tpu_custom_call" | custom-call | tf_op jit(solution)/shard_map/pallas_call | solution.py:326
  405.8 4.6 shard_map.516
  410.4 4.6 shard_map.517
  415.1 4.1 collective-permute-done.35.refs_1_
  437.4 8.0 %collective-permute-start.42 = (bf16[104,800]{1,0:T(8,128)(2,1)S(1)}, bf16[104,800]{1,0:T(8,128)(2,1)S(1)}, u32[]{:S(2)}, u32[]{:S(2)}) collective-permute-start(bf16[104,800]{1,0:T(8,128)(2,1)S(1)} %get-tuple-element.413), channel_id=1, source_target_pairs={{5,0},{0,1},{4,2},{1,3},{7,4},{2,5},{6,6},{3,7},{13,8},{8,9},{12,1... | collective-permute-start | bytes 499208 | tf_op jit(solution)/shard_map/ppermute | solution.py:834
  445.4 25.3 %shard_map.520 = (bf16[3,448,1024]{2,1,0:T(8,128)(2,1)}, bf16[3,448,1024]{2,1,0:T(8,128)(2,1)}) custom-call(s32[4]{0:T(128)} %get-tuple-element.172.meta, s32[25,4]{1,0:T(8,128)} %copy-done.5, bf16[3,448,1024]{2,1,0:T(8,128)(2,1)} %get-tuple-element.177.refs_0_, bf16[3,448,1024]{2,1,0:T(8,128)(2,1)} %get-tuple-element.181.refs_1_, ...), custom_call_target="tpu_custom_call" | custom-call | tf_op jit(solution)/shard_map/pallas_call | solution.py:157
  474.8 5.9 collective-permute-start.47
  487.6 4.6 add_convert_fusion.2
  492.3 6.4 shard_map.523
  507.2 6.4 shard_map.525
  516.9 7.3 %collective-permute-done.51.refs_6_ = bf16[4,104,800]{2,1,0:T(8,128)(2,1)S(1)} collective-permute-done((bf16[4,104,800]{2,1,0:T(8,128)(2,1)}, bf16[4,104,800]{2,1,0:T(8,128)(2,1)S(1)}, u32[]{:S(2)}, u32[]{:S(2)}) %collective-permute-start.51) | collective-permute-done | bytes 665632 | tf_op jit(solution)/shard_map/ppermute | solution.py:588
  526.5 5.0 collective-permute-start.55
  534.0 14.3 %shard_map.527 = (bf16[4,416,1024]{2,1,0:T(8,128)(2,1)}, f32[1600,2]{1,0:T(8,128)}) custom-call(s32[1]{0:T(128)} %bitcast.88.col_ref, bf16[1344,1600]{1,0:T(8,128)(2,1)} %get-tuple-element.173.a_ref, bf16[1344,1024]{1,0:T(8,128)(2,1)} %get-tuple-element.291.b_ref.refs_1_, bf16[1600,1024]{1,0:T(8,128)(2,1)} %fusion.5.b_ref.n_ref, ...), custom_call_target="tpu_custom_call" | custom-call | tf_op jit(solution)/shard_map/pallas_call | solution.py:401
  567.9 4.6 collective-permute-done.61
  575.1 6.5 %concatenate.67.refs_4_ = f32[400,3200]{1,0:T(8,128)} concatenate(f32[400,800]{1,0:T(8,128)} %get-tuple-element.352, f32[400,800]{1,0:T(8,128)} %get-tuple-element.351, f32[400,800]{1,0:T(8,128)S(1)} %get-tuple-element.350, f32[400,800]{1,0:T(8,128)S(1)} %get-tuple-element.349), dimensions={1} | concatenate | bytes 10240000 | tf_op jit(solution)/shard_map/concatenate | solution.py:1076
  599.2 20.3 %reduce-scatter.11.cloned.1.call-done = bf16[1,416,1024]{2,1,0:T(8,128)(2,1)} async-done(((bf16[4,416,1024]{2,1,0:T(8,128)(2,1)}), bf16[1,416,1024]{2,1,0:T(8,128)(2,1)}) %reduce-scatter.11.cloned.1.call-update) | async-done | bytes 851984 | tf_op jit(solution)/shard_map/reduce_scatter | solution.py:1069
  (452 shorter events, 221.9 us)
Async XLA Ops:
  7.2 79.8 %all-gather.4.cloned.1.call-start = ((), (), s32[]{:S(2)}) async-start(), calls=%async_computation.4 | async-start | bytes 4096000 | tf_op jit(solution)/shard_map/all_gather | solution.py:837
  17.7 147.2 %all-gather.6.cloned.1.call-start = ((), (), s32[]{:S(2)}) async-start(), calls=%async_computation.5 | async-start | bytes 4096000 | tf_op jit(solution)/shard_map/all_gather | solution.py:871
  30.2 24.4 %collective-permute-start.6 = (bf16[800,1600]{1,0:T(8,128)(2,1)}, bf16[800,1600]{1,0:T(8,128)(2,1)}, u32[]{:S(2)}, u32[]{:S(2)}) collective-permute-start(bf16[800,1600]{1,0:T(8,128)(2,1)} %param.47), channel_id=1, source_target_pairs={{0,4},{4,0},{1,5},{5,1},{2,6},{6,2},{3,7},{7,3},{8,12},{12,8},{9,1... | collective-permute-start | bytes 7680008 | tf_op jit(solution)/shard_map/ppermute | solution.py:573
  87.0 18.7 %collective-permute-start.7 = (bf16[112,800]{1,0:T(8,128)(2,1)}, bf16[112,800]{1,0:T(8,128)(2,1)}, u32[]{:S(2)}, u32[]{:S(2)}) collective-permute-start(bf16[112,800]{1,0:T(8,128)(2,1)} %get-tuple-element.176), channel_id=1, source_target_pairs={{0,3},{1,0},{2,1},{3,2},{4,7},{5,4},{6,5},{7,6},{8,11},{9,8},{10,9... | collective-permute-start | bytes 537608 | tf_op jit(solution)/shard_map/ppermute | solution.py:573
  87.8 21.3 %collective-permute-start.8 = (bf16[112,800]{1,0:T(8,128)(2,1)}, bf16[112,800]{1,0:T(8,128)(2,1)}, u32[]{:S(2)}, u32[]{:S(2)}) collective-permute-start(bf16[112,800]{1,0:T(8,128)(2,1)} %get-tuple-element.176), channel_id=1, source_target_pairs={{0,2},{1,3},{2,0},{3,1},{4,6},{5,7},{6,4},{7,5},{8,10},{9,11},{10,... | collective-permute-start | bytes 537608 | tf_op jit(solution)/shard_map/ppermute | solution.py:573
  87.8 21.3 %collective-permute-start.9 = (bf16[112,800]{1,0:T(8,128)(2,1)}, bf16[112,800]{1,0:T(8,128)(2,1)}, u32[]{:S(2)}, u32[]{:S(2)}) collective-permute-start(bf16[112,800]{1,0:T(8,128)(2,1)} %get-tuple-element.176), channel_id=1, source_target_pairs={{0,1},{1,2},{2,3},{3,0},{4,5},{5,6},{6,7},{7,4},{8,9},{9,10},{10,1... | collective-permute-start | bytes 537608 | tf_op jit(solution)/shard_map/ppermute | solution.py:573
  93.2 185.2 %all-gather.8.cloned.1.call-start = ((), (), s32[]{:S(2)}) async-start(), calls=%async_computation.6 | async-start | bytes 4096000 | tf_op jit(solution)/shard_map/all_gather | solution.py:923
  114.5 24.0 %collective-permute-start.11 = (bf16[4,112,800]{2,1,0:T(8,128)(2,1)}, bf16[4,112,800]{2,1,0:T(8,128)(2,1)}, u32[]{:S(2)}, u32[]{:S(2)}) collective-permute-start(bf16[4,112,800]{2,1,0:T(8,128)(2,1)} %get-tuple-element.184.refs_0_), channel_id=1, source_target_pairs={{0,8},{8,0},{16,24},{24,16},{1,9},{9,1},{17,25},{25,17},{2,10},{10... | collective-permute-start | bytes 2150408 | tf_op jit(solution)/shard_map/ppermute | solution.py:588
  116.0 24.4 %collective-permute-start.12 = (bf16[4,112,800]{2,1,0:T(8,128)(2,1)}, bf16[4,112,800]{2,1,0:T(8,128)(2,1)}, u32[]{:S(2)}, u32[]{:S(2)}) collective-permute-start(bf16[4,112,800]{2,1,0:T(8,128)(2,1)} %get-tuple-element.184.refs_0_), channel_id=1, source_target_pairs={{0,16},{8,24},{16,0},{24,8},{1,17},{9,25},{17,1},{25,9},{2,18},{10... | collective-permute-start | bytes 2150408 | tf_op jit(solution)/shard_map/ppermute | solution.py:588
  142.2 22.6 %collective-permute-start.16 = (bf16[2,112,800]{2,1,0:T(8,128)(2,1)}, bf16[2,112,800]{2,1,0:T(8,128)(2,1)}, u32[]{:S(2)}, u32[]{:S(2)}) collective-permute-start(bf16[2,112,800]{2,1,0:T(8,128)(2,1)} %get-tuple-element.190), channel_id=1, source_target_pairs={{0,16},{8,24},{16,0},{24,8},{1,17},{9,25},{17,1},{25,9},{2,18},{10... | collective-permute-start | bytes 1075208 | tf_op jit(solution)/shard_map/ppermute | solution.py:588
  142.8 22.0 %collective-permute-start.17 = (bf16[2,112,800]{2,1,0:T(8,128)(2,1)}, bf16[2,112,800]{2,1,0:T(8,128)(2,1)}, u32[]{:S(2)}, u32[]{:S(2)}) collective-permute-start(bf16[2,112,800]{2,1,0:T(8,128)(2,1)} %get-tuple-element.191), channel_id=1, source_target_pairs={{0,8},{8,0},{16,24},{24,16},{1,9},{9,1},{17,25},{25,17},{2,10},{10... | collective-permute-start | bytes 1075208 | tf_op jit(solution)/shard_map/ppermute | solution.py:588
  145.2 19.6 %collective-permute-start.15 = (bf16[112,800]{1,0:T(8,128)(2,1)S(1)}, bf16[112,800]{1,0:T(8,128)(2,1)}, u32[]{:S(2)}, u32[]{:S(2)}) collective-permute-start(bf16[112,800]{1,0:T(8,128)(2,1)S(1)} %get-tuple-element.417), channel_id=1, source_target_pairs={{0,5},{1,0},{2,4},{3,1},{4,7},{5,2},{6,6},{7,3},{8,13},{9,8},{10,1... | collective-permute-start | bytes 537608 | tf_op jit(solution)/shard_map/ppermute | solution.py:834
  168.3 23.9 %collective-permute-start.21 = (bf16[4,400,800]{2,1,0:T(8,128)(2,1)}, bf16[4,400,800]{2,1,0:T(8,128)(2,1)}, u32[]{:S(2)}, u32[]{:S(2)}) collective-permute-start(bf16[4,400,800]{2,1,0:T(8,128)(2,1)} %shard_map.494), channel_id=1, source_target_pairs={{0,4},{4,0},{1,5},{5,1},{2,6},{6,2},{3,7},{7,3},{8,12},{12,8},{9,1... | collective-permute-start | bytes 7680008 | tf_op jit(solution)/shard_map/ppermute | solution.py:573
  173.4 18.7 %collective-permute-start.19 = (bf16[448,256]{1,0:T(8,128)(2,1)S(1)}, bf16[448,256]{1,0:T(8,128)(2,1)}, u32[]{:S(2)}, u32[]{:S(2)}) collective-permute-start(bf16[448,256]{1,0:T(8,128)(2,1)S(1)} %get-tuple-element.390), channel_id=1, source_target_pairs={{0,2},{1,3},{2,0},{3,1},{4,6},{5,7},{6,4},{7,5},{8,10},{9,11},{10,... | collective-permute-start | bytes 688136 | tf_op jit(solution)/shard_map/ppermute | solution.py:573
  212.7 167.9 %reduce-scatter.7.cloned.1.call-start = ((), (), s32[]{:S(2)}) async-start(), calls=%async_computation.7 | async-start | bytes 4096000 | tf_op jit(solution)/shard_map/reduce_scatter | solution.py:949
  213.3 21.9 %collective-permute-start.24 = (bf16[4,112,800]{2,1,0:T(8,128)(2,1)}, bf16[4,112,800]{2,1,0:T(8,128)(2,1)S(1)}, u32[]{:S(2)}, u32[]{:S(2)}) collective-permute-start(bf16[4,112,800]{2,1,0:T(8,128)(2,1)} %get-tuple-element.208.refs_0_), channel_id=1, source_target_pairs={{0,8},{8,0},{16,24},{24,16},{1,9},{9,1},{17,25},{25,17},{2,10},{10... | collective-permute-start | bytes 2150408 | tf_op jit(solution)/shard_map/ppermute | solution.py:588
  216.2 37.2 %collective-permute-start.25 = (bf16[4,112,800]{2,1,0:T(8,128)(2,1)}, bf16[4,112,800]{2,1,0:T(8,128)(2,1)S(1)}, u32[]{:S(2)}, u32[]{:S(2)}) collective-permute-start(bf16[4,112,800]{2,1,0:T(8,128)(2,1)} %get-tuple-element.208.refs_0_), channel_id=1, source_target_pairs={{0,16},{8,24},{16,0},{24,8},{1,17},{9,25},{17,1},{25,9},{2,18},{10... | collective-permute-start | bytes 2150408 | tf_op jit(solution)/shard_map/ppermute | solution.py:588
  217.7 35.8 %collective-permute-start.26 = (bf16[4,112,800]{2,1,0:T(8,128)(2,1)}, bf16[4,112,800]{2,1,0:T(8,128)(2,1)S(1)}, u32[]{:S(2)}, u32[]{:S(2)}) collective-permute-start(bf16[4,112,800]{2,1,0:T(8,128)(2,1)} %get-tuple-element.208.refs_0_), channel_id=1, source_target_pairs={{0,24},{8,16},{16,8},{24,0},{1,25},{9,17},{17,9},{25,1},{2,26},{10... | collective-permute-start | bytes 2150408 | tf_op jit(solution)/shard_map/ppermute | solution.py:588
  312.9 19.1 %collective-permute-start.28 = (bf16[800,1600]{1,0:T(8,128)(2,1)}, bf16[800,1600]{1,0:T(8,128)(2,1)S(1)}, u32[]{:S(2)}, u32[]{:S(2)}) collective-permute-start(bf16[800,1600]{1,0:T(8,128)(2,1)} %get-tuple-element.221), channel_id=1, source_target_pairs={{0,4},{4,0},{1,5},{5,1},{2,6},{6,2},{3,7},{7,3},{8,12},{12,8},{9,1... | collective-permute-start | bytes 7680008 | tf_op jit(solution)/shard_map/ppermute | solution.py:573
  313.0 191.9 %reduce-scatter.9.cloned.1.call-start = ((), (), s32[]{:S(2)}) async-start(), calls=%async_computation.8 | async-start | bytes 4096000 | tf_op jit(solution)/shard_map/reduce_scatter | solution.py:1008
  341.4 20.7 %collective-permute-start.30 = (bf16[2,104,1600]{2,1,0:T(8,128)(2,1)}, bf16[2,104,1600]{2,1,0:T(8,128)(2,1)}, u32[]{:S(2)}, u32[]{:S(2)}) collective-permute-start(bf16[2,104,1600]{2,1,0:T(8,128)(2,1)} %get-tuple-element.233), channel_id=1, source_target_pairs={{0,8},{8,0},{16,24},{24,16},{1,9},{9,1},{17,25},{25,17},{2,10},{10... | collective-permute-start | bytes 1996808 | tf_op jit(solution)/shard_map/ppermute | solution.py:588
  360.5 18.9 %collective-permute-start.31 = (bf16[4,104,800]{2,1,0:T(8,128)(2,1)}, bf16[4,104,800]{2,1,0:T(8,128)(2,1)S(1)}, u32[]{:S(2)}, u32[]{:S(2)}) collective-permute-start(bf16[4,104,800]{2,1,0:T(8,128)(2,1)} %get-tuple-element.234), channel_id=1, source_target_pairs={{0,16},{8,24},{16,0},{24,8},{1,17},{9,25},{17,1},{25,9},{2,18},{10... | collective-permute-start | bytes 1996808 | tf_op jit(solution)/shard_map/ppermute | solution.py:588
  399.1 20.0 %collective-permute-start.37 = (bf16[2,104,1600]{2,1,0:T(8,128)(2,1)}, bf16[2,104,1600]{2,1,0:T(8,128)(2,1)}, u32[]{:S(2)}, u32[]{:S(2)}) collective-permute-start(bf16[2,104,1600]{2,1,0:T(8,128)(2,1)} %get-tuple-element.252), channel_id=1, source_target_pairs={{0,16},{8,24},{16,0},{24,8},{1,17},{9,25},{17,1},{25,9},{2,18},{10... | collective-permute-start | bytes 1996808 | tf_op jit(solution)/shard_map/ppermute | solution.py:588
  400.7 18.5 %collective-permute-start.38 = (bf16[4,104,800]{2,1,0:T(8,128)(2,1)}, bf16[4,104,800]{2,1,0:T(8,128)(2,1)}, u32[]{:S(2)}, u32[]{:S(2)}) collective-permute-start(bf16[4,104,800]{2,1,0:T(8,128)(2,1)} %get-tuple-element.253), channel_id=1, source_target_pairs={{0,8},{8,0},{16,24},{24,16},{1,9},{9,1},{17,25},{25,17},{2,10},{10... | collective-permute-start | bytes 1996808 | tf_op jit(solution)/shard_map/ppermute | solution.py:588
  424.6 126.6 %reduce-scatter.13.cloned.1.call-start = ((), (), s32[]{:S(2)}) async-start(), calls=%async_computation.10 | async-start | bytes 931840
  435.0 35.8 %collective-permute-start.43 = (bf16[2,4,104,800]{3,2,1,0:T(8,128)(2,1)}, bf16[2,4,104,800]{3,2,1,0:T(8,128)(2,1)}, u32[]{:S(2)}, u32[]{:S(2)}) collective-permute-start(bf16[2,4,104,800]{3,2,1,0:T(8,128)(2,1)} %get-tuple-element.270), channel_id=1, source_target_pairs={{0,8},{8,0},{16,24},{24,16},{1,9},{9,1},{17,25},{25,17},{2,10},{10... | collective-permute-start | bytes 3993608 | tf_op jit(solution)/shard_map/ppermute | solution.py:588
  435.2 35.6 %collective-permute-start.44 = (bf16[2,104,1600]{2,1,0:T(8,128)(2,1)}, bf16[2,104,1600]{2,1,0:T(8,128)(2,1)}, u32[]{:S(2)}, u32[]{:S(2)}) collective-permute-start(bf16[2,104,1600]{2,1,0:T(8,128)(2,1)} %get-tuple-element.271.refs_6_), channel_id=1, source_target_pairs={{0,16},{8,24},{16,0},{24,8},{1,17},{9,25},{17,1},{25,9},{2,18},{10... | collective-permute-start | bytes 1996808 | tf_op jit(solution)/shard_map/ppermute | solution.py:588
  436.7 34.0 %collective-permute-start.41 = (bf16[104,800]{1,0:T(8,128)(2,1)S(1)}, bf16[104,800]{1,0:T(8,128)(2,1)S(1)}, u32[]{:S(2)}, u32[]{:S(2)}) collective-permute-start(bf16[104,800]{1,0:T(8,128)(2,1)S(1)} %get-tuple-element.414), channel_id=1, source_target_pairs={{0,0},{4,1},{1,2},{5,3},{2,4},{6,5},{3,6},{7,7},{8,8},{12,9},{9,10... | collective-permute-start | bytes 499208 | tf_op jit(solution)/shard_map/ppermute | solution.py:834
  437.4 33.3 %collective-permute-start.42 = (bf16[104,800]{1,0:T(8,128)(2,1)S(1)}, bf16[104,800]{1,0:T(8,128)(2,1)S(1)}, u32[]{:S(2)}, u32[]{:S(2)}) collective-permute-start(bf16[104,800]{1,0:T(8,128)(2,1)S(1)} %get-tuple-element.413), channel_id=1, source_target_pairs={{5,0},{0,1},{4,2},{1,3},{7,4},{2,5},{6,6},{3,7},{13,8},{8,9},{12,1... | collective-permute-start | bytes 499208 | tf_op jit(solution)/shard_map/ppermute | solution.py:834
  472.8 25.9 %collective-permute-start.46 = (bf16[104,800]{1,0:T(8,128)(2,1)S(1)}, bf16[104,800]{1,0:T(8,128)(2,1)S(1)}, u32[]{:S(2)}, u32[]{:S(2)}) collective-permute-start(bf16[104,800]{1,0:T(8,128)(2,1)S(1)} %get-tuple-element.412), channel_id=1, source_target_pairs={{1,0},{5,1},{0,2},{4,3},{3,4},{7,5},{2,6},{6,7},{9,8},{13,9},{8,10... | collective-permute-start | bytes 499208 | tf_op jit(solution)/shard_map/ppermute | solution.py:834
  474.8 23.9 %collective-permute-start.47 = (bf16[104,800]{1,0:T(8,128)(2,1)S(1)}, bf16[104,800]{1,0:T(8,128)(2,1)S(1)}, u32[]{:S(2)}, u32[]{:S(2)}) collective-permute-start(bf16[104,800]{1,0:T(8,128)(2,1)S(1)} %get-tuple-element.411), channel_id=1, source_target_pairs={{4,0},{1,1},{5,2},{0,3},{6,4},{3,5},{7,6},{2,7},{12,8},{9,9},{13,1... | collective-permute-start | bytes 499208 | tf_op jit(solution)/shard_map/ppermute | solution.py:834
  480.7 24.2 %collective-permute-start.48 = (bf16[2,104,1600]{2,1,0:T(8,128)(2,1)}, bf16[2,104,1600]{2,1,0:T(8,128)(2,1)}, u32[]{:S(2)}, u32[]{:S(2)}) collective-permute-start(bf16[2,104,1600]{2,1,0:T(8,128)(2,1)} %get-tuple-element.283), channel_id=1, source_target_pairs={{0,8},{8,0},{16,24},{24,16},{1,9},{9,1},{17,25},{25,17},{2,10},{10... | collective-permute-start | bytes 1996808 | tf_op jit(solution)/shard_map/ppermute | solution.py:588
  484.0 18.6 %collective-permute-start.49 = (bf16[4,104,800]{2,1,0:T(8,128)(2,1)}, bf16[4,104,800]{2,1,0:T(8,128)(2,1)S(1)}, u32[]{:S(2)}, u32[]{:S(2)}) collective-permute-start(bf16[4,104,800]{2,1,0:T(8,128)(2,1)} %fusion.11), channel_id=1, source_target_pairs={{0,16},{8,24},{16,0},{24,8},{1,17},{9,25},{17,1},{25,9},{2,18},{10... | collective-permute-start | bytes 1996808 | tf_op jit(solution)/shard_map/ppermute | solution.py:588
  504.9 19.3 %collective-permute-start.51 = (bf16[4,104,800]{2,1,0:T(8,128)(2,1)}, bf16[4,104,800]{2,1,0:T(8,128)(2,1)S(1)}, u32[]{:S(2)}, u32[]{:S(2)}) collective-permute-start(bf16[4,104,800]{2,1,0:T(8,128)(2,1)} %get-tuple-element.286.refs_0_), channel_id=1, source_target_pairs={{0,8},{8,0},{16,24},{24,16},{1,9},{9,1},{17,25},{25,17},{2,10},{10... | collective-permute-start | bytes 1996808 | tf_op jit(solution)/shard_map/ppermute | solution.py:588
  505.9 19.0 %collective-permute-start.52 = (bf16[4,104,800]{2,1,0:T(8,128)(2,1)}, bf16[4,104,800]{2,1,0:T(8,128)(2,1)}, u32[]{:S(2)}, u32[]{:S(2)}) collective-permute-start(bf16[4,104,800]{2,1,0:T(8,128)(2,1)} %get-tuple-element.286.refs_0_), channel_id=1, source_target_pairs={{0,16},{8,24},{16,0},{24,8},{1,17},{9,25},{17,1},{25,9},{2,18},{10... | collective-permute-start | bytes 1996808 | tf_op jit(solution)/shard_map/ppermute | solution.py:588
  525.1 94.4 %reduce-scatter.11.cloned.1.call-start = ((), (), s32[]{:S(2)}) async-start(), calls=%async_computation.9 | async-start | bytes 4259840 | tf_op jit(solution)/shard_map/reduce_scatter | solution.py:1069
  525.2 23.2 %collective-permute-start.56 = (bf16[3,48,800]{2,1,0:T(8,128)(2,1)}, bf16[3,48,800]{2,1,0:T(8,128)(2,1)S(1)}, u32[]{:S(2)}, u32[]{:S(2)}) collective-permute-start(bf16[3,48,800]{2,1,0:T(8,128)(2,1)} %get-tuple-element.299), channel_id=1, source_target_pairs={{1,0},{2,1},{3,2},{5,4},{6,5},{7,6},{9,8},{10,9},{11,10},{13,12},{... | collective-permute-start | bytes 691208 | tf_op jit(solution)/shard_map/ppermute | solution.py:689
  526.5 21.9 %collective-permute-start.55 = (bf16[3,48,800]{2,1,0:T(8,128)(2,1)}, bf16[3,48,800]{2,1,0:T(8,128)(2,1)S(1)}, u32[]{:S(2)}, u32[]{:S(2)}) collective-permute-start(bf16[3,48,800]{2,1,0:T(8,128)(2,1)} %get-tuple-element.298), channel_id=1, source_target_pairs={{0,1},{1,2},{2,3},{4,5},{5,6},{6,7},{8,9},{9,10},{10,11},{12,13},{... | collective-permute-start | bytes 691208 | tf_op jit(solution)/shard_map/ppermute | solution.py:685
  531.4 19.7 %collective-permute-start.54 = (bf16[2,104,1600]{2,1,0:T(8,128)(2,1)}, bf16[2,104,1600]{2,1,0:T(8,128)(2,1)S(1)}, u32[]{:S(2)}, u32[]{:S(2)}) collective-permute-start(bf16[2,104,1600]{2,1,0:T(8,128)(2,1)} %get-tuple-element.295), channel_id=1, source_target_pairs={{0,16},{8,24},{16,0},{24,8},{1,17},{9,25},{17,1},{25,9},{2,18},{10... | collective-permute-start | bytes 1996808 | tf_op jit(solution)/shard_map/ppermute | solution.py:588
  533.0 18.1 %collective-permute-start.53 = (bf16[4,104,800]{2,1,0:T(8,128)(2,1)}, bf16[4,104,800]{2,1,0:T(8,128)(2,1)S(1)}, u32[]{:S(2)}, u32[]{:S(2)}) collective-permute-start(bf16[4,104,800]{2,1,0:T(8,128)(2,1)} %get-tuple-element.294), channel_id=1, source_target_pairs={{0,8},{8,0},{16,24},{24,16},{1,9},{9,1},{17,25},{25,17},{2,10},{10... | collective-permute-start | bytes 1996808 | tf_op jit(solution)/shard_map/ppermute | solution.py:588
  553.8 29.7 %collective-permute-start.59 = (bf16[3,104,800]{2,1,0:T(8,128)(2,1)}, bf16[3,104,800]{2,1,0:T(8,128)(2,1)}, u32[]{:S(2)}, u32[]{:S(2)}) collective-permute-start(bf16[3,104,800]{2,1,0:T(8,128)(2,1)} %get-tuple-element.306.refs_7_), channel_id=1, source_target_pairs={{0,24},{8,16},{16,8},{24,0},{1,25},{9,17},{17,9},{25,1},{2,26},{10... | collective-permute-start | bytes 1497608 | tf_op jit(solution)/shard_map/ppermute | solution.py:588
  554.7 28.8 %collective-permute-start.58 = (bf16[3,104,800]{2,1,0:T(8,128)(2,1)}, bf16[3,104,800]{2,1,0:T(8,128)(2,1)}, u32[]{:S(2)}, u32[]{:S(2)}) collective-permute-start(bf16[3,104,800]{2,1,0:T(8,128)(2,1)} %get-tuple-element.305.refs_6_), channel_id=1, source_target_pairs={{0,16},{8,24},{16,0},{24,8},{1,17},{9,25},{17,1},{25,9},{2,18},{10... | collective-permute-start | bytes 1497608 | tf_op jit(solution)/shard_map/ppermute | solution.py:588
  556.3 27.2 %collective-permute-start.57 = (bf16[3,104,800]{2,1,0:T(8,128)(2,1)}, bf16[3,104,800]{2,1,0:T(8,128)(2,1)}, u32[]{:S(2)}, u32[]{:S(2)}) collective-permute-start(bf16[3,104,800]{2,1,0:T(8,128)(2,1)} %get-tuple-element.304.refs_5_), channel_id=1, source_target_pairs={{0,8},{8,0},{16,24},{24,16},{1,9},{9,1},{17,25},{25,17},{2,10},{10... | collective-permute-start | bytes 1497608 | tf_op jit(solution)/shard_map/ppermute | solution.py:588
  561.0 25.3 %collective-permute-start.63 = (bf16[1,104,800]{2,1,0:T(8,128)(2,1)}, bf16[1,104,800]{2,1,0:T(8,128)(2,1)S(1)}, u32[]{:S(2)}, u32[]{:S(2)}) collective-permute-start(bf16[1,104,800]{2,1,0:T(8,128)(2,1)} %get-tuple-element.314), channel_id=1, source_target_pairs={{0,8},{8,0},{16,24},{24,16},{1,9},{9,1},{17,25},{25,17},{2,10},{10... | collective-permute-start | bytes 499208 | tf_op jit(solution)/shard_map/ppermute | solution.py:588
  588.6 34.2 %collective-permute-start.66 = (bf16[324,800]{1,0:T(8,128)(2,1)}, bf16[324,800]{1,0:T(8,128)(2,1)S(1)}, u32[]{:S(2)}, u32[]{:S(2)}) collective-permute-start(bf16[324,800]{1,0:T(8,128)(2,1)} %get-tuple-element.320), channel_id=1, source_target_pairs={{0,8},{8,0},{16,24},{24,16},{1,9},{9,1},{17,25},{25,17},{2,10},{10... | collective-permute-start | bytes 1555208 | tf_op jit(solution)/shard_map/ppermute | solution.py:588
  589.7 33.1 %collective-permute-start.67 = (bf16[324,800]{1,0:T(8,128)(2,1)}, bf16[324,800]{1,0:T(8,128)(2,1)S(1)}, u32[]{:S(2)}, u32[]{:S(2)}) collective-permute-start(bf16[324,800]{1,0:T(8,128)(2,1)} %get-tuple-element.320), channel_id=1, source_target_pairs={{0,16},{8,24},{16,0},{24,8},{1,17},{9,25},{17,1},{25,9},{2,18},{10... | collective-permute-start | bytes 1555208 | tf_op jit(solution)/shard_map/ppermute | solution.py:588
  591.4 31.5 %collective-permute-start.68 = (bf16[324,800]{1,0:T(8,128)(2,1)}, bf16[324,800]{1,0:T(8,128)(2,1)S(1)}, u32[]{:S(2)}, u32[]{:S(2)}) collective-permute-start(bf16[324,800]{1,0:T(8,128)(2,1)} %get-tuple-element.320), channel_id=1, source_target_pairs={{0,24},{8,16},{16,8},{24,0},{1,25},{9,17},{17,9},{25,1},{2,26},{10... | collective-permute-start | bytes 1555208 | tf_op jit(solution)/shard_map/ppermute | solution.py:588
  592.1 30.7 %collective-permute-start.65 = (bf16[1,104,800]{2,1,0:T(8,128)(2,1)}, bf16[1,104,800]{2,1,0:T(8,128)(2,1)S(1)}, u32[]{:S(2)}, u32[]{:S(2)}) collective-permute-start(bf16[1,104,800]{2,1,0:T(8,128)(2,1)} %get-tuple-element.318.refs_0_), channel_id=1, source_target_pairs={{0,16},{8,24},{16,0},{24,8},{1,17},{9,25},{17,1},{25,9},{2,18},{10... | collective-permute-start | bytes 499208 | tf_op jit(solution)/shard_map/ppermute | solution.py:588
  (107 other events, 952.9 us)
Sparse Core Ops, SparseCore 0:
  17.7 69.2 all-gather.3
  93.4 68.2 all-gather.5
  212.8 65.5 all-gather.7
  313.1 60.6 reduce-scatter.6
  424.8 74.8 reduce-scatter.8
  525.2 25.2 reduce-scatter.12
  553.5 65.9 reduce-scatter.10

commit v5 on v4

--- a/solution.py
+++ b/solution.py
@@ -668,6 +668,33 @@
     )(me, *parts)
 
 
+def join_wide(parts, shares, me):
+    wide = parts[0].shape[1]
+    size = shares.size
+
+    def kernel(me_ref, *refs):
+        o_ref = refs[4]
+        for m in range(4):
+            for s in range(4):
+
+                @pl.when(me_ref[0] ^ m == s)
+                def move():
+                    first, rows = shares.starts[s], shares.lengths[s]
+                    held = refs[m][...].astype(F32)
+                    for k in range(3):
+                        cut = held[k * size : k * size + rows]
+                        o_ref[k, first : first + rows, :] = cut
+
+    return pl.pallas_call(
+        kernel,
+        out_shape=jax.ShapeDtypeStruct((3, shares.rows, wide), F32),
+        in_specs=[SM] + [V] * 4,
+        out_specs=V,
+        compiler_params=ROOM,
+        cost_estimate=FREE,
+    )(me, *parts)
+
+
 def small_sum(value, axes):
     for axis in axes:
         size = lax.axis_size(axis)
@@ -1110,8 +1137,7 @@
     small = sum(v[ends:].astype(F32) for v in (payload, a, b, c))
     small = (small[:deep] + small[deep:]).reshape(-1)
     sums, local = small[: 7 * width].reshape(7, width), small[7 * width : 8 * width + ff]
-    qkv_all = [v[:ends].reshape(3, fine.size, in_rows) for v in (payload, a, b, c)]
-    qkv_grad = fine.join(qkv_all, dp, 1).astype(F32)
+    qkv_grad = join_wide([payload, a, b, c], fine, dp[None].astype(jnp.int32))
     return (
         outputs.T.reshape(tokens.shape),
         input_grad.T.reshape(tokens.shape),

time: 651 us -> 650 us (level)
  Pallas kernels: 188 us -> 200 us
  starting transfers between devices: 109 us -> 101 us
    unnamed x161 -> x157, local copies, waits for them, and re-layouts: 27.7 us -> 27.1 us
  transfers between devices with their start and end apart: 76 -> 76, of which waited for: 24 -> 22; matrix products, arithmetic and copies ran while one was open for 22% -> 22% of each run, Pallas kernels for 23% -> 25%
where the time goes in v5:
time: 650 us; the launch traced here: 641 us
  Pallas kernels  200 us (31%)
  waiting for transfers between devices  144 us (22%)
  starting transfers between devices  101 us (16%)
  other arithmetic  97 us (15%)
  local copies, waits for them, and re-layouts  75.6 us (12%)
  between operations  23.1 us (4%)
    ppermute x30, waiting for transfers between devices, swap_with(): return lax.ppermute(value, 'dp', [(i, i ^ bit) for i in range(4)])  50.5 us
    pallas_call x8, Pallas kernels, token_product(): pl.pallas_call(kernel, out_shape=jax.ShapeDtypeStruct((rows_a, rows_b), B...  49.9 us
    ppermute x8, starting transfers between devices, between_owners(): got.append(lax.ppermute(value_of(step), ('row', 'col'), pairs))  34 us
    ppermute x30, starting transfers between devices, swap_with(): return lax.ppermute(value, 'dp', [(i, i ^ bit) for i in range(4)])  32.2 us
    pallas_call x1, Pallas kernels, attn_bwd(): pl.pallas_call(functools.partial(bwd_kernel, n_row, n_slots, hd, ks.shape...  29.4 us
    pallas_call x1, Pallas kernels, hidden_layer(): pl.pallas_call(kernel, out_shape=[jax.ShapeDtypeStruct((ff, tokens), BF16...  27.8 us
    unnamed x157, local copies, waits for them, and re-layouts  27.1 us
    ppermute x24, waiting for transfers between devices, turn(): lax.ppermute(value, axis, [(i, (i + steps) % size) for i in range(size)])  26.6 us
  transfers between devices with their start and end apart: 76, of which 22 were waited for; matrix products, arithmetic and copies ran while one was open for 22% of the time, Pallas kernels for 25%

profile of v5, /device:TPU:0, one launch (start us, length us, event | category | flops | bytes accessed | tf_op | source)
XLA Modules:
  0.0 640.8 jit_solution(6770222520765080298)
XLA Ops:
  11.3 4.9 collective-permute-start
  17.7 4.3 collective-permute-done
  22.0 3.8 collective-permute-done.1
  25.8 4.4 fusion.8
  41.0 4.3 copy.214
  51.1 3.5 pad_maximum_fusion
  54.6 5.2 copy.215
  62.2 4.1 maximum_bitcast_fusion.refs_8_.up_ref
  66.3 20.7 %all-gather.4.cloned.1.call-done.refs_0_ = bf16[1600,1024]{1,0:T(8,128)(2,1)} async-done(((bf16[400,1024]{1,0:T(8,128)(2,1)}), bf16[1600,1024]{1,0:T(8,128)(2,1)}) %all-gather.4.cloned.1.call-update) | async-done | bytes 3276816 | tf_op jit(solution)/shard_map/all_gather | solution.py:864
  96.2 9.4 %shard_map.488 = bf16[1344,1024]{1,0:T(8,128)(2,1)} custom-call(bf16[1344,1600]{1,0:T(8,128)(2,1)} %get-tuple-element.173.a_ref, bf16[1600,1024]{1,0:T(8,128)(2,1)} %fusion.5.b_ref.n_ref, f32[1344,1]{1,0:T(8,128)} %get-tuple-element.175.bias_ref), custom_call_target="tpu_custom_call" | custom-call | tf_op jit(solution)/shard_map/pallas_call | solution.py:189
  105.7 3.4 collective-permute-done.8.refs_2_
  117.6 20.7 %shard_map.491 = (bf16[448,1024]{1,0:T(8,128)(2,1)S(1)}, bf16[448,1024]{1,0:T(8,128)(2,1)S(1)}, bf16[448,2048]{1,0:T(8,128)(2,1)S(1)}, f32[7,2048]{1,0:T(8,128)S(1)}) custom-call(s32[4]{0:T(128)S(1)} %copy-done.7, s32[25,4]{1,0:T(8,128)S(1)} %copy.220.ks, bf16[3,448,1024]{2,1,0:T(8,128)(2,1)} %get-tuple-element.177.refs_0_, ...), custom_call_target="tpu_custom_call" | custom-call | tf_op jit(solution)/shard_map/pallas_call | solution.py:148
  148.7 12.9 %collective-permute-start.15 = (bf16[112,800]{1,0:T(8,128)(2,1)S(1)}, bf16[112,800]{1,0:T(8,128)(2,1)}, u32[]{:S(2)}, u32[]{:S(2)}) collective-permute-start(bf16[112,800]{1,0:T(8,128)(2,1)S(1)} %get-tuple-element.413), channel_id=1, source_target_pairs={{0,5},{1,0},{2,4},{3,1},{4,7},{5,2},{6,6},{7,3},{8,13},{9,8},{10,1... | collective-permute-start | bytes 537608 | tf_op jit(solution)/shard_map/ppermute | solution.py:861
  166.8 3.4 shard_map.494
  180.1 3.3 collective-permute-done.18.refs_2_
  183.4 9.1 %collective-permute-done.19.refs_3_ = bf16[448,256]{1,0:T(8,128)(2,1)} collective-permute-done((bf16[448,256]{1,0:T(8,128)(2,1)S(1)}, bf16[448,256]{1,0:T(8,128)(2,1)}, u32[]{:S(2)}, u32[]{:S(2)}) %collective-permute-start.19) | collective-permute-done | bytes 229408 | tf_op jit(solution)/shard_map/ppermute | solution.py:573
  196.1 4.2 collective-permute-start.22
  201.3 8.2 %shard_map.496 = (f32[1600,256]{1,0:T(8,128)}, f32[1600,256]{1,0:T(8,128)}, bf16[1600,256]{1,0:T(8,128)(2,1)}, f32[1,256]{1,0:T(1,128)}) custom-call(s32[1]{0:T(128)} %bitcast.9.row_ref, bf16[1600,256]{1,0:T(8,128)(2,1)} %pad_add_fusion.b_ref, f32[1600,6]{1,0:T(8,128)} %get-tuple-element.200.c_ref.bias_ref.g_ref, ...), custom_call_target="tpu_custom_call" | custom-call | tf_op jit(solution)/shard_map/pallas_call | solution.py:262
  219.0 17.5 %collective-permute-done.24.refs_1_ = bf16[4,112,800]{2,1,0:T(8,128)(2,1)S(1)} collective-permute-done((bf16[4,112,800]{2,1,0:T(8,128)(2,1)}, bf16[4,112,800]{2,1,0:T(8,128)(2,1)S(1)}, u32[]{:S(2)}, u32[]{:S(2)}) %collective-permute-start.24) | collective-permute-done | bytes 716832 | tf_op jit(solution)/shard_map/ppermute | solution.py:588
  236.5 17.5 %collective-permute-done.25.refs_2_ = bf16[4,112,800]{2,1,0:T(8,128)(2,1)S(1)} collective-permute-done((bf16[4,112,800]{2,1,0:T(8,128)(2,1)}, bf16[4,112,800]{2,1,0:T(8,128)(2,1)S(1)}, u32[]{:S(2)}, u32[]{:S(2)}) %collective-permute-start.25) | collective-permute-done | bytes 716832 | tf_op jit(solution)/shard_map/ppermute | solution.py:588
  255.8 3.5 shard_map.498
  261.4 3.6 collective-permute-done.27
  265.0 6.9 %shard_map.499.refs_1_ = bf16[1600,1600]{1,0:T(8,128)(2,1)} custom-call(bf16[1600,800]{1,0:T(8,128)(2,1)} %bitcast.185, bf16[1600,800]{1,0:T(8,128)(2,1)} %bitcast.54.refs_1_), custom_call_target="tpu_custom_call" | custom-call | tf_op jit(solution)/shard_map/pallas_call | solution.py:544
  272.0 7.1 %all-gather.8.cloned.1.call-done.refs_0_ = bf16[1600,1024]{1,0:T(8,128)(2,1)} async-done(((bf16[1600,256]{1,0:T(8,128)(2,1)}), bf16[1600,1024]{1,0:T(8,128)(2,1)}) %all-gather.8.cloned.1.call-update) | async-done | bytes 3276816 | tf_op jit(solution)/shard_map/all_gather | solution.py:950
  279.0 27.8 %shard_map.501 = (bf16[1600,1024]{1,0:T(8,128)(2,1)}, bf16[1600,1024]{1,0:T(8,128)(2,1)}, bf16[1600,1024]{1,0:T(8,128)(2,1)}, f32[1600,1]{1,0:T(8,128)}) custom-call(s32[1]{0:T(128)} %bitcast.9.row_ref, bf16[1600,1600]{1,0:T(8,128)(2,1)} %maximum_bitcast_fusion.refs_8_.up_ref, bf16[1600,1600]{1,0:T(8,128)(2,1)} %get-tuple-element.210.down_ref, ...), custom_call_target="tpu_custom_call" | custom-call | tf_op jit(solution)/shard_map/pallas_call | solution.py:498
  306.8 6.7 %shard_map.503.refs_2_ = bf16[800,1600]{1,0:T(8,128)(2,1)} custom-call(s32[1]{0:T(128)} %bitcast.55.index_ref, bf16[1600,1024]{1,0:T(8,128)(2,1)} %get-tuple-element.211.n_ref.a_ref.refs_0_, bf16[1600,1024]{1,0:T(8,128)(2,1)} %get-tuple-element.218.b_ref), custom_call_target="tpu_custom_call" | custom-call | tf_op jit(solution)/shard_map/pallas_call | solution.py:442
  318.8 7.2 %shard_map.506 = bf16[1600,800]{1,0:T(8,128)(2,1)} custom-call(s32[1]{0:T(128)} %bitcast.55.index_ref, bf16[1600,1024]{1,0:T(8,128)(2,1)} %get-tuple-element.212.g_ref.a_ref, bf16[1600,1024]{1,0:T(8,128)(2,1)} %get-tuple-element.219.b_ref.refs_0_), custom_call_target="tpu_custom_call" | custom-call | tf_op jit(solution)/shard_map/pallas_call | solution.py:442
  326.0 6.7 %shard_map.505.refs_1_ = bf16[800,1600]{1,0:T(8,128)(2,1)} custom-call(s32[1]{0:T(128)} %bitcast.56.index_ref, bf16[1600,1024]{1,0:T(8,128)(2,1)} %get-tuple-element.220.a_ref, bf16[1600,1024]{1,0:T(8,128)(2,1)} %get-tuple-element.218.b_ref), custom_call_target="tpu_custom_call" | custom-call | tf_op jit(solution)/shard_map/pallas_call | solution.py:442
  347.6 7.2 %shard_map.509 = bf16[1600,800]{1,0:T(8,128)(2,1)} custom-call(s32[1]{0:T(128)} %bitcast.56.index_ref, bf16[1600,1024]{1,0:T(8,128)(2,1)} %get-tuple-element.212.g_ref.a_ref, bf16[1600,1024]{1,0:T(8,128)(2,1)} %get-tuple-element.226.b_ref.refs_0_), custom_call_target="tpu_custom_call" | custom-call | tf_op jit(solution)/shard_map/pallas_call | solution.py:442
  356.4 3.4 add_convert_fusion.1
  364.9 11.2 %shard_map.512 = bf16[1600,1024]{1,0:T(8,128)(2,1)} custom-call(s32[1]{0:T(128)} %bitcast.9.row_ref, bf16[1600,1024]{1,0:T(8,128)(2,1)} %get-tuple-element.231.b_ref, f32[1600,6]{1,0:T(8,128)} %get-tuple-element.200.c_ref.bias_ref.g_ref, bf16[1600,800]{1,0:T(8,128)(2,1)} %bitcast.186, bf16[1600,800]{1,0:T(8,128)(2,1)} %bitcast.54.refs_1_), custom_call_target="tpu_custom_call" | custom-call | tf_op jit(solution)/shard_map/pallas_call | solution.py:217
  383.2 10.5 %shard_map.514 = (f32[1600,256]{1,0:T(8,128)}, bf16[1600,256]{1,0:T(8,128)(2,1)}, bf16[1600,256]{1,0:T(8,128)(2,1)}, f32[1600,3]{1,0:T(8,128)}) custom-call(s32[1]{0:T(128)} %bitcast.9.row_ref, bf16[1600,256]{1,0:T(8,128)(2,1)} %get-tuple-element.236.dn_ref, f32[1600,256]{1,0:T(8,128)} %get-tuple-element.237.hat_ref, f32[1,256]{1,0:T(1,128)} %get-tuple-element.238.scale_ref, ...), custom_call_target="tpu_custom_call" | custom-call | tf_op jit(solution)/shard_map/pallas_call | solution.py:326
  406.3 4.6 shard_map.516
  410.9 4.6 shard_map.517
  415.6 4.1 collective-permute-done.35.refs_1_
  438.2 7.9 %collective-permute-start.42 = (bf16[104,800]{1,0:T(8,128)(2,1)S(1)}, bf16[104,800]{1,0:T(8,128)(2,1)S(1)}, u32[]{:S(2)}, u32[]{:S(2)}) collective-permute-start(bf16[104,800]{1,0:T(8,128)(2,1)S(1)} %get-tuple-element.409), channel_id=1, source_target_pairs={{5,0},{0,1},{4,2},{1,3},{7,4},{2,5},{6,6},{3,7},{13,8},{8,9},{12,1... | collective-permute-start | bytes 499208 | tf_op jit(solution)/shard_map/ppermute | solution.py:861
  446.1 29.4 %shard_map.520 = (bf16[3,448,1024]{2,1,0:T(8,128)(2,1)}, bf16[3,448,1024]{2,1,0:T(8,128)(2,1)}) custom-call(s32[4]{0:T(128)} %get-tuple-element.172.meta, s32[25,4]{1,0:T(8,128)} %copy-done.5, bf16[3,448,1024]{2,1,0:T(8,128)(2,1)} %get-tuple-element.177.refs_0_, bf16[3,448,1024]{2,1,0:T(8,128)(2,1)} %get-tuple-element.181.refs_1_, ...), custom_call_target="tpu_custom_call" | custom-call | tf_op jit(solution)/shard_map/pallas_call | solution.py:157
  477.7 5.7 collective-permute-start.47
  490.3 4.7 add_convert_fusion.2
  494.9 6.4 %shard_map.523 = bf16[1344,800]{1,0:T(8,128)(2,1)} custom-call(s32[1]{0:T(128)} %bitcast.55.index_ref, bf16[1344,1024]{1,0:T(8,128)(2,1)} %bitcast.175, bf16[1600,1024]{1,0:T(8,128)(2,1)} %fusion.5.b_ref.n_ref), custom_call_target="tpu_custom_call" | custom-call | tf_op jit(solution)/shard_map/pallas_call | solution.py:442
  508.4 6.4 shard_map.525
  518.1 8.0 %collective-permute-done.51.refs_6_ = bf16[4,104,800]{2,1,0:T(8,128)(2,1)S(1)} collective-permute-done((bf16[4,104,800]{2,1,0:T(8,128)(2,1)}, bf16[4,104,800]{2,1,0:T(8,128)(2,1)S(1)}, u32[]{:S(2)}, u32[]{:S(2)}) %collective-permute-start.51) | collective-permute-done | bytes 665632 | tf_op jit(solution)/shard_map/ppermute | solution.py:588
  528.4 5.0 collective-permute-start.55
  534.9 14.3 %shard_map.527 = (bf16[4,416,1024]{2,1,0:T(8,128)(2,1)}, f32[1600,2]{1,0:T(8,128)}) custom-call(s32[1]{0:T(128)} %bitcast.88.col_ref, bf16[1344,1600]{1,0:T(8,128)(2,1)} %get-tuple-element.173.a_ref, bf16[1344,1024]{1,0:T(8,128)(2,1)} %get-tuple-element.291.b_ref.refs_1_, bf16[1600,1024]{1,0:T(8,128)(2,1)} %fusion.5.b_ref.n_ref, ...), custom_call_target="tpu_custom_call" | custom-call | tf_op jit(solution)/shard_map/pallas_call | solution.py:401
  568.8 4.6 collective-permute-done.61
  576.3 6.6 %concatenate.64.refs_4_ = f32[400,3200]{1,0:T(8,128)} concatenate(f32[400,800]{1,0:T(8,128)} %get-tuple-element.352, f32[400,800]{1,0:T(8,128)} %get-tuple-element.351, f32[400,800]{1,0:T(8,128)S(1)} %get-tuple-element.350, f32[400,800]{1,0:T(8,128)S(1)} %get-tuple-element.349), dimensions={1} | concatenate | bytes 10240000 | tf_op jit(solution)/shard_map/concatenate | solution.py:1103
  599.6 20.8 %reduce-scatter.11.cloned.1.call-done = bf16[1,416,1024]{2,1,0:T(8,128)(2,1)} async-done(((bf16[4,416,1024]{2,1,0:T(8,128)(2,1)}), bf16[1,416,1024]{2,1,0:T(8,128)(2,1)}) %reduce-scatter.11.cloned.1.call-update) | async-done | bytes 851984 | tf_op jit(solution)/shard_map/reduce_scatter | solution.py:1096
  625.1 4.2 shard_map.532
  (445 shorter events, 213.8 us)
Async XLA Ops:
  7.2 79.8 %all-gather.4.cloned.1.call-start = ((), (), s32[]{:S(2)}) async-start(), calls=%async_computation.4 | async-start | bytes 4096000 | tf_op jit(solution)/shard_map/all_gather | solution.py:864
  17.7 149.1 %all-gather.6.cloned.1.call-start = ((), (), s32[]{:S(2)}) async-start(), calls=%async_computation.5 | async-start | bytes 4096000 | tf_op jit(solution)/shard_map/all_gather | solution.py:898
  30.2 18.0 %collective-permute-start.2 = (bf16[3,448,800]{2,1,0:T(8,128)(2,1)}, bf16[3,448,800]{2,1,0:T(8,128)(2,1)}, u32[]{:S(2)}, u32[]{:S(2)}) collective-permute-start(bf16[3,448,800]{2,1,0:T(8,128)(2,1)} %fusion.8), channel_id=1, source_target_pairs={{0,4},{4,0},{1,5},{5,1},{2,6},{6,2},{3,7},{7,3},{8,12},{12,8},{9,1... | collective-permute-start | bytes 6451208 | tf_op jit(solution)/shard_map/ppermute | solution.py:573
  30.2 24.4 %collective-permute-start.6 = (bf16[800,1600]{1,0:T(8,128)(2,1)}, bf16[800,1600]{1,0:T(8,128)(2,1)}, u32[]{:S(2)}, u32[]{:S(2)}) collective-permute-start(bf16[800,1600]{1,0:T(8,128)(2,1)} %param.47), channel_id=1, source_target_pairs={{0,4},{4,0},{1,5},{5,1},{2,6},{6,2},{3,7},{7,3},{8,12},{12,8},{9,1... | collective-permute-start | bytes 7680008 | tf_op jit(solution)/shard_map/ppermute | solution.py:573
  87.0 18.7 %collective-permute-start.7 = (bf16[112,800]{1,0:T(8,128)(2,1)}, bf16[112,800]{1,0:T(8,128)(2,1)}, u32[]{:S(2)}, u32[]{:S(2)}) collective-permute-start(bf16[112,800]{1,0:T(8,128)(2,1)} %get-tuple-element.176), channel_id=1, source_target_pairs={{0,3},{1,0},{2,1},{3,2},{4,7},{5,4},{6,5},{7,6},{8,11},{9,8},{10,9... | collective-permute-start | bytes 537608 | tf_op jit(solution)/shard_map/ppermute | solution.py:573
  87.8 21.3 %collective-permute-start.8 = (bf16[112,800]{1,0:T(8,128)(2,1)}, bf16[112,800]{1,0:T(8,128)(2,1)}, u32[]{:S(2)}, u32[]{:S(2)}) collective-permute-start(bf16[112,800]{1,0:T(8,128)(2,1)} %get-tuple-element.176), channel_id=1, source_target_pairs={{0,2},{1,3},{2,0},{3,1},{4,6},{5,7},{6,4},{7,5},{8,10},{9,11},{10,... | collective-permute-start | bytes 537608 | tf_op jit(solution)/shard_map/ppermute | solution.py:573
  87.8 21.3 %collective-permute-start.9 = (bf16[112,800]{1,0:T(8,128)(2,1)}, bf16[112,800]{1,0:T(8,128)(2,1)}, u32[]{:S(2)}, u32[]{:S(2)}) collective-permute-start(bf16[112,800]{1,0:T(8,128)(2,1)} %get-tuple-element.176), channel_id=1, source_target_pairs={{0,1},{1,2},{2,3},{3,0},{4,5},{5,6},{6,7},{7,4},{8,9},{9,10},{10,1... | collective-permute-start | bytes 537608 | tf_op jit(solution)/shard_map/ppermute | solution.py:573
  93.2 185.8 %all-gather.8.cloned.1.call-start = ((), (), s32[]{:S(2)}) async-start(), calls=%async_computation.6 | async-start | bytes 4096000 | tf_op jit(solution)/shard_map/all_gather | solution.py:950
  114.5 27.5 %collective-permute-start.11 = (bf16[4,112,800]{2,1,0:T(8,128)(2,1)}, bf16[4,112,800]{2,1,0:T(8,128)(2,1)}, u32[]{:S(2)}, u32[]{:S(2)}) collective-permute-start(bf16[4,112,800]{2,1,0:T(8,128)(2,1)} %get-tuple-element.184.refs_0_), channel_id=1, source_target_pairs={{0,8},{8,0},{16,24},{24,16},{1,9},{9,1},{17,25},{25,17},{2,10},{10... | collective-permute-start | bytes 2150408 | tf_op jit(solution)/shard_map/ppermute | solution.py:588
  116.0 27.8 %collective-permute-start.12 = (bf16[4,112,800]{2,1,0:T(8,128)(2,1)}, bf16[4,112,800]{2,1,0:T(8,128)(2,1)}, u32[]{:S(2)}, u32[]{:S(2)}) collective-permute-start(bf16[4,112,800]{2,1,0:T(8,128)(2,1)} %get-tuple-element.184.refs_0_), channel_id=1, source_target_pairs={{0,16},{8,24},{16,0},{24,8},{1,17},{9,25},{17,1},{25,9},{2,18},{10... | collective-permute-start | bytes 2150408 | tf_op jit(solution)/shard_map/ppermute | solution.py:588
  145.6 21.2 %collective-permute-start.16 = (bf16[2,112,800]{2,1,0:T(8,128)(2,1)}, bf16[2,112,800]{2,1,0:T(8,128)(2,1)}, u32[]{:S(2)}, u32[]{:S(2)}) collective-permute-start(bf16[2,112,800]{2,1,0:T(8,128)(2,1)} %get-tuple-element.190), channel_id=1, source_target_pairs={{0,16},{8,24},{16,0},{24,8},{1,17},{9,25},{17,1},{25,9},{2,18},{10... | collective-permute-start | bytes 1075208 | tf_op jit(solution)/shard_map/ppermute | solution.py:588
  146.2 20.6 %collective-permute-start.17 = (bf16[2,112,800]{2,1,0:T(8,128)(2,1)}, bf16[2,112,800]{2,1,0:T(8,128)(2,1)}, u32[]{:S(2)}, u32[]{:S(2)}) collective-permute-start(bf16[2,112,800]{2,1,0:T(8,128)(2,1)} %get-tuple-element.191), channel_id=1, source_target_pairs={{0,8},{8,0},{16,24},{24,16},{1,9},{9,1},{17,25},{25,17},{2,10},{10... | collective-permute-start | bytes 1075208 | tf_op jit(solution)/shard_map/ppermute | solution.py:588
  148.7 18.1 %collective-permute-start.15 = (bf16[112,800]{1,0:T(8,128)(2,1)S(1)}, bf16[112,800]{1,0:T(8,128)(2,1)}, u32[]{:S(2)}, u32[]{:S(2)}) collective-permute-start(bf16[112,800]{1,0:T(8,128)(2,1)S(1)} %get-tuple-element.413), channel_id=1, source_target_pairs={{0,5},{1,0},{2,4},{3,1},{4,7},{5,2},{6,6},{7,3},{8,13},{9,8},{10,1... | collective-permute-start | bytes 537608 | tf_op jit(solution)/shard_map/ppermute | solution.py:861
  170.3 22.3 %collective-permute-start.21 = (bf16[4,400,800]{2,1,0:T(8,128)(2,1)}, bf16[4,400,800]{2,1,0:T(8,128)(2,1)}, u32[]{:S(2)}, u32[]{:S(2)}) collective-permute-start(bf16[4,400,800]{2,1,0:T(8,128)(2,1)} %shard_map.494), channel_id=1, source_target_pairs={{0,4},{4,0},{1,5},{5,1},{2,6},{6,2},{3,7},{7,3},{8,12},{12,8},{9,1... | collective-permute-start | bytes 7680008 | tf_op jit(solution)/shard_map/ppermute | solution.py:573
  174.2 18.3 %collective-permute-start.19 = (bf16[448,256]{1,0:T(8,128)(2,1)S(1)}, bf16[448,256]{1,0:T(8,128)(2,1)}, u32[]{:S(2)}, u32[]{:S(2)}) collective-permute-start(bf16[448,256]{1,0:T(8,128)(2,1)S(1)} %get-tuple-element.386), channel_id=1, source_target_pairs={{0,2},{1,3},{2,0},{3,1},{4,6},{5,7},{6,4},{7,5},{8,10},{9,11},{10,... | collective-permute-start | bytes 688136 | tf_op jit(solution)/shard_map/ppermute | solution.py:573
  214.9 166.2 %reduce-scatter.7.cloned.1.call-start = ((), (), s32[]{:S(2)}) async-start(), calls=%async_computation.7 | async-start | bytes 4096000 | tf_op jit(solution)/shard_map/reduce_scatter | solution.py:976
  215.5 21.0 %collective-permute-start.24 = (bf16[4,112,800]{2,1,0:T(8,128)(2,1)}, bf16[4,112,800]{2,1,0:T(8,128)(2,1)S(1)}, u32[]{:S(2)}, u32[]{:S(2)}) collective-permute-start(bf16[4,112,800]{2,1,0:T(8,128)(2,1)} %get-tuple-element.208.refs_0_), channel_id=1, source_target_pairs={{0,8},{8,0},{16,24},{24,16},{1,9},{9,1},{17,25},{25,17},{2,10},{10... | collective-permute-start | bytes 2150408 | tf_op jit(solution)/shard_map/ppermute | solution.py:588
  217.0 37.0 %collective-permute-start.25 = (bf16[4,112,800]{2,1,0:T(8,128)(2,1)}, bf16[4,112,800]{2,1,0:T(8,128)(2,1)S(1)}, u32[]{:S(2)}, u32[]{:S(2)}) collective-permute-start(bf16[4,112,800]{2,1,0:T(8,128)(2,1)} %get-tuple-element.208.refs_0_), channel_id=1, source_target_pairs={{0,16},{8,24},{16,0},{24,8},{1,17},{9,25},{17,1},{25,9},{2,18},{10... | collective-permute-start | bytes 2150408 | tf_op jit(solution)/shard_map/ppermute | solution.py:588
  218.4 35.6 %collective-permute-start.26 = (bf16[4,112,800]{2,1,0:T(8,128)(2,1)}, bf16[4,112,800]{2,1,0:T(8,128)(2,1)S(1)}, u32[]{:S(2)}, u32[]{:S(2)}) collective-permute-start(bf16[4,112,800]{2,1,0:T(8,128)(2,1)} %get-tuple-element.208.refs_0_), channel_id=1, source_target_pairs={{0,24},{8,16},{16,8},{24,0},{1,25},{9,17},{17,9},{25,1},{2,26},{10... | collective-permute-start | bytes 2150408 | tf_op jit(solution)/shard_map/ppermute | solution.py:588
  313.6 19.1 %collective-permute-start.28 = (bf16[800,1600]{1,0:T(8,128)(2,1)}, bf16[800,1600]{1,0:T(8,128)(2,1)S(1)}, u32[]{:S(2)}, u32[]{:S(2)}) collective-permute-start(bf16[800,1600]{1,0:T(8,128)(2,1)} %get-tuple-element.221), channel_id=1, source_target_pairs={{0,4},{4,0},{1,5},{5,1},{2,6},{6,2},{3,7},{7,3},{8,12},{12,8},{9,1... | collective-permute-start | bytes 7680008 | tf_op jit(solution)/shard_map/ppermute | solution.py:573
  313.6 193.3 %reduce-scatter.9.cloned.1.call-start = ((), (), s32[]{:S(2)}) async-start(), calls=%async_computation.8 | async-start | bytes 4096000 | tf_op jit(solution)/shard_map/reduce_scatter | solution.py:1035
  342.0 20.6 %collective-permute-start.30 = (bf16[2,104,1600]{2,1,0:T(8,128)(2,1)}, bf16[2,104,1600]{2,1,0:T(8,128)(2,1)}, u32[]{:S(2)}, u32[]{:S(2)}) collective-permute-start(bf16[2,104,1600]{2,1,0:T(8,128)(2,1)} %get-tuple-element.233), channel_id=1, source_target_pairs={{0,8},{8,0},{16,24},{24,16},{1,9},{9,1},{17,25},{25,17},{2,10},{10... | collective-permute-start | bytes 1996808 | tf_op jit(solution)/shard_map/ppermute | solution.py:588
  361.1 18.9 %collective-permute-start.31 = (bf16[4,104,800]{2,1,0:T(8,128)(2,1)}, bf16[4,104,800]{2,1,0:T(8,128)(2,1)S(1)}, u32[]{:S(2)}, u32[]{:S(2)}) collective-permute-start(bf16[4,104,800]{2,1,0:T(8,128)(2,1)} %get-tuple-element.234), channel_id=1, source_target_pairs={{0,16},{8,24},{16,0},{24,8},{1,17},{9,25},{17,1},{25,9},{2,18},{10... | collective-permute-start | bytes 1996808 | tf_op jit(solution)/shard_map/ppermute | solution.py:588
  399.7 20.0 %collective-permute-start.37 = (bf16[2,104,1600]{2,1,0:T(8,128)(2,1)}, bf16[2,104,1600]{2,1,0:T(8,128)(2,1)}, u32[]{:S(2)}, u32[]{:S(2)}) collective-permute-start(bf16[2,104,1600]{2,1,0:T(8,128)(2,1)} %get-tuple-element.252), channel_id=1, source_target_pairs={{0,16},{8,24},{16,0},{24,8},{1,17},{9,25},{17,1},{25,9},{2,18},{10... | collective-permute-start | bytes 1996808 | tf_op jit(solution)/shard_map/ppermute | solution.py:588
  401.2 18.5 %collective-permute-start.38 = (bf16[4,104,800]{2,1,0:T(8,128)(2,1)}, bf16[4,104,800]{2,1,0:T(8,128)(2,1)}, u32[]{:S(2)}, u32[]{:S(2)}) collective-permute-start(bf16[4,104,800]{2,1,0:T(8,128)(2,1)} %get-tuple-element.253), channel_id=1, source_target_pairs={{0,8},{8,0},{16,24},{24,16},{1,9},{9,1},{17,25},{25,17},{2,10},{10... | collective-permute-start | bytes 1996808 | tf_op jit(solution)/shard_map/ppermute | solution.py:588
  425.3 126.8 %reduce-scatter.13.cloned.1.call-start = ((), (), s32[]{:S(2)}) async-start(), calls=%async_computation.10 | async-start | bytes 931840
  435.7 39.9 %collective-permute-start.43 = (bf16[2,4,104,800]{3,2,1,0:T(8,128)(2,1)}, bf16[2,4,104,800]{3,2,1,0:T(8,128)(2,1)}, u32[]{:S(2)}, u32[]{:S(2)}) collective-permute-start(bf16[2,4,104,800]{3,2,1,0:T(8,128)(2,1)} %get-tuple-element.270), channel_id=1, source_target_pairs={{0,8},{8,0},{16,24},{24,16},{1,9},{9,1},{17,25},{25,17},{2,10},{10... | collective-permute-start | bytes 3993608 | tf_op jit(solution)/shard_map/ppermute | solution.py:588
  435.9 39.7 %collective-permute-start.44 = (bf16[2,104,1600]{2,1,0:T(8,128)(2,1)}, bf16[2,104,1600]{2,1,0:T(8,128)(2,1)}, u32[]{:S(2)}, u32[]{:S(2)}) collective-permute-start(bf16[2,104,1600]{2,1,0:T(8,128)(2,1)} %get-tuple-element.271.refs_6_), channel_id=1, source_target_pairs={{0,16},{8,24},{16,0},{24,8},{1,17},{9,25},{17,1},{25,9},{2,18},{10... | collective-permute-start | bytes 1996808 | tf_op jit(solution)/shard_map/ppermute | solution.py:588
  437.5 38.1 %collective-permute-start.41 = (bf16[104,800]{1,0:T(8,128)(2,1)S(1)}, bf16[104,800]{1,0:T(8,128)(2,1)S(1)}, u32[]{:S(2)}, u32[]{:S(2)}) collective-permute-start(bf16[104,800]{1,0:T(8,128)(2,1)S(1)} %get-tuple-element.410), channel_id=1, source_target_pairs={{0,0},{4,1},{1,2},{5,3},{2,4},{6,5},{3,6},{7,7},{8,8},{12,9},{9,10... | collective-permute-start | bytes 499208 | tf_op jit(solution)/shard_map/ppermute | solution.py:861
  438.2 37.4 %collective-permute-start.42 = (bf16[104,800]{1,0:T(8,128)(2,1)S(1)}, bf16[104,800]{1,0:T(8,128)(2,1)S(1)}, u32[]{:S(2)}, u32[]{:S(2)}) collective-permute-start(bf16[104,800]{1,0:T(8,128)(2,1)S(1)} %get-tuple-element.409), channel_id=1, source_target_pairs={{5,0},{0,1},{4,2},{1,3},{7,4},{2,5},{6,6},{3,7},{13,8},{8,9},{12,1... | collective-permute-start | bytes 499208 | tf_op jit(solution)/shard_map/ppermute | solution.py:861
  477.6 23.7 %collective-permute-start.46 = (bf16[104,800]{1,0:T(8,128)(2,1)S(1)}, bf16[104,800]{1,0:T(8,128)(2,1)S(1)}, u32[]{:S(2)}, u32[]{:S(2)}) collective-permute-start(bf16[104,800]{1,0:T(8,128)(2,1)S(1)} %get-tuple-element.408), channel_id=1, source_target_pairs={{1,0},{5,1},{0,2},{4,3},{3,4},{7,5},{2,6},{6,7},{9,8},{13,9},{8,10... | collective-permute-start | bytes 499208 | tf_op jit(solution)/shard_map/ppermute | solution.py:861
  477.7 23.6 %collective-permute-start.47 = (bf16[104,800]{1,0:T(8,128)(2,1)S(1)}, bf16[104,800]{1,0:T(8,128)(2,1)S(1)}, u32[]{:S(2)}, u32[]{:S(2)}) collective-permute-start(bf16[104,800]{1,0:T(8,128)(2,1)S(1)} %get-tuple-element.407), channel_id=1, source_target_pairs={{4,0},{1,1},{5,2},{0,3},{6,4},{3,5},{7,6},{2,7},{12,8},{9,9},{13,1... | collective-permute-start | bytes 499208 | tf_op jit(solution)/shard_map/ppermute | solution.py:861
  483.4 23.5 %collective-permute-start.48 = (bf16[2,104,1600]{2,1,0:T(8,128)(2,1)}, bf16[2,104,1600]{2,1,0:T(8,128)(2,1)}, u32[]{:S(2)}, u32[]{:S(2)}) collective-permute-start(bf16[2,104,1600]{2,1,0:T(8,128)(2,1)} %get-tuple-element.283), channel_id=1, source_target_pairs={{0,8},{8,0},{16,24},{24,16},{1,9},{9,1},{17,25},{25,17},{2,10},{10... | collective-permute-start | bytes 1996808 | tf_op jit(solution)/shard_map/ppermute | solution.py:588
  506.9 19.3 %collective-permute-start.51 = (bf16[4,104,800]{2,1,0:T(8,128)(2,1)}, bf16[4,104,800]{2,1,0:T(8,128)(2,1)S(1)}, u32[]{:S(2)}, u32[]{:S(2)}) collective-permute-start(bf16[4,104,800]{2,1,0:T(8,128)(2,1)} %get-tuple-element.286.refs_0_), channel_id=1, source_target_pairs={{0,8},{8,0},{16,24},{24,16},{1,9},{9,1},{17,25},{25,17},{2,10},{10... | collective-permute-start | bytes 1996808 | tf_op jit(solution)/shard_map/ppermute | solution.py:588
  507.6 19.0 %collective-permute-start.52 = (bf16[4,104,800]{2,1,0:T(8,128)(2,1)}, bf16[4,104,800]{2,1,0:T(8,128)(2,1)}, u32[]{:S(2)}, u32[]{:S(2)}) collective-permute-start(bf16[4,104,800]{2,1,0:T(8,128)(2,1)} %get-tuple-element.286.refs_0_), channel_id=1, source_target_pairs={{0,16},{8,24},{16,0},{24,8},{1,17},{9,25},{17,1},{25,9},{2,18},{10... | collective-permute-start | bytes 1996808 | tf_op jit(solution)/shard_map/ppermute | solution.py:588
  527.1 93.4 %reduce-scatter.11.cloned.1.call-start = ((), (), s32[]{:S(2)}) async-start(), calls=%async_computation.9 | async-start | bytes 4259840 | tf_op jit(solution)/shard_map/reduce_scatter | solution.py:1096
  527.1 22.1 %collective-permute-start.56 = (bf16[3,48,800]{2,1,0:T(8,128)(2,1)}, bf16[3,48,800]{2,1,0:T(8,128)(2,1)S(1)}, u32[]{:S(2)}, u32[]{:S(2)}) collective-permute-start(bf16[3,48,800]{2,1,0:T(8,128)(2,1)} %get-tuple-element.299), channel_id=1, source_target_pairs={{1,0},{2,1},{3,2},{5,4},{6,5},{7,6},{9,8},{10,9},{11,10},{13,12},{... | collective-permute-start | bytes 691208 | tf_op jit(solution)/shard_map/ppermute | solution.py:716
  528.4 20.8 %collective-permute-start.55 = (bf16[3,48,800]{2,1,0:T(8,128)(2,1)}, bf16[3,48,800]{2,1,0:T(8,128)(2,1)S(1)}, u32[]{:S(2)}, u32[]{:S(2)}) collective-permute-start(bf16[3,48,800]{2,1,0:T(8,128)(2,1)} %get-tuple-element.298), channel_id=1, source_target_pairs={{0,1},{1,2},{2,3},{4,5},{5,6},{6,7},{8,9},{9,10},{10,11},{12,13},{... | collective-permute-start | bytes 691208 | tf_op jit(solution)/shard_map/ppermute | solution.py:712
  533.4 18.7 %collective-permute-start.54 = (bf16[2,104,1600]{2,1,0:T(8,128)(2,1)}, bf16[2,104,1600]{2,1,0:T(8,128)(2,1)S(1)}, u32[]{:S(2)}, u32[]{:S(2)}) collective-permute-start(bf16[2,104,1600]{2,1,0:T(8,128)(2,1)} %get-tuple-element.295), channel_id=1, source_target_pairs={{0,16},{8,24},{16,0},{24,8},{1,17},{9,25},{17,1},{25,9},{2,18},{10... | collective-permute-start | bytes 1996808 | tf_op jit(solution)/shard_map/ppermute | solution.py:588
  533.9 18.2 %collective-permute-start.53 = (bf16[4,104,800]{2,1,0:T(8,128)(2,1)}, bf16[4,104,800]{2,1,0:T(8,128)(2,1)S(1)}, u32[]{:S(2)}, u32[]{:S(2)}) collective-permute-start(bf16[4,104,800]{2,1,0:T(8,128)(2,1)} %get-tuple-element.294), channel_id=1, source_target_pairs={{0,8},{8,0},{16,24},{24,16},{1,9},{9,1},{17,25},{25,17},{2,10},{10... | collective-permute-start | bytes 1996808 | tf_op jit(solution)/shard_map/ppermute | solution.py:588
  554.7 29.9 %collective-permute-start.59 = (bf16[3,104,800]{2,1,0:T(8,128)(2,1)}, bf16[3,104,800]{2,1,0:T(8,128)(2,1)}, u32[]{:S(2)}, u32[]{:S(2)}) collective-permute-start(bf16[3,104,800]{2,1,0:T(8,128)(2,1)} %get-tuple-element.306.refs_7_), channel_id=1, source_target_pairs={{0,24},{8,16},{16,8},{24,0},{1,25},{9,17},{17,9},{25,1},{2,26},{10... | collective-permute-start | bytes 1497608 | tf_op jit(solution)/shard_map/ppermute | solution.py:588
  556.7 27.9 %collective-permute-start.58 = (bf16[3,104,800]{2,1,0:T(8,128)(2,1)}, bf16[3,104,800]{2,1,0:T(8,128)(2,1)}, u32[]{:S(2)}, u32[]{:S(2)}) collective-permute-start(bf16[3,104,800]{2,1,0:T(8,128)(2,1)} %get-tuple-element.305.refs_6_), channel_id=1, source_target_pairs={{0,16},{8,24},{16,0},{24,8},{1,17},{9,25},{17,1},{25,9},{2,18},{10... | collective-permute-start | bytes 1497608 | tf_op jit(solution)/shard_map/ppermute | solution.py:588
  557.2 27.4 %collective-permute-start.57 = (bf16[3,104,800]{2,1,0:T(8,128)(2,1)}, bf16[3,104,800]{2,1,0:T(8,128)(2,1)}, u32[]{:S(2)}, u32[]{:S(2)}) collective-permute-start(bf16[3,104,800]{2,1,0:T(8,128)(2,1)} %get-tuple-element.304.refs_5_), channel_id=1, source_target_pairs={{0,8},{8,0},{16,24},{24,16},{1,9},{9,1},{17,25},{25,17},{2,10},{10... | collective-permute-start | bytes 1497608 | tf_op jit(solution)/shard_map/ppermute | solution.py:588
  561.8 25.6 %collective-permute-start.63 = (bf16[1,104,800]{2,1,0:T(8,128)(2,1)}, bf16[1,104,800]{2,1,0:T(8,128)(2,1)S(1)}, u32[]{:S(2)}, u32[]{:S(2)}) collective-permute-start(bf16[1,104,800]{2,1,0:T(8,128)(2,1)} %get-tuple-element.314), channel_id=1, source_target_pairs={{0,8},{8,0},{16,24},{24,16},{1,9},{9,1},{17,25},{25,17},{2,10},{10... | collective-permute-start | bytes 499208 | tf_op jit(solution)/shard_map/ppermute | solution.py:588
  589.7 34.1 %collective-permute-start.66 = (bf16[324,800]{1,0:T(8,128)(2,1)}, bf16[324,800]{1,0:T(8,128)(2,1)S(1)}, u32[]{:S(2)}, u32[]{:S(2)}) collective-permute-start(bf16[324,800]{1,0:T(8,128)(2,1)} %get-tuple-element.318.refs_0_), channel_id=1, source_target_pairs={{0,8},{8,0},{16,24},{24,16},{1,9},{9,1},{17,25},{25,17},{2,10},{10... | collective-permute-start | bytes 1555208 | tf_op jit(solution)/shard_map/ppermute | solution.py:588
  590.8 33.0 %collective-permute-start.67 = (bf16[324,800]{1,0:T(8,128)(2,1)}, bf16[324,800]{1,0:T(8,128)(2,1)S(1)}, u32[]{:S(2)}, u32[]{:S(2)}) collective-permute-start(bf16[324,800]{1,0:T(8,128)(2,1)} %get-tuple-element.318.refs_0_), channel_id=1, source_target_pairs={{0,16},{8,24},{16,0},{24,8},{1,17},{9,25},{17,1},{25,9},{2,18},{10... | collective-permute-start | bytes 1555208 | tf_op jit(solution)/shard_map/ppermute | solution.py:588
  592.2 31.6 %collective-permute-start.68 = (bf16[324,800]{1,0:T(8,128)(2,1)}, bf16[324,800]{1,0:T(8,128)(2,1)S(1)}, u32[]{:S(2)}, u32[]{:S(2)}) collective-permute-start(bf16[324,800]{1,0:T(8,128)(2,1)} %get-tuple-element.318.refs_0_), channel_id=1, source_target_pairs={{0,24},{8,16},{16,8},{24,0},{1,25},{9,17},{17,9},{25,1},{2,26},{10... | collective-permute-start | bytes 1555208 | tf_op jit(solution)/shard_map/ppermute | solution.py:588
  593.1 30.6 %collective-permute-start.65 = (bf16[1,104,800]{2,1,0:T(8,128)(2,1)}, bf16[1,104,800]{2,1,0:T(8,128)(2,1)S(1)}, u32[]{:S(2)}, u32[]{:S(2)}) collective-permute-start(bf16[1,104,800]{2,1,0:T(8,128)(2,1)} %get-tuple-element.319.refs_0_), channel_id=1, source_target_pairs={{0,16},{8,24},{16,0},{24,8},{1,17},{9,25},{17,1},{25,9},{2,18},{10... | collective-permute-start | bytes 499208 | tf_op jit(solution)/shard_map/ppermute | solution.py:588
  (105 other events, 956.7 us)
Sparse Core Ops, SparseCore 0:
  17.7 69.2 all-gather.3
  93.4 70.2 all-gather.5
  215.0 63.9 all-gather.7
  313.7 60.6 reduce-scatter.6
  425.4 74.8 reduce-scatter.8
  527.2 24.3 reduce-scatter.12
  554.5 65.8 reduce-scatter.10

commit v6 on v5

--- a/solution.py
+++ b/solution.py
@@ -668,7 +668,7 @@
     )(me, *parts)
 
 
-def join_wide(parts, shares, me):
+def join_wide(parts, shares, me, count):
     wide = parts[0].shape[1]
     size = shares.size
 
@@ -681,13 +681,13 @@
                 def move():
                     first, rows = shares.starts[s], shares.lengths[s]
                     held = refs[m][...].astype(F32)
-                    for k in range(3):
+                    for k in range(count):
                         cut = held[k * size : k * size + rows]
                         o_ref[k, first : first + rows, :] = cut
 
     return pl.pallas_call(
         kernel,
-        out_shape=jax.ShapeDtypeStruct((3, shares.rows, wide), F32),
+        out_shape=jax.ShapeDtypeStruct((count, shares.rows, wide), F32),
         in_specs=[SM] + [V] * 4,
         out_specs=V,
         compiler_params=ROOM,
@@ -1133,11 +1133,11 @@
     input_grad = input_grad.astype(BF16)
     *out_all, a, b, c = gate(out_all + qkv_all, [up_grad, input_grad])
 
-    out_grad = fine.join([out_home] + out_all, dp, 1).astype(F32)[0]
+    out_grad = join_wide([v[0] for v in [out_home] + out_all], fine, dp_at, 1)[0]
     small = sum(v[ends:].astype(F32) for v in (payload, a, b, c))
     small = (small[:deep] + small[deep:]).reshape(-1)
     sums, local = small[: 7 * width].reshape(7, width), small[7 * width : 8 * width + ff]
-    qkv_grad = join_wide([payload, a, b, c], fine, dp[None].astype(jnp.int32))
+    qkv_grad = join_wide([payload, a, b, c], fine, dp_at, 3)
     return (
         outputs.T.reshape(tokens.shape),
         input_grad.T.reshape(tokens.shape),

time: 650 us -> 651 us (level)
  starting transfers between devices: 101 us -> 113 us
  Pallas kernels: 200 us -> 193 us
    ppermute x8, starting transfers between devices: 34 us -> 41.8 us  [between_owners(): got.append(lax.ppermute(value_of(step), ('row', 'col'), pairs))]
    unnamed x157 -> x151, local copies, waits for them, and re-layouts: 27.1 us -> 26 us
  transfers between devices with their start and end apart: 76 -> 76, of which waited for: 22 -> 24; matrix products, arithmetic and copies ran while one was open for 22% -> 22% of each run, Pallas kernels for 25% -> 23%
where the time goes in v6:
time: 651 us; the launch traced here: 643 us
  Pallas kernels  193 us (30%)
  waiting for transfers between devices  146 us (22%)
  starting transfers between devices  113 us (17%)
  other arithmetic  94.4 us (15%)
  local copies, waits for them, and re-layouts  74.3 us (11%)
  between operations  23.1 us (4%)
    ppermute x30, waiting for transfers between devices, swap_with(): return lax.ppermute(value, 'dp', [(i, i ^ bit) for i in range(4)])  51.5 us
    pallas_call x8, Pallas kernels, token_product(): pl.pallas_call(kernel, out_shape=jax.ShapeDtypeStruct((rows_a, rows_b), B...  49.9 us
    ppermute x8, starting transfers between devices, between_owners(): got.append(lax.ppermute(value_of(step), ('row', 'col'), pairs))  41.8 us
    ppermute x30, starting transfers between devices, swap_with(): return lax.ppermute(value, 'dp', [(i, i ^ bit) for i in range(4)])  34 us
    pallas_call x1, Pallas kernels, hidden_layer(): pl.pallas_call(kernel, out_shape=[jax.ShapeDtypeStruct((ff, tokens), BF16...  27.8 us
    ppermute x24, waiting for transfers between devices, turn(): lax.ppermute(value, axis, [(i, (i + steps) % size) for i in range(size)])  26.5 us
    unnamed x151, local copies, waits for them, and re-layouts  26 us
    pallas_call x1, Pallas kernels, attn_bwd(): pl.pallas_call(functools.partial(bwd_kernel, n_row, n_slots, hd, ks.shape...  24.5 us
  transfers between devices with their start and end apart: 76, of which 24 were waited for; matrix products, arithmetic and copies ran while one was open for 22% of the time, Pallas kernels for 23%

profile of v6, /device:TPU:0, one launch (start us, length us, event | category | flops | bytes accessed | tf_op | source)
XLA Modules:
  0.0 643.2 jit_solution(4034980369835251722)
XLA Ops:
  11.3 4.9 collective-permute-start
  17.7 4.3 collective-permute-done
  22.0 3.8 collective-permute-done.1
  25.8 4.4 fusion.8
  41.0 4.3 copy.214
  51.1 3.5 pad_maximum_fusion
  54.6 5.2 copy.215
  62.2 4.1 maximum_bitcast_fusion.refs_8_.up_ref
  66.3 20.7 %all-gather.4.cloned.1.call-done.refs_0_ = bf16[1600,1024]{1,0:T(8,128)(2,1)} async-done(((bf16[400,1024]{1,0:T(8,128)(2,1)}), bf16[1600,1024]{1,0:T(8,128)(2,1)}) %all-gather.4.cloned.1.call-update) | async-done | bytes 3276816 | tf_op jit(solution)/shard_map/all_gather | solution.py:864
  96.2 9.4 %shard_map.488 = bf16[1344,1024]{1,0:T(8,128)(2,1)} custom-call(bf16[1344,1600]{1,0:T(8,128)(2,1)} %get-tuple-element.173.a_ref, bf16[1600,1024]{1,0:T(8,128)(2,1)} %fusion.5.b_ref.n_ref, f32[1344,1]{1,0:T(8,128)} %get-tuple-element.175.bias_ref), custom_call_target="tpu_custom_call" | custom-call | tf_op jit(solution)/shard_map/pallas_call | solution.py:189
  105.6 3.4 collective-permute-done.8.refs_2_
  117.6 16.6 %shard_map.491 = (bf16[448,1024]{1,0:T(8,128)(2,1)S(1)}, bf16[448,1024]{1,0:T(8,128)(2,1)S(1)}, bf16[448,2048]{1,0:T(8,128)(2,1)S(1)}, f32[7,2048]{1,0:T(8,128)S(1)}) custom-call(s32[4]{0:T(128)S(1)} %copy-done.7, s32[25,4]{1,0:T(8,128)S(1)} %copy.220.ks, bf16[3,448,1024]{2,1,0:T(8,128)(2,1)} %get-tuple-element.177.refs_0_, ...), custom_call_target="tpu_custom_call" | custom-call | tf_op jit(solution)/shard_map/pallas_call | solution.py:148
  144.5 18.5 %collective-permute-start.15 = (bf16[112,800]{1,0:T(8,128)(2,1)S(1)}, bf16[112,800]{1,0:T(8,128)(2,1)}, u32[]{:S(2)}, u32[]{:S(2)}) collective-permute-start(bf16[112,800]{1,0:T(8,128)(2,1)S(1)} %get-tuple-element.404), channel_id=1, source_target_pairs={{0,5},{1,0},{2,4},{3,1},{4,7},{5,2},{6,6},{7,3},{8,13},{9,8},{10,1... | collective-permute-start | bytes 537608 | tf_op jit(solution)/shard_map/ppermute | solution.py:861
  168.3 3.5 shard_map.494
  181.6 3.3 collective-permute-done.18.refs_2_
  184.9 9.1 %collective-permute-done.19.refs_3_ = bf16[448,256]{1,0:T(8,128)(2,1)} collective-permute-done((bf16[448,256]{1,0:T(8,128)(2,1)S(1)}, bf16[448,256]{1,0:T(8,128)(2,1)}, u32[]{:S(2)}, u32[]{:S(2)}) %collective-permute-start.19) | collective-permute-done | bytes 229408 | tf_op jit(solution)/shard_map/ppermute | solution.py:573
  197.6 4.2 collective-permute-start.22
  202.8 8.2 %shard_map.496 = (f32[1600,256]{1,0:T(8,128)}, f32[1600,256]{1,0:T(8,128)}, bf16[1600,256]{1,0:T(8,128)(2,1)}, f32[1,256]{1,0:T(1,128)}) custom-call(s32[1]{0:T(128)} %bitcast.9.row_ref, bf16[1600,256]{1,0:T(8,128)(2,1)} %pad_add_fusion.b_ref, f32[1600,6]{1,0:T(8,128)} %get-tuple-element.200.c_ref.bias_ref.g_ref, ...), custom_call_target="tpu_custom_call" | custom-call | tf_op jit(solution)/shard_map/pallas_call | solution.py:262
  220.6 17.5 %collective-permute-done.24.refs_1_ = bf16[4,112,800]{2,1,0:T(8,128)(2,1)S(1)} collective-permute-done((bf16[4,112,800]{2,1,0:T(8,128)(2,1)}, bf16[4,112,800]{2,1,0:T(8,128)(2,1)S(1)}, u32[]{:S(2)}, u32[]{:S(2)}) %collective-permute-start.24) | collective-permute-done | bytes 716832 | tf_op jit(solution)/shard_map/ppermute | solution.py:588
  238.0 17.5 %collective-permute-done.25.refs_2_ = bf16[4,112,800]{2,1,0:T(8,128)(2,1)S(1)} collective-permute-done((bf16[4,112,800]{2,1,0:T(8,128)(2,1)}, bf16[4,112,800]{2,1,0:T(8,128)(2,1)S(1)}, u32[]{:S(2)}, u32[]{:S(2)}) %collective-permute-start.25) | collective-permute-done | bytes 716832 | tf_op jit(solution)/shard_map/ppermute | solution.py:588
  257.3 3.5 shard_map.498
  262.9 3.6 collective-permute-done.27
  266.5 6.9 %shard_map.499.refs_1_ = bf16[1600,1600]{1,0:T(8,128)(2,1)} custom-call(bf16[1600,800]{1,0:T(8,128)(2,1)} %bitcast.182, bf16[1600,800]{1,0:T(8,128)(2,1)} %bitcast.54.refs_1_), custom_call_target="tpu_custom_call" | custom-call | tf_op jit(solution)/shard_map/pallas_call | solution.py:544
  273.4 7.1 %all-gather.8.cloned.1.call-done.refs_0_ = bf16[1600,1024]{1,0:T(8,128)(2,1)} async-done(((bf16[1600,256]{1,0:T(8,128)(2,1)}), bf16[1600,1024]{1,0:T(8,128)(2,1)}) %all-gather.8.cloned.1.call-update) | async-done | bytes 3276816 | tf_op jit(solution)/shard_map/all_gather | solution.py:950
  280.5 27.8 %shard_map.501 = (bf16[1600,1024]{1,0:T(8,128)(2,1)}, bf16[1600,1024]{1,0:T(8,128)(2,1)}, bf16[1600,1024]{1,0:T(8,128)(2,1)}, f32[1600,1]{1,0:T(8,128)}) custom-call(s32[1]{0:T(128)} %bitcast.9.row_ref, bf16[1600,1600]{1,0:T(8,128)(2,1)} %maximum_bitcast_fusion.refs_8_.up_ref, bf16[1600,1600]{1,0:T(8,128)(2,1)} %get-tuple-element.210.down_ref, ...), custom_call_target="tpu_custom_call" | custom-call | tf_op jit(solution)/shard_map/pallas_call | solution.py:498
  308.3 6.7 %shard_map.503.refs_2_ = bf16[800,1600]{1,0:T(8,128)(2,1)} custom-call(s32[1]{0:T(128)} %bitcast.55.index_ref, bf16[1600,1024]{1,0:T(8,128)(2,1)} %get-tuple-element.211.n_ref.a_ref.refs_0_, bf16[1600,1024]{1,0:T(8,128)(2,1)} %get-tuple-element.218.b_ref), custom_call_target="tpu_custom_call" | custom-call | tf_op jit(solution)/shard_map/pallas_call | solution.py:442
  320.2 7.2 %shard_map.506 = bf16[1600,800]{1,0:T(8,128)(2,1)} custom-call(s32[1]{0:T(128)} %bitcast.55.index_ref, bf16[1600,1024]{1,0:T(8,128)(2,1)} %get-tuple-element.212.g_ref.a_ref, bf16[1600,1024]{1,0:T(8,128)(2,1)} %get-tuple-element.219.b_ref.refs_0_), custom_call_target="tpu_custom_call" | custom-call | tf_op jit(solution)/shard_map/pallas_call | solution.py:442
  327.4 6.7 %shard_map.505.refs_1_ = bf16[800,1600]{1,0:T(8,128)(2,1)} custom-call(s32[1]{0:T(128)} %bitcast.56.index_ref, bf16[1600,1024]{1,0:T(8,128)(2,1)} %get-tuple-element.220.a_ref, bf16[1600,1024]{1,0:T(8,128)(2,1)} %get-tuple-element.218.b_ref), custom_call_target="tpu_custom_call" | custom-call | tf_op jit(solution)/shard_map/pallas_call | solution.py:442
  349.1 7.2 %shard_map.509 = bf16[1600,800]{1,0:T(8,128)(2,1)} custom-call(s32[1]{0:T(128)} %bitcast.56.index_ref, bf16[1600,1024]{1,0:T(8,128)(2,1)} %get-tuple-element.212.g_ref.a_ref, bf16[1600,1024]{1,0:T(8,128)(2,1)} %get-tuple-element.226.b_ref.refs_0_), custom_call_target="tpu_custom_call" | custom-call | tf_op jit(solution)/shard_map/pallas_call | solution.py:442
  357.9 3.4 add_convert_fusion.1
  366.4 11.2 %shard_map.512 = bf16[1600,1024]{1,0:T(8,128)(2,1)} custom-call(s32[1]{0:T(128)} %bitcast.9.row_ref, bf16[1600,1024]{1,0:T(8,128)(2,1)} %get-tuple-element.231.b_ref, f32[1600,6]{1,0:T(8,128)} %get-tuple-element.200.c_ref.bias_ref.g_ref, bf16[1600,800]{1,0:T(8,128)(2,1)} %bitcast.183, bf16[1600,800]{1,0:T(8,128)(2,1)} %bitcast.54.refs_1_), custom_call_target="tpu_custom_call" | custom-call | tf_op jit(solution)/shard_map/pallas_call | solution.py:217
  384.7 10.4 %shard_map.514 = (f32[1600,256]{1,0:T(8,128)}, bf16[1600,256]{1,0:T(8,128)(2,1)}, bf16[1600,256]{1,0:T(8,128)(2,1)}, f32[1600,3]{1,0:T(8,128)}) custom-call(s32[1]{0:T(128)} %bitcast.9.row_ref, bf16[1600,256]{1,0:T(8,128)(2,1)} %get-tuple-element.236.dn_ref, f32[1600,256]{1,0:T(8,128)} %get-tuple-element.237.hat_ref, f32[1,256]{1,0:T(1,128)} %get-tuple-element.238.scale_ref, ...), custom_call_target="tpu_custom_call" | custom-call | tf_op jit(solution)/shard_map/pallas_call | solution.py:326
  407.8 4.6 shard_map.516
  412.4 4.7 shard_map.517
  417.0 4.0 collective-permute-done.35.refs_1_
  439.6 8.0 %collective-permute-start.42 = (bf16[104,800]{1,0:T(8,128)(2,1)S(1)}, bf16[104,800]{1,0:T(8,128)(2,1)S(1)}, u32[]{:S(2)}, u32[]{:S(2)}) collective-permute-start(bf16[104,800]{1,0:T(8,128)(2,1)S(1)} %get-tuple-element.400), channel_id=1, source_target_pairs={{5,0},{0,1},{4,2},{1,3},{7,4},{2,5},{6,6},{3,7},{13,8},{8,9},{12,1... | collective-permute-start | bytes 499208 | tf_op jit(solution)/shard_map/ppermute | solution.py:861
  447.6 24.5 %shard_map.520 = (bf16[3,448,1024]{2,1,0:T(8,128)(2,1)}, bf16[3,448,1024]{2,1,0:T(8,128)(2,1)}) custom-call(s32[4]{0:T(128)} %get-tuple-element.172.meta, s32[25,4]{1,0:T(8,128)} %copy-done.5, bf16[3,448,1024]{2,1,0:T(8,128)(2,1)} %get-tuple-element.177.refs_0_, bf16[3,448,1024]{2,1,0:T(8,128)(2,1)} %get-tuple-element.181.refs_1_, ...), custom_call_target="tpu_custom_call" | custom-call | tf_op jit(solution)/shard_map/pallas_call | solution.py:157
  474.2 5.8 collective-permute-start.46
  489.2 4.7 add_convert_fusion.2
  493.9 6.4 shard_map.523
  509.6 6.4 shard_map.525
  519.3 7.3 %collective-permute-done.51.refs_6_ = bf16[4,104,800]{2,1,0:T(8,128)(2,1)S(1)} collective-permute-done((bf16[4,104,800]{2,1,0:T(8,128)(2,1)}, bf16[4,104,800]{2,1,0:T(8,128)(2,1)S(1)}, u32[]{:S(2)}, u32[]{:S(2)}) %collective-permute-start.51) | collective-permute-done | bytes 665632 | tf_op jit(solution)/shard_map/ppermute | solution.py:588
  528.9 5.0 collective-permute-start.55
  536.1 14.3 %shard_map.527 = (bf16[4,416,1024]{2,1,0:T(8,128)(2,1)}, f32[1600,2]{1,0:T(8,128)}) custom-call(s32[1]{0:T(128)} %bitcast.88.col_ref, bf16[1344,1600]{1,0:T(8,128)(2,1)} %get-tuple-element.173.a_ref, bf16[1344,1024]{1,0:T(8,128)(2,1)} %get-tuple-element.291.b_ref.refs_1_, bf16[1600,1024]{1,0:T(8,128)(2,1)} %fusion.5.b_ref.n_ref, ...), custom_call_target="tpu_custom_call" | custom-call | tf_op jit(solution)/shard_map/pallas_call | solution.py:401
  570.3 4.9 collective-permute-done.61
  578.8 6.5 %concatenate.50.refs_4_ = f32[400,3200]{1,0:T(8,128)} concatenate(f32[400,800]{1,0:T(8,128)} %get-tuple-element.346, f32[400,800]{1,0:T(8,128)} %get-tuple-element.345, f32[400,800]{1,0:T(8,128)S(1)} %get-tuple-element.344, f32[400,800]{1,0:T(8,128)S(1)} %get-tuple-element.343), dimensions={1} | concatenate | bytes 10240000 | tf_op jit(solution)/shard_map/concatenate | solution.py:1103
  602.3 20.3 %reduce-scatter.11.cloned.1.call-done = bf16[1,416,1024]{2,1,0:T(8,128)(2,1)} async-done(((bf16[4,416,1024]{2,1,0:T(8,128)(2,1)}), bf16[1,416,1024]{2,1,0:T(8,128)(2,1)}) %reduce-scatter.11.cloned.1.call-update) | async-done | bytes 851984 | tf_op jit(solution)/shard_map/reduce_scatter | solution.py:1096
  627.3 4.2 shard_map.532
  (436 shorter events, 220.5 us)
Async XLA Ops:
  7.2 79.8 %all-gather.4.cloned.1.call-start = ((), (), s32[]{:S(2)}) async-start(), calls=%async_computation.4 | async-start | bytes 4096000 | tf_op jit(solution)/shard_map/all_gather | solution.py:864
  17.7 150.6 %all-gather.6.cloned.1.call-start = ((), (), s32[]{:S(2)}) async-start(), calls=%async_computation.5 | async-start | bytes 4096000 | tf_op jit(solution)/shard_map/all_gather | solution.py:898
  30.2 24.4 %collective-permute-start.6 = (bf16[800,1600]{1,0:T(8,128)(2,1)}, bf16[800,1600]{1,0:T(8,128)(2,1)}, u32[]{:S(2)}, u32[]{:S(2)}) collective-permute-start(bf16[800,1600]{1,0:T(8,128)(2,1)} %param.47), channel_id=1, source_target_pairs={{0,4},{4,0},{1,5},{5,1},{2,6},{6,2},{3,7},{7,3},{8,12},{12,8},{9,1... | collective-permute-start | bytes 7680008 | tf_op jit(solution)/shard_map/ppermute | solution.py:573
  87.0 18.6 %collective-permute-start.7 = (bf16[112,800]{1,0:T(8,128)(2,1)}, bf16[112,800]{1,0:T(8,128)(2,1)}, u32[]{:S(2)}, u32[]{:S(2)}) collective-permute-start(bf16[112,800]{1,0:T(8,128)(2,1)} %get-tuple-element.176), channel_id=1, source_target_pairs={{0,3},{1,0},{2,1},{3,2},{4,7},{5,4},{6,5},{7,6},{8,11},{9,8},{10,9... | collective-permute-start | bytes 537608 | tf_op jit(solution)/shard_map/ppermute | solution.py:573
  87.8 21.3 %collective-permute-start.8 = (bf16[112,800]{1,0:T(8,128)(2,1)}, bf16[112,800]{1,0:T(8,128)(2,1)}, u32[]{:S(2)}, u32[]{:S(2)}) collective-permute-start(bf16[112,800]{1,0:T(8,128)(2,1)} %get-tuple-element.176), channel_id=1, source_target_pairs={{0,2},{1,3},{2,0},{3,1},{4,6},{5,7},{6,4},{7,5},{8,10},{9,11},{10,... | collective-permute-start | bytes 537608 | tf_op jit(solution)/shard_map/ppermute | solution.py:573
  87.8 21.3 %collective-permute-start.9 = (bf16[112,800]{1,0:T(8,128)(2,1)}, bf16[112,800]{1,0:T(8,128)(2,1)}, u32[]{:S(2)}, u32[]{:S(2)}) collective-permute-start(bf16[112,800]{1,0:T(8,128)(2,1)} %get-tuple-element.176), channel_id=1, source_target_pairs={{0,1},{1,2},{2,3},{3,0},{4,5},{5,6},{6,7},{7,4},{8,9},{9,10},{10,1... | collective-permute-start | bytes 537608 | tf_op jit(solution)/shard_map/ppermute | solution.py:573
  93.2 187.3 %all-gather.8.cloned.1.call-start = ((), (), s32[]{:S(2)}) async-start(), calls=%async_computation.6 | async-start | bytes 4096000 | tf_op jit(solution)/shard_map/all_gather | solution.py:950
  114.5 23.3 %collective-permute-start.11 = (bf16[4,112,800]{2,1,0:T(8,128)(2,1)}, bf16[4,112,800]{2,1,0:T(8,128)(2,1)}, u32[]{:S(2)}, u32[]{:S(2)}) collective-permute-start(bf16[4,112,800]{2,1,0:T(8,128)(2,1)} %get-tuple-element.184.refs_0_), channel_id=1, source_target_pairs={{0,8},{8,0},{16,24},{24,16},{1,9},{9,1},{17,25},{25,17},{2,10},{10... | collective-permute-start | bytes 2150408 | tf_op jit(solution)/shard_map/ppermute | solution.py:588
  116.0 23.7 %collective-permute-start.12 = (bf16[4,112,800]{2,1,0:T(8,128)(2,1)}, bf16[4,112,800]{2,1,0:T(8,128)(2,1)}, u32[]{:S(2)}, u32[]{:S(2)}) collective-permute-start(bf16[4,112,800]{2,1,0:T(8,128)(2,1)} %get-tuple-element.184.refs_0_), channel_id=1, source_target_pairs={{0,16},{8,24},{16,0},{24,8},{1,17},{9,25},{17,1},{25,9},{2,18},{10... | collective-permute-start | bytes 2150408 | tf_op jit(solution)/shard_map/ppermute | solution.py:588
  141.5 21.6 %collective-permute-start.13 = (bf16[448,1024]{1,0:T(8,128)(2,1)}, bf16[448,1024]{1,0:T(8,128)(2,1)}, u32[]{:S(2)}, u32[]{:S(2)}) collective-permute-start(bf16[448,1024]{1,0:T(8,128)(2,1)} %get-tuple-element.187), channel_id=1, source_target_pairs={{0,4},{4,0},{1,5},{5,1},{2,6},{6,2},{3,7},{7,3},{8,12},{12,8},{9,1... | collective-permute-start | bytes 2752520 | tf_op jit(solution)/shard_map/ppermute | solution.py:573
  141.5 26.8 %collective-permute-start.16 = (bf16[2,112,800]{2,1,0:T(8,128)(2,1)}, bf16[2,112,800]{2,1,0:T(8,128)(2,1)}, u32[]{:S(2)}, u32[]{:S(2)}) collective-permute-start(bf16[2,112,800]{2,1,0:T(8,128)(2,1)} %get-tuple-element.190), channel_id=1, source_target_pairs={{0,16},{8,24},{16,0},{24,8},{1,17},{9,25},{17,1},{25,9},{2,18},{10... | collective-permute-start | bytes 1075208 | tf_op jit(solution)/shard_map/ppermute | solution.py:588
  142.0 26.2 %collective-permute-start.17 = (bf16[2,112,800]{2,1,0:T(8,128)(2,1)}, bf16[2,112,800]{2,1,0:T(8,128)(2,1)}, u32[]{:S(2)}, u32[]{:S(2)}) collective-permute-start(bf16[2,112,800]{2,1,0:T(8,128)(2,1)} %get-tuple-element.191), channel_id=1, source_target_pairs={{0,8},{8,0},{16,24},{24,16},{1,9},{9,1},{17,25},{25,17},{2,10},{10... | collective-permute-start | bytes 1075208 | tf_op jit(solution)/shard_map/ppermute | solution.py:588
  143.8 22.0 %collective-permute-start.14 = (bf16[112,800]{1,0:T(8,128)(2,1)S(1)}, bf16[112,800]{1,0:T(8,128)(2,1)S(1)}, u32[]{:S(2)}, u32[]{:S(2)}) collective-permute-start(bf16[112,800]{1,0:T(8,128)(2,1)S(1)} %get-tuple-element.405), channel_id=1, source_target_pairs={{0,0},{1,4},{2,1},{3,5},{4,2},{5,6},{6,3},{7,7},{8,8},{9,12},{10,9... | collective-permute-start | bytes 537608 | tf_op jit(solution)/shard_map/ppermute | solution.py:861
  144.5 23.8 %collective-permute-start.15 = (bf16[112,800]{1,0:T(8,128)(2,1)S(1)}, bf16[112,800]{1,0:T(8,128)(2,1)}, u32[]{:S(2)}, u32[]{:S(2)}) collective-permute-start(bf16[112,800]{1,0:T(8,128)(2,1)S(1)} %get-tuple-element.404), channel_id=1, source_target_pairs={{0,5},{1,0},{2,4},{3,1},{4,7},{5,2},{6,6},{7,3},{8,13},{9,8},{10,1... | collective-permute-start | bytes 537608 | tf_op jit(solution)/shard_map/ppermute | solution.py:861
  171.8 22.3 %collective-permute-start.21 = (bf16[4,400,800]{2,1,0:T(8,128)(2,1)}, bf16[4,400,800]{2,1,0:T(8,128)(2,1)}, u32[]{:S(2)}, u32[]{:S(2)}) collective-permute-start(bf16[4,400,800]{2,1,0:T(8,128)(2,1)} %shard_map.494), channel_id=1, source_target_pairs={{0,4},{4,0},{1,5},{5,1},{2,6},{6,2},{3,7},{7,3},{8,12},{12,8},{9,1... | collective-permute-start | bytes 7680008 | tf_op jit(solution)/shard_map/ppermute | solution.py:573
  216.4 166.2 %reduce-scatter.7.cloned.1.call-start = ((), (), s32[]{:S(2)}) async-start(), calls=%async_computation.7 | async-start | bytes 4096000 | tf_op jit(solution)/shard_map/reduce_scatter | solution.py:976
  217.0 21.0 %collective-permute-start.24 = (bf16[4,112,800]{2,1,0:T(8,128)(2,1)}, bf16[4,112,800]{2,1,0:T(8,128)(2,1)S(1)}, u32[]{:S(2)}, u32[]{:S(2)}) collective-permute-start(bf16[4,112,800]{2,1,0:T(8,128)(2,1)} %get-tuple-element.208.refs_0_), channel_id=1, source_target_pairs={{0,8},{8,0},{16,24},{24,16},{1,9},{9,1},{17,25},{25,17},{2,10},{10... | collective-permute-start | bytes 2150408 | tf_op jit(solution)/shard_map/ppermute | solution.py:588
  218.5 37.0 %collective-permute-start.25 = (bf16[4,112,800]{2,1,0:T(8,128)(2,1)}, bf16[4,112,800]{2,1,0:T(8,128)(2,1)S(1)}, u32[]{:S(2)}, u32[]{:S(2)}) collective-permute-start(bf16[4,112,800]{2,1,0:T(8,128)(2,1)} %get-tuple-element.208.refs_0_), channel_id=1, source_target_pairs={{0,16},{8,24},{16,0},{24,8},{1,17},{9,25},{17,1},{25,9},{2,18},{10... | collective-permute-start | bytes 2150408 | tf_op jit(solution)/shard_map/ppermute | solution.py:588
  219.9 35.6 %collective-permute-start.26 = (bf16[4,112,800]{2,1,0:T(8,128)(2,1)}, bf16[4,112,800]{2,1,0:T(8,128)(2,1)S(1)}, u32[]{:S(2)}, u32[]{:S(2)}) collective-permute-start(bf16[4,112,800]{2,1,0:T(8,128)(2,1)} %get-tuple-element.208.refs_0_), channel_id=1, source_target_pairs={{0,24},{8,16},{16,8},{24,0},{1,25},{9,17},{17,9},{25,1},{2,26},{10... | collective-permute-start | bytes 2150408 | tf_op jit(solution)/shard_map/ppermute | solution.py:588
  315.1 19.1 %collective-permute-start.28 = (bf16[800,1600]{1,0:T(8,128)(2,1)}, bf16[800,1600]{1,0:T(8,128)(2,1)S(1)}, u32[]{:S(2)}, u32[]{:S(2)}) collective-permute-start(bf16[800,1600]{1,0:T(8,128)(2,1)} %get-tuple-element.221), channel_id=1, source_target_pairs={{0,4},{4,0},{1,5},{5,1},{2,6},{6,2},{3,7},{7,3},{8,12},{12,8},{9,1... | collective-permute-start | bytes 7680008 | tf_op jit(solution)/shard_map/ppermute | solution.py:573
  315.1 192.2 %reduce-scatter.9.cloned.1.call-start = ((), (), s32[]{:S(2)}) async-start(), calls=%async_computation.8 | async-start | bytes 4096000 | tf_op jit(solution)/shard_map/reduce_scatter | solution.py:1035
  343.4 20.7 %collective-permute-start.30 = (bf16[2,104,1600]{2,1,0:T(8,128)(2,1)}, bf16[2,104,1600]{2,1,0:T(8,128)(2,1)}, u32[]{:S(2)}, u32[]{:S(2)}) collective-permute-start(bf16[2,104,1600]{2,1,0:T(8,128)(2,1)} %get-tuple-element.233), channel_id=1, source_target_pairs={{0,8},{8,0},{16,24},{24,16},{1,9},{9,1},{17,25},{25,17},{2,10},{10... | collective-permute-start | bytes 1996808 | tf_op jit(solution)/shard_map/ppermute | solution.py:588
  362.5 18.9 %collective-permute-start.31 = (bf16[4,104,800]{2,1,0:T(8,128)(2,1)}, bf16[4,104,800]{2,1,0:T(8,128)(2,1)S(1)}, u32[]{:S(2)}, u32[]{:S(2)}) collective-permute-start(bf16[4,104,800]{2,1,0:T(8,128)(2,1)} %get-tuple-element.234), channel_id=1, source_target_pairs={{0,16},{8,24},{16,0},{24,8},{1,17},{9,25},{17,1},{25,9},{2,18},{10... | collective-permute-start | bytes 1996808 | tf_op jit(solution)/shard_map/ppermute | solution.py:588
  401.1 20.0 %collective-permute-start.37 = (bf16[2,104,1600]{2,1,0:T(8,128)(2,1)}, bf16[2,104,1600]{2,1,0:T(8,128)(2,1)}, u32[]{:S(2)}, u32[]{:S(2)}) collective-permute-start(bf16[2,104,1600]{2,1,0:T(8,128)(2,1)} %get-tuple-element.252), channel_id=1, source_target_pairs={{0,16},{8,24},{16,0},{24,8},{1,17},{9,25},{17,1},{25,9},{2,18},{10... | collective-permute-start | bytes 1996808 | tf_op jit(solution)/shard_map/ppermute | solution.py:588
  402.6 18.4 %collective-permute-start.38 = (bf16[4,104,800]{2,1,0:T(8,128)(2,1)}, bf16[4,104,800]{2,1,0:T(8,128)(2,1)}, u32[]{:S(2)}, u32[]{:S(2)}) collective-permute-start(bf16[4,104,800]{2,1,0:T(8,128)(2,1)} %get-tuple-element.253), channel_id=1, source_target_pairs={{0,8},{8,0},{16,24},{24,16},{1,9},{9,1},{17,25},{25,17},{2,10},{10... | collective-permute-start | bytes 1996808 | tf_op jit(solution)/shard_map/ppermute | solution.py:588
  426.8 127.4 %reduce-scatter.13.cloned.1.call-start = ((), (), s32[]{:S(2)}) async-start(), calls=%async_computation.10 | async-start | bytes 931840
  437.1 35.1 %collective-permute-start.43 = (bf16[2,4,104,800]{3,2,1,0:T(8,128)(2,1)}, bf16[2,4,104,800]{3,2,1,0:T(8,128)(2,1)}, u32[]{:S(2)}, u32[]{:S(2)}) collective-permute-start(bf16[2,4,104,800]{3,2,1,0:T(8,128)(2,1)} %get-tuple-element.270), channel_id=1, source_target_pairs={{0,8},{8,0},{16,24},{24,16},{1,9},{9,1},{17,25},{25,17},{2,10},{10... | collective-permute-start | bytes 3993608 | tf_op jit(solution)/shard_map/ppermute | solution.py:588
  437.5 34.7 %collective-permute-start.44 = (bf16[2,104,1600]{2,1,0:T(8,128)(2,1)}, bf16[2,104,1600]{2,1,0:T(8,128)(2,1)}, u32[]{:S(2)}, u32[]{:S(2)}) collective-permute-start(bf16[2,104,1600]{2,1,0:T(8,128)(2,1)} %get-tuple-element.271.refs_6_), channel_id=1, source_target_pairs={{0,16},{8,24},{16,0},{24,8},{1,17},{9,25},{17,1},{25,9},{2,18},{10... | collective-permute-start | bytes 1996808 | tf_op jit(solution)/shard_map/ppermute | solution.py:588
  438.9 33.2 %collective-permute-start.41 = (bf16[104,800]{1,0:T(8,128)(2,1)S(1)}, bf16[104,800]{1,0:T(8,128)(2,1)S(1)}, u32[]{:S(2)}, u32[]{:S(2)}) collective-permute-start(bf16[104,800]{1,0:T(8,128)(2,1)S(1)} %get-tuple-element.401), channel_id=1, source_target_pairs={{0,0},{4,1},{1,2},{5,3},{2,4},{6,5},{3,6},{7,7},{8,8},{12,9},{9,10... | collective-permute-start | bytes 499208 | tf_op jit(solution)/shard_map/ppermute | solution.py:861
  439.6 32.5 %collective-permute-start.42 = (bf16[104,800]{1,0:T(8,128)(2,1)S(1)}, bf16[104,800]{1,0:T(8,128)(2,1)S(1)}, u32[]{:S(2)}, u32[]{:S(2)}) collective-permute-start(bf16[104,800]{1,0:T(8,128)(2,1)S(1)} %get-tuple-element.400), channel_id=1, source_target_pairs={{5,0},{0,1},{4,2},{1,3},{7,4},{2,5},{6,6},{3,7},{13,8},{8,9},{12,1... | collective-permute-start | bytes 499208 | tf_op jit(solution)/shard_map/ppermute | solution.py:861
  474.2 26.1 %collective-permute-start.46 = (bf16[104,800]{1,0:T(8,128)(2,1)S(1)}, bf16[104,800]{1,0:T(8,128)(2,1)S(1)}, u32[]{:S(2)}, u32[]{:S(2)}) collective-permute-start(bf16[104,800]{1,0:T(8,128)(2,1)S(1)} %get-tuple-element.399), channel_id=1, source_target_pairs={{1,0},{5,1},{0,2},{4,3},{3,4},{7,5},{2,6},{6,7},{9,8},{13,9},{8,10... | collective-permute-start | bytes 499208 | tf_op jit(solution)/shard_map/ppermute | solution.py:861
  480.0 20.3 %collective-permute-start.47 = (bf16[104,800]{1,0:T(8,128)(2,1)S(1)}, bf16[104,800]{1,0:T(8,128)(2,1)S(1)}, u32[]{:S(2)}, u32[]{:S(2)}) collective-permute-start(bf16[104,800]{1,0:T(8,128)(2,1)S(1)} %get-tuple-element.398), channel_id=1, source_target_pairs={{4,0},{1,1},{5,2},{0,3},{6,4},{3,5},{7,6},{2,7},{12,8},{9,9},{13,1... | collective-permute-start | bytes 499208 | tf_op jit(solution)/shard_map/ppermute | solution.py:861
  482.1 25.2 %collective-permute-start.48 = (bf16[2,104,1600]{2,1,0:T(8,128)(2,1)}, bf16[2,104,1600]{2,1,0:T(8,128)(2,1)}, u32[]{:S(2)}, u32[]{:S(2)}) collective-permute-start(bf16[2,104,1600]{2,1,0:T(8,128)(2,1)} %get-tuple-element.283), channel_id=1, source_target_pairs={{0,8},{8,0},{16,24},{24,16},{1,9},{9,1},{17,25},{25,17},{2,10},{10... | collective-permute-start | bytes 1996808 | tf_op jit(solution)/shard_map/ppermute | solution.py:588
  486.0 19.0 %collective-permute-start.49 = (bf16[4,104,800]{2,1,0:T(8,128)(2,1)}, bf16[4,104,800]{2,1,0:T(8,128)(2,1)S(1)}, u32[]{:S(2)}, u32[]{:S(2)}) collective-permute-start(bf16[4,104,800]{2,1,0:T(8,128)(2,1)} %fusion.11), channel_id=1, source_target_pairs={{0,16},{8,24},{16,0},{24,8},{1,17},{9,25},{17,1},{25,9},{2,18},{10... | collective-permute-start | bytes 1996808 | tf_op jit(solution)/shard_map/ppermute | solution.py:588
  507.3 19.3 %collective-permute-start.51 = (bf16[4,104,800]{2,1,0:T(8,128)(2,1)}, bf16[4,104,800]{2,1,0:T(8,128)(2,1)S(1)}, u32[]{:S(2)}, u32[]{:S(2)}) collective-permute-start(bf16[4,104,800]{2,1,0:T(8,128)(2,1)} %get-tuple-element.286.refs_0_), channel_id=1, source_target_pairs={{0,8},{8,0},{16,24},{24,16},{1,9},{9,1},{17,25},{25,17},{2,10},{10... | collective-permute-start | bytes 1996808 | tf_op jit(solution)/shard_map/ppermute | solution.py:588
  507.9 19.1 %collective-permute-start.52 = (bf16[4,104,800]{2,1,0:T(8,128)(2,1)}, bf16[4,104,800]{2,1,0:T(8,128)(2,1)}, u32[]{:S(2)}, u32[]{:S(2)}) collective-permute-start(bf16[4,104,800]{2,1,0:T(8,128)(2,1)} %get-tuple-element.286.refs_0_), channel_id=1, source_target_pairs={{0,16},{8,24},{16,0},{24,8},{1,17},{9,25},{17,1},{25,9},{2,18},{10... | collective-permute-start | bytes 1996808 | tf_op jit(solution)/shard_map/ppermute | solution.py:588
  527.5 95.1 %reduce-scatter.11.cloned.1.call-start = ((), (), s32[]{:S(2)}) async-start(), calls=%async_computation.9 | async-start | bytes 4259840 | tf_op jit(solution)/shard_map/reduce_scatter | solution.py:1096
  527.6 22.8 %collective-permute-start.56 = (bf16[3,48,800]{2,1,0:T(8,128)(2,1)}, bf16[3,48,800]{2,1,0:T(8,128)(2,1)S(1)}, u32[]{:S(2)}, u32[]{:S(2)}) collective-permute-start(bf16[3,48,800]{2,1,0:T(8,128)(2,1)} %get-tuple-element.299), channel_id=1, source_target_pairs={{1,0},{2,1},{3,2},{5,4},{6,5},{7,6},{9,8},{10,9},{11,10},{13,12},{... | collective-permute-start | bytes 691208 | tf_op jit(solution)/shard_map/ppermute | solution.py:716
  528.9 21.5 %collective-permute-start.55 = (bf16[3,48,800]{2,1,0:T(8,128)(2,1)}, bf16[3,48,800]{2,1,0:T(8,128)(2,1)S(1)}, u32[]{:S(2)}, u32[]{:S(2)}) collective-permute-start(bf16[3,48,800]{2,1,0:T(8,128)(2,1)} %get-tuple-element.298), channel_id=1, source_target_pairs={{0,1},{1,2},{2,3},{4,5},{5,6},{6,7},{8,9},{9,10},{10,11},{12,13},{... | collective-permute-start | bytes 691208 | tf_op jit(solution)/shard_map/ppermute | solution.py:712
  533.8 19.4 %collective-permute-start.54 = (bf16[2,104,1600]{2,1,0:T(8,128)(2,1)}, bf16[2,104,1600]{2,1,0:T(8,128)(2,1)S(1)}, u32[]{:S(2)}, u32[]{:S(2)}) collective-permute-start(bf16[2,104,1600]{2,1,0:T(8,128)(2,1)} %get-tuple-element.295), channel_id=1, source_target_pairs={{0,16},{8,24},{16,0},{24,8},{1,17},{9,25},{17,1},{25,9},{2,18},{10... | collective-permute-start | bytes 1996808 | tf_op jit(solution)/shard_map/ppermute | solution.py:588
  555.8 30.8 %collective-permute-start.59 = (bf16[3,104,800]{2,1,0:T(8,128)(2,1)}, bf16[3,104,800]{2,1,0:T(8,128)(2,1)}, u32[]{:S(2)}, u32[]{:S(2)}) collective-permute-start(bf16[3,104,800]{2,1,0:T(8,128)(2,1)} %get-tuple-element.306.refs_7_), channel_id=1, source_target_pairs={{0,24},{8,16},{16,8},{24,0},{1,25},{9,17},{17,9},{25,1},{2,26},{10... | collective-permute-start | bytes 1497608 | tf_op jit(solution)/shard_map/ppermute | solution.py:588
  557.9 28.8 %collective-permute-start.58 = (bf16[3,104,800]{2,1,0:T(8,128)(2,1)}, bf16[3,104,800]{2,1,0:T(8,128)(2,1)}, u32[]{:S(2)}, u32[]{:S(2)}) collective-permute-start(bf16[3,104,800]{2,1,0:T(8,128)(2,1)} %get-tuple-element.305.refs_6_), channel_id=1, source_target_pairs={{0,16},{8,24},{16,0},{24,8},{1,17},{9,25},{17,1},{25,9},{2,18},{10... | collective-permute-start | bytes 1497608 | tf_op jit(solution)/shard_map/ppermute | solution.py:588
  558.3 28.3 %collective-permute-start.57 = (bf16[3,104,800]{2,1,0:T(8,128)(2,1)}, bf16[3,104,800]{2,1,0:T(8,128)(2,1)}, u32[]{:S(2)}, u32[]{:S(2)}) collective-permute-start(bf16[3,104,800]{2,1,0:T(8,128)(2,1)} %get-tuple-element.304.refs_5_), channel_id=1, source_target_pairs={{0,8},{8,0},{16,24},{24,16},{1,9},{9,1},{17,25},{25,17},{2,10},{10... | collective-permute-start | bytes 1497608 | tf_op jit(solution)/shard_map/ppermute | solution.py:588
  562.7 26.7 %collective-permute-start.63 = (bf16[1,104,800]{2,1,0:T(8,128)(2,1)}, bf16[1,104,800]{2,1,0:T(8,128)(2,1)S(1)}, u32[]{:S(2)}, u32[]{:S(2)}) collective-permute-start(bf16[1,104,800]{2,1,0:T(8,128)(2,1)} %get-tuple-element.314), channel_id=1, source_target_pairs={{0,8},{8,0},{16,24},{24,16},{1,9},{9,1},{17,25},{25,17},{2,10},{10... | collective-permute-start | bytes 499208 | tf_op jit(solution)/shard_map/ppermute | solution.py:588
  592.2 33.7 %collective-permute-start.66 = (bf16[324,800]{1,0:T(8,128)(2,1)}, bf16[324,800]{1,0:T(8,128)(2,1)S(1)}, u32[]{:S(2)}, u32[]{:S(2)}) collective-permute-start(bf16[324,800]{1,0:T(8,128)(2,1)} %get-tuple-element.318.refs_0_), channel_id=1, source_target_pairs={{0,8},{8,0},{16,24},{24,16},{1,9},{9,1},{17,25},{25,17},{2,10},{10... | collective-permute-start | bytes 1555208 | tf_op jit(solution)/shard_map/ppermute | solution.py:588
  593.5 32.5 %collective-permute-start.67 = (bf16[324,800]{1,0:T(8,128)(2,1)}, bf16[324,800]{1,0:T(8,128)(2,1)S(1)}, u32[]{:S(2)}, u32[]{:S(2)}) collective-permute-start(bf16[324,800]{1,0:T(8,128)(2,1)} %get-tuple-element.318.refs_0_), channel_id=1, source_target_pairs={{0,16},{8,24},{16,0},{24,8},{1,17},{9,25},{17,1},{25,9},{2,18},{10... | collective-permute-start | bytes 1555208 | tf_op jit(solution)/shard_map/ppermute | solution.py:588
  594.6 31.4 %collective-permute-start.68 = (bf16[324,800]{1,0:T(8,128)(2,1)}, bf16[324,800]{1,0:T(8,128)(2,1)S(1)}, u32[]{:S(2)}, u32[]{:S(2)}) collective-permute-start(bf16[324,800]{1,0:T(8,128)(2,1)} %get-tuple-element.318.refs_0_), channel_id=1, source_target_pairs={{0,24},{8,16},{16,8},{24,0},{1,25},{9,17},{17,9},{25,1},{2,26},{10... | collective-permute-start | bytes 1555208 | tf_op jit(solution)/shard_map/ppermute | solution.py:588
  595.7 30.2 %collective-permute-start.65 = (bf16[1,104,800]{2,1,0:T(8,128)(2,1)}, bf16[1,104,800]{2,1,0:T(8,128)(2,1)S(1)}, u32[]{:S(2)}, u32[]{:S(2)}) collective-permute-start(bf16[1,104,800]{2,1,0:T(8,128)(2,1)} %get-tuple-element.319.refs_0_), channel_id=1, source_target_pairs={{0,16},{8,24},{16,0},{24,8},{1,17},{9,25},{17,1},{25,9},{2,18},{10... | collective-permute-start | bytes 499208 | tf_op jit(solution)/shard_map/ppermute | solution.py:588
  (102 other events, 942.8 us)
Sparse Core Ops, SparseCore 0:
  17.7 69.2 all-gather.3
  93.4 70.3 all-gather.5
  216.5 63.9 all-gather.7
  315.2 60.6 reduce-scatter.6
  426.9 74.8 reduce-scatter.8
  527.6 26.5 reduce-scatter.12
  557.2 65.3 reduce-scatter.10
